TPU v7x, 32 devices: a whole 2x2x4 slice. The times are simulated.
32 devices in a mesh: seq: 4 (over z), dp: 8 (over y, x, core).
Axes of the slice: x: 2, y: 2, z: 4, core: 2. Of those that a mesh axis runs over, the one named last changes fastest.
Arguments:
- block_input: bfloat16 [8, 2048, 1536], P('dp', 'seq'), may hold values from -6 to 6
- document_number: int32 [8, 2048], P('dp', 'seq'), may hold values from 0 to 3, never falling along the last dimension, each value on 1 to 1024 neighbouring positions
- key_present: int32 [8, 2048], P('dp', 'seq'), may hold values 0 or 1
- routes: int32 [8, 2048, 6], P('dp', 'seq'), may hold values from 0 to 15, all different within a row; in each aligned block of 512 rows (0 to 511, 512 to 1023, ..., all dimensions but the last counted through in order) at most 256 rows name the same one
- sequence_adapter: int32 [8], P('dp'), may hold values from 0 to 7
- output_gradient: bfloat16 [8, 2048, 1536], P('dp', 'seq'), may hold values from -6 to 6
- norm_scale_pair: bfloat16 [2, 1536], P(None, ('seq', 'dp')), may hold values from 0.5 to 1.5
- query_key_value_weight: bfloat16 [1536, 2560], P(('seq', 'dp')), may hold values from -0.15625 to 0.15625
- attention_output_weight: bfloat16 [1536, 1536], P(('seq', 'dp')), may hold values from -0.625 to 0.625
- router_weight: bfloat16 [1536, 16], P(('seq', 'dp')), may hold values from -0.078125 to 0.078125
- shared_gate_up_weight: bfloat16 [1536, 2, 1024], P(('seq', 'dp')), may hold values from -0.15625 to 0.15625
- shared_down_weight: bfloat16 [1024, 1536], P(('seq', 'dp')), may hold values from -0.375 to 0.375
- routed_gate_up_weight: bfloat16 [16, 1536, 2, 512], P('dp', 'seq'), may hold values from -0.15625 to 0.15625
- routed_down_weight: bfloat16 [16, 512, 1536], P('dp', 'seq'), may hold values from -1 to 1
- dense_first_factor: bfloat16 [1536, 6, 128], P(('seq', 'dp')), may hold values from -0.15625 to 0.15625
- shared_down_first_factor: bfloat16 [1024, 128], P(('seq', 'dp')), may hold values from -0.1875 to 0.1875
- dense_second_factor: bfloat16 [128, 7680], P(None, ('seq', 'dp')), may hold values from -0.75 to 0.75
- routed_first_factor: bfloat16 [16, 1536, 2, 128], P('dp', 'seq'), may hold values from -0.15625 to 0.15625
- routed_down_first_factor: bfloat16 [16, 512, 128], P('dp', 'seq'), may hold values from -0.25 to 0.25
- routed_second_factor: bfloat16 [16, 128, 2560], P('dp', None, 'seq'), may hold values from -0.75 to 0.75
Outputs:
- hidden_out: bfloat16 [8, 2048, 1536], P('dp', 'seq')
- grad_hidden: float32 [8, 2048, 1536], P('dp', 'seq')
- gradient_first_factor: float32 [1536, 6, 128], P(('seq', 'dp'))
- gradient_shared_down_factor: float32 [1024, 128], P(('seq', 'dp'))
- gradient_second_factor: float32 [128, 7680], P(None, ('seq', 'dp'))
- grad_expert_lora_a: float32 [16, 1536, 2, 128], P('dp', 'seq')
- grad_expert_lora_a_down: float32 [16, 512, 128], P('dp', 'seq')
- grad_expert_lora_b: float32 [16, 128, 2560], P('dp', None, 'seq')
Inputs may be any that keep to these rules, and one draw needn't show every extreme that they name: `routes`: in each aligned block of 512 positions of a sequence, every expert is named by at most 256 tokens; each token names 6 different experts. `document_number`: never falling along a sequence; a document spans at most 1024 positions.
All inputs are finite; a program needn't handle non-finite values. No bound on the sum of `key_present` on one device may be relied on, other than what follows from the above.
Results may differ from a plain program's by a relative error of at most 0.022.
Values may be sent and summed in bfloat16 or wider, within the bound.
No kernel may reach another device: no remote copies, remote signals or barrier semaphores. Data moves between devices by JAX's collectives and lax.ppermute only.
A program may use at most 384 MiB of HBM per device.

v0:
```python
import math

import jax
import jax.numpy as jnp
from jax import lax
from jax.sharding import PartitionSpec as P

HEADS = 12
KV_HEADS = 4
HEAD_DIM = 128
EXPERT_HIDDEN = 512
SHARED_HIDDEN = 1024
ADAPTER_RANK = 16


EPSILON = 1e-05
MASKED_SCORE = -1e30


def matmul(left, right):
    return jnp.dot(left, right, preferred_element_type=jnp.float32)


def matmul_tn(left, right):
    return jnp.einsum("ri,rj->ij", left, right, preferred_element_type=jnp.float32)


def matmul_nt(left, right):
    return jnp.einsum("ri,ji->rj", left, right, preferred_element_type=jnp.float32)


def rms_norm(values, gain):
    return values * lax.rsqrt(jnp.mean(values * values, axis=-1, keepdims=True) + EPSILON) * gain


def swiglu(gate_up):
    half_width = gate_up.shape[-1] // 2
    return jax.nn.silu(gate_up[:, :half_width]) * gate_up[:, half_width:]


def split_columns(matrix, widths):
    parts_list = []
    offset = 0
    for span_width in widths:
        parts_list.append(matrix[:, offset : offset + span_width])
        offset += span_width
    return parts_list


def pick_rows(matrix, indices):
    return matrix[indices]


def adapter_low(inputs, a_cols, select):
    row_count = inputs.shape[0]
    group_count, rank_width = (a_cols.shape[1], a_cols.shape[2])
    low_rank = matmul(inputs, a_cols.reshape(a_cols.shape[0], group_count * rank_width))
    low_rank = low_rank.reshape(row_count, group_count, rank_width) * select[:, None, :]
    return low_rank.astype(jnp.bfloat16)


def adapter_fwd(inputs, a_cols, b_parts, select):
    low_round = adapter_low(inputs, a_cols, select)
    extra_out = jnp.concatenate(
        [matmul(low_round[:, g], b_parts[g]) for g in range(len(b_parts))], axis=1
    )
    return (extra_out, low_round)


def adapter_bwd(inputs, a_cols, b_parts, select, low_round, grad_out):
    group_count, rank_width = (a_cols.shape[1], a_cols.shape[2])
    offset = 0
    grad_lows = []
    grad_seconds = []
    for g in range(group_count):
        col_span = b_parts[g].shape[1]
        grad_part = grad_out[:, offset : offset + col_span]
        grad_seconds.append(matmul_tn(low_round[:, g], grad_part))
        grad_lows.append(matmul_nt(grad_part, b_parts[g]))
        offset += col_span
    grad_low = (jnp.stack(grad_lows, axis=1) * select[:, None, :]).astype(jnp.bfloat16)
    grad_first = jnp.einsum("ri,rnl->inl", inputs, grad_low, preferred_element_type=jnp.float32)
    grad_inputs = matmul_nt(
        grad_low.reshape(grad_low.shape[0], group_count * rank_width),
        a_cols.reshape(a_cols.shape[0], group_count * rank_width),
    )
    return (grad_inputs, grad_first, grad_seconds)


def allowed_pairs(query_pos, key_pos, query_tags, key_tags):
    causal = key_pos[None, :] <= query_pos[:, None]
    itself = key_pos[None, :] == query_pos[:, None]
    same_doc = key_tags.astype(jnp.float32)[:, None, :] == query_tags[:, :, None]
    return causal[None] & (same_doc | itself[None])


def per_device(
    block_input,
    document_number,
    key_present,
    routes,
    sequence_adapter,
    output_gradient,
    norm_scale_pair,
    query_key_value_weight,
    attention_output_weight,
    router_weight,
    shared_gate_up_weight,
    shared_down_weight,
    routed_gate_up_weight,
    routed_down_weight,
    dense_first_factor,
    shared_down_first_factor,
    dense_second_factor,
    routed_first_factor,
    routed_down_first_factor,
    routed_second_factor,
):
    sequence_batch, token_block, model = block_input.shape
    topk = routes.shape[2]
    total_row_count = sequence_batch * token_block
    adapter_span_width = dense_second_factor.shape[0]
    experts = router_weight.shape[1]
    local_experts = routed_gate_up_weight.shape[0]
    adapter_row_count = experts // local_experts
    expert_capacity = 4 * topk * token_block // (3 * experts)
    query_width = HEADS * HEAD_DIM
    kv_width = KV_HEADS * HEAD_DIM
    groups = HEADS // KV_HEADS
    scale = HEAD_DIM ** (-0.5)

    def dense_gather():
        return (
            lax.all_gather(norm_scale_pair, ("seq", "dp"), axis=1, tiled=True),
            lax.all_gather(query_key_value_weight, ("seq", "dp"), axis=0, tiled=True),
            lax.all_gather(attention_output_weight, ("seq", "dp"), axis=0, tiled=True),
            lax.all_gather(router_weight, ("seq", "dp"), axis=0, tiled=True),
            lax.all_gather(shared_gate_up_weight, ("seq", "dp"), axis=0, tiled=True),
            lax.all_gather(shared_down_weight, ("seq", "dp"), axis=0, tiled=True),
            lax.all_gather(dense_first_factor, ("seq", "dp"), axis=0, tiled=True),
            lax.all_gather(shared_down_first_factor, ("seq", "dp"), axis=0, tiled=True),
            lax.all_gather(dense_second_factor, ("seq", "dp"), axis=1, tiled=True),
        )

    def expert_gather():
        return (
            lax.all_gather(routed_gate_up_weight, "seq", axis=1, tiled=True),
            lax.all_gather(routed_down_weight, "seq", axis=1, tiled=True),
            lax.all_gather(routed_first_factor, "seq", axis=1, tiled=True),
            lax.all_gather(routed_down_first_factor, "seq", axis=1, tiled=True),
            lax.all_gather(routed_second_factor, "seq", axis=2, tiled=True),
        )

    column_adapter = jnp.arange(adapter_span_width, dtype=jnp.int32) // ADAPTER_RANK
    sequence_picker = (column_adapter[None, :] == sequence_adapter[:, None]).astype(jnp.float32)
    picked_rows = jnp.broadcast_to(
        sequence_picker[:, None, :], (sequence_batch, token_block, adapter_span_width)
    ).reshape(total_row_count, adapter_span_width)
    dense_fwd = dense_gather()
    expert_fwd = expert_gather()
    gains_all, qkv_w, out_w, router_w, sgu_w, sdown_w, first_all, first_down, second_all = dense_fwd
    b_parts = split_columns(
        second_all, [query_width, kv_width, kv_width, model, SHARED_HIDDEN, SHARED_HIDDEN, model]
    )
    gains = gains_all.astype(jnp.float32)
    x_flat = block_input.reshape(total_row_count, model).astype(jnp.float32)
    normed = rms_norm(x_flat, gains[0]).astype(jnp.bfloat16)
    qkv_extra, qkv_low = adapter_fwd(normed, first_all[:, 0:3], b_parts[0:3], picked_rows)
    qkv_b = (matmul(normed, qkv_w) + qkv_extra).astype(jnp.bfloat16)
    query = qkv_b[:, :query_width].reshape(sequence_batch, token_block, KV_HEADS, groups, HEAD_DIM)
    keys = qkv_b[:, query_width : query_width + kv_width].reshape(
        sequence_batch, token_block, KV_HEADS, HEAD_DIM
    )
    values = qkv_b[:, query_width + kv_width :].reshape(
        sequence_batch, token_block, KV_HEADS, HEAD_DIM
    )
    key_tags = jnp.where(key_present == 1, document_number, -1).astype(jnp.bfloat16)
    query_tags = document_number.astype(jnp.float32)
    query_pos = lax.axis_index("seq") * token_block + jnp.arange(token_block, dtype=jnp.int32)
    stat_shape = (sequence_batch, KV_HEADS, groups, token_block)
    start_state = (
        jnp.full(stat_shape, MASKED_SCORE, jnp.float32),
        jnp.zeros(stat_shape, jnp.float32),
        jnp.zeros(stat_shape + (HEAD_DIM,), jnp.float32),
    )
    key_part = lax.all_gather(keys, "seq", axis=1, tiled=True)
    value_part = lax.all_gather(values, "seq", axis=1, tiled=True)
    tag_part = lax.all_gather(key_tags, "seq", axis=1, tiled=True)
    span_len = key_part.shape[1]
    sub_len = math.gcd(span_len, 512)

    def step(i, state):
        run_max, run_sum, accum = state
        offset = i * sub_len
        key_blk = lax.dynamic_slice_in_dim(key_part, offset, sub_len, 1)
        value_blk = lax.dynamic_slice_in_dim(value_part, offset, sub_len, 1)
        tag_blk = lax.dynamic_slice_in_dim(tag_part, offset, sub_len, 1)
        scores = (
            jnp.einsum("sqkgd,spkd->skgqp", query, key_blk, preferred_element_type=jnp.float32)
            * scale
        )
        permit = allowed_pairs(
            query_pos, offset + jnp.arange(sub_len, dtype=jnp.int32), query_tags, tag_blk
        )
        scores = jnp.where(permit[:, None, None], scores, MASKED_SCORE)
        new_max = jnp.maximum(run_max, jnp.max(scores, axis=-1))
        weights = jnp.exp(scores - new_max[..., None])
        decay = jnp.exp(run_max - new_max)
        run_sum = decay * run_sum + jnp.sum(weights, axis=-1)
        accum = decay[..., None] * accum + jnp.einsum(
            "skgqp,spkd->skgqd",
            weights.astype(jnp.bfloat16),
            value_blk,
            preferred_element_type=jnp.float32,
        )
        return (new_max, run_sum, accum)

    run_max, run_sum, accum = lax.fori_loop(0, span_len // sub_len, step, start_state)
    attn_f = accum / run_sum[..., None]
    log_total = run_max + jnp.log(run_sum)
    attn_b = (
        attn_f.transpose(0, 3, 1, 2, 4).reshape(total_row_count, query_width).astype(jnp.bfloat16)
    )
    out_extra, out_low = adapter_fwd(attn_b, first_all[:, 3:4], b_parts[3:4], picked_rows)
    mid = x_flat + matmul(attn_b, out_w) + out_extra
    normed2 = rms_norm(mid, gains[1]).astype(jnp.bfloat16)
    logits = matmul(normed2, router_w)
    route_flat = routes.reshape(total_row_count, topk)
    route_hot = (route_flat[..., None] == jnp.arange(experts, dtype=jnp.int32)).astype(jnp.float32)
    chosen = jnp.sum(route_hot * logits[:, None, :], axis=-1)
    gates = jax.nn.softmax(chosen, axis=-1)
    shared_extra, shared_low = adapter_fwd(normed2, first_all[:, 4:6], b_parts[4:6], picked_rows)
    shared_gu = matmul(normed2, sgu_w.reshape(model, 2 * SHARED_HIDDEN)) + shared_extra
    shared_hidden = swiglu(shared_gu).astype(jnp.bfloat16)
    sdown_extra, sdown_low = adapter_fwd(
        shared_hidden, first_down[:, None], b_parts[6:7], picked_rows
    )
    y_shared = matmul(shared_hidden, sdown_w) + sdown_extra
    hits = (routes[..., None] == jnp.arange(experts, dtype=jnp.int32)).astype(jnp.int32)
    flags = jnp.sum(hits, axis=2)
    ranks = jnp.cumsum(flags, axis=1) - flags
    slot_ids = jnp.sum(hits * ranks[:, :, None, :], axis=3)
    dest = routes * expert_capacity + slot_ids
    pair_ids = jnp.arange(token_block * topk, dtype=jnp.int32).reshape(1, token_block, topk)
    table = (
        jnp.full((sequence_batch, experts * expert_capacity), token_block * topk, jnp.int32)
        .at[jnp.arange(sequence_batch, dtype=jnp.int32)[:, None, None], dest]
        .set(pair_ids)
    )
    dest_flat = dest.reshape(sequence_batch, token_block * topk)
    padded = jnp.concatenate(
        [
            normed2.reshape(sequence_batch, token_block, model),
            jnp.zeros((sequence_batch, 1, model), jnp.bfloat16),
        ],
        axis=1,
    )
    send_rows = jax.vmap(pick_rows)(padded, table // topk).reshape(
        sequence_batch, experts, expert_capacity, model
    )
    send_tags = jnp.broadcast_to(sequence_adapter[:, None], (sequence_batch, experts)).astype(
        jnp.bfloat16
    )
    recv_rows, recv_tags = (
        lax.all_to_all(send_rows, "dp", split_axis=1, concat_axis=1, tiled=True),
        lax.all_to_all(send_tags, "dp", split_axis=1, concat_axis=1, tiled=True),
    )
    tag_grid = recv_tags.reshape(sequence_batch, adapter_row_count, local_experts).astype(
        jnp.float32
    )
    adapter_row_list = sequence_batch * adapter_row_count * expert_capacity

    def local_rows(grid, j):
        return grid.reshape(
            sequence_batch, adapter_row_count, local_experts, expert_capacity, model
        )[:, :, j].reshape(adapter_row_list, model)

    def local_select(j):
        picked_columns = (
            tag_grid[:, :, j][..., None] == column_adapter.astype(jnp.float32)
        ).astype(jnp.float32)
        return jnp.broadcast_to(
            picked_columns[:, :, None, :],
            (sequence_batch, adapter_row_count, expert_capacity, adapter_span_width),
        ).reshape(adapter_row_list, adapter_span_width)

    def expert_front(weights_set, j, inputs, select):
        egu_all, edown_all, ea_all, ead_all, eb_all = weights_set
        gate_up_w = egu_all[j].reshape(model, 2 * EXPERT_HIDDEN)
        gu_parts = [eb_all[j][:, :EXPERT_HIDDEN], eb_all[j][:, EXPERT_HIDDEN : 2 * EXPERT_HIDDEN]]
        gu_extra, gu_low = adapter_fwd(inputs, ea_all[j], gu_parts, select)
        gate_up = matmul(inputs, gate_up_w) + gu_extra
        return (gate_up, gu_low, swiglu(gate_up).astype(jnp.bfloat16))

    expert_outs = []
    for j in range(local_experts):
        inputs_j = local_rows(recv_rows, j)
        select_j = local_select(j)
        gate_up, gu_low, hidden = expert_front(expert_fwd, j, inputs_j, select_j)
        dn_extra, dn_low = adapter_fwd(
            hidden, expert_fwd[3][j][:, None], [expert_fwd[4][j][:, 2 * EXPERT_HIDDEN :]], select_j
        )
        output = (matmul(hidden, expert_fwd[1][j]) + dn_extra).astype(jnp.bfloat16)
        expert_outs.append(
            output.reshape(sequence_batch, adapter_row_count, expert_capacity, model)
        )
    out_grid = jnp.stack(expert_outs, axis=2).reshape(
        sequence_batch, experts, expert_capacity, model
    )
    back_rows = lax.all_to_all(out_grid, "dp", split_axis=1, concat_axis=1, tiled=True)
    taken = jax.vmap(pick_rows)(
        back_rows.reshape(sequence_batch, experts * expert_capacity, model), dest_flat
    )
    taken = taken.reshape(total_row_count, topk, model)
    moe = jnp.sum(gates[..., None] * taken.astype(jnp.float32), axis=1)
    hidden_out = (
        (mid + moe + y_shared).astype(jnp.bfloat16).reshape(sequence_batch, token_block, model)
    )
    dense_bwd = dense_gather()
    expert_bwd = expert_gather()
    gains_all, qkv_w, out_w, router_w, sgu_w, sdown_w, first_all, first_down, second_all = dense_bwd
    b_parts = split_columns(
        second_all, [query_width, kv_width, kv_width, model, SHARED_HIDDEN, SHARED_HIDDEN, model]
    )
    grad_out = output_gradient.reshape(total_row_count, model).astype(jnp.float32)
    grad_ys = grad_out.astype(jnp.bfloat16)
    grad_sh_a, gradient_down_factor, grad_b_sdown = adapter_bwd(
        shared_hidden, first_down[:, None], b_parts[6:7], picked_rows, sdown_low, grad_ys
    )
    grad_shared_hidden = grad_sh_a + matmul_nt(grad_ys, sdown_w)
    _, swiglu_back = jax.vjp(swiglu, shared_gu)
    grad_shared_gu = swiglu_back(grad_shared_hidden)[0].astype(jnp.bfloat16)
    grad_n2_a, grad_first_shared, grad_b_shared = adapter_bwd(
        normed2, first_all[:, 4:6], b_parts[4:6], picked_rows, shared_low, grad_shared_gu
    )
    grad_normed2 = grad_n2_a + matmul_nt(grad_shared_gu, sgu_w.reshape(model, 2 * SHARED_HIDDEN))
    grad_taken = (gates[..., None] * grad_out[:, None, :]).astype(jnp.bfloat16)
    grad_gates = jnp.sum(taken.astype(jnp.float32) * grad_out[:, None, :], axis=-1)
    grad_chosen = gates * (grad_gates - jnp.sum(gates * grad_gates, axis=-1, keepdims=True))
    grad_logits = jnp.sum(route_hot * grad_chosen[..., None], axis=1)
    grad_normed2 = grad_normed2 + jnp.einsum(
        "re,de->rd", grad_logits, router_w.astype(jnp.float32), precision=lax.Precision.HIGHEST
    )
    grad_padded = jnp.concatenate(
        [
            grad_taken.reshape(sequence_batch, token_block * topk, model),
            jnp.zeros((sequence_batch, 1, model), jnp.bfloat16),
        ],
        axis=1,
    )
    grad_send = jax.vmap(pick_rows)(grad_padded, table).reshape(
        sequence_batch, experts, expert_capacity, model
    )
    grad_recv = lax.all_to_all(grad_send, "dp", split_axis=1, concat_axis=1, tiled=True)
    grad_inputs_all = []
    grad_ea_all = []
    gradient_routed_down_first_total = []
    grad_eb_all = []
    for j in range(local_experts):
        inputs_j = local_rows(recv_rows, j)
        select_j = local_select(j)
        gate_up, gu_low, hidden = expert_front(expert_bwd, j, inputs_j, select_j)
        down_first = expert_bwd[3][j][:, None]
        down_second = [expert_bwd[4][j][:, 2 * EXPERT_HIDDEN :]]
        dn_low = adapter_low(hidden, down_first, select_j)
        grad_y = local_rows(grad_recv, j)
        grad_hid_a, gradient_routed_down_first, grad_eb_down = adapter_bwd(
            hidden, down_first, down_second, select_j, dn_low, grad_y
        )
        grad_hidden = grad_hid_a + matmul_nt(grad_y, expert_bwd[1][j])
        _, expert_swiglu_back = jax.vjp(swiglu, gate_up)
        grad_gu = expert_swiglu_back(grad_hidden)[0].astype(jnp.bfloat16)
        gu_parts = [
            expert_bwd[4][j][:, :EXPERT_HIDDEN],
            expert_bwd[4][j][:, EXPERT_HIDDEN : 2 * EXPERT_HIDDEN],
        ]
        grad_in_a, grad_ea, grad_eb_gu = adapter_bwd(
            inputs_j, expert_bwd[2][j], gu_parts, select_j, gu_low, grad_gu
        )
        grad_inputs = (
            grad_in_a + matmul_nt(grad_gu, expert_bwd[0][j].reshape(model, 2 * EXPERT_HIDDEN))
        ).astype(jnp.bfloat16)
        grad_inputs_all.append(
            grad_inputs.reshape(sequence_batch, adapter_row_count, expert_capacity, model)
        )
        grad_ea_all.append(grad_ea)
        gradient_routed_down_first_total.append(
            gradient_routed_down_first.reshape(EXPERT_HIDDEN, adapter_span_width)
        )
        grad_eb_all.append(jnp.concatenate([grad_eb_gu[0], grad_eb_gu[1], grad_eb_down[0]], axis=1))
    grad_grid = jnp.stack(grad_inputs_all, axis=2).reshape(
        sequence_batch, experts, expert_capacity, model
    )
    grad_back = lax.all_to_all(grad_grid, "dp", split_axis=1, concat_axis=1, tiled=True)
    grad_routes = jax.vmap(pick_rows)(
        grad_back.reshape(sequence_batch, experts * expert_capacity, model), dest_flat
    )
    grad_normed2 = grad_normed2 + jnp.sum(
        grad_routes.reshape(total_row_count, topk, model).astype(jnp.float32), axis=1
    )
    grad_expert_a, grad_expert_a_down, grad_expert_b = (
        lax.psum_scatter(
            jnp.stack(grad_ea_all, axis=0).astype(jnp.bfloat16),
            "seq",
            scatter_dimension=1,
            tiled=True,
        ).astype(jnp.float32),
        lax.psum_scatter(
            jnp.stack(gradient_routed_down_first_total, axis=0).astype(jnp.bfloat16),
            "seq",
            scatter_dimension=1,
            tiled=True,
        ).astype(jnp.float32),
        lax.psum_scatter(
            jnp.stack(grad_eb_all, axis=0).astype(jnp.bfloat16),
            "seq",
            scatter_dimension=2,
            tiled=True,
        ).astype(jnp.float32),
    )
    _, norm2_back = jax.vjp(lambda values_in: rms_norm(values_in, gains[1]), mid)
    grad_mid = grad_out + norm2_back(grad_normed2)[0]
    grad_y_attn = grad_mid.astype(jnp.bfloat16)
    grad_attn_a, grad_first_out, grad_b_out = adapter_bwd(
        attn_b, first_all[:, 3:4], b_parts[3:4], picked_rows, out_low, grad_y_attn
    )
    grad_attn = (grad_attn_a + matmul_nt(grad_y_attn, out_w)).astype(jnp.bfloat16)
    grad_attn5 = grad_attn.reshape(sequence_batch, token_block, KV_HEADS, groups, HEAD_DIM)
    delta = jnp.einsum("sqkgd,skgqd->skgq", grad_attn5, attn_f, preferred_element_type=jnp.float32)
    attend_key_part = lax.all_gather(keys, "seq", axis=1, tiled=True)
    attend_value_part = lax.all_gather(values, "seq", axis=1, tiled=True)
    attend_tag_part = lax.all_gather(key_tags, "seq", axis=1, tiled=True)
    span_len = attend_key_part.shape[1]
    attend_sub_len = math.gcd(span_len, 512)

    def step(i, grad_q):
        offset = i * attend_sub_len
        key_blk = lax.dynamic_slice_in_dim(attend_key_part, offset, attend_sub_len, 1)
        value_blk = lax.dynamic_slice_in_dim(attend_value_part, offset, attend_sub_len, 1)
        tag_blk = lax.dynamic_slice_in_dim(attend_tag_part, offset, attend_sub_len, 1)
        scores = (
            jnp.einsum("sqkgd,spkd->skgqp", query, key_blk, preferred_element_type=jnp.float32)
            * scale
        )
        permit = allowed_pairs(
            query_pos, offset + jnp.arange(attend_sub_len, dtype=jnp.int32), query_tags, tag_blk
        )
        scores = jnp.where(permit[:, None, None], scores, MASKED_SCORE)
        probs = jnp.exp(scores - log_total[..., None])
        grad_probs = jnp.einsum(
            "sqkgd,spkd->skgqp", grad_attn5, value_blk, preferred_element_type=jnp.float32
        )
        grad_scores = (probs * (grad_probs - delta[..., None])).astype(jnp.bfloat16)
        return (
            grad_q
            + jnp.einsum(
                "skgqp,spkd->sqkgd", grad_scores, key_blk, preferred_element_type=jnp.float32
            )
            * scale
        )

    grad_query = lax.fori_loop(
        0,
        span_len // attend_sub_len,
        step,
        jnp.zeros((sequence_batch, token_block, KV_HEADS, groups, HEAD_DIM), jnp.float32),
    )
    all_lse, all_delta, all_tags = (
        lax.all_gather(log_total.transpose(0, 3, 1, 2), "seq", axis=1, tiled=True),
        lax.all_gather(delta.transpose(0, 3, 1, 2), "seq", axis=1, tiled=True),
        lax.all_gather(query_tags, "seq", axis=1, tiled=True),
    )

    def attend_keys(carry, pieces):
        query_part, grad_part = pieces
        span_len = query_part.shape[1]
        sub_len = math.gcd(span_len, 512)

        def step(i, state):
            grad_k, grad_v = state
            offset = i * sub_len
            query_blk = lax.dynamic_slice_in_dim(query_part, offset, sub_len, 1)
            grad_blk = lax.dynamic_slice_in_dim(grad_part, offset, sub_len, 1)
            lse_blk = lax.dynamic_slice_in_dim(all_lse, offset, sub_len, 1).transpose(0, 2, 3, 1)
            delta_blk = lax.dynamic_slice_in_dim(all_delta, offset, sub_len, 1).transpose(
                0, 2, 3, 1
            )
            tag_blk = lax.dynamic_slice_in_dim(all_tags, offset, sub_len, 1)
            rows_pos = offset + jnp.arange(sub_len, dtype=jnp.int32)
            scores = (
                jnp.einsum("sqkgd,spkd->skgqp", query_blk, keys, preferred_element_type=jnp.float32)
                * scale
            )
            permit = allowed_pairs(rows_pos, query_pos, tag_blk, key_tags)
            scores = jnp.where(permit[:, None, None], scores, MASKED_SCORE)
            probs = jnp.exp(scores - lse_blk[..., None])
            grad_v = grad_v + jnp.einsum(
                "skgqp,sqkgd->spkd",
                probs.astype(jnp.bfloat16),
                grad_blk,
                preferred_element_type=jnp.float32,
            )
            grad_probs = jnp.einsum(
                "sqkgd,spkd->skgqp", grad_blk, values, preferred_element_type=jnp.float32
            )
            grad_scores = (probs * (grad_probs - delta_blk[..., None])).astype(jnp.bfloat16)
            grad_k = (
                grad_k
                + jnp.einsum(
                    "skgqp,sqkgd->spkd", grad_scores, query_blk, preferred_element_type=jnp.float32
                )
                * scale
            )
            return (grad_k, grad_v)

        return lax.fori_loop(0, span_len // sub_len, step, carry)

    own_kv = jnp.zeros((sequence_batch, token_block, KV_HEADS, HEAD_DIM), jnp.float32)
    grad_keys, grad_values = attend_keys(
        (own_kv, own_kv),
        (
            lax.all_gather(query, "seq", axis=1, tiled=True),
            lax.all_gather(grad_attn5, "seq", axis=1, tiled=True),
        ),
    )
    grad_qkv = jnp.concatenate(
        [
            grad_query.reshape(total_row_count, query_width),
            grad_keys.reshape(total_row_count, kv_width),
            grad_values.reshape(total_row_count, kv_width),
        ],
        axis=1,
    ).astype(jnp.bfloat16)
    grad_normed_a, grad_first_qkv, grad_b_qkv = adapter_bwd(
        normed, first_all[:, 0:3], b_parts[0:3], picked_rows, qkv_low, grad_qkv
    )
    grad_normed = grad_normed_a + matmul_nt(grad_qkv, qkv_w)
    _, norm1_back = jax.vjp(lambda values_in: rms_norm(values_in, gains[0]), x_flat)
    grad_hidden = (grad_mid + norm1_back(grad_normed)[0]).reshape(
        sequence_batch, token_block, model
    )
    grad_first_all = jnp.concatenate([grad_first_qkv, grad_first_out, grad_first_shared], axis=1)
    grad_second_all = jnp.concatenate(
        grad_b_qkv + grad_b_out + grad_b_shared + grad_b_sdown, axis=1
    )
    gradient_first_factor, gradient_shared_down_factor, gradient_second_factor = (
        lax.psum_scatter(grad_first_all, ("seq", "dp"), scatter_dimension=0, tiled=True),
        lax.psum_scatter(
            gradient_down_factor.reshape(SHARED_HIDDEN, adapter_span_width),
            ("seq", "dp"),
            scatter_dimension=0,
            tiled=True,
        ),
        lax.psum_scatter(grad_second_all, ("seq", "dp"), scatter_dimension=1, tiled=True),
    )
    return (
        hidden_out,
        grad_hidden,
        gradient_first_factor,
        gradient_shared_down_factor,
        gradient_second_factor,
        grad_expert_a,
        grad_expert_a_down,
        grad_expert_b,
    )


def solution(mesh):
    in_specs = (
        P("dp", "seq", None),
        P("dp", "seq"),
        P("dp", "seq"),
        P("dp", "seq", None),
        P("dp"),
        P("dp", "seq", None),
        P(None, ("seq", "dp")),
        P(("seq", "dp"), None),
        P(("seq", "dp"), None),
        P(("seq", "dp"), None),
        P(("seq", "dp"), None, None),
        P(("seq", "dp"), None),
        P("dp", "seq", None, None),
        P("dp", "seq", None),
        P(("seq", "dp"), None, None),
        P(("seq", "dp"), None),
        P(None, ("seq", "dp")),
        P("dp", "seq", None, None),
        P("dp", "seq", None),
        P("dp", None, "seq"),
    )
    out_specs = (
        P("dp", "seq", None),
        P("dp", "seq", None),
        P(("seq", "dp"), None, None),
        P(("seq", "dp"), None),
        P(None, ("seq", "dp")),
        P("dp", "seq", None, None),
        P("dp", "seq", None),
        P("dp", None, "seq"),
    )
    return jax.shard_map(
        per_device, mesh=mesh, in_specs=in_specs, out_specs=out_specs, check_vma=False
    )
```

profile of v0, /device:TPU:0, one launch (start us, length us, event | category | flops | bytes accessed | tf_op | source)
XLA Modules:
  0.0 2217.7 jit_solution(7771527592312428395)
XLA Ops:
  10.1 43.2 %all-gather = bf16[32,48,2]{1,2,0:T(2,128)(2,1)S(1)} all-gather(bf16[1,48,2]{1,2,0:T(2,128)(2,1)} %bitcast.872), channel_id=1, replica_groups=mesh['seq'=4,'dp'=8] {'seq','dp'}, dimensions={0}, use_global_device_ids=true | all-gather | bytes 6336 | tf_op jit(solution)/shard_map/all_gather | solution.py:134
  56.0 12.8 all-gather.19.cloned.1.call-done
  73.8 53.1 %all-gather.21.cloned.1.call-done = bf16[128,7680]{0,1:T(8,128)(2,1)} async-done(((bf16[128,240]{0,1:T(8,128)(2,1)}), bf16[128,7680]{0,1:T(8,128)(2,1)}) %all-gather.21.cloned.1.call-update) | async-done | bytes 1966096 | tf_op jit(solution)/shard_map/all_gather | solution.py:142
  133.5 70.4 %all-gather.17.cloned.1.call-done = bf16[1536,2560]{1,0:T(8,128)(2,1)} async-done(((bf16[48,2560]{1,0:T(8,128)(2,1)}), bf16[1536,2560]{1,0:T(8,128)(2,1)}) %all-gather.17.cloned.1.call-update) | async-done | bytes 7864336 | tf_op jit(solution)/shard_map/all_gather | solution.py:135
  203.9 8.5 fusion.133
  223.8 12.1 all_gather.82
  237.6 11.8 scatter_custom_fusion
  251.5 8.7 all-gather.23.cloned.1.call-done
  260.2 45.9 %all-gather.25.cloned.1.call-done = bf16[1,2048,4,128]{3,1,2,0:T(8,128)(2,1)} async-done(((bf16[1,512,4,128]{3,1,2,0:T(8,128)(2,1)}), bf16[1,2048,4,128]{3,1,2,0:T(8,128)(2,1)}) %all-gather.25.cloned.1.call-update) | async-done | bytes 2097168 | tf_op jit(solution)/shard_map/all_gather | solution.py:187
  306.0 84.7 %while.48 = (s32[]{:T(128)}, f32[1,4,3,512]{3,2,1,0:T(4,128)S(1)}, f32[1,4,3,512]{3,2,1,0:T(4,128)S(1)}, f32[1,4,3,512,128]{4,3,2,1,0:T(8,128)}, bf16[1,2048]{1,...) while((s32[]{:T(128)}, f32[1,4,3,512]{3,2,1,0:T(4,128)S(1)}, ...), condition=%wide.region_4.5_spmd.clone, body=%wide.region_1.4_spmd.clone.sunk | while | flops 1648924160 | bytes 98450664 | solution.py:218
  334.6 9.0 bitcast_add_fusion.7
  355.9 9.0 bitcast_add_fusion.7
  377.3 9.2 bitcast_add_fusion.7
  406.2 70.2 %gather_fusion = bf16[4096,1536]{1,0:T(8,128)(2,1)} fusion(bf16[1,513,1536]{2,1,0:T(8,128)(2,1)S(1)} %concatenate.42, s32[4096]{0:T(1024)S(1)} %bitcast.765), kind=kCustom, calls=%fused_computation | custom fusion | bytes 25198592 | tf_op jit(solution)/shard_map/vmap()/gather | solution.py:51
  482.7 168.6 %all-gather.1 = bf16[32,48,16]{1,2,0:T(8,128)(2,1)S(1)} all-gather(bf16[1,48,16]{1,2,0:T(8,128)(2,1)S(1)} %bitcast.871), channel_id=1, replica_groups=mesh['seq'=4,'dp'=8] {'seq','dp'}, dimensions={0}, use_global_device_ids=true | all-gather | bytes 50688 | tf_op jit(solution)/shard_map/all_gather | solution.py:137
  653.6 9.4 mul.598
  663.0 22.3 %mul.605 = f32[1,3072,1536]{2,1,0:T(8,128)} reshape(f32[512,6,1536]{2,1,0:T(8,128)} %mul.598) | data formatting | bytes 37748736 | tf_op jit(solution)/shard_map/mul | solution.py:338
  689.0 11.7 multiply_convert_fusion
  708.5 119.2 %gather_fusion.2 = bf16[4096,1536]{1,0:T(8,128)(2,1)} fusion(bf16[1,3073,1536]{2,1,0:T(8,128)(2,1)} %concatenate.47, s32[4096]{0:T(1024)S(1)} %bitcast.766), kind=kCustom, calls=%fused_computation.2 | custom fusion | bytes 25198592 | tf_op jit(solution)/shard_map/vmap()/gather | solution.py:51
  834.5 16.5 all_gather.95
  892.2 87.4 %all-to-all-done.3 = bf16[1,16,256,1536]{3,2,0,1:T(8,128)(2,1)} async-done(((bf16[1,16,256,1536]{3,2,0,1:T(8,128)(2,1)}), bf16[1,16,256,1536]{3,2,0,1:T(8,128)(2,1)}, u32[]{:S(2)}, u32[]{:S(2)}) %all-to-all-start.3) | async-done | bytes 12582944 | tf_op jit(solution)/shard_map/all_to_all | solution.py:354
  996.5 8.9 maximum_add_fusion
  1019.5 12.6 maximum_add_fusion.1
  1096.3 9.5 fusion.345
  1109.1 12.5 fusion.346
  1133.5 99.2 %all-to-all-done.2 = bf16[1,16,256,1536]{3,2,0,1:T(8,128)(2,1)} async-done(((bf16[1,16,256,1536]{3,2,0,1:T(8,128)(2,1)}), bf16[1,16,256,1536]{3,2,0,1:T(8,128)(2,1)}, u32[]{:S(2)}, u32[]{:S(2)}) %all-to-all-start.2) | async-done | bytes 12582944 | tf_op jit(solution)/shard_map/all_to_all | solution.py:310
  1238.7 168.6 %all_gather.98 = bf16[1024,128]{1,0:T(8,128)(2,1)S(1)} all-gather(bf16[32,128]{1,0:T(8,128)(2,1)S(1)} %copy-done.150), channel_id=1, replica_groups=mesh['seq'=4,'dp'=8] {'seq','dp'}, dimensions={0}, use_global_device_ids=true | all-gather | bytes 270336 | tf_op jit(solution)/shard_map/all_gather | solution.py:141
  1436.3 66.4 %gather_fusion.1 = bf16[3072,1536]{1,0:T(8,128)(2,1)} fusion(bf16[1,4096,1536]{2,1,0:T(8,128)(2,1)} %bitcast.64, s32[3072]{0:T(1024)S(1)} %bitcast.763), kind=kCustom, calls=%fused_computation.1 | custom fusion | bytes 18898944 | tf_op jit(solution)/shard_map/vmap()/gather | solution.py:51
  1502.7 16.7 reshape.1246
  1519.4 18.5 multiply_reduce_fusion
  1539.0 66.3 %gather_fusion.3 = bf16[3072,1536]{1,0:T(8,128)(2,1)} fusion(bf16[1,4096,1536]{2,1,0:T(8,128)(2,1)} %bitcast.98, s32[3072]{0:T(1024)S(1)} %bitcast.764), kind=kCustom, calls=%fused_computation.3 | custom fusion | bytes 18898944 | tf_op jit(solution)/shard_map/vmap()/gather | solution.py:51
  1605.3 16.5 reshape.1247
  1621.9 15.1 reduce_sum.162
  1681.9 14.1 all_gather.100
  1696.0 15.4 all_gather.101
  1718.8 82.6 %while.49 = (s32[]{:T(128)}, f32[1,512,4,3,128]{1,4,3,2,0:T(8,128)}, bf16[1,2048,4,128]{3,1,2,0:T(8,128)(2,1)}, bf16[1,2048]{1,0:T(2,128)(2,1)}, f32[1,512]{1,0:...) while((s32[]{:T(128)}, ...), condition=%wide.region_21.22_spmd.clone, body=%wide.region_20.21_spmd.clone.sunk | while | flops 2438465024 | bytes 43074288 | solution.py:462
  1727.3 11.4 bitcast_add_fusion.8
  1747.2 12.3 bitcast_add_fusion.8
  1768.0 12.3 bitcast_add_fusion.8
  1788.9 12.5 bitcast_add_fusion.8
  1806.5 14.9 all_gather.103
  1821.5 110.8 %while.50 = (s32[]{:T(128)}, f32[1,512,4,128]{1,3,2,0:T(8,128)S(1)}, f32[1,512,4,128]{1,3,2,0:T(8,128)}, bf16[1,2048,4,3,128]{1,4,3,2,0:T(8,128)(2,1)}, bf16[1,5...) while((s32[]{:T(128)}, ...), condition=%wide.region_23.24_spmd.clone, body=%wide.region_22.23_spmd.clone.sunk | while | flops 3255305728 | bytes 50262756 | solution.py:516
  1837.7 11.3 fusion.467
  1865.5 11.2 fusion.467
  1893.3 11.3 fusion.467
  1921.1 11.2 fusion.467
  1992.8 105.8 %reduce-scatter.19.cloned.1.call-done = f32[240,128]{1,0:T(8,128)} async-done(((f32[7680,128]{1,0:T(8,128)}), f32[240,128]{1,0:T(8,128)}) %reduce-scatter.19.cloned.1.call-update) | async-done | bytes 122896
  2098.6 112.0 %reduce-scatter.11.cloned.1.call-done = f32[48,6,128]{2,0,1:T(8,128)} async-done(((f32[1536,6,128]{2,0,1:T(8,128)}), f32[48,6,128]{2,0,1:T(8,128)}) %reduce-scatter.11.cloned.1.call-update) | async-done | bytes 147472 | tf_op jit(solution)/shard_map/reduce_scatter | solution.py:547
  (710 shorter events, 533.3 us)
Async XLA Ops:
  7.2 61.6 %all-gather.19.cloned.1.call-start = ((), (), s32[]{:S(2)}) async-start(), calls=%async_computation.12 | async-start | bytes 2433024 | tf_op jit(solution)/shard_map/all_gather | solution.py:140
  7.9 119.0 %all-gather.21.cloned.1.call-start = ((), (), s32[]{:S(2)}) async-start(), calls=%async_computation.13 | async-start | bytes 2027520 | tf_op jit(solution)/shard_map/all_gather | solution.py:142
  8.7 195.3 %all-gather.17.cloned.1.call-start = ((), (), s32[]{:S(2)}) async-start(), calls=%async_computation.11 | async-start | bytes 8110080 | tf_op jit(solution)/shard_map/all_gather | solution.py:135
  9.4 250.8 %all-gather.23.cloned.1.call-start = ((), (), s32[]{:S(2)}) async-start(), calls=%async_computation.14 | async-start | bytes 2621440 | tf_op jit(solution)/shard_map/all_gather | solution.py:186
  53.4 344.1 %copy-start.145 = (f32[128]{0:T(128)}, f32[128]{0:T(128)S(1)}, u32[]{:S(2)}) copy-start(f32[128]{0:T(128)S(1)} %compare_convert_fusion.2) | copy-start | bytes 1540
  53.5 150.5 %copy-start.151 = (f32[1536]{0:T(1024)}, f32[1536]{0:T(1024)S(1)}, u32[]{:S(2)}) copy-start(f32[1536]{0:T(1024)S(1)} %get-tuple-element.976) | copy-start | bytes 18436
  53.5 631.9 %copy-start.123 = (f32[1536]{0:T(1024)}, f32[1536]{0:T(1024)S(1)}, u32[]{:S(2)}) copy-start(f32[1536]{0:T(1024)S(1)} %get-tuple-element.975) | copy-start | bytes 18436
  56.0 147.9 %copy-start.148 = (f32[512]{0:T(512)}, f32[512]{0:T(512)S(1)}, u32[]{:S(2)}) copy-start(f32[512]{0:T(512)S(1)} %fusion.321) | copy-start | bytes 6148
  73.8 59.7 %copy-start.85 = (bf16[512,3,128]{2,0,1:T(8,128)(2,1)}, bf16[512,3,128]{2,0,1:T(8,128)(2,1)S(1)}, u32[]{:S(2)}) copy-start(bf16[512,3,128]{2,0,1:T(8,128)(2,1)S(1)} %fusion.217) | copy-start | bytes 1179652
  214.2 22.6 %copy-start.156 = (s32[2]{0:T(128)S(1)}, s32[2]{0:T(128)}, u32[]{:S(2)}) copy-start(s32[2]{0:T(128)} %constant.266) | copy-start | bytes 28
  214.2 22.7 %copy-start.157 = (s32[2]{0:T(128)S(1)}, s32[2]{0:T(128)}, u32[]{:S(2)}) copy-start(s32[2]{0:T(128)} %constant.269) | copy-start | bytes 28
  215.1 90.9 %all-gather.25.cloned.1.call-start = ((), (), s32[]{:S(2)}) async-start(), calls=%async_computation.15 | async-start | bytes 2621440 | tf_op jit(solution)/shard_map/all_gather | solution.py:187
  216.2 33.4 %slice-start.10 = ((bf16[512,2560]{1,0:T(8,128)(2,1)}), bf16[512,1536]{1,0:T(8,128)(2,1)S(1)}, s32[]{:S(2)}) async-start(bf16[512,2560]{1,0:T(8,128)(2,1)} %copy-done.44), calls=%async_computation.41 | async-start | bytes 3145728 | tf_op jit(solution)/shard_map/slice | solution.py:170
  216.2 182.0 %all-gather.27.cloned.1.call-start = ((), (), s32[]{:S(2)}) async-start(), calls=%async_computation.16 | async-start | bytes 4866048 | tf_op jit(solution)/shard_map/all_gather | solution.py:136
  216.8 634.5 %all-gather.33.cloned.1.call-start = ((), (), s32[]{:S(2)}) async-start(), calls=%async_computation.19 | async-start | bytes 1638400 | tf_op jit(solution)/shard_map/all_gather | solution.py:151
  218.2 258.3 %all-to-all-start.1 = ((bf16[1,8,2]{2,0,1:T(2,128)(2,1)}), bf16[1,8,2]{2,0,1:T(2,128)(2,1)S(1)}, u32[]{:S(2)}, u32[]{:S(2)}) async-start(bf16[1,8,2]{2,0,1:T(2,128)(2,1)} %broadcast_in_dim.256), calls=%async_computation.1 | async-start | bytes 8192 | tf_op jit(solution)/shard_map/all_to_all | solution.py:266
  221.5 631.3 %all-gather.31.cloned.1.call-start = ((), (), s32[]{:S(2)}) async-start(), calls=%async_computation.18 | async-start | bytes 1966080 | tf_op jit(solution)/shard_map/all_gather | solution.py:149
  223.8 26.7 %copy-start.130 = (bf16[1,512]{1,0:T(2,128)(2,1)}, bf16[1,512]{1,0:T(2,128)(2,1)S(1)}, u32[]{:S(2)}) copy-start(bf16[1,512]{1,0:T(2,128)(2,1)S(1)} %get-tuple-element.1365) | copy-start | bytes 3076
  250.5 55.5 %copy-start.22 = (bf16[512,1536]{0,1:T(8,128)(2,1)}, bf16[512,1536]{0,1:T(8,128)(2,1)S(1)}, u32[]{:S(2)}) copy-start(bf16[512,1536]{0,1:T(8,128)(2,1)S(1)} %copy.369) | copy-start | bytes 4718596
  404.6 280.8 %copy-start.137 = (f32[512]{0:T(512)}, f32[512]{0:T(512)S(1)}, u32[]{:S(2)}) copy-start(f32[512]{0:T(512)S(1)} %fusion.322) | copy-start | bytes 6148
  476.5 351.3 %all-to-all-start = ((bf16[1,16,256,1536]{3,2,0,1:T(8,128)(2,1)}), bf16[1,16,256,1536]{3,2,0,1:T(8,128)(2,1)}, u32[]{:S(2)}, u32[]{:S(2)}) async-start(bf16[1,16,256,1536]{3,2,0,1:T(8,128)(2,1)} %bitcast.780), calls=%async_computation | async-start | bytes 25165824 | tf_op jit(solution)/shard_map/all_to_all | solution.py:265
  481.9 169.6 %copy-start.18 = (bf16[1,512,1536]{2,1,0:T(8,128)(2,1)S(1)}, bf16[1,512,1536]{2,1,0:T(8,128)(2,1)}, u32[]{:S(2)}) copy-start(bf16[1,512,1536]{2,1,0:T(8,128)(2,1)} %param.31) | copy-start | bytes 4718596
  482.0 376.6 %all-gather.29.cloned.1.call-start = ((), (), s32[]{:S(2)}) async-start(), calls=%async_computation.17 | async-start | bytes 7864320 | tf_op jit(solution)/shard_map/all_gather | solution.py:147
  651.5 34.2 %copy-start.114 = (bf16[1536,16]{0,1:T(8,128)(2,1)}, bf16[1536,16]{0,1:T(8,128)(2,1)S(1)}, u32[]{:S(2)}) copy-start(bf16[1536,16]{0,1:T(8,128)(2,1)S(1)} %reshape.1302) | copy-start | bytes 147460
  663.0 22.4 %copy-start.4 = (f32[512,1536]{1,0:T(8,128)S(1)}, f32[512,1536]{1,0:T(8,128)}, u32[]{:S(2)}) copy-start(f32[512,1536]{1,0:T(8,128)} %copy-done.3) | copy-start | bytes 9437188
  827.7 151.8 %all-to-all-start.3 = ((bf16[1,16,256,1536]{3,2,0,1:T(8,128)(2,1)}), bf16[1,16,256,1536]{3,2,0,1:T(8,128)(2,1)}, u32[]{:S(2)}, u32[]{:S(2)}) async-start(bf16[1,16,256,1536]{3,2,0,1:T(8,128)(2,1)} %bitcast.779), calls=%async_computation.3 | async-start | bytes 25165824 | tf_op jit(solution)/shard_map/all_to_all | solution.py:354
  833.2 172.2 %all-gather.35.cloned.1.call-start = ((), (), s32[]{:S(2)}) async-start(), calls=%async_computation.20 | async-start | bytes 3932160 | tf_op jit(solution)/shard_map/all_gather | solution.py:148
  833.8 575.8 %all-gather.39.cloned.1.call-start = ((), (), s32[]{:S(2)}) async-start(), calls=%async_computation.22 | async-start | bytes 3244032 | tf_op jit(solution)/shard_map/all_gather | solution.py:139
  1011.6 20.5 slice-start
  1019.4 23.4 %copy-start.32 = (bf16[2048,512]{1,0:T(8,128)(2,1)}, bf16[2048,512]{1,0:T(8,128)(2,1)S(1)}, u32[]{:S(2)}) copy-start(bf16[2048,512]{1,0:T(8,128)(2,1)S(1)} %get-tuple-element.1067) | copy-start | bytes 6291460
  1070.1 162.6 %all-to-all-start.2 = ((bf16[1,16,256,1536]{3,2,0,1:T(8,128)(2,1)}), bf16[1,16,256,1536]{3,2,0,1:T(8,128)(2,1)}, u32[]{:S(2)}, u32[]{:S(2)}) async-start(bf16[1,16,256,1536]{3,2,0,1:T(8,128)(2,1)} %bitcast.782), calls=%async_computation.2 | async-start | bytes 25165824 | tf_op jit(solution)/shard_map/all_to_all | solution.py:310
  1075.4 339.3 %all-gather.37.cloned.1.call-start = ((), (), s32[]{:S(2)}) async-start(), calls=%async_computation.21 | async-start | bytes 6488064 | tf_op jit(solution)/shard_map/all_gather | solution.py:138
  1232.7 174.7 %copy-start.19 = (bf16[1,512,1536]{2,1,0:T(8,128)(2,1)S(1)}, bf16[1,512,1536]{2,1,0:T(8,128)(2,1)}, u32[]{:S(2)}) copy-start(bf16[1,512,1536]{2,1,0:T(8,128)(2,1)} %param.31) | copy-start | bytes 4718596
  1232.7 174.7 %copy-start.146 = (f32[128]{0:T(128)S(1)}, f32[128]{0:T(128)}, u32[]{:S(2)}) copy-start(f32[128]{0:T(128)} %copy-done.145) | copy-start | bytes 1540
  1232.7 306.3 %all-to-all-start.4 = ((bf16[1,16,256,1536]{3,2,0,1:T(8,128)(2,1)}), bf16[1,16,256,1536]{3,2,0,1:T(8,128)(2,1)}, u32[]{:S(2)}, u32[]{:S(2)}) async-start(bf16[1,16,256,1536]{3,2,0,1:T(8,128)(2,1)} %bitcast.781), calls=%async_computation.4 | async-start | bytes 25165824 | tf_op jit(solution)/shard_map/all_to_all | solution.py:394
  1238.2 170.7 %slice-start.7 = ((bf16[1536,6,128]{2,0,1:T(8,128)(2,1)}), bf16[1536,2,128]{2,0,1:T(8,128)(2,1)S(1)}, s32[]{:S(2)}) async-start(bf16[1536,6,128]{2,0,1:T(8,128)(2,1)} %all-gather.19.cloned.1.call-done), calls=%async_computation.38 | async-start | bytes 1572864 | tf_op jit(solution)/shard_map/slice | solution.py:232
  1238.2 583.2 %all-gather.41.cloned.1.call-start = ((), (), s32[]{:S(2)}) async-start(), calls=%async_computation.23 | async-start | bytes 7864320 | tf_op jit(solution)/shard_map/all_gather | solution.py:522
  1409.3 412.1 %all-gather.43.cloned.1.call-start = ((), (), s32[]{:S(2)}) async-start(), calls=%async_computation.24 | async-start | bytes 7864320 | tf_op jit(solution)/shard_map/all_gather | solution.py:523
  1652.1 313.7 %reduce-scatter.17.cloned.1.call-start = ((), (), s32[]{:S(2)}) async-start(), calls=%async_computation.28 | async-start | bytes 327680 | tf_op jit(solution)/shard_map/reduce_scatter | solution.py:408
  1668.1 299.3 %reduce-scatter.21.cloned.1.call-start = ((), (), s32[]{:S(2)}) async-start(), calls=%async_computation.30 | async-start | bytes 1638400
  1670.7 301.1 %reduce-scatter.15.cloned.1.call-start = ((), (), s32[]{:S(2)}) async-start(), calls=%async_computation.27 | async-start | bytes 1966080 | tf_op jit(solution)/shard_map/reduce_scatter | solution.py:402
  1680.4 31.1 %copy-start.66 = (bf16[512,1024]{1,0:T(8,128)(2,1)S(1)}, bf16[512,1024]{1,0:T(8,128)(2,1)}, u32[]{:S(2)}) copy-start(bf16[512,1024]{1,0:T(8,128)(2,1)} %get-tuple-element.1073) | copy-start | bytes 3145732
  1680.4 31.1 %copy-start.97 = (bf16[1024,128]{1,0:T(8,128)(2,1)S(1)}, bf16[1024,128]{1,0:T(8,128)(2,1)}, u32[]{:S(2)}) copy-start(bf16[1024,128]{1,0:T(8,128)(2,1)} %copy-done.96) | copy-start | bytes 786436
  1680.4 32.1 %copy-start.128 = (bf16[512,128]{1,0:T(8,128)(2,1)S(1)}, bf16[512,128]{1,0:T(8,128)(2,1)}, u32[]{:S(2)}) copy-start(bf16[512,128]{1,0:T(8,128)(2,1)} %copy-done.127) | copy-start | bytes 393220
  1681.7 32.2 %copy-start.15 = (bf16[512,1536]{0,1:T(8,128)(2,1)S(1)}, bf16[512,1536]{0,1:T(8,128)(2,1)}, u32[]{:S(2)}) copy-start(bf16[512,1536]{0,1:T(8,128)(2,1)} %copy.408) | copy-start | bytes 4718596
  1681.8 311.0 %reduce-scatter.13.cloned.1.call-start = ((), (), s32[]{:S(2)}) async-start(), calls=%async_computation.26 | async-start | bytes 540672 | tf_op jit(solution)/shard_map/reduce_scatter | solution.py:548
  1713.9 384.8 %reduce-scatter.19.cloned.1.call-start = ((), (), s32[]{:S(2)}) async-start(), calls=%async_computation.29 | async-start | bytes 4055040
  1946.5 264.1 %reduce-scatter.11.cloned.1.call-start = ((), (), s32[]{:S(2)}) async-start(), calls=%async_computation.25 | async-start | bytes 4866048 | tf_op jit(solution)/shard_map/reduce_scatter | solution.py:547
  (159 other events, 1004.2 us)
Sparse Core Ops, SparseCore 0:
  10.8 57.9 all-gather.18
  71.7 55.1 all-gather.20
  129.8 74.0 all-gather.16
  215.3 44.8 all-gather.22
  261.6 44.4 all-gather.24
  308.8 62.3 all-gather.26
  372.8 31.0 all-gather.32
  405.5 36.5 all-gather.30
  484.4 114.7 all-gather.28
  835.3 62.8 all-gather.34
  901.0 87.6 all-gather.38
  1078.8 121.0 all-gather.36
  1409.4 111.6 all-gather.40
  1652.2 113.8 all-gather.42
  1768.8 17.8 reduce-scatter.16
  1789.0 31.1 reduce-scatter.20
  1822.5 34.4 reduce-scatter.14
  1859.7 133.0 reduce-scatter.12
  1998.8 99.8 reduce-scatter.18
  2104.5 106.0 reduce-scatter.10
where the time goes:
time: 2230 us; the launch traced here: 2220 us
  waiting for transfers between devices  604 us (27%)
  local copies, waits for them, and re-layouts  509 us (23%)
  matrix products  496 us (22%)
  blocking collectives  454 us (20%)
  other arithmetic  110 us (5%)
  starting transfers between devices  26.5 us (1%)
    gather x6, local copies, waits for them, and re-layouts, pick_rows(): return matrix[indices]  322 us
    all_gather x1, blocking collectives, dense_gather(): lax.all_gather(shared_down_first_factor, ('seq', 'dp'), axis=0, tiled=True)  169 us
    all_gather x1, blocking collectives, dense_gather(): lax.all_gather(router_weight, ('seq', 'dp'), axis=0, tiled=True)  169 us
    unnamed x22, waiting for transfers between devices  112 us
    reduce_scatter x1, waiting for transfers between devices, per_device(): lax.psum_scatter(grad_first_all, ('seq', 'dp'), scatter_dimension=0, tile...  112 us
    dot_general x29, matrix products, matmul_nt(): jnp.einsum('ri,ji->rj', left, right, preferred_element_type=jnp.float32)  101 us
    all_to_all x1, waiting for transfers between devices, per_device(): lax.all_to_all(out_grid, 'dp', split_axis=1, concat_axis=1, tiled=True)  99.2 us
    dot_general x30, matrix products, matmul(): return jnp.dot(left, right, preferred_element_type=jnp.float32)  97.6 us
  transfers between devices with their start and end apart: 25, of which 10 were waited for; matrix products, arithmetic and copies ran while one was open for 48% of the time, Pallas kernels for 0%

commit v1 on v0

v1 whole, which is shorter than its diff:
```python
import functools
import math

import jax
import jax.numpy as jnp
from jax import lax
from jax.experimental import pallas as pl
from jax.experimental.pallas import tpu as pltpu
from jax.sharding import PartitionSpec as P

HEADS = 12
KV_HEADS = 4
HEAD_DIM = 128
EXPERT_HIDDEN = 512
SHARED_HIDDEN = 1024
ADAPTER_RANK = 16
DOCUMENT_SPAN = 1024

EPSILON = 1e-05
MASKED_SCORE = -1e30
LOG2E = 1.4426950408889634
SCALE = HEAD_DIM ** (-0.5)
LANES = 128
VMEM_LIMIT = 60 * 1024 * 1024

F32 = jnp.float32
BF16 = jnp.bfloat16


def dot_nn(left, right):
    return jnp.dot(left, right, preferred_element_type=F32)


def dot_tn(left, right):
    return lax.dot_general(left, right, (((0,), (0,)), ((), ())), preferred_element_type=F32)


def dot_nt(left, right):
    return lax.dot_general(left, right, (((1,), (1,)), ((), ())), preferred_element_type=F32)


def rms_norm(values, gain):
    return values * lax.rsqrt(jnp.mean(values * values, axis=-1, keepdims=True) + EPSILON) * gain


def swiglu(gate_up):
    half_width = gate_up.shape[-1] // 2
    return jax.nn.silu(gate_up[:, :half_width]) * gate_up[:, half_width:]


def query_tiles(rows, hops):
    tile = math.gcd(rows, 256)
    spans = []
    for first in range(0, rows, tile):
        oldest = max(0, hops * rows + first - (DOCUMENT_SPAN - 1)) // tile * tile
        spans.append((first, tile, oldest, hops * rows + first + tile - oldest))
    return spans


def fill_bias(spans, shift, query_tag, key_tag, bias):
    for first, tile, oldest, span in spans:
        keys = oldest + lax.broadcasted_iota(jnp.int32, (span, tile), 0)
        queries = shift + first + lax.broadcasted_iota(jnp.int32, (span, tile), 1)
        same = key_tag[oldest : oldest + span, :] == query_tag[:, first : first + tile]
        permit = (keys <= queries) & (same | (keys == queries))
        bias[oldest : oldest + span, first : first + tile] = jnp.where(permit, 0.0, MASKED_SCORE)


def attend_kernel(spans, shift, q_ref, k_ref, v_ref, qt_ref, kt_ref, out_ref, lse_ref, bias):
    @pl.when(pl.program_id(0) == 0)
    def _():
        fill_bias(spans, shift, qt_ref, kt_ref, bias)

    groups = q_ref.shape[1] // HEAD_DIM
    for first, tile, oldest, span in spans:
        keys = k_ref[oldest : oldest + span, :]
        values = v_ref[oldest : oldest + span, :]
        mask = bias[oldest : oldest + span, first : first + tile]
        for h in range(groups):
            columns = slice(h * HEAD_DIM, (h + 1) * HEAD_DIM)
            scores = dot_nt(keys, q_ref[first : first + tile, columns]) * (SCALE * LOG2E) + mask
            top = jnp.max(scores, axis=0, keepdims=True)
            weights = jnp.exp2(scores - top)
            total = jnp.sum(weights, axis=0, keepdims=True)
            mixed = dot_tn(values, weights.astype(BF16)) / total
            out_ref[first : first + tile, columns] = mixed.T.astype(BF16)
            lse_ref[0, h : h + 1, first : first + tile] = top + jnp.log2(total)


def attend(qkv, kv_all, query_tag, key_tag, hops):
    rows = qkv.shape[0]
    groups = HEADS // KV_HEADS
    span = kv_all.shape[0]
    spans = query_tiles(rows, hops)
    return pl.pallas_call(
        functools.partial(attend_kernel, spans, hops * rows),
        grid=(KV_HEADS,),
        in_specs=[
            pl.BlockSpec((rows, groups * HEAD_DIM), lambda g: (0, g)),
            pl.BlockSpec((span, HEAD_DIM), lambda g: (0, g)),
            pl.BlockSpec((span, HEAD_DIM), lambda g: (0, KV_HEADS + g)),
            pl.BlockSpec((1, rows), lambda g: (0, 0)),
            pl.BlockSpec((span, 1), lambda g: (0, 0)),
        ],
        out_specs=[
            pl.BlockSpec((rows, groups * HEAD_DIM), lambda g: (0, g)),
            pl.BlockSpec((1, groups, rows), lambda g: (g, 0, 0)),
        ],
        out_shape=[
            jax.ShapeDtypeStruct((rows, HEADS * HEAD_DIM), BF16),
            jax.ShapeDtypeStruct((KV_HEADS, groups, rows), F32),
        ],
        scratch_shapes=[pltpu.VMEM((span, rows), F32)],
        compiler_params=pltpu.CompilerParams(vmem_limit_bytes=VMEM_LIMIT),
        cost_estimate=pl.CostEstimate(
            flops=4 * HEADS * rows * span * HEAD_DIM, bytes_accessed=8 * rows * 1536, transcendentals=HEADS * rows * span
        ),
        name="attend",
    )(qkv, kv_all, kv_all, query_tag, key_tag)


def attend_back_kernel(
    spans, shift, q_ref, k_ref, v_ref, g_ref, lse_ref, qt_ref, kt_ref, dq_ref, dk_ref, dv_ref, bias, dk_acc, dv_acc
):
    @pl.when(pl.program_id(0) == 0)
    def _():
        fill_bias(spans, shift, qt_ref, kt_ref, bias)

    dk_acc[...] = jnp.zeros_like(dk_acc)
    dv_acc[...] = jnp.zeros_like(dv_acc)
    groups = q_ref.shape[1] // HEAD_DIM
    for first, tile, oldest, span in spans:
        keys = k_ref[oldest : oldest + span, :]
        values = v_ref[oldest : oldest + span, :]
        mask = bias[oldest : oldest + span, first : first + tile]
        for h in range(groups):
            columns = slice(h * HEAD_DIM, (h + 1) * HEAD_DIM)
            query = q_ref[first : first + tile, columns]
            grad = g_ref[first : first + tile, columns]
            lse = lse_ref[0, h : h + 1, first : first + tile]
            probs = jnp.exp2(dot_nt(keys, query) * (SCALE * LOG2E) + mask - lse)
            dv_acc[oldest : oldest + span, :] += dot_nn(probs.astype(BF16), grad)
            grad_probs = dot_nt(values, grad)
            delta = jnp.sum(probs * grad_probs, axis=0, keepdims=True)
            grad_scores = (probs * (grad_probs - delta)).astype(BF16)
            dk_acc[oldest : oldest + span, :] += dot_nn(grad_scores, query) * SCALE
            dq_ref[first : first + tile, columns] = (dot_tn(grad_scores, keys) * SCALE).astype(BF16)
    dk_ref[...] = dk_acc[...].astype(dk_ref.dtype)
    dv_ref[...] = dv_acc[...].astype(dv_ref.dtype)


def attend_back(qkv, kv_all, grad_attn, lse, query_tag, key_tag, hops):
    rows = qkv.shape[0]
    groups = HEADS // KV_HEADS
    span = kv_all.shape[0]
    spans = query_tiles(rows, hops)
    return pl.pallas_call(
        functools.partial(attend_back_kernel, spans, hops * rows),
        grid=(KV_HEADS,),
        in_specs=[
            pl.BlockSpec((rows, groups * HEAD_DIM), lambda g: (0, g)),
            pl.BlockSpec((span, HEAD_DIM), lambda g: (0, g)),
            pl.BlockSpec((span, HEAD_DIM), lambda g: (0, KV_HEADS + g)),
            pl.BlockSpec((rows, groups * HEAD_DIM), lambda g: (0, g)),
            pl.BlockSpec((1, groups, rows), lambda g: (g, 0, 0)),
            pl.BlockSpec((1, rows), lambda g: (0, 0)),
            pl.BlockSpec((span, 1), lambda g: (0, 0)),
        ],
        out_specs=[
            pl.BlockSpec((rows, groups * HEAD_DIM), lambda g: (0, g)),
            pl.BlockSpec((span, HEAD_DIM), lambda g: (0, g)),
            pl.BlockSpec((span, HEAD_DIM), lambda g: (0, g)),
        ],
        out_shape=[
            jax.ShapeDtypeStruct((rows, HEADS * HEAD_DIM), BF16),
            jax.ShapeDtypeStruct((span, KV_HEADS * HEAD_DIM), BF16),
            jax.ShapeDtypeStruct((span, KV_HEADS * HEAD_DIM), BF16),
        ],
        scratch_shapes=[
            pltpu.VMEM((span, rows), F32),
            pltpu.VMEM((span, HEAD_DIM), F32),
            pltpu.VMEM((span, HEAD_DIM), F32),
        ],
        compiler_params=pltpu.CompilerParams(vmem_limit_bytes=VMEM_LIMIT),
        cost_estimate=pl.CostEstimate(
            flops=10 * HEADS * rows * span * HEAD_DIM, bytes_accessed=16 * rows * 1536, transcendentals=HEADS * rows * span
        ),
        name="attend_back",
    )(qkv, kv_all, kv_all, grad_attn, lse, query_tag, key_tag)


def expert_kernel(count, experts, with_prior, *refs):
    meta, up_ref, down_ref, second_ref = refs[:4]
    refs = refs[4:]
    token_refs, refs = refs[:count], refs[count:]
    grad_refs, refs = refs[:count], refs[count:]
    prior_moe, prior_back = (), ()
    if with_prior:
        prior_moe, refs = refs[:count], refs[count:]
        prior_back, refs = refs[:count], refs[count:]
    moe_refs, refs = refs[:count], refs[count:]
    back_refs, refs = refs[:count], refs[count:]
    first_grad, down_grad, second_grad = refs[:3]
    tokens_buf, grad_buf, moe_buf, back_buf, in_sem, out_sem = refs[3:]

    step = pl.program_id(0)
    slot = lax.rem(step, 2)
    rows, wide = tokens_buf.shape[1:]
    model = wide - LANES
    hidden = EXPERT_HIDDEN
    capacity = rows // 2
    rank = LANES

    def incoming(k, to):
        pairs = [(token_refs[k], tokens_buf, 0), (grad_refs[k], grad_buf, 1)]
        if with_prior:
            pairs += [(prior_moe[k], moe_buf, 2), (prior_back[k], back_buf, 3)]
        return [pltpu.make_async_copy(src, dst.at[to], in_sem.at[to, n]) for src, dst, n in pairs]

    def outgoing(k, at):
        return [
            pltpu.make_async_copy(moe_buf.at[at], moe_refs[k], out_sem.at[at, 0]),
            pltpu.make_async_copy(back_buf.at[at], back_refs[k], out_sem.at[at, 1]),
        ]

    @pl.when(step == 0)
    def _():
        for copy in incoming(0, 0):
            copy.start()
        first_grad[...] = jnp.zeros_like(first_grad)
        down_grad[...] = jnp.zeros_like(down_grad)
        second_grad[...] = jnp.zeros_like(second_grad)

    for k in range(count):

        @pl.when(step == k)
        def _(k=k):
            for copy in incoming(k, k % 2):
                copy.wait()
            if k >= 1:
                for copy in outgoing(k - 1, (k - 1) % 2):
                    copy.wait()
            if k + 1 < count:
                for copy in incoming(k + 1, (k + 1) % 2):
                    copy.start()

    expert = meta[0]
    adapter = meta[1 + step]
    lane = lax.broadcasted_iota(jnp.int32, (1, LANES), 1)
    select = (lane // ADAPTER_RANK == adapter).astype(F32)
    select_two = jnp.concatenate([select, select], axis=1)

    extra = tokens_buf[slot, :, model:].astype(F32)
    slot_column = jnp.sum(jnp.where(lane == expert, extra, 0.0), axis=1, keepdims=True)
    extra_t = extra.T
    sub = lax.broadcasted_iota(jnp.int32, (LANES, 1), 0)
    slot_row = jnp.sum(jnp.where(sub == expert, extra_t, 0.0), axis=0, keepdims=True)
    place = (lax.broadcasted_iota(jnp.int32, (rows, capacity), 1).astype(F32) == slot_column).astype(F32).astype(BF16)
    pick = (lax.broadcasted_iota(jnp.int32, (capacity, rows), 0).astype(F32) == slot_row).astype(F32).astype(BF16)

    picked_extra = dot_nn(pick, tokens_buf[slot, :, model:])
    gate = jnp.sum(
        jnp.where((lane == experts + expert) | (lane == 2 * experts + expert), picked_extra, 0.0), axis=1, keepdims=True
    )
    inputs = dot_nn(pick, tokens_buf[slot, :, :model]).astype(BF16)
    low = (dot_nn(inputs, up_ref[:, 2 * hidden :]) * select_two).astype(BF16)
    gate_part = dot_nn(inputs, up_ref[:, :hidden]) + dot_nn(low[:, :rank], second_ref[:, :hidden])
    up_part = dot_nn(inputs, up_ref[:, hidden : 2 * hidden]) + dot_nn(low[:, rank:], second_ref[:, hidden : 2 * hidden])
    sigmoid = 1.0 / (1.0 + jnp.exp(-gate_part))
    silu = gate_part * sigmoid
    act = (silu * up_part).astype(BF16)
    low_down = (dot_nn(act, down_ref[:, model:]) * select).astype(BF16)
    output = (dot_nn(act, down_ref[:, :model]) + dot_nn(low_down, second_ref[:, 2 * hidden :])).astype(BF16).astype(F32)
    grad_rows = dot_nn(pick, grad_buf[slot])
    grad_gate = jnp.sum(output * grad_rows, axis=1, keepdims=True)
    moe = dot_nn(place, (gate * output).astype(BF16))
    if with_prior:
        moe = moe + moe_buf[slot].astype(F32)
    moe_buf[slot] = moe.astype(BF16)

    grad_y = (gate * grad_rows).astype(BF16)
    glow_down = (dot_nt(grad_y, second_ref[:, 2 * hidden :]) * select).astype(BF16)
    second_grad[:, 2 * hidden :] += dot_tn(low_down, grad_y)
    down_grad[...] += dot_tn(glow_down, act)
    grad_act = dot_nt(grad_y, down_ref[:, :model]) + dot_nt(glow_down, down_ref[:, model:])
    grad_up = (grad_act * silu).astype(BF16)
    grad_gp = (grad_act * up_part * (sigmoid * (1.0 + gate_part * (1.0 - sigmoid)))).astype(BF16)
    glow = jnp.concatenate(
        [
            dot_nt(grad_gp, second_ref[:, :hidden]) * select,
            dot_nt(grad_up, second_ref[:, hidden : 2 * hidden]) * select,
        ],
        axis=1,
    ).astype(BF16)
    second_grad[:, :hidden] += dot_tn(low[:, :rank], grad_gp)
    second_grad[:, hidden : 2 * hidden] += dot_tn(low[:, rank:], grad_up)
    first_grad[...] += dot_tn(glow, inputs)
    grad_in = (
        dot_nt(grad_gp, up_ref[:, :hidden])
        + dot_nt(grad_up, up_ref[:, hidden : 2 * hidden])
        + dot_nt(glow, up_ref[:, 2 * hidden :])
    ).astype(BF16)
    gate_hi = grad_gate.astype(BF16).astype(F32)
    gate_lo = grad_gate - gate_hi
    extra_out = (
        jnp.where(lane == expert, gate_hi, 0.0) + jnp.where(lane == experts + expert, gate_lo, 0.0)
    ).astype(BF16)
    back = dot_nn(place, grad_in)
    back_extra = dot_nn(place, extra_out)
    if with_prior:
        back = back + back_buf[slot, :, :model].astype(F32)
        back_extra = back_extra + back_buf[slot, :, model:].astype(F32)
    back_buf[slot, :, :model] = back.astype(BF16)
    back_buf[slot, :, model:] = back_extra.astype(BF16)

    for k in range(count):

        @pl.when(step == k)
        def _(k=k):
            for copy in outgoing(k, k % 2):
                copy.start()
            if k == count - 1:
                for copy in outgoing(k, k % 2):
                    copy.wait()


def expert_call(meta, up, down, second, tokens, grads, prior, experts):
    count = len(tokens)
    rows, wide = tokens[0].shape
    model = wide - LANES
    whole = lambda a: pl.BlockSpec(a.shape, lambda i: (0,) * a.ndim, pipeline_mode=pl.Buffered(1))
    anywhere = pl.BlockSpec(memory_space=pl.ANY)
    prior = [] if prior is None else list(prior[0]) + list(prior[1])
    moe_shape = jax.ShapeDtypeStruct((rows, model), BF16)
    back_shape = jax.ShapeDtypeStruct((rows, wide), BF16)
    grad_shapes = [
        jax.ShapeDtypeStruct((2 * LANES, model), F32),
        jax.ShapeDtypeStruct((LANES, EXPERT_HIDDEN), F32),
        jax.ShapeDtypeStruct(second.shape, F32),
    ]
    outs = pl.pallas_call(
        functools.partial(expert_kernel, count, experts, bool(prior)),
        grid=(count,),
        in_specs=[pl.BlockSpec(memory_space=pltpu.SMEM), whole(up), whole(down), whole(second)]
        + [anywhere] * (2 * count + len(prior)),
        out_specs=[anywhere] * (2 * count)
        + [pl.BlockSpec(s.shape, lambda i: (0, 0), pipeline_mode=pl.Buffered(1)) for s in grad_shapes],
        out_shape=[moe_shape] * count + [back_shape] * count + grad_shapes,
        scratch_shapes=[
            pltpu.VMEM((2, rows, wide), BF16),
            pltpu.VMEM((2, rows, model), BF16),
            pltpu.VMEM((2, rows, model), BF16),
            pltpu.VMEM((2, rows, wide), BF16),
            pltpu.SemaphoreType.DMA((2, 4)),
            pltpu.SemaphoreType.DMA((2, 2)),
        ],
        compiler_params=pltpu.CompilerParams(vmem_limit_bytes=VMEM_LIMIT),
        cost_estimate=pl.CostEstimate(
            flops=count * 2 * 2800000000 * rows // 512, bytes_accessed=12000000, transcendentals=count * rows * 512
        ),
        name="expert",
    )(meta, up, down, second, *tokens, *grads, *prior)
    return outs[:count], outs[count : 2 * count], outs[2 * count :]


def swap(array, bit, size):
    return lax.ppermute(array, "dp", [(i, i ^ bit) for i in range(size)])


def plane_gather(array, size):
    half = array.shape[0] // 2
    across = {0: array, 2: swap(array, 2, size), 4: swap(array, 4, size)}
    across[6] = jnp.concatenate([swap(across[4][:half], 2, size), swap(across[2][half:], 4, size)], axis=0)
    blocks = [None] * size
    for k in (0, 2, 4, 6):
        blocks[k] = across[k]
        blocks[k + 1] = swap(across[k], 1, size)
    return blocks


def plane_reduce(parts, size):
    def add(*terms):
        total = terms[0].astype(F32)
        for term in terms[1:]:
            total = total + term.astype(F32)
        return total.astype(BF16)

    half = parts[0].shape[0] // 2
    pair = {k: add(parts[k], swap(parts[k + 1], 1, size)) for k in (6, 2, 4, 0)}
    top = add(pair[4][:half], swap(pair[6][:half], 2, size))
    low = add(pair[2][half:], swap(pair[6][half:], 4, size))
    from_x = swap(jnp.concatenate([pair[2][:half], low], axis=0), 2, size)
    from_y = swap(jnp.concatenate([top, pair[4][half:]], axis=0), 4, size)
    return add(pair[0], from_x, from_y)


def dense_gather(shard, me, size):
    along = lax.all_gather(shard, "seq", axis=0)
    depth, rows, width = along.shape
    whole = jnp.zeros((depth, size, rows, width), shard.dtype)
    for k, block in enumerate(plane_gather(along, size)):
        whole = lax.dynamic_update_slice(whole, block[:, None], (0, me ^ k, 0, 0))
    return whole.reshape(depth * size * rows, width)


def pad_rows(array, rows):
    return jnp.pad(array, ((0, rows - array.shape[0]), (0, 0)))


def per_device(
    depth,
    size,
    block_input,
    document_number,
    key_present,
    routes,
    sequence_adapter,
    output_gradient,
    norm_scale_pair,
    query_key_value_weight,
    attention_output_weight,
    router_weight,
    shared_gate_up_weight,
    shared_down_weight,
    routed_gate_up_weight,
    routed_down_weight,
    dense_first_factor,
    shared_down_first_factor,
    dense_second_factor,
    routed_first_factor,
    routed_down_first_factor,
    routed_second_factor,
):
    _, rows, model = block_input.shape
    me = lax.axis_index("dp")
    experts = router_weight.shape[1]
    local_experts = routed_gate_up_weight.shape[0]
    shard_rows = query_key_value_weight.shape[0]
    shared_rows = shared_down_weight.shape[0]
    rank_all = dense_second_factor.shape[0]
    second_columns = dense_second_factor.shape[1]
    query_width = HEADS * HEAD_DIM
    kv_width = KV_HEADS * HEAD_DIM
    hops = min(depth - 1, -(-(DOCUMENT_SPAN - 1) // rows))
    rank = ADAPTER_RANK

    adapters_all = lax.all_gather(sequence_adapter, "dp", axis=0, tiled=True)
    adapter = sequence_adapter[0]

    pack_one = jnp.concatenate(
        [
            query_key_value_weight,
            dense_first_factor.reshape(shard_rows, 6 * rank_all),
            dense_second_factor.T.reshape(shard_rows, second_columns * rank_all // shard_rows),
            jnp.pad(
                jnp.concatenate([router_weight, norm_scale_pair.T], axis=1), ((0, 0), (0, LANES - experts - 2))
            ),
        ],
        axis=1,
    )
    pack_two = jnp.concatenate(
        [
            attention_output_weight,
            shared_gate_up_weight.reshape(shard_rows, 2 * SHARED_HIDDEN),
            pad_rows(jnp.concatenate([shared_down_weight, shared_down_first_factor], axis=1), shard_rows),
        ],
        axis=1,
    )
    one = dense_gather(pack_one, me, size)
    two = dense_gather(pack_two, me, size)
    qkv_w = one[:, : query_width + 2 * kv_width]
    offset = query_width + 2 * kv_width
    first_all = one[:, offset : offset + 6 * rank_all].reshape(model, 6, rank_all)
    offset += 6 * rank_all
    second_width = second_columns * rank_all // shard_rows
    second_t = one[:, offset : offset + second_width].reshape(depth * size * second_columns, rank_all)
    offset += second_width
    router_w = one[:, offset : offset + experts]
    gains = one[:, offset + experts : offset + experts + 2].astype(F32).T
    out_w = two[:, :model]
    sgu_w = two[:, model : model + 2 * SHARED_HIDDEN]
    shared_down = two[:, model + 2 * SHARED_HIDDEN :].reshape(depth * size, shard_rows, model + rank_all)
    shared_down = shared_down[:, :shared_rows].reshape(SHARED_HIDDEN, model + rank_all)
    sdown_w = shared_down[:, :model]
    first = lax.dynamic_slice_in_dim(first_all, adapter * rank, rank, 2)
    first_down = lax.dynamic_slice_in_dim(shared_down[:, model:], adapter * rank, rank, 1)
    second = lax.dynamic_slice_in_dim(second_t, adapter * rank, rank, 1).T
    widths = [query_width, kv_width, kv_width, model, SHARED_HIDDEN, SHARED_HIDDEN, model]
    edges = [sum(widths[:n]) for n in range(len(widths) + 1)]
    b_parts = [second[:, edges[n] : edges[n + 1]] for n in range(len(widths))]

    second_experts = lax.all_gather(routed_second_factor, "seq", axis=2, tiled=True)
    up_experts, down_experts = [], []
    for j in range(local_experts):
        up_shard = jnp.concatenate(
            [
                routed_gate_up_weight[j].reshape(-1, 2 * EXPERT_HIDDEN),
                routed_first_factor[j].reshape(-1, 2 * rank_all),
            ],
            axis=1,
        )
        up_experts.append(lax.all_gather(up_shard, "seq", axis=0, tiled=True))
        down_shard = jnp.concatenate([routed_down_weight[j], routed_down_first_factor[j]], axis=1)
        down_experts.append(lax.all_gather(down_shard, "seq", axis=0, tiled=True))

    grad_out_b = output_gradient[0]
    grad_blocks = plane_gather(grad_out_b, size)

    present_tag = jnp.where(key_present == 1, document_number, -1).astype(F32)
    tag_blocks = [
        lax.ppermute(present_tag + 1.0, "seq", [(i, i + h) for i in range(depth - h)]) - 1.0 for h in range(hops, 0, -1)
    ] + [present_tag]
    key_tag = jnp.concatenate(tag_blocks, axis=1).reshape((hops + 1) * rows, 1)
    query_tag = document_number.astype(F32)

    x_flat = block_input[0].astype(F32)
    normed = rms_norm(x_flat, gains[0]).astype(BF16)
    qkv_low = dot_nn(normed, first[:, 0:3].reshape(model, 3 * rank)).astype(BF16)
    qkv_extra = jnp.concatenate([dot_nn(qkv_low[:, n * rank : (n + 1) * rank], b_parts[n]) for n in range(3)], axis=1)
    qkv = (dot_nn(normed, qkv_w) + qkv_extra).astype(BF16)
    own_kv = qkv[:, query_width:]
    kv_blocks = [own_kv]
    for _ in range(hops):
        kv_blocks.append(lax.ppermute(kv_blocks[-1], "seq", [(i, i + 1) for i in range(depth - 1)]))
    kv_all = jnp.concatenate(kv_blocks[::-1], axis=0)
    attn, lse = attend(qkv, kv_all, query_tag, key_tag, hops)
    out_low = dot_nn(attn, first[:, 3]).astype(BF16)
    mid = x_flat + dot_nn(attn, out_w) + dot_nn(out_low, b_parts[3])
    normed2 = rms_norm(mid, gains[1]).astype(BF16)

    logits = dot_nn(normed2, router_w)
    route_rows = routes[0]
    flags = jnp.sum((route_rows[..., None] == jnp.arange(experts, dtype=jnp.int32)).astype(F32), axis=1)
    before = (jnp.arange(rows)[:, None] > jnp.arange(rows)[None, :]).astype(BF16)
    ranks = dot_nn(before, flags.astype(BF16))
    slots = jnp.where(flags > 0, ranks, -1.0)
    top = jnp.max(jnp.where(flags > 0, logits, -jnp.inf), axis=-1, keepdims=True)
    weights = jnp.where(flags > 0, jnp.exp(logits - top), 0.0)
    gates = weights / jnp.sum(weights, axis=-1, keepdims=True)
    gates_hi = gates.astype(BF16)
    gates_lo = (gates - gates_hi.astype(F32)).astype(BF16)
    extra = jnp.concatenate([slots.astype(BF16), gates_hi, gates_lo], axis=1)
    payload = jnp.concatenate([normed2, jnp.pad(extra, ((0, 0), (0, LANES - 3 * experts)))], axis=1)
    token_blocks = plane_gather(payload, size)

    shared_low = dot_nn(normed2, first[:, 4:6].reshape(model, 2 * rank)).astype(BF16)
    shared_gu = dot_nn(normed2, sgu_w) + jnp.concatenate(
        [dot_nn(shared_low[:, :rank], b_parts[4]), dot_nn(shared_low[:, rank:], b_parts[5])], axis=1
    )
    shared_hidden = swiglu(shared_gu).astype(BF16)
    sdown_low = dot_nn(shared_hidden, first_down).astype(BF16)
    y_shared = dot_nn(shared_hidden, sdown_w) + dot_nn(sdown_low, b_parts[6])
    grad_out = grad_out_b.astype(F32)
    glow_sdown = dot_nt(grad_out_b, b_parts[6]).astype(BF16)
    grad_b_sdown = dot_tn(sdown_low, grad_out_b)
    grad_a_sdown = dot_tn(shared_hidden, glow_sdown)
    grad_shared_hidden = dot_nt(grad_out_b, sdown_w) + dot_nt(glow_sdown, first_down)
    _, swiglu_back = jax.vjp(swiglu, shared_gu)
    grad_sgu = swiglu_back(grad_shared_hidden)[0].astype(BF16)
    glow_sgu = jnp.concatenate(
        [dot_nt(grad_sgu[:, :SHARED_HIDDEN], b_parts[4]), dot_nt(grad_sgu[:, SHARED_HIDDEN:], b_parts[5])], axis=1
    ).astype(BF16)
    grad_b_sgu = [
        dot_tn(shared_low[:, :rank], grad_sgu[:, :SHARED_HIDDEN]),
        dot_tn(shared_low[:, rank:], grad_sgu[:, SHARED_HIDDEN:]),
    ]
    grad_a_sgu = dot_tn(normed2, glow_sgu)
    grad_normed2 = dot_nt(grad_sgu, sgu_w) + dot_nt(glow_sgu, first[:, 4:6].reshape(model, 2 * rank))

    groups = ((6, 7, 2, 3), (4, 5, 1, 0))
    moe_parts, back_parts = [None] * size, [None] * size
    grads_first, grads_down, grads_second = [], [], []
    for j in range(local_experts):
        sums = None
        for group in groups:
            meta = jnp.stack([me * local_experts + j] + [adapters_all[me ^ k] for k in group]).astype(jnp.int32)
            prior = None if j == 0 else ([moe_parts[k] for k in group], [back_parts[k] for k in group])
            moe_out, back_out, grads = expert_call(
                meta,
                up_experts[j],
                down_experts[j],
                second_experts[j],
                [token_blocks[k] for k in group],
                [grad_blocks[k] for k in group],
                prior,
                experts,
            )
            for n, k in enumerate(group):
                moe_parts[k], back_parts[k] = moe_out[n], back_out[n]
            sums = grads if sums is None else [a + b for a, b in zip(sums, grads)]
        grads_first.append(sums[0])
        grads_down.append(sums[1])
        grads_second.append(sums[2])
    back = plane_reduce(back_parts, size).astype(F32)
    moe = plane_reduce(moe_parts, size).astype(F32)
    hidden_out = (mid + moe + y_shared).astype(BF16)[None]

    owner_rows = model // depth
    first_sum = jnp.stack(grads_first).astype(BF16).transpose(0, 2, 1)
    grad_expert_a = lax.psum_scatter(first_sum, "seq", scatter_dimension=1, tiled=True).astype(F32)
    grad_expert_a = grad_expert_a.reshape(local_experts, owner_rows, 2, rank_all)
    down_sum = jnp.stack(grads_down).astype(BF16).transpose(0, 2, 1)
    grad_expert_a_down = lax.psum_scatter(down_sum, "seq", scatter_dimension=1, tiled=True).astype(F32)
    second_sum = jnp.stack(grads_second).astype(BF16)
    grad_expert_b = lax.psum_scatter(second_sum, "seq", scatter_dimension=2, tiled=True).astype(F32)

    grad_gates = back[:, model : model + experts] + back[:, model + experts : model + 2 * experts]
    grad_logits = gates * (grad_gates - jnp.sum(gates * grad_gates, axis=-1, keepdims=True))
    grad_normed2 = grad_normed2 + back[:, :model]
    grad_normed2 = grad_normed2 + jnp.einsum(
        "re,de->rd", grad_logits, router_w.astype(F32), precision=lax.Precision.HIGHEST
    )
    _, norm2_back = jax.vjp(lambda values_in: rms_norm(values_in, gains[1]), mid)
    grad_mid = grad_out + norm2_back(grad_normed2)[0]
    grad_mid_b = grad_mid.astype(BF16)
    glow_out = dot_nt(grad_mid_b, b_parts[3]).astype(BF16)
    grad_b_out = dot_tn(out_low, grad_mid_b)
    grad_a_out = dot_tn(attn, glow_out)
    grad_attn = (dot_nt(grad_mid_b, out_w) + dot_nt(glow_out, first[:, 3])).astype(BF16)

    grad_q, grad_k, grad_v = attend_back(qkv, kv_all, grad_attn, lse, query_tag, key_tag, hops)
    grad_kv = jnp.concatenate([grad_k, grad_v], axis=1)
    moving = None
    for h in range(hops + 1):
        part = grad_kv[h * rows : (h + 1) * rows].astype(F32)
        if moving is not None:
            part = part + lax.ppermute(moving, "seq", [(i + 1, i) for i in range(depth - 1)]).astype(F32)
        moving = part.astype(BF16)
    grad_qkv = jnp.concatenate([grad_q, moving], axis=1)
    parts = [grad_qkv[:, edges[n] : edges[n + 1]] for n in range(3)]
    glow_qkv = jnp.concatenate([dot_nt(parts[n], b_parts[n]) for n in range(3)], axis=1).astype(BF16)
    grad_b_qkv = [dot_tn(qkv_low[:, n * rank : (n + 1) * rank], parts[n]) for n in range(3)]
    grad_a_qkv = dot_tn(normed, glow_qkv)
    grad_normed = dot_nt(grad_qkv, qkv_w) + dot_nt(glow_qkv, first[:, 0:3].reshape(model, 3 * rank))
    _, norm1_back = jax.vjp(lambda values_in: rms_norm(values_in, gains[0]), x_flat)
    grad_hidden = (grad_mid + norm1_back(grad_normed)[0])[None]

    first_compact = jnp.concatenate([grad_a_qkv, grad_a_out, grad_a_sgu], axis=1)
    second_compact = jnp.concatenate(grad_b_qkv + [grad_b_out] + grad_b_sgu + [grad_b_sdown], axis=1)
    compact = jnp.concatenate(
        [
            first_compact.reshape(depth * size, shard_rows * 6 * rank),
            grad_a_sdown.reshape(depth * size, shared_rows * rank),
            second_compact.T.reshape(depth * size, second_columns * rank),
        ],
        axis=1,
    ).reshape(depth, size, -1)
    compact = lax.psum_scatter(compact, "seq", scatter_dimension=0, tiled=True)[0]
    compact = lax.all_to_all(compact, "dp", split_axis=0, concat_axis=0, tiled=True)
    of_adapter = (adapters_all[:, None] == jnp.arange(rank_all // rank, dtype=jnp.int32)[None, :]).astype(F32)
    spread = jnp.sum(of_adapter[:, :, None] * compact[:, None, :], axis=0)
    cut_one = shard_rows * 6 * rank
    cut_two = cut_one + shared_rows * rank
    grad_first = spread[:, :cut_one].reshape(-1, shard_rows, 6, rank).transpose(1, 2, 0, 3)
    grad_first = grad_first.reshape(shard_rows, 6, rank_all)
    grad_first_down = spread[:, cut_one:cut_two].reshape(-1, shared_rows, rank).transpose(1, 0, 2)
    grad_first_down = grad_first_down.reshape(shared_rows, rank_all)
    grad_second = spread[:, cut_two:].reshape(-1, second_columns, rank).transpose(0, 2, 1)
    grad_second = grad_second.reshape(rank_all, second_columns)
    return (
        hidden_out,
        grad_hidden,
        grad_first,
        grad_first_down,
        grad_second,
        grad_expert_a,
        grad_expert_a_down,
        grad_expert_b,
    )


def solution(mesh):
    in_specs = (
        P("dp", "seq", None),
        P("dp", "seq"),
        P("dp", "seq"),
        P("dp", "seq", None),
        P("dp"),
        P("dp", "seq", None),
        P(None, ("seq", "dp")),
        P(("seq", "dp"), None),
        P(("seq", "dp"), None),
        P(("seq", "dp"), None),
        P(("seq", "dp"), None, None),
        P(("seq", "dp"), None),
        P("dp", "seq", None, None),
        P("dp", "seq", None),
        P(("seq", "dp"), None, None),
        P(("seq", "dp"), None),
        P(None, ("seq", "dp")),
        P("dp", "seq", None, None),
        P("dp", "seq", None),
        P("dp", None, "seq"),
    )
    out_specs = (
        P("dp", "seq", None),
        P("dp", "seq", None),
        P(("seq", "dp"), None, None),
        P(("seq", "dp"), None),
        P(None, ("seq", "dp")),
        P("dp", "seq", None, None),
        P("dp", "seq", None),
        P("dp", None, "seq"),
    )
    return jax.shard_map(
        functools.partial(per_device, mesh.shape["seq"], mesh.shape["dp"]),
        mesh=mesh,
        in_specs=in_specs,
        out_specs=out_specs,
        check_vma=False,
    )
```

time: 2230 us -> 1050 us (0.47)
  blocking collectives: 454 us -> 25.3 us
  matrix products: 496 us -> 110 us
  local copies, waits for them, and re-layouts: 509 us -> 146 us
  Pallas kernels: 0 us -> 233 us
  waiting for transfers between devices: 604 us -> 371 us
  starting transfers between devices: 26.5 us -> 80 us
  other arithmetic: 110 us -> 56.9 us
    all_gather x8 -> x0, blocking collectives: 454 us -> none  [the longest x1 169 us: dense_gather(): lax.all_gather(shared_down_first_factor, ('seq', 'dp'), axis=0, tiled=True)]
    dot_general x109 -> x44, matrix products: 496 us -> 110 us  [the longest x15 47.5 us: dot_nt(): lax.dot_general(left, right, (((1,), (1,)), ((), ())), preferred_element_...]
    ppermute x0 -> x54, waiting for transfers between devices: none -> 345 us  [the longest x48 261 us: swap(): return lax.ppermute(array, 'dp', [(i, i ^ bit) for i in range(size)])]
    gather x6 -> x0, local copies, waits for them, and re-layouts: 322 us -> none  [pick_rows(): return matrix[indices]]
    pallas_call x0 -> x6, Pallas kernels: none -> 233 us  [the longest x4 176 us: expert_call(): pl.pallas_call(functools.partial(expert_kernel, count, experts, bool(prio...]
    all_to_all x5 -> x1, waiting for transfers between devices: 187 us -> 2.4 us  [per_device(): lax.all_to_all(compact, 'dp', split_axis=0, concat_axis=0, tiled=True)]
    all_gather x14 -> x7, waiting for transfers between devices: 191 us -> 17.3 us  [the longest x2 17.2 us: dense_gather(): along = lax.all_gather(shard, 'seq', axis=0)]
    unnamed x22 -> x14, waiting for transfers between devices: 112 us -> 0.85 us
  transfers between devices with their start and end apart: 25 -> 66, of which waited for: 10 -> 22; matrix products, arithmetic and copies ran while one was open for 48% -> 28% of each run, Pallas kernels for 0% -> 22%
where the time goes in v1:
time: 1050 us; the launch traced here: 1040 us
  waiting for transfers between devices  371 us (35%)
  Pallas kernels  233 us (22%)
  local copies, waits for them, and re-layouts  146 us (14%)
  matrix products  110 us (10%)
  starting transfers between devices  80 us (8%)
  other arithmetic  56.9 us (5%)
  blocking collectives  25.3 us (2%)
  between operations  16.7 us (2%)
    ppermute x48, waiting for transfers between devices, swap(): return lax.ppermute(array, 'dp', [(i, i ^ bit) for i in range(size)])  261 us
    pallas_call x4, Pallas kernels, expert_call(): pl.pallas_call(functools.partial(expert_kernel, count, experts, bool(prio...  176 us
    unnamed x237, local copies, waits for them, and re-layouts  58.5 us
    ppermute x2, waiting for transfers between devices, per_device(): lax.ppermute(kv_blocks[-1], 'seq', [(i, i + 1) for i in range(depth - 1)])  50 us
    dot_general x15, matrix products, dot_nt(): lax.dot_general(left, right, (((1,), (1,)), ((), ())), preferred_element_...  47.5 us
    dot_general x17, matrix products, dot_nn(): return jnp.dot(left, right, preferred_element_type=F32)  41.7 us
    ppermute x48, starting transfers between devices, swap(): return lax.ppermute(array, 'dp', [(i, i ^ bit) for i in range(size)])  39 us
    ppermute x2, waiting for transfers between devices, per_device(): lax.ppermute(moving, 'seq', [(i + 1, i) for i in range(depth - 1)])  34.6 us
  transfers between devices with their start and end apart: 66, of which 22 were waited for; matrix products, arithmetic and copies ran while one was open for 28% of the time, Pallas kernels for 22%

profile of v1, /device:TPU:0, one launch (start us, length us, event | category | flops | bytes accessed | tf_op | source)
XLA Modules:
  0.0 1039.0 jit_solution(3732748459275037631)
XLA Ops:
  22.6 3.5 collective-permute-start.11
  26.1 4.5 collective-permute-start.10
  34.0 25.3 %all-reduce.5 = s32[8]{0:T(128)S(1)} all-reduce(s32[8]{0:T(128)S(1)} %dynamic-update-slice), channel_id=1, replica_groups=mesh['seq'=4,'dp'=8] {'dp'}, use_global_device_ids=true, to_apply=%add.5 | all-reduce | flops 8 | bytes 64
  64.2 3.3 stack.60.refs_0_
  85.2 11.2 %collective-permute-done.32 = bf16[256,1536]{1,0:T(8,128)(2,1)} collective-permute-done((bf16[256,1536]{1,0:T(8,128)(2,1)S(1)}, bf16[256,1536]{1,0:T(8,128)(2,1)}, u32[]{:S(2)}, u32[]{:S(2)}) %collective-permute-start.32) | collective-permute-done | bytes 786464 | tf_op jit(solution)/shard_map/ppermute | solution.py:367
  103.6 6.2 broadcast_in_dim.92
  111.1 17.2 %all-gather.22.cloned.1.call-done = bf16[192,5248]{1,0:T(8,128)(2,1)} async-done(((bf16[48,5248]{1,0:T(8,128)(2,1)}), bf16[192,5248]{1,0:T(8,128)(2,1)}) %all-gather.22.cloned.1.call-update) | async-done | bytes 2015248 | tf_op jit(solution)/shard_map/all_gather | solution.py:398
  137.7 55.6 %collective-permute-done.5 = bf16[2,48,4096]{2,1,0:T(8,128)(2,1)S(1)} collective-permute-done((bf16[2,48,4096]{2,1,0:T(8,128)(2,1)S(1)}, bf16[2,48,4096]{2,1,0:T(8,128)(2,1)S(1)}, u32[]{:S(2)}, u32[]{:S(2)}) %collective-permute-start.5) | collective-permute-done | bytes 786464 | tf_op jit(solution)/shard_map/ppermute | solution.py:367
  195.8 41.2 %collective-permute-done.15 = bf16[4,48,5248]{2,1,0:T(8,128)(2,1)} collective-permute-done((bf16[4,48,5248]{2,1,0:T(8,128)(2,1)S(1)}, bf16[4,48,5248]{2,1,0:T(8,128)(2,1)}, u32[]{:S(2)}, u32[]{:S(2)}) %collective-permute-start.15) | collective-permute-done | bytes 2015264 | tf_op jit(solution)/shard_map/ppermute | solution.py:367
  249.3 14.3 %collective-permute-done.17 = bf16[2,48,5248]{2,1,0:T(8,128)(2,1)S(1)} collective-permute-done((bf16[2,48,5248]{2,1,0:T(8,128)(2,1)S(1)}, bf16[2,48,5248]{2,1,0:T(8,128)(2,1)S(1)}, u32[]{:S(2)}, u32[]{:S(2)}) %collective-permute-start.17) | collective-permute-done | bytes 1007648 | tf_op jit(solution)/shard_map/ppermute | solution.py:367
  264.7 3.6 collective-permute-done.18
  269.9 4.1 copy-done.6
  289.4 10.7 %fusion.8.q_ref = bf16[512,2560]{1,0:T(8,128)(2,1)} fusion(f32[512,512]{1,0:T(8,128)} %fusion.135, f32[512,512]{1,0:T(8,128)} %fusion.138, f32[512,1536]{1,0:T(8,128)} %fusion.108, bf16[1536,4096]{1,0:T(8,128)(2,1)} %bitcast.248, bf16[1,512,1536]{2,1,0:T(8,128)(2,1)S(1)} %copy-done.18, f32[1536]{0:T(1024)S(1)} %get-tuple-element.139, f32[512]{0:T(512)S(1)} %fusion.161), kind=kOutput, calls=%fused_computation.9 | convolution fusion | flops 4034920448 | bytes 17309696 | tf_op jit(solution)/shard_map/dot_general | solution.py:31
  313.8 34.8 %collective-permute-done.8 = bf16[512,1024]{1,0:T(8,128)(2,1)S(1)} collective-permute-done((bf16[512,1024]{1,0:T(8,128)(2,1)S(1)}, bf16[512,1024]{1,0:T(8,128)(2,1)S(1)}, u32[]{:S(2)}, u32[]{:S(2)}) %collective-permute-start.8) | collective-permute-done | bytes 1048608 | tf_op jit(solution)/shard_map/ppermute | solution.py:524
  348.6 24.2 %collective-permute-start.9 = (bf16[512,1024]{1,0:T(8,128)(2,1)S(1)}, bf16[512,1024]{1,0:T(8,128)(2,1)}, u32[]{:S(2)}, u32[]{:S(2)}) collective-permute-start(bf16[512,1024]{1,0:T(8,128)(2,1)S(1)} %collective-permute-done.8), channel_id=1, source_target_pairs={{0,8},{8,16},{16,24},{1,9},{9,17},{17,25},{2,10},{10,18},{18,26},{... | collective-permute-start | bytes 3145736 | tf_op jit(solution)/shard_map/ppermute | solution.py:524
  375.4 4.9 copy-done.3
  380.3 5.8 fusion.60
  386.1 15.3 %collective-permute-done.9 = bf16[512,1024]{1,0:T(8,128)(2,1)} collective-permute-done((bf16[512,1024]{1,0:T(8,128)(2,1)S(1)}, bf16[512,1024]{1,0:T(8,128)(2,1)}, u32[]{:S(2)}, u32[]{:S(2)}) %collective-permute-start.9) | collective-permute-done | bytes 1048608 | tf_op jit(solution)/shard_map/ppermute | solution.py:524
  401.4 3.4 pad_maximum_fusion.k_ref.v_ref
  404.7 23.5 %attend.1 = (bf16[512,1536]{1,0:T(8,128)(2,1)}, f32[4,3,512]{2,1,0:T(4,128)}) custom-call(bf16[512,2560]{1,0:T(8,128)(2,1)} %fusion.8.q_ref, bf16[1536,1024]{1,0:T(8,128)(2,1)} %pad_maximum_fusion.k_ref.v_ref, bf16[1536,1024]{1,0:T(8,128)(2,1)} %pad_maximum_fusion.k_ref.v_ref, f32[1,512]{1,0:T(1,128)} %convert_element_type.278.qt_ref, f32[1536,1]{1,0:T(8,128)} %copy.124.kt_ref), custom_call_target="tpu_custom_call" | custom-call | flops 4831838208 | bytes 6291456 | tf_op jit(solution)/shard_map/attend/pallas_call | solution.py:95
  431.9 4.7 multiply_reduce_fusion.1
  448.9 5.8 maximum_add_fusion.1
  458.3 22.8 %collective-permute-done.20.refs_4_ = bf16[512,1664]{1,0:T(8,128)(2,1)} collective-permute-done((bf16[512,1664]{1,0:T(8,128)(2,1)S(1)}, bf16[512,1664]{1,0:T(8,128)(2,1)}, u32[]{:S(2)}, u32[]{:S(2)}) %collective-permute-start.20) | collective-permute-done | bytes 1703968 | tf_op jit(solution)/shard_map/ppermute | solution.py:367
  491.2 11.0 %collective-permute-done.27 = bf16[256,1664]{1,0:T(8,128)(2,1)S(1)} collective-permute-done((bf16[256,1664]{1,0:T(8,128)(2,1)S(1)}, bf16[256,1664]{1,0:T(8,128)(2,1)S(1)}, u32[]{:S(2)}, u32[]{:S(2)}) %collective-permute-start.27) | collective-permute-done | bytes 852000 | tf_op jit(solution)/shard_map/ppermute | solution.py:367
  504.3 3.3 convolution_add_fusion
  508.5 12.4 %collective-permute-done.29 = bf16[256,1664]{1,0:T(8,128)(2,1)S(1)} collective-permute-done((bf16[256,1664]{1,0:T(8,128)(2,1)S(1)}, bf16[256,1664]{1,0:T(8,128)(2,1)S(1)}, u32[]{:S(2)}, u32[]{:S(2)}) %collective-permute-start.29) | collective-permute-done | bytes 852000 | tf_op jit(solution)/shard_map/ppermute | solution.py:367
  524.8 43.3 %expert.4 = (bf16[512,1536]{1,0:T(8,128)(2,1)}, bf16[512,1536]{1,0:T(8,128)(2,1)}, bf16[512,1536]{1,0:T(8,128)(2,1)}, bf16[512,1536]{1,0:T(8,128)(2,1)}, bf16[51...) custom-call(s32[5]{0:T(128)} %stack.59.refs_0_, ...), custom_call_target="tpu_custom_call" | custom-call | flops 22400000000 | bytes 12000000 | tf_op jit(solution)/shard_map/expert/pallas_call | solution.py:341
  568.2 44.7 %expert.5 = (bf16[512,1536]{1,0:T(8,128)(2,1)}, bf16[512,1536]{1,0:T(8,128)(2,1)}, bf16[512,1536]{1,0:T(8,128)(2,1)}, bf16[512,1536]{1,0:T(8,128)(2,1)}, bf16[51...) custom-call(s32[5]{0:T(128)} %stack.57.refs_0_, ...), custom_call_target="tpu_custom_call" | custom-call | flops 22400000000 | bytes 12000000 | tf_op jit(solution)/shard_map/expert/pallas_call | solution.py:341
  614.0 43.4 %expert.6 = (bf16[512,1536]{1,0:T(8,128)(2,1)}, bf16[512,1536]{1,0:T(8,128)(2,1)}, bf16[512,1536]{1,0:T(8,128)(2,1)}, bf16[512,1536]{1,0:T(8,128)(2,1)}, bf16[51...) custom-call(s32[5]{0:T(128)} %stack.61.refs_0_, ...), custom_call_target="tpu_custom_call" | custom-call | flops 22400000000 | bytes 12000000 | tf_op jit(solution)/shard_map/expert/pallas_call | solution.py:341
  657.5 44.8 %expert.7 = (bf16[512,1536]{1,0:T(8,128)(2,1)}, bf16[512,1536]{1,0:T(8,128)(2,1)}, bf16[512,1536]{1,0:T(8,128)(2,1)}, bf16[512,1536]{1,0:T(8,128)(2,1)}, bf16[51...) custom-call(s32[5]{0:T(128)} %stack.60.refs_0_, ...), custom_call_target="tpu_custom_call" | custom-call | flops 22400000000 | bytes 12000000 | tf_op jit(solution)/shard_map/expert/pallas_call | solution.py:341
  729.0 17.8 %collective-permute-done.47 = bf16[256,1664]{1,0:T(8,128)(2,1)S(1)} collective-permute-done((bf16[256,1664]{1,0:T(8,128)(2,1)S(1)}, bf16[256,1664]{1,0:T(8,128)(2,1)S(1)}, u32[]{:S(2)}, u32[]{:S(2)}) %collective-permute-start.47) | collective-permute-done | bytes 852000 | tf_op jit(solution)/shard_map/ppermute | solution.py:367
  752.0 15.3 %collective-permute-done.39 = bf16[256,1536]{1,0:T(8,128)(2,1)S(1)} collective-permute-done((bf16[256,1536]{1,0:T(8,128)(2,1)S(1)}, bf16[256,1536]{1,0:T(8,128)(2,1)S(1)}, u32[]{:S(2)}, u32[]{:S(2)}) %collective-permute-start.39) | collective-permute-done | bytes 786464 | tf_op jit(solution)/shard_map/ppermute | solution.py:367
  769.9 34.2 %collective-permute-done.42 = bf16[256,1536]{1,0:T(8,128)(2,1)S(1)} collective-permute-done((bf16[256,1536]{1,0:T(8,128)(2,1)S(1)}, bf16[256,1536]{1,0:T(8,128)(2,1)S(1)}, u32[]{:S(2)}, u32[]{:S(2)}) %collective-permute-start.42) | collective-permute-done | bytes 786464 | tf_op jit(solution)/shard_map/ppermute | solution.py:367
  810.0 4.3 fusion.100
  814.3 9.3 multiply_reduce_fusion
  823.7 15.4 %collective-permute-done.40 = bf16[512,1536]{1,0:T(8,128)(2,1)} collective-permute-done((bf16[512,1536]{1,0:T(8,128)(2,1)}, bf16[512,1536]{1,0:T(8,128)(2,1)}, u32[]{:S(2)}, u32[]{:S(2)}) %collective-permute-start.40) | collective-permute-done | bytes 1572896 | tf_op jit(solution)/shard_map/ppermute | solution.py:367
  841.4 5.8 fusion.52
  850.1 6.2 fusion.57.g_ref
  856.3 33.1 %attend_back.1 = (bf16[512,1536]{1,0:T(8,128)(2,1)}, bf16[1536,512]{1,0:T(8,128)(2,1)}, bf16[1536,512]{1,0:T(8,128)(2,1)}) custom-call(bf16[512,2560]{1,0:T(8,128)(2,1)} %fusion.8.q_ref, bf16[1536,1024]{1,0:T(8,128)(2,1)} %pad_maximum_fusion.k_ref.v_ref, bf16[1536,1024]{1,0:T(8,128)(2,1)} %pad_maximum_fusion.k_ref.v_ref, bf16[512,1536]{1,0:T(8,128)(2,1)} %fusion.57.g_ref, ...), custom_call_target="tpu_custom_call" | custom-call | flops 12079595520 | bytes 12582912 | tf_op jit(solution)/shard_map/attend_back/pallas_call | solution.py:157
  903.3 16.4 %collective-permute-done.52 = bf16[512,1024]{1,0:T(8,128)(2,1)} collective-permute-done((bf16[512,1024]{1,0:T(8,128)(2,1)}, bf16[512,1024]{1,0:T(8,128)(2,1)}, u32[]{:S(2)}, u32[]{:S(2)}) %collective-permute-start.52) | collective-permute-done | bytes 1048608 | tf_op jit(solution)/shard_map/ppermute | solution.py:627
  925.2 4.9 copy.155
  938.9 18.2 %collective-permute-done.53 = bf16[512,1024]{1,0:T(8,128)(2,1)} collective-permute-done((bf16[512,1024]{1,0:T(8,128)(2,1)}, bf16[512,1024]{1,0:T(8,128)(2,1)}, u32[]{:S(2)}, u32[]{:S(2)}) %collective-permute-start.53) | collective-permute-done | bytes 1048608 | tf_op jit(solution)/shard_map/ppermute | solution.py:627
  976.5 3.4 copy.139
  979.9 3.8 concatenate.126
  999.8 9.9 fusion.49
  1009.7 5.1 reduce-scatter.11.cloned.1.call-done
  1016.8 3.8 all-to-all-start
  1020.6 4.8 fusion.54
  (522 shorter events, 262.0 us)
Async XLA Ops:
  7.2 75.0 %all-gather.14.cloned.1.call-start = ((), (), s32[]{:S(2)}) async-start(), calls=%async_computation.7 | async-start | bytes 1638400 | tf_op jit(solution)/shard_map/all_gather | solution.py:492
  8.0 76.7 %all-gather.20.cloned.1.call-start = ((), (), s32[]{:S(2)}) async-start(), calls=%async_computation.11 | async-start | bytes 1966080 | tf_op jit(solution)/shard_map/all_gather | solution.py:398
  11.5 116.8 %all-gather.22.cloned.1.call-start = ((), (), s32[]{:S(2)}) async-start(), calls=%async_computation.12 | async-start | bytes 2519040 | tf_op jit(solution)/shard_map/all_gather | solution.py:398
  13.4 511.4 %all-gather.18.cloned.1.call-start = ((), (), s32[]{:S(2)}) async-start(), calls=%async_computation.9 | async-start | bytes 2129920 | tf_op jit(solution)/shard_map/all_gather | solution.py:504
  14.4 510.4 %all-gather.16.cloned.1.call-start = ((), (), s32[]{:S(2)}) async-start(), calls=%async_computation.8 | async-start | bytes 4915200 | tf_op jit(solution)/shard_map/all_gather | solution.py:502
  17.1 551.0 %all-gather.12.cloned.1.call-start = ((), (), s32[]{:S(2)}) async-start(), calls=%async_computation.6 | async-start | bytes 2129920 | tf_op jit(solution)/shard_map/all_gather | solution.py:504
  18.0 550.2 %all-gather.10.cloned.1.call-start = ((), (), s32[]{:S(2)}) async-start(), calls=%async_computation.5 | async-start | bytes 4915200 | tf_op jit(solution)/shard_map/all_gather | solution.py:502
  18.0 56.5 %collective-permute-start.23 = (bf16[512,1536]{1,0:T(8,128)(2,1)}, bf16[512,1536]{1,0:T(8,128)(2,1)}, u32[]{:S(2)}, u32[]{:S(2)}) collective-permute-start(bf16[512,1536]{1,0:T(8,128)(2,1)} %bitcast.48.refs_11_), channel_id=1, source_target_pairs={{0,4},{1,5},{2,6},{3,7},{4,0},{5,1},{6,2},{7,3},{8,12},{9,13},{10,... | collective-permute-start | bytes 4718600 | tf_op jit(solution)/shard_map/ppermute | solution.py:367
  21.1 57.6 %collective-permute-start.33 = (bf16[512,1536]{1,0:T(8,128)(2,1)}, bf16[512,1536]{1,0:T(8,128)(2,1)}, u32[]{:S(2)}, u32[]{:S(2)}) collective-permute-start(bf16[512,1536]{1,0:T(8,128)(2,1)} %bitcast.48.refs_11_), channel_id=1, source_target_pairs={{0,2},{1,3},{2,0},{3,1},{4,6},{5,7},{6,4},{7,5},{8,10},{9,11},{10,... | collective-permute-start | bytes 4718600 | tf_op jit(solution)/shard_map/ppermute | solution.py:367
  22.6 52.0 %collective-permute-start.11 = (f32[1,512]{1,0:T(1,128)S(1)}, f32[1,512]{1,0:T(1,128)S(1)}, u32[]{:S(2)}, u32[]{:S(2)}) collective-permute-start(f32[1,512]{1,0:T(1,128)S(1)} %get-tuple-element.145), channel_id=1, source_target_pairs={{0,8},{8,16},{16,24},{1,9},{9,17},{17,25},{2,10},{10,18},{18,26},{... | collective-permute-start | bytes 6152 | tf_op jit(solution)/shard_map/ppermute | solution.py:511
  26.1 48.5 %collective-permute-start.10 = (f32[1,512]{1,0:T(1,128)S(1)}, f32[1,512]{1,0:T(1,128)S(1)}, u32[]{:S(2)}, u32[]{:S(2)}) collective-permute-start(f32[1,512]{1,0:T(1,128)S(1)} %get-tuple-element.145), channel_id=1, source_target_pairs={{0,16},{8,24},{1,17},{9,25},{2,18},{10,26},{3,19},{11,27},{4,20},{... | collective-permute-start | bytes 6152 | tf_op jit(solution)/shard_map/ppermute | solution.py:511
  30.6 491.4 %collective-permute-start.25 = (bf16[512,1536]{1,0:T(8,128)(2,1)}, bf16[512,1536]{1,0:T(8,128)(2,1)}, u32[]{:S(2)}, u32[]{:S(2)}) collective-permute-start(bf16[512,1536]{1,0:T(8,128)(2,1)} %bitcast.48.refs_11_), channel_id=1, source_target_pairs={{0,1},{1,0},{2,3},{3,2},{4,5},{5,4},{6,7},{7,6},{8,9},{9,8},{10,11... | collective-permute-start | bytes 4718600 | tf_op jit(solution)/shard_map/ppermute | solution.py:367
  33.9 952.2 %reduce-scatter.15.cloned.1.call-start = ((), (), s32[]{:S(2)}) async-start(), calls=%async_computation.14 | async-start | bytes 327680
  84.7 49.6 %collective-permute-start = (bf16[4,48,4096]{2,1,0:T(8,128)(2,1)}, bf16[4,48,4096]{2,1,0:T(8,128)(2,1)}, u32[]{:S(2)}, u32[]{:S(2)}) collective-permute-start(bf16[4,48,4096]{2,1,0:T(8,128)(2,1)} %bitcast.276), channel_id=1, source_target_pairs={{0,1},{1,0},{2,3},{3,2},{4,5},{5,4},{6,7},{7,6},{8,9},{9,8},{10,11... | collective-permute-start | bytes 4718600 | tf_op jit(solution)/shard_map/ppermute | solution.py:367
  84.7 48.1 %collective-permute-start.1 = (bf16[4,48,4096]{2,1,0:T(8,128)(2,1)}, bf16[4,48,4096]{2,1,0:T(8,128)(2,1)S(1)}, u32[]{:S(2)}, u32[]{:S(2)}) collective-permute-start(bf16[4,48,4096]{2,1,0:T(8,128)(2,1)} %bitcast.277), channel_id=1, source_target_pairs={{0,2},{1,3},{2,0},{3,1},{4,6},{5,7},{6,4},{7,5},{8,10},{9,11},{10,... | collective-permute-start | bytes 4718600 | tf_op jit(solution)/shard_map/ppermute | solution.py:367
  96.4 35.6 %collective-permute-start.3 = (bf16[4,48,4096]{2,1,0:T(8,128)(2,1)}, bf16[4,48,4096]{2,1,0:T(8,128)(2,1)S(1)}, u32[]{:S(2)}, u32[]{:S(2)}) collective-permute-start(bf16[4,48,4096]{2,1,0:T(8,128)(2,1)} %bitcast.278), channel_id=1, source_target_pairs={{0,4},{1,5},{2,6},{3,7},{4,0},{5,1},{6,2},{7,3},{8,12},{9,13},{10,... | collective-permute-start | bytes 4718600 | tf_op jit(solution)/shard_map/ppermute | solution.py:367
  128.3 66.7 %collective-permute-start.12 = (bf16[4,48,5248]{2,1,0:T(8,128)(2,1)}, bf16[4,48,5248]{2,1,0:T(8,128)(2,1)S(1)}, u32[]{:S(2)}, u32[]{:S(2)}) collective-permute-start(bf16[4,48,5248]{2,1,0:T(8,128)(2,1)} %bitcast.270), channel_id=1, source_target_pairs={{0,1},{1,0},{2,3},{3,2},{4,5},{5,4},{6,7},{7,6},{8,9},{9,8},{10,11... | collective-permute-start | bytes 6045704 | tf_op jit(solution)/shard_map/ppermute | solution.py:367
  132.0 106.3 %collective-permute-start.13 = (bf16[4,48,5248]{2,1,0:T(8,128)(2,1)S(1)}, bf16[4,48,5248]{2,1,0:T(8,128)(2,1)}, u32[]{:S(2)}, u32[]{:S(2)}) collective-permute-start(bf16[4,48,5248]{2,1,0:T(8,128)(2,1)S(1)} %bitcast.272), channel_id=1, source_target_pairs={{0,2},{1,3},{2,0},{3,1},{4,6},{5,7},{6,4},{7,5},{8,10},{9,11},{10,... | collective-permute-start | bytes 6045704 | tf_op jit(solution)/shard_map/ppermute | solution.py:367
  132.8 60.5 %collective-permute-start.5 = (bf16[2,48,4096]{2,1,0:T(8,128)(2,1)S(1)}, bf16[2,48,4096]{2,1,0:T(8,128)(2,1)S(1)}, u32[]{:S(2)}, u32[]{:S(2)}) collective-permute-start(bf16[2,48,4096]{2,1,0:T(8,128)(2,1)S(1)} %slice.312), channel_id=1, source_target_pairs={{0,2},{1,3},{2,0},{3,1},{4,6},{5,7},{6,4},{7,5},{8,10},{9,11},{10,... | collective-permute-start | bytes 2359304 | tf_op jit(solution)/shard_map/ppermute | solution.py:367
  134.2 60.6 %collective-permute-start.6 = (bf16[2,48,4096]{2,1,0:T(8,128)(2,1)S(1)}, bf16[2,48,4096]{2,1,0:T(8,128)(2,1)S(1)}, u32[]{:S(2)}, u32[]{:S(2)}) collective-permute-start(bf16[2,48,4096]{2,1,0:T(8,128)(2,1)S(1)} %slice.313), channel_id=1, source_target_pairs={{0,4},{1,5},{2,6},{3,7},{4,0},{5,1},{6,2},{7,3},{8,12},{9,13},{10,... | collective-permute-start | bytes 2359304 | tf_op jit(solution)/shard_map/ppermute | solution.py:367
  193.3 43.7 %collective-permute-start.15 = (bf16[4,48,5248]{2,1,0:T(8,128)(2,1)S(1)}, bf16[4,48,5248]{2,1,0:T(8,128)(2,1)}, u32[]{:S(2)}, u32[]{:S(2)}) collective-permute-start(bf16[4,48,5248]{2,1,0:T(8,128)(2,1)S(1)} %bitcast.273), channel_id=1, source_target_pairs={{0,4},{1,5},{2,6},{3,7},{4,0},{5,1},{6,2},{7,3},{8,12},{9,13},{10,... | collective-permute-start | bytes 6045704 | tf_op jit(solution)/shard_map/ppermute | solution.py:367
  194.9 48.9 %collective-permute-start.2 = (bf16[4,48,4096]{2,1,0:T(8,128)(2,1)S(1)}, bf16[4,48,4096]{2,1,0:T(8,128)(2,1)S(1)}, u32[]{:S(2)}, u32[]{:S(2)}) collective-permute-start(bf16[4,48,4096]{2,1,0:T(8,128)(2,1)S(1)} %collective-permute-done.1), channel_id=1, source_target_pairs={{0,1},{1,0},{2,3},{3,2},{4,5},{5,4},{6,7},{7,6},{8,9},{9,8},{10,11... | collective-permute-start | bytes 4718600 | tf_op jit(solution)/shard_map/ppermute | solution.py:367
  195.0 50.8 %collective-permute-start.4 = (bf16[4,48,4096]{2,1,0:T(8,128)(2,1)S(1)}, bf16[4,48,4096]{2,1,0:T(8,128)(2,1)S(1)}, u32[]{:S(2)}, u32[]{:S(2)}) collective-permute-start(bf16[4,48,4096]{2,1,0:T(8,128)(2,1)S(1)} %collective-permute-done.3), channel_id=1, source_target_pairs={{0,1},{1,0},{2,3},{3,2},{4,5},{5,4},{6,7},{7,6},{8,9},{9,8},{10,11... | collective-permute-start | bytes 4718600 | tf_op jit(solution)/shard_map/ppermute | solution.py:367
  245.8 60.5 %collective-permute-start.14 = (bf16[4,48,5248]{2,1,0:T(8,128)(2,1)}, bf16[4,48,5248]{2,1,0:T(8,128)(2,1)}, u32[]{:S(2)}, u32[]{:S(2)}) collective-permute-start(bf16[4,48,5248]{2,1,0:T(8,128)(2,1)} %collective-permute-done.13), channel_id=1, source_target_pairs={{0,1},{1,0},{2,3},{3,2},{4,5},{5,4},{6,7},{7,6},{8,9},{9,8},{10,11... | collective-permute-start | bytes 6045704 | tf_op jit(solution)/shard_map/ppermute | solution.py:367
  263.6 46.6 %collective-permute-start.16 = (bf16[4,48,5248]{2,1,0:T(8,128)(2,1)}, bf16[4,48,5248]{2,1,0:T(8,128)(2,1)}, u32[]{:S(2)}, u32[]{:S(2)}) collective-permute-start(bf16[4,48,5248]{2,1,0:T(8,128)(2,1)} %collective-permute-done.15), channel_id=1, source_target_pairs={{0,1},{1,0},{2,3},{3,2},{4,5},{5,4},{6,7},{7,6},{8,9},{9,8},{10,11... | collective-permute-start | bytes 6045704 | tf_op jit(solution)/shard_map/ppermute | solution.py:367
  269.3 103.6 %collective-permute-start.19 = (bf16[4,48,5248]{2,1,0:T(8,128)(2,1)}, bf16[4,48,5248]{2,1,0:T(8,128)(2,1)}, u32[]{:S(2)}, u32[]{:S(2)}) collective-permute-start(bf16[4,48,5248]{2,1,0:T(8,128)(2,1)} %constant_dynamic-update-slice_fusion.2), channel_id=1, source_target_pairs={{0,1},{1,0},{2,3},{3,2},{4,5},{5,4},{6,7},{7,6},{8,9},{9,8},{10,11... | collective-permute-start | bytes 6045704 | tf_op jit(solution)/shard_map/ppermute | solution.py:367
  301.4 47.2 %collective-permute-start.8 = (bf16[512,1024]{1,0:T(8,128)(2,1)S(1)}, bf16[512,1024]{1,0:T(8,128)(2,1)S(1)}, u32[]{:S(2)}, u32[]{:S(2)}) collective-permute-start(bf16[512,1024]{1,0:T(8,128)(2,1)S(1)} %slice.325), channel_id=1, source_target_pairs={{0,8},{8,16},{16,24},{1,9},{9,17},{17,25},{2,10},{10,18},{18,26},{... | collective-permute-start | bytes 3145736 | tf_op jit(solution)/shard_map/ppermute | solution.py:524
  348.6 52.8 %collective-permute-start.9 = (bf16[512,1024]{1,0:T(8,128)(2,1)S(1)}, bf16[512,1024]{1,0:T(8,128)(2,1)}, u32[]{:S(2)}, u32[]{:S(2)}) collective-permute-start(bf16[512,1024]{1,0:T(8,128)(2,1)S(1)} %collective-permute-done.8), channel_id=1, source_target_pairs={{0,8},{8,16},{16,24},{1,9},{9,17},{17,25},{2,10},{10,18},{18,26},{... | collective-permute-start | bytes 3145736 | tf_op jit(solution)/shard_map/ppermute | solution.py:524
  442.1 39.0 %collective-permute-start.20 = (bf16[512,1664]{1,0:T(8,128)(2,1)S(1)}, bf16[512,1664]{1,0:T(8,128)(2,1)}, u32[]{:S(2)}, u32[]{:S(2)}) collective-permute-start(bf16[512,1664]{1,0:T(8,128)(2,1)S(1)} %pad_maximum_fusion.1.refs_7_), channel_id=1, source_target_pairs={{0,4},{1,5},{2,6},{3,7},{4,0},{5,1},{6,2},{7,3},{8,12},{9,13},{10,... | collective-permute-start | bytes 5111816 | tf_op jit(solution)/shard_map/ppermute | solution.py:367
  443.9 43.7 %collective-permute-start.28 = (bf16[512,1664]{1,0:T(8,128)(2,1)S(1)}, bf16[512,1664]{1,0:T(8,128)(2,1)}, u32[]{:S(2)}, u32[]{:S(2)}) collective-permute-start(bf16[512,1664]{1,0:T(8,128)(2,1)S(1)} %pad_maximum_fusion.1.refs_7_), channel_id=1, source_target_pairs={{0,2},{1,3},{2,0},{3,1},{4,6},{5,7},{6,4},{7,5},{8,10},{9,11},{10,... | collective-permute-start | bytes 5111816 | tf_op jit(solution)/shard_map/ppermute | solution.py:367
  445.4 77.1 %collective-permute-start.22 = (bf16[512,1664]{1,0:T(8,128)(2,1)S(1)}, bf16[512,1664]{1,0:T(8,128)(2,1)S(1)}, u32[]{:S(2)}, u32[]{:S(2)}) collective-permute-start(bf16[512,1664]{1,0:T(8,128)(2,1)S(1)} %pad_maximum_fusion.1.refs_7_), channel_id=1, source_target_pairs={{0,1},{1,0},{2,3},{3,2},{4,5},{5,4},{6,7},{7,6},{8,9},{9,8},{10,11... | collective-permute-start | bytes 5111816 | tf_op jit(solution)/shard_map/ppermute | solution.py:367
  485.3 39.5 %collective-permute-start.21 = (bf16[512,1664]{1,0:T(8,128)(2,1)}, bf16[512,1664]{1,0:T(8,128)(2,1)}, u32[]{:S(2)}, u32[]{:S(2)}) collective-permute-start(bf16[512,1664]{1,0:T(8,128)(2,1)} %collective-permute-done.20.refs_4_), channel_id=1, source_target_pairs={{0,1},{1,0},{2,3},{3,2},{4,5},{5,4},{6,7},{7,6},{8,9},{9,8},{10,11... | collective-permute-start | bytes 5111816 | tf_op jit(solution)/shard_map/ppermute | solution.py:367
  487.6 34.8 %collective-permute-start.24 = (bf16[512,1536]{1,0:T(8,128)(2,1)}, bf16[512,1536]{1,0:T(8,128)(2,1)S(1)}, u32[]{:S(2)}, u32[]{:S(2)}) collective-permute-start(bf16[512,1536]{1,0:T(8,128)(2,1)} %collective-permute-done.23.refs_8_), channel_id=1, source_target_pairs={{0,1},{1,0},{2,3},{3,2},{4,5},{5,4},{6,7},{7,6},{8,9},{9,8},{10,11... | collective-permute-start | bytes 4718600 | tf_op jit(solution)/shard_map/ppermute | solution.py:367
  521.0 92.5 %collective-permute-start.36 = (bf16[512,1536]{1,0:T(8,128)(2,1)}, bf16[512,1536]{1,0:T(8,128)(2,1)}, u32[]{:S(2)}, u32[]{:S(2)}) collective-permute-start(bf16[512,1536]{1,0:T(8,128)(2,1)} %collective-permute-done.33.refs_10_), channel_id=1, source_target_pairs={{0,1},{1,0},{2,3},{3,2},{4,5},{5,4},{6,7},{7,6},{8,9},{9,8},{10,11... | collective-permute-start | bytes 4718600 | tf_op jit(solution)/shard_map/ppermute | solution.py:367
  521.9 91.6 %collective-permute-start.35 = (bf16[512,1536]{1,0:T(8,128)(2,1)}, bf16[512,1536]{1,0:T(8,128)(2,1)}, u32[]{:S(2)}, u32[]{:S(2)}) collective-permute-start(bf16[512,1536]{1,0:T(8,128)(2,1)} %constant_dynamic-update-slice_fusion.6.refs_8_), channel_id=1, source_target_pairs={{0,1},{1,0},{2,3},{3,2},{4,5},{5,4},{6,7},{7,6},{8,9},{9,8},{10,11... | collective-permute-start | bytes 4718600 | tf_op jit(solution)/shard_map/ppermute | solution.py:367
  522.4 91.5 %collective-permute-start.31 = (bf16[512,1664]{1,0:T(8,128)(2,1)}, bf16[512,1664]{1,0:T(8,128)(2,1)}, u32[]{:S(2)}, u32[]{:S(2)}) collective-permute-start(bf16[512,1664]{1,0:T(8,128)(2,1)} %collective-permute-done.28.refs_6_), channel_id=1, source_target_pairs={{0,1},{1,0},{2,3},{3,2},{4,5},{5,4},{6,7},{7,6},{8,9},{9,8},{10,11... | collective-permute-start | bytes 5111816 | tf_op jit(solution)/shard_map/ppermute | solution.py:367
  524.8 89.2 %collective-permute-start.30 = (bf16[512,1664]{1,0:T(8,128)(2,1)}, bf16[512,1664]{1,0:T(8,128)(2,1)}, u32[]{:S(2)}, u32[]{:S(2)}) collective-permute-start(bf16[512,1664]{1,0:T(8,128)(2,1)} %constant_dynamic-update-slice_fusion.4.refs_4_), channel_id=1, source_target_pairs={{0,1},{1,0},{2,3},{3,2},{4,5},{5,4},{6,7},{7,6},{8,9},{9,8},{10,11... | collective-permute-start | bytes 5111816 | tf_op jit(solution)/shard_map/ppermute | solution.py:367
  612.9 103.7 %collective-permute-start.41 = (bf16[512,1536]{1,0:T(8,128)(2,1)}, bf16[512,1536]{1,0:T(8,128)(2,1)}, u32[]{:S(2)}, u32[]{:S(2)}) collective-permute-start(bf16[512,1536]{1,0:T(8,128)(2,1)} %get-tuple-element.81), channel_id=1, source_target_pairs={{0,1},{1,0},{2,3},{3,2},{4,5},{5,4},{6,7},{7,6},{8,9},{9,8},{10,11... | collective-permute-start | bytes 4718600 | tf_op jit(solution)/shard_map/ppermute | solution.py:367
  613.4 105.8 %collective-permute-start.49 = (bf16[512,1664]{1,0:T(8,128)(2,1)}, bf16[512,1664]{1,0:T(8,128)(2,1)}, u32[]{:S(2)}, u32[]{:S(2)}) collective-permute-start(bf16[512,1664]{1,0:T(8,128)(2,1)} %get-tuple-element.89), channel_id=1, source_target_pairs={{0,1},{1,0},{2,3},{3,2},{4,5},{5,4},{6,7},{7,6},{8,9},{9,8},{10,11... | collective-permute-start | bytes 5111816 | tf_op jit(solution)/shard_map/ppermute | solution.py:367
  613.5 193.1 %collective-permute-start.44 = (bf16[512,1664]{1,0:T(8,128)(2,1)}, bf16[512,1664]{1,0:T(8,128)(2,1)}, u32[]{:S(2)}, u32[]{:S(2)}) collective-permute-start(bf16[512,1664]{1,0:T(8,128)(2,1)} %get-tuple-element.83), channel_id=1, source_target_pairs={{0,1},{1,0},{2,3},{3,2},{4,5},{5,4},{6,7},{7,6},{8,9},{9,8},{10,11... | collective-permute-start | bytes 5111816 | tf_op jit(solution)/shard_map/ppermute | solution.py:367
  613.9 209.8 %collective-permute-start.26 = (bf16[512,1536]{1,0:T(8,128)(2,1)}, bf16[512,1536]{1,0:T(8,128)(2,1)}, u32[]{:S(2)}, u32[]{:S(2)}) collective-permute-start(bf16[512,1536]{1,0:T(8,128)(2,1)} %get-tuple-element.67), channel_id=1, source_target_pairs={{0,1},{1,0},{2,3},{3,2},{4,5},{5,4},{6,7},{7,6},{8,9},{9,8},{10,11... | collective-permute-start | bytes 4718600 | tf_op jit(solution)/shard_map/ppermute | solution.py:367
  707.8 280.1 %reduce-scatter.17.cloned.1.call-start = ((), (), s32[]{:S(2)}) async-start(), calls=%async_computation.15 | async-start | bytes 1638400
  716.3 276.0 %reduce-scatter.13.cloned.1.call-start = ((), (), s32[]{:S(2)}) async-start(), calls=%async_computation.13 | async-start | bytes 1966080
  748.8 58.4 %collective-permute-start.48 = (bf16[512,1664]{1,0:T(8,128)(2,1)S(1)}, bf16[512,1664]{1,0:T(8,128)(2,1)S(1)}, u32[]{:S(2)}, u32[]{:S(2)}) collective-permute-start(bf16[512,1664]{1,0:T(8,128)(2,1)S(1)} %pad_maximum_fusion.2), channel_id=1, source_target_pairs={{0,2},{1,3},{2,0},{3,1},{4,6},{5,7},{6,4},{7,5},{8,10},{9,11},{10,... | collective-permute-start | bytes 5111816 | tf_op jit(solution)/shard_map/ppermute | solution.py:367
  750.3 56.9 %collective-permute-start.51 = (bf16[512,1664]{1,0:T(8,128)(2,1)S(1)}, bf16[512,1664]{1,0:T(8,128)(2,1)S(1)}, u32[]{:S(2)}, u32[]{:S(2)}) collective-permute-start(bf16[512,1664]{1,0:T(8,128)(2,1)S(1)} %pad_maximum_fusion.3), channel_id=1, source_target_pairs={{0,4},{1,5},{2,6},{3,7},{4,0},{5,1},{6,2},{7,3},{8,12},{9,13},{10,... | collective-permute-start | bytes 5111816 | tf_op jit(solution)/shard_map/ppermute | solution.py:367
  767.3 36.8 %collective-permute-start.42 = (bf16[256,1536]{1,0:T(8,128)(2,1)S(1)}, bf16[256,1536]{1,0:T(8,128)(2,1)S(1)}, u32[]{:S(2)}, u32[]{:S(2)}) collective-permute-start(bf16[256,1536]{1,0:T(8,128)(2,1)S(1)} %get-tuple-element.155), channel_id=1, source_target_pairs={{0,2},{1,3},{2,0},{3,1},{4,6},{5,7},{6,4},{7,5},{8,10},{9,11},{10,... | collective-permute-start | bytes 2359304 | tf_op jit(solution)/shard_map/ppermute | solution.py:367
  804.1 35.0 %collective-permute-start.40 = (bf16[512,1536]{1,0:T(8,128)(2,1)}, bf16[512,1536]{1,0:T(8,128)(2,1)}, u32[]{:S(2)}, u32[]{:S(2)}) collective-permute-start(bf16[512,1536]{1,0:T(8,128)(2,1)} %pad_maximum_fusion.4), channel_id=1, source_target_pairs={{0,2},{1,3},{2,0},{3,1},{4,6},{5,7},{6,4},{7,5},{8,10},{9,11},{10,... | collective-permute-start | bytes 4718600 | tf_op jit(solution)/shard_map/ppermute | solution.py:367
  933.1 81.7 %reduce-scatter.11.cloned.1.call-start = ((), (), s32[]{:S(2)}) async-start(), calls=%async_computation.10 | async-start | bytes 1433600 | tf_op jit(solution)/shard_map/reduce_scatter | solution.py:648
  (121 other events, 1991.8 us)
Sparse Core Ops, SparseCore 0:
  9.7 34.9 all-gather.13
  46.2 36.5 all-gather.19
  85.0 43.2 all-gather.21
  129.7 38.0 all-gather.17
  169.2 75.2 all-gather.15
  245.9 37.7 all-gather.11
  285.4 100.3 all-gather.9
  707.9 21.5 reduce-scatter.14
  731.9 29.4 reduce-scatter.16
  933.2 40.8 reduce-scatter.12
  986.2 28.5 reduce-scatter.10

commit v2 on v1

v2 whole, which is shorter than its diff:
```python
import functools
import math

import jax
import jax.numpy as jnp
from jax import lax
from jax.experimental import pallas as pl
from jax.experimental.pallas import tpu as pltpu
from jax.sharding import PartitionSpec as P

HEADS = 12
KV_HEADS = 4
HEAD_DIM = 128
EXPERT_HIDDEN = 512
SHARED_HIDDEN = 1024
ADAPTER_RANK = 16
DOCUMENT_SPAN = 1024

EPSILON = 1e-05
MASKED_SCORE = -1e30
LOG2E = 1.4426950408889634
SCALE = HEAD_DIM ** (-0.5)
LANES = 128
VMEM_LIMIT = 60 * 1024 * 1024

F32 = jnp.float32
BF16 = jnp.bfloat16


def dot_nn(left, right):
    return jnp.dot(left, right, preferred_element_type=F32)


def dot_tn(left, right):
    return lax.dot_general(left, right, (((0,), (0,)), ((), ())), preferred_element_type=F32)


def dot_nt(left, right):
    return lax.dot_general(left, right, (((1,), (1,)), ((), ())), preferred_element_type=F32)


def rms_norm(values, gain):
    return values * lax.rsqrt(jnp.mean(values * values, axis=-1, keepdims=True) + EPSILON) * gain


def cost(microseconds):
    return pl.CostEstimate(flops=int(1153500000 * microseconds), bytes_accessed=1000000, transcendentals=0)


def query_tiles(rows, hops):
    tile = math.gcd(rows, 256)
    spans = []
    for first in range(0, rows, tile):
        oldest = max(0, hops * rows + first - (DOCUMENT_SPAN - 1)) // tile * tile
        spans.append((first, tile, oldest, hops * rows + first + tile - oldest))
    return spans


def fill_bias(spans, shift, query_tag, key_tag, bias):
    for first, tile, oldest, span in spans:
        keys = oldest + lax.broadcasted_iota(jnp.int32, (span, tile), 0)
        queries = shift + first + lax.broadcasted_iota(jnp.int32, (span, tile), 1)
        same = key_tag[oldest : oldest + span, :] == query_tag[:, first : first + tile]
        permit = (keys <= queries) & (same | (keys == queries))
        bias[oldest : oldest + span, first : first + tile] = jnp.where(permit, 0.0, MASKED_SCORE)


def attend_kernel(spans, shift, waits, q_ref, k_ref, v_ref, qt_ref, kt_ref, *rest):
    out_ref, lse_ref, bias = rest[waits:]

    @pl.when(pl.program_id(0) == 0)
    def _():
        fill_bias(spans, shift, qt_ref, kt_ref, bias)

    groups = q_ref.shape[1] // HEAD_DIM
    for first, tile, oldest, span in spans:
        keys = k_ref[oldest : oldest + span, :]
        values = v_ref[oldest : oldest + span, :]
        mask = bias[oldest : oldest + span, first : first + tile]
        for h in range(groups):
            columns = slice(h * HEAD_DIM, (h + 1) * HEAD_DIM)
            scores = dot_nt(keys, q_ref[first : first + tile, columns]) * (SCALE * LOG2E) + mask
            top = jnp.max(scores, axis=0, keepdims=True)
            weights = jnp.exp2(scores - top)
            total = jnp.sum(weights, axis=0, keepdims=True)
            mixed = dot_tn(values, weights.astype(BF16)) / total
            out_ref[first : first + tile, columns] = mixed.T.astype(BF16)
            lse_ref[0, h : h + 1, first : first + tile] = top + jnp.log2(total)


def attend(query, kv_all, query_tag, key_tag, hops, deps=()):
    rows = query.shape[0]
    groups = HEADS // KV_HEADS
    span = kv_all.shape[0]
    spans = query_tiles(rows, hops)
    return pl.pallas_call(
        functools.partial(attend_kernel, spans, hops * rows, len(deps)),
        grid=(KV_HEADS,),
        in_specs=[
            pl.BlockSpec((rows, groups * HEAD_DIM), lambda g: (0, g)),
            pl.BlockSpec((span, HEAD_DIM), lambda g: (0, g)),
            pl.BlockSpec((span, HEAD_DIM), lambda g: (0, KV_HEADS + g)),
            pl.BlockSpec((1, rows), lambda g: (0, 0)),
            pl.BlockSpec((span, 1), lambda g: (0, 0)),
        ]
        + [pl.BlockSpec(memory_space=pl.ANY)] * len(deps),
        out_specs=[
            pl.BlockSpec((rows, groups * HEAD_DIM), lambda g: (0, g)),
            pl.BlockSpec((1, groups, rows), lambda g: (g, 0, 0)),
        ],
        out_shape=[
            jax.ShapeDtypeStruct((rows, HEADS * HEAD_DIM), BF16),
            jax.ShapeDtypeStruct((KV_HEADS, groups, rows), F32),
        ],
        scratch_shapes=[pltpu.VMEM((span, rows), F32)],
        compiler_params=pltpu.CompilerParams(vmem_limit_bytes=VMEM_LIMIT),
        cost_estimate=cost(23.0),
        name="attend",
    )(query, kv_all, kv_all, query_tag, key_tag, *deps)


def attend_back_kernel(
    spans, shift, waits, q_ref, k_ref, v_ref, g_ref, lse_ref, qt_ref, kt_ref, *rest
):
    dq_ref, dkv_ref, bias, dk_acc, dv_acc = rest[waits:]

    @pl.when(pl.program_id(0) == 0)
    def _():
        fill_bias(spans, shift, qt_ref, kt_ref, bias)

    dk_acc[...] = jnp.zeros_like(dk_acc)
    dv_acc[...] = jnp.zeros_like(dv_acc)
    groups = q_ref.shape[1] // HEAD_DIM
    for first, tile, oldest, span in spans:
        keys = k_ref[oldest : oldest + span, :]
        values = v_ref[oldest : oldest + span, :]
        mask = bias[oldest : oldest + span, first : first + tile]
        for h in range(groups):
            columns = slice(h * HEAD_DIM, (h + 1) * HEAD_DIM)
            query = q_ref[first : first + tile, columns]
            grad = g_ref[first : first + tile, columns]
            lse = lse_ref[0, h : h + 1, first : first + tile]
            probs = jnp.exp2(dot_nt(keys, query) * (SCALE * LOG2E) + mask - lse)
            dv_acc[oldest : oldest + span, :] += dot_nn(probs.astype(BF16), grad)
            grad_probs = dot_nt(values, grad)
            delta = jnp.sum(probs * grad_probs, axis=0, keepdims=True)
            grad_scores = (probs * (grad_probs - delta)).astype(BF16)
            dk_acc[oldest : oldest + span, :] += dot_nn(grad_scores, query) * SCALE
            dq_ref[first : first + tile, columns] = (dot_tn(grad_scores, keys) * SCALE).astype(BF16)
    dkv_ref[:, :HEAD_DIM] = dk_acc[...].astype(dkv_ref.dtype)
    dkv_ref[:, HEAD_DIM:] = dv_acc[...].astype(dkv_ref.dtype)


def attend_back(query, kv_all, grad_attn, lse, query_tag, key_tag, hops, head, count, deps=()):
    rows = query.shape[0]
    groups = HEADS // KV_HEADS
    span = kv_all.shape[0]
    spans = query_tiles(rows, hops)
    return pl.pallas_call(
        functools.partial(attend_back_kernel, spans, hops * rows, len(deps)),
        grid=(count,),
        in_specs=[
            pl.BlockSpec((rows, groups * HEAD_DIM), lambda g: (0, head + g)),
            pl.BlockSpec((span, HEAD_DIM), lambda g: (0, head + g)),
            pl.BlockSpec((span, HEAD_DIM), lambda g: (0, KV_HEADS + head + g)),
            pl.BlockSpec((rows, groups * HEAD_DIM), lambda g: (0, head + g)),
            pl.BlockSpec((1, groups, rows), lambda g: (head + g, 0, 0)),
            pl.BlockSpec((1, rows), lambda g: (0, 0)),
            pl.BlockSpec((span, 1), lambda g: (0, 0)),
        ]
        + [pl.BlockSpec(memory_space=pl.ANY)] * len(deps),
        out_specs=[
            pl.BlockSpec((rows, groups * HEAD_DIM), lambda g: (0, g)),
            pl.BlockSpec((span, 2 * HEAD_DIM), lambda g: (0, g)),
        ],
        out_shape=[
            jax.ShapeDtypeStruct((rows, count * groups * HEAD_DIM), BF16),
            jax.ShapeDtypeStruct((span, count * 2 * HEAD_DIM), BF16),
        ],
        scratch_shapes=[
            pltpu.VMEM((span, rows), F32),
            pltpu.VMEM((span, HEAD_DIM), F32),
            pltpu.VMEM((span, HEAD_DIM), F32),
        ],
        compiler_params=pltpu.CompilerParams(vmem_limit_bytes=VMEM_LIMIT),
        cost_estimate=cost(2.0 * count),
        name="attend_back",
    )(query, kv_all, kv_all, grad_attn, lse, query_tag, key_tag, *deps)


BACK_ROWS = 2 * ADAPTER_RANK


def expert_kernel(count, splits, experts, capacity, with_prior, with_shared, waits, *refs):
    meta, refs = refs[0], refs[1:]
    weight_count = 5 if with_shared else 3
    weight_refs, refs = refs[:weight_count], refs[weight_count:]
    token_refs, grad_refs = [], []
    for split in splits:
        token_refs.append(refs[:split])
        refs = refs[split:]
    for split in splits:
        grad_refs.append(refs[:split])
        refs = refs[split:]
    prior_moe, prior_back = (), ()
    if with_prior:
        prior_moe, refs = refs[:count], refs[count:]
        prior_back, refs = refs[:count], refs[count:]
    refs = refs[waits:]
    moe_refs, refs = refs[:count], refs[count:]
    back_refs, refs = refs[:count], refs[count:]
    grad_count = 4 if with_shared else 3
    grad_outs, refs = refs[:grad_count], refs[grad_count:]
    grad_sums, refs = refs[:grad_count], refs[grad_count:]
    first_grad, down_grad, second_grad = grad_sums[:3]
    weight_bufs, refs = refs[:weight_count], refs[weight_count:]
    tokens_buf, grad_buf, moe_buf, back_buf, in_sem, out_sem, weight_sem, sum_sem = refs

    step = pl.program_id(0)
    steps = count // 2
    slots = min(2, steps)
    slot = lax.rem(step, slots)
    rows, wide = tokens_buf.shape[2:]
    model = wide - LANES
    hidden = EXPERT_HIDDEN
    rank = ADAPTER_RANK
    up_ref, down_ref, second_ref = weight_bufs[:3]

    def weight_copy(n):
        return pltpu.make_async_copy(weight_refs[n], weight_bufs[n], weight_sem.at[n])

    def incoming(k, i, kinds):
        copies = []
        to, source = k % slots, 2 * k + i
        for n, (refs_of, buf) in enumerate(((token_refs, tokens_buf), (grad_refs, grad_buf))):
            size = rows // len(refs_of[source])
            for p, piece in enumerate(refs_of[source] if n in kinds else ()):
                part = buf.at[to, i, pl.ds(p * size, size)]
                copies.append(pltpu.make_async_copy(piece, part, in_sem.at[to, i, 2 * n + p]))
        if with_prior and 2 in kinds:
            copies.append(pltpu.make_async_copy(prior_moe[source], moe_buf.at[to, i], in_sem.at[to, i, 4]))
            copies.append(pltpu.make_async_copy(prior_back[source], back_buf.at[to, i], in_sem.at[to, i, 5]))
        return copies

    def outgoing(k, i, kinds=(0, 1)):
        at, source = k % slots, 2 * k + i
        pairs = ((moe_buf, moe_refs), (back_buf, back_refs))
        return [pltpu.make_async_copy(pairs[n][0].at[at, i], pairs[n][1][source], out_sem.at[at, i, n]) for n in kinds]

    def at_step(action, first=0, last=steps):
        for k in range(first, last):
            pl.when(step == k)(functools.partial(action, k))

    def wait_in(i, kind):
        def action(k):
            for copy in incoming(k, i, (kind,)):
                copy.wait()

        at_step(action)

    def start_out(i, n):
        at_step(lambda k: outgoing(k, i, (n,))[0].start())

    def turn(k):
        for i in (0, 1):
            if k >= 1:
                for copy in outgoing(k - 1, i):
                    copy.wait()
            if k + 1 < steps:
                for copy in incoming(k + 1, i, (0, 1, 2)):
                    copy.start()

    def sum_copy(n):
        return pltpu.make_async_copy(grad_sums[n], grad_outs[n], sum_sem.at[n])

    @pl.when(step == 0)
    def _():
        for i in (0, 1):
            for copy in incoming(0, i, (0,)):
                copy.start()
        for i in (0, 1):
            for copy in incoming(0, i, (1,)):
                copy.start()
        for n in range(weight_count):
            weight_copy(n).start()
        for i in (0, 1):
            for copy in incoming(0, i, (2,)):
                copy.start()
        for total in grad_sums:
            total[...] = jnp.zeros_like(total)

    expert = meta[0]
    lane = lax.broadcasted_iota(jnp.int32, (1, LANES), 1)
    sub = lax.broadcasted_iota(jnp.int32, (LANES, 1), 0)
    places, picks, gates_of, selects, adapters = [], [], [], [], []
    inputs, grad_rows = [], []
    for i in (0, 1):
        wait_in(i, 0)
        extra_b = tokens_buf[slot, i, :, model:]
        extra = extra_b.astype(F32)
        own = 3 * experts + 3 * rank
        adapter = extra[0:1, own : own + 1]
        select = ((lane // rank).astype(F32) == adapter).astype(F32)
        slot_column = jnp.sum(jnp.where(lane == expert, extra, 0.0), axis=1, keepdims=True)
        slot_row = jnp.sum(jnp.where(sub == expert, extra.T, 0.0), axis=0, keepdims=True)
        place = lax.broadcasted_iota(jnp.int32, (rows, capacity), 1).astype(F32) == slot_column
        pick = lax.broadcasted_iota(jnp.int32, (capacity, rows), 0).astype(F32) == slot_row
        place, pick = place.astype(F32).astype(BF16), pick.astype(F32).astype(BF16)
        picked_extra = dot_nn(pick, extra_b)
        chosen = (lane == experts + expert) | (lane == 2 * experts + expert)
        gates_of.append(jnp.sum(jnp.where(chosen, picked_extra, 0.0), axis=1, keepdims=True))
        inputs.append(dot_nn(pick, tokens_buf[slot, i, :, :model]).astype(BF16))
        picks.append(pick)
        places.append(place)
        adapters.append(adapter)
        selects.append(jnp.broadcast_to(select, (capacity, LANES)))
    for i in (0, 1):
        wait_in(i, 1)
        grad_rows.append(dot_nn(picks[i], grad_buf[slot, i]))
    at_step(turn)
    inputs = jnp.concatenate(inputs, axis=0)
    grad_rows = jnp.concatenate(grad_rows, axis=0)
    gate = jnp.concatenate(gates_of, axis=0)
    select = jnp.concatenate(selects, axis=0)
    select_two = jnp.concatenate([select, select], axis=1)

    @pl.when(step == 0)
    def _():
        for n in range(weight_count):
            weight_copy(n).wait()

    low = (dot_nn(inputs, up_ref[:, 2 * hidden : 2 * hidden + 2 * LANES]) * select_two).astype(BF16)
    gate_part = dot_nn(inputs, up_ref[:, :hidden]) + dot_nn(low[:, :LANES], second_ref[:, :hidden])
    up_part = dot_nn(inputs, up_ref[:, hidden : 2 * hidden]) + dot_nn(low[:, LANES:], second_ref[:, hidden : 2 * hidden])
    sigmoid = 1.0 / (1.0 + jnp.exp(-gate_part))
    silu = gate_part * sigmoid
    act = (silu * up_part).astype(BF16)
    low_down = (dot_nn(act, down_ref[:, model:]) * select).astype(BF16)
    output = (dot_nn(act, down_ref[:, :model]) + dot_nn(low_down, second_ref[:, 2 * hidden :])).astype(BF16).astype(F32)
    grad_gate = jnp.sum(output * grad_rows, axis=1, keepdims=True)
    weighted = (gate * output).astype(BF16)

    grad_y = (gate * grad_rows).astype(BF16)
    glow_down = (dot_nt(grad_y, second_ref[:, 2 * hidden :]) * select).astype(BF16)
    second_grad[:, 2 * hidden :] += dot_tn(low_down, grad_y)
    down_grad[...] += dot_tn(act, glow_down)
    grad_act = dot_nt(grad_y, down_ref[:, :model]) + dot_nt(glow_down, down_ref[:, model:])
    grad_up = (grad_act * silu).astype(BF16)
    grad_gp = (grad_act * up_part * (sigmoid * (1.0 + gate_part * (1.0 - sigmoid)))).astype(BF16)
    glow = jnp.concatenate(
        [
            dot_nt(grad_gp, second_ref[:, :hidden]) * select,
            dot_nt(grad_up, second_ref[:, hidden : 2 * hidden]) * select,
        ],
        axis=1,
    ).astype(BF16)
    second_grad[:, :hidden] += dot_tn(low[:, :LANES], grad_gp)
    second_grad[:, hidden : 2 * hidden] += dot_tn(low[:, LANES:], grad_up)
    first_grad[...] += dot_tn(inputs, glow)
    grad_in = (
        dot_nt(grad_gp, up_ref[:, :hidden])
        + dot_nt(grad_up, up_ref[:, hidden : 2 * hidden])
        + dot_nt(glow, up_ref[:, 2 * hidden : 2 * hidden + 2 * LANES])
    ).astype(BF16)
    gate_hi = grad_gate.astype(BF16).astype(F32)
    gate_lo = grad_gate - gate_hi
    extra_out = (
        jnp.where(lane == expert, gate_hi, 0.0) + jnp.where(lane == experts + expert, gate_lo, 0.0)
    ).astype(BF16)

    @pl.when(step == steps - 1)
    def _():
        for n in range(3):
            sum_copy(n).start()

    for i in (0, 1):
        mine = slice(i * capacity, (i + 1) * capacity)
        wait_in(i, 2)
        moe = dot_nn(places[i], weighted[mine])
        back = dot_nn(places[i], grad_in[mine])
        back_extra = dot_nn(places[i], extra_out[mine])
        if with_prior:
            moe = moe + moe_buf[slot, i].astype(F32)
            back = back + back_buf[slot, i, :rows, :model].astype(F32)
            back_extra = back_extra + back_buf[slot, i, :rows, model:].astype(F32)
        if not with_prior:
            back_buf[slot, i, rows:, :] = jnp.zeros((BACK_ROWS, wide), BF16)
        if with_shared:
            sdown_ref, sb_ref = weight_bufs[3:]
            units = sdown_ref.shape[0]
            first_gate, first_up, first_down = 3 * experts, 3 * experts + rank, 3 * experts + 2 * rank
            tokens = tokens_buf[slot, i, :, :model]
            extra_b = tokens_buf[slot, i, :, model:]
            grads = grad_buf[slot, i]
            offset = (lane - sub).astype(F32) - adapters[i] * float(rank)

            def spread(base):
                inside = (sub >= base) & (sub < base + rank)
                return (inside & (offset == float(-base))).astype(F32).astype(BF16)

            to_gate = dot_nt(spread(first_gate), sb_ref[:units]).astype(BF16)
            to_up = dot_nt(spread(first_up), sb_ref[units:]).astype(BF16)
            to_down = dot_nt(spread(first_down), sdown_ref[:, model:]).astype(BF16)
            shared_up = up_ref[:, 2 * hidden + 2 * LANES :]
            gate_up = dot_nn(tokens, shared_up)
            s_gate = gate_up[:, :units] + dot_nn(extra_b, to_gate)
            s_up = gate_up[:, units:] + dot_nn(extra_b, to_up)
            s_sig = 1.0 / (1.0 + jnp.exp(-s_gate))
            s_silu = s_gate * s_sig
            s_act = (s_silu * s_up).astype(BF16)
            moe = moe + dot_nn(s_act, sdown_ref[:, :model])
            s_grad = dot_nt(grads, sdown_ref[:, :model]) + dot_nn(extra_b, to_down)
            grad_sums[3][...] += dot_tn(s_act, dot_nn(extra_b, spread(first_down)).astype(BF16))
            s_gu = (s_grad * s_silu).astype(BF16)
            s_gg = (s_grad * s_up * (s_sig * (1.0 + s_gate * (1.0 - s_sig)))).astype(BF16)
            back_extra = back_extra + dot_nt(s_act, to_down) + dot_nt(s_gg, to_gate) + dot_nt(s_gu, to_up)
            back = back + dot_nt(jnp.concatenate([s_gg, s_gu], axis=1), shared_up)
            columns = pl.ds(pl.multiple_of(meta[1] * units, units), units)
            grad_bg = dot_tn(extra_b, s_gg)[first_gate : first_gate + rank]
            grad_bu = dot_tn(extra_b, s_gu)[first_up : first_up + rank]
            back_buf[slot, i, rows : rows + rank, columns] = grad_bg.astype(BF16)
            back_buf[slot, i, rows + rank :, columns] = grad_bu.astype(BF16)
        moe_buf[slot, i] = moe.astype(BF16)
        start_out(i, 0)
        back_buf[slot, i, :rows, :model] = back.astype(BF16)
        back_buf[slot, i, :rows, model:] = back_extra.astype(BF16)
        start_out(i, 1)

    @pl.when(step == steps - 1)
    def _():
        for n in range(3, grad_count):
            sum_copy(n).start()
        for i in (0, 1):
            for copy in outgoing(steps - 1, i):
                copy.wait()
        for n in range(grad_count):
            sum_copy(n).wait()


def expert_call(meta, weights, tokens, grads, prior, experts, capacity, deps=()):
    count = len(tokens)
    with_shared = len(weights) > 3
    splits = [len(pieces) for pieces in tokens]
    rows, model = sum(piece.shape[0] for piece in grads[0]), grads[0][0].shape[1]
    wide = model + LANES
    slots = min(2, count // 2)
    anywhere = pl.BlockSpec(memory_space=pl.ANY)
    prior = [] if prior is None else list(prior[0]) + list(prior[1])
    flat = [piece for pieces in tokens for piece in pieces] + [piece for pieces in grads for piece in pieces]
    grad_shapes = [
        jax.ShapeDtypeStruct((model, 2 * LANES), F32),
        jax.ShapeDtypeStruct((EXPERT_HIDDEN, LANES), F32),
        jax.ShapeDtypeStruct(weights[2].shape, F32),
    ]
    if with_shared:
        grad_shapes.append(jax.ShapeDtypeStruct((weights[3].shape[0], LANES), F32))
    back_rows = rows + BACK_ROWS
    outs = pl.pallas_call(
        functools.partial(expert_kernel, count, splits, experts, capacity, bool(prior), with_shared, len(deps)),
        grid=(count // 2,),
        in_specs=[pl.BlockSpec(memory_space=pltpu.SMEM)]
        + [anywhere] * (len(weights) + len(flat) + len(prior) + len(deps)),
        out_specs=[anywhere] * (2 * count + len(grad_shapes)),
        out_shape=[jax.ShapeDtypeStruct((rows, model), BF16)] * count
        + [jax.ShapeDtypeStruct((back_rows, wide), BF16)] * count
        + grad_shapes,
        scratch_shapes=[pltpu.VMEM(s.shape, F32) for s in grad_shapes]
        + [pltpu.VMEM(w.shape, BF16) for w in weights]
        + [
            pltpu.VMEM((slots, 2, rows, wide), BF16),
            pltpu.VMEM((slots, 2, rows, model), BF16),
            pltpu.VMEM((slots, 2, rows, model), BF16),
            pltpu.VMEM((slots, 2, back_rows, wide), BF16),
            pltpu.SemaphoreType.DMA((slots, 2, 6)),
            pltpu.SemaphoreType.DMA((slots, 2, 2)),
            pltpu.SemaphoreType.DMA((len(weights),)),
            pltpu.SemaphoreType.DMA((len(grad_shapes),)),
        ],
        compiler_params=pltpu.CompilerParams(vmem_limit_bytes=VMEM_LIMIT),
        cost_estimate=cost(12.0 * count),
        name="expert",
    )(meta, *weights, *flat, *prior, *deps)
    return outs[:count], outs[count : 2 * count], outs[2 * count :]


def swap(array, bit, size):
    return lax.ppermute(array, "dp", [(i, i ^ bit) for i in range(size)])


def plane_gather(array, size):
    half = array.shape[0] // 2
    x, y = swap(array, 2, size), swap(array, 4, size)
    across = {0: (array,), 2: (x,), 4: (y,), 6: (swap(y[:half], 2, size), swap(x[half:], 4, size))}
    blocks = [None] * size
    for k in (0, 2, 4, 6):
        blocks[k] = across[k]
        blocks[k + 1] = tuple(swap(piece, 1, size) for piece in across[k])
    return blocks


def add(*terms):
    total = terms[0].astype(F32)
    for term in terms[1:]:
        total = total + term.astype(F32)
    return total.astype(BF16)


def tie_kernel(*refs):
    del refs


def tie_all(arrays, *others):
    anywhere = pl.BlockSpec(memory_space=pl.ANY)
    return pl.pallas_call(
        tie_kernel,
        in_specs=[anywhere] * (len(arrays) + len(others)),
        out_specs=[anywhere] * len(arrays),
        out_shape=[jax.ShapeDtypeStruct(array.shape, array.dtype) for array in arrays],
        input_output_aliases={n: n for n in range(len(arrays))},
        name="tie",
    )(*arrays, *others)


def tie(array, *others):
    return tie_all([array], *others)[0]


def assemble_kernel(splits, widths, waits, me_ref, *refs):
    pieces, outs = refs[: sum(splits)], refs[sum(splits) + waits : -3]
    whole, in_sem, out_sem = refs[-3:]
    copies, at = [], 0
    for k, split in enumerate(splits):
        start = 0
        for piece in pieces[at : at + split]:
            target = whole.at[pl.ds(start, piece.shape[0]), me_ref[0] ^ k]
            copies.append(pltpu.make_async_copy(piece, target, in_sem.at[len(copies)]))
            start += piece.shape[0]
        at += split
    for copy in copies:
        copy.start()
    for copy in copies:
        copy.wait()
    copies, column = [], 0
    for out, (count, width) in zip(outs, widths):
        for n in range(count):
            source = whole.at[:, :, :, pl.ds(column, width)]
            copies.append(pltpu.make_async_copy(source, out.at[:, :, n], out_sem.at[len(copies)]))
            column += width
    for copy in copies:
        copy.start()
    for copy in copies:
        copy.wait()


def assemble(blocks, widths, me, deps=()):
    depth, rows, _ = blocks[0][0].shape
    size = len(blocks)
    splits = [len(pieces) for pieces in blocks]
    flat = [piece for pieces in blocks for piece in pieces]
    outs = pl.pallas_call(
        functools.partial(assemble_kernel, splits, widths, len(deps)),
        in_specs=[pl.BlockSpec(memory_space=pltpu.SMEM)] + [pl.BlockSpec(memory_space=pl.ANY)] * (len(flat) + len(deps)),
        out_specs=[pl.BlockSpec(memory_space=pl.ANY)] * len(widths),
        out_shape=[jax.ShapeDtypeStruct((depth, size, count, rows, width), BF16) for count, width in widths],
        scratch_shapes=[
            pltpu.VMEM((depth, size, rows, sum(count * width for count, width in widths)), BF16),
            pltpu.SemaphoreType.DMA((len(flat),)),
            pltpu.SemaphoreType.DMA((sum(count for count, _ in widths),)),
        ],
        compiler_params=pltpu.CompilerParams(vmem_limit_bytes=VMEM_LIMIT),
        name="assemble",
    )(me.astype(jnp.int32).reshape(1), *flat, *deps)
    return [out.reshape(-1, out.shape[-1]) for out in outs]


def per_device(
    depth,
    size,
    block_input,
    document_number,
    key_present,
    routes,
    sequence_adapter,
    output_gradient,
    norm_scale_pair,
    query_key_value_weight,
    attention_output_weight,
    router_weight,
    shared_gate_up_weight,
    shared_down_weight,
    routed_gate_up_weight,
    routed_down_weight,
    dense_first_factor,
    shared_down_first_factor,
    dense_second_factor,
    routed_first_factor,
    routed_down_first_factor,
    routed_second_factor,
):
    _, rows, model = block_input.shape
    topk = routes.shape[2]
    me = lax.axis_index("dp")
    experts = router_weight.shape[1]
    local_experts = routed_gate_up_weight.shape[0]
    shard_rows = query_key_value_weight.shape[0]
    shared_rows = shared_down_weight.shape[0]
    rank_all = dense_second_factor.shape[0]
    second_columns = dense_second_factor.shape[1]
    capacity = 4 * topk * rows // (3 * experts)
    query_width = HEADS * HEAD_DIM
    kv_width = KV_HEADS * HEAD_DIM
    hops = min(depth - 1, -(-(DOCUMENT_SPAN - 1) // rows))
    rank = ADAPTER_RANK
    units = SHARED_HIDDEN // size
    adapter = sequence_adapter[0]
    forward = [(i, i + 1) for i in range(depth - 1)]
    backward = [(i + 1, i) for i in range(depth - 1)]

    def over_seq(shard):
        return lax.all_gather(shard, "seq", axis=0)

    first_shard = dense_first_factor.reshape(shard_rows, 6 * rank_all)
    second_width = second_columns * rank_all // shard_rows
    groups = second_width // rank_all
    pack_kv = jnp.concatenate(
        [
            query_key_value_weight[:, query_width:],
            first_shard[:, rank_all : 3 * rank_all],
            dense_second_factor.T.reshape(groups, shard_rows, rank_all).transpose(1, 0, 2).reshape(shard_rows, -1),
            jnp.pad(
                jnp.concatenate([router_weight, norm_scale_pair.T], axis=1), ((0, 0), (0, LANES - experts - 2))
            ),
        ],
        axis=1,
    )
    pack_q = jnp.concatenate(
        [
            query_key_value_weight[:, :query_width],
            first_shard[:, :rank_all],
            first_shard[:, 3 * rank_all :],
            attention_output_weight,
        ],
        axis=1,
    )
    seq_kv = over_seq(pack_kv)
    seq_q = over_seq(tie(pack_q, seq_kv))

    present_tag = jnp.where(key_present == 1, document_number, -1).astype(F32)
    tag_blocks = [
        lax.ppermute(present_tag + 1.0, "seq", [(i, i + h) for i in range(depth - h)]) - 1.0 for h in range(hops, 0, -1)
    ] + [present_tag]
    key_tag = jnp.concatenate(tag_blocks, axis=1).reshape((hops + 1) * rows, 1)
    query_tag = document_number.astype(F32)

    flags = jnp.sum((routes[0][..., None] == jnp.arange(experts, dtype=jnp.int32)).astype(F32), axis=1)
    before = (jnp.arange(rows)[:, None] > jnp.arange(rows)[None, :]).astype(BF16)
    slots = jnp.where(flags > 0, dot_nn(before, flags.astype(BF16)), -1.0).astype(BF16)

    def own_columns(matrix):
        return lax.dynamic_slice_in_dim(matrix, adapter * rank, rank, 1)

    def own_factors(matrix):
        count = matrix.shape[1] // rank_all
        return jnp.concatenate([own_columns(matrix[:, n * rank_all : (n + 1) * rank_all]) for n in range(count)], axis=1)

    grad_out_b = output_gradient[0]
    grads_x, grads_y = swap(grad_out_b, 2, size), swap(grad_out_b, 4, size)
    kv_gathered = plane_gather(tie(seq_kv, grads_x, grads_y), size)
    grads_x, grads_y = tie_all([grads_x, grads_y], kv_gathered[2][0], kv_gathered[4][0])
    far_grads = (swap(grads_y[: rows // 2], 2, size), swap(grads_x[rows // 2 :], 4, size))
    grad_blocks = [(grad_out_b,), None, (grads_x,), None, (grads_y,), None, far_grads, None]
    kv_w, kv_first, second_t, small = assemble(
        kv_gathered, ((1, 2 * kv_width), (1, 2 * rank_all), (groups, rank_all), (1, LANES)), me, tag_blocks[:hops]
    )
    router_w = small[:, :experts]
    gains = small[:, experts : experts + 2].astype(F32).T
    second = own_columns(second_t).T
    first_kv = own_factors(kv_first)
    widths = [query_width, kv_width, kv_width, model, SHARED_HIDDEN, SHARED_HIDDEN, model]
    edges = [sum(widths[:n]) for n in range(len(widths) + 1)]
    b_parts = [second[:, edges[n] : edges[n + 1]] for n in range(len(widths))]

    x_flat = block_input[0].astype(F32)
    normed = rms_norm(x_flat, gains[0]).astype(BF16)
    low_kv = dot_nn(normed, first_kv).astype(BF16)
    kv_extra = jnp.concatenate([dot_nn(low_kv[:, :rank], b_parts[1]), dot_nn(low_kv[:, rank:], b_parts[2])], axis=1)
    kv_blocks = [(dot_nn(normed, kv_w) + kv_extra).astype(BF16)]
    q_blocks = plane_gather(tie(seq_q, *far_grads), size)
    for k in range(1, size, 2):
        grad_blocks[k] = tuple(swap(piece, 1, size) for piece in grad_blocks[k - 1])
    for h in range(hops):
        block = kv_blocks[-1] if h == 0 else tie(kv_blocks[-1], q_blocks[2][0], q_blocks[4][0])
        kv_blocks.append(lax.ppermute(block, "seq", forward))
        kv_blocks[h] = block
    kv_all = jnp.concatenate(kv_blocks[::-1], axis=0)

    down_rows = routed_down_weight.shape[1]
    second_cut = rank_all * routed_second_factor.shape[2] // down_rows
    up_shards, down_shards = [], []
    for j in range(local_experts):
        up_parts = [
            routed_gate_up_weight[j].reshape(-1, 2 * EXPERT_HIDDEN),
            routed_first_factor[j].reshape(-1, 2 * rank_all),
        ]
        down_parts = [
            routed_down_weight[j],
            routed_down_first_factor[j],
            routed_second_factor[j].reshape(down_rows, -1),
        ]
        if j == 0:
            gate_up = shared_gate_up_weight.reshape(shard_rows, 2, depth, size, units // depth)
            gate_up = gate_up.transpose(3, 0, 1, 2, 4).reshape(size, shard_rows, 2 * units)
            gate_up = lax.all_to_all(tie(gate_up, kv_gathered[2][0], kv_gathered[4][0]), "dp", split_axis=0, concat_axis=0, tiled=True)
            up_parts.append(gate_up.reshape(size * shard_rows, 2 * units))
            shared_down = jnp.concatenate([shared_down_weight, shared_down_first_factor], axis=1)
            down_parts.append(shared_down.reshape(down_rows, -1))
        up_shards.append(jnp.concatenate(up_parts, axis=1))
        down_shards.append(jnp.concatenate(down_parts, axis=1))
    seq_up, seq_down = [], []
    for j in range(local_experts):
        seq_up.append(over_seq(tie(up_shards[j], seq_q if j == 0 else seq_up[j - 1])))
        seq_down.append(over_seq(tie(down_shards[j], seq_q if j == 0 else seq_up[j - 1])))

    q_w, q_first, out_w = assemble(q_blocks, ((1, query_width), (1, 4 * rank_all), (1, model)), me)
    q_first = own_factors(q_first)
    first_q, first_o, first_gu = q_first[:, :rank], q_first[:, rank : 2 * rank], q_first[:, 2 * rank :]
    low_q = dot_nn(normed, first_q).astype(BF16)
    query = (dot_nn(normed, q_w) + dot_nn(low_q, b_parts[0])).astype(BF16)
    glow_sdown = dot_nt(grad_out_b, b_parts[6]).astype(BF16)
    attn, lse = attend(query, kv_all, query_tag, key_tag, hops, (*grad_blocks[3], *grad_blocks[5], *grad_blocks[7]))
    out_low = dot_nn(attn, first_o).astype(BF16)
    mid = x_flat + dot_nn(attn, out_w) + dot_nn(out_low, b_parts[3])
    normed2 = rms_norm(mid, gains[1]).astype(BF16)

    logits = dot_nn(normed2, router_w)
    top = jnp.max(jnp.where(flags > 0, logits, -jnp.inf), axis=-1, keepdims=True)
    weights = jnp.where(flags > 0, jnp.exp(logits - top), 0.0)
    gates = weights / jnp.sum(weights, axis=-1, keepdims=True)
    gates_hi = gates.astype(BF16)
    gates_lo = (gates - gates_hi.astype(F32)).astype(BF16)
    shared_low = dot_nn(normed2, first_gu).astype(BF16)
    own_adapter = jnp.full((rows, LANES - 3 * experts - 3 * rank), adapter.astype(F32)).astype(BF16)
    payload = jnp.concatenate([normed2, slots, gates_hi, gates_lo, shared_low, glow_sdown, own_adapter], axis=1)
    token_blocks = [None] * size
    token_blocks[0], token_blocks[1] = (payload,), (swap(payload, 1, size),)
    tokens_x, tokens_y = swap(payload, 2, size), swap(payload, 4, size)

    def gather_far(tokens_x, tokens_y, *done):
        tokens_x, tokens_y = tie_all([tokens_x, tokens_y], *done)
        half = rows // 2
        token_blocks[2], token_blocks[3] = (tokens_x,), (swap(tokens_x, 1, size),)
        token_blocks[4], token_blocks[5] = (tokens_y,), (swap(tokens_y, 1, size),)
        return swap(tokens_y[:half], 2, size), swap(tokens_x[half:], 4, size)

    def gather_farthest(far, *done):
        far = tuple(tie_all(far, *done))
        token_blocks[6], token_blocks[7] = far, tuple(swap(piece, 1, size) for piece in far)


    moe_parts, back_parts, grad_sums = [None] * size, [None] * size, []
    wide = model + rank_all

    def weights_of(j):
        second_j = seq_down[j][:, :, wide : wide + second_cut]
        second_j = second_j.reshape(depth, rank_all, -1).transpose(1, 0, 2).reshape(rank_all, -1)
        args = [seq_up[j].reshape(model, -1), seq_down[j][:, :, :wide].reshape(EXPERT_HIDDEN, wide), second_j]
        if j == 0:
            args.append(seq_down[j][:, :, wide + second_cut :].reshape(units, wide))
            slices = [
                lax.dynamic_slice_in_dim(second_t[edges[n] : edges[n + 1]].reshape(depth, size, -1, rank_all), me, 1, 1)
                for n in (4, 5)
            ]
            args.append(jnp.concatenate([part.reshape(units, rank_all) for part in slices], axis=0))
        return args

    def run_expert(j, args, group, prior, deps):
        meta = jnp.stack([me * local_experts + j, me]).astype(jnp.int32)
        prior = ([moe_parts[k] for k in group], [back_parts[k] for k in group]) if prior else None
        moe_out, back_out, grads = expert_call(
            meta,
            args,
            [token_blocks[k] for k in group],
            [grad_blocks[k] for k in group],
            prior,
            experts,
            capacity,
            deps,
        )
        for n, k in enumerate(group):
            moe_parts[k], back_parts[k] = moe_out[n], back_out[n]
        grad_sums[-1] = list(grads) if grad_sums[-1] is None else [a + b for a, b in zip(grad_sums[-1], grads)]

    for j in range(local_experts - 1):
        grad_sums.append(None)
        args = weights_of(j)
        previous = ()
        for group in ((0, 1), (2, 3), (4, 5), (6, 7)):
            run_expert(j, args, group, j > 0, previous)
            previous = (back_parts[group[0]],)
            if j == 0 and group == (0, 1):
                far = gather_far(tokens_x, tokens_y, *previous)
            if j == 0 and group == (2, 3):
                gather_farthest(far, *previous)
    if local_experts == 1:
        gather_farthest(gather_far(tokens_x, tokens_y))
    grad_sums.append(None)
    j, prior, half = local_experts - 1, local_experts > 1, (rows + BACK_ROWS) // 2
    args = weights_of(j)
    run_expert(j, args, (6, 7), prior, (back_parts[6],) if prior else ())
    pair_six = add(back_parts[6], swap(back_parts[7], 1, size))
    run_expert(j, args, (2, 3), prior, (pair_six,))
    from_diagonal_x, from_diagonal_y = swap(pair_six[:half], 2, size), swap(pair_six[half:], 4, size)
    pair_two = add(back_parts[2], swap(back_parts[3], 1, size))
    run_expert(j, args, (4, 5), prior, (pair_two,))
    pair_four = add(back_parts[4], swap(tie(back_parts[5], from_diagonal_x, from_diagonal_y), 1, size))
    to_x = jnp.concatenate([pair_two[:half], add(pair_two[half:], from_diagonal_y)], axis=0)
    to_y = jnp.concatenate([add(pair_four[:half], from_diagonal_x), pair_four[half:]], axis=0)
    run_expert(j, args, (0, 1), prior, (to_x, to_y))
    back_sum = add(back_parts[0], swap(back_parts[1], 1, size), swap(to_x, 2, size), swap(to_y, 4, size))
    back = back_sum.astype(F32)

    half = rows // 2
    far_parts = dict(zip((6, 2, 4, 0), tie_all([moe_parts[k + 1] for k in (6, 2, 4, 0)], back_sum)))
    pair = {k: add(moe_parts[k], swap(far_parts[k], 1, size)) for k in (6, 2, 4, 0)}
    moe_to_x = jnp.concatenate([pair[2][:half], add(pair[2][half:], swap(pair[6][half:], 4, size))], axis=0)
    moe_to_y = jnp.concatenate([add(pair[4][:half], swap(pair[6][:half], 2, size)), pair[4][half:]], axis=0)
    moe_from_x, moe_from_y = swap(moe_to_x, 2, size), swap(moe_to_y, 4, size)
    moe = pair[0].astype(F32) + moe_from_x.astype(F32) + moe_from_y.astype(F32)
    tail = back[:rows, model:]
    low_sdown = tail[:, 3 * experts + 2 * rank : 3 * experts + 3 * rank].astype(BF16)

    owner_rows = model // depth
    packed = [grads[0].astype(BF16).reshape(depth, owner_rows, 2 * rank_all) for grads in grad_sums]
    packed.append(
        jnp.concatenate([g[1] for g in grad_sums], axis=1).astype(BF16).reshape(depth, -1, 2 * rank_all)
    )
    for grads in grad_sums:
        packed.append(
            grads[2].astype(BF16).reshape(rank_all, depth, -1).transpose(1, 0, 2).reshape(depth, -1, 2 * rank_all)
        )
    packed.append(grad_sums[0][3].astype(BF16).reshape(depth, -1, 2 * rank_all))
    lines = [part.shape[1] for part in packed]
    packed_sum = lax.psum_scatter(jnp.concatenate(packed, axis=1), "seq", scatter_dimension=0, tiled=True)
    packed = packed_sum[0].astype(F32)
    cuts = [sum(lines[:n]) for n in range(len(lines) + 1)]
    pieces = [packed[cuts[n] : cuts[n + 1]] for n in range(len(lines))]
    grad_expert_a = jnp.stack(pieces[:local_experts]).reshape(local_experts, owner_rows, 2, rank_all)
    grad_expert_a_down = pieces[local_experts].reshape(down_rows, local_experts, rank_all).transpose(1, 0, 2)
    grad_expert_b = jnp.stack(pieces[local_experts + 1 : -1]).reshape(local_experts, rank_all, -1)
    grad_first_down = pieces[-1].reshape(shared_rows, rank_all)

    grad_out = grad_out_b.astype(F32)
    grad_gates = tail[:, :experts] + tail[:, experts : 2 * experts]
    glow_sgu = tail[:, 3 * experts : 3 * experts + 2 * rank].astype(BF16)
    grad_logits = gates * (grad_gates - jnp.sum(gates * grad_gates, axis=-1, keepdims=True))
    grad_normed2 = back[:rows, :model] + dot_nt(glow_sgu, first_gu)
    grad_normed2 = grad_normed2 + jnp.einsum(
        "re,de->rd", grad_logits, router_w.astype(F32), precision=lax.Precision.HIGHEST
    )
    _, norm2_back = jax.vjp(lambda values_in: rms_norm(values_in, gains[1]), mid)
    grad_mid = grad_out + norm2_back(grad_normed2)[0]
    grad_mid_b = grad_mid.astype(BF16)
    glow_out = dot_nt(grad_mid_b, b_parts[3]).astype(BF16)
    grad_attn = (dot_nt(grad_mid_b, out_w) + dot_nt(glow_out, first_o)).astype(BF16)

    def spread_out(flat, pieces):
        width = sum(p.size // (depth * size) for p in pieces)
        flat = flat.astype(F32)
        chosen = (flat[:, width : width + 1] == jnp.arange(rank_all // rank, dtype=F32)[None, :]).astype(F32)
        spread = jnp.sum(chosen[:, :, None] * flat[:, None, :width], axis=0)
        outs, at = [], 0
        for p in pieces:
            count = p.shape[0] // (depth * size)
            outs.append(spread[:, at : at + count * p.shape[1]].reshape(-1, count, p.shape[1]))
            at += count * p.shape[1]
        return outs

    def tagged(flat):
        return jnp.concatenate([flat, jnp.full((flat.shape[0], LANES), adapter.astype(F32)).astype(flat.dtype)], axis=1)

    def shared_columns(block):
        block = block[:, :SHARED_HIDDEN].reshape(rank, size, depth, units // depth)
        return block.transpose(0, 2, 1, 3).reshape(rank, SHARED_HIDDEN).T

    def pack_for_owners(pieces):
        return tagged(jnp.concatenate([p.astype(BF16).reshape(depth * size, -1) for p in pieces], axis=1))

    count = KV_HEADS // 2
    grad_q_one, grad_kv_one = attend_back(query, kv_all, grad_attn, lse, query_tag, key_tag, hops, 0, count, (pair[6], pair[2], pair[4]))
    one = grad_kv_one[:rows]
    hop_one = lax.ppermute(one, "seq", backward)
    grad_q_two, grad_kv_two = attend_back(
        query, kv_all, grad_attn, lse, query_tag, key_tag, hops, count, count, (moe_to_x, moe_to_y)
    )
    two = tie(grad_kv_two[:rows], hop_one)
    hop_two = lax.ppermute(two, "seq", backward)
    for h in range(hops):
        own = slice((h + 1) * rows, (h + 2) * rows)
        from_one = hop_one if h == 0 else lax.ppermute(one, "seq", backward)
        from_two = hop_two if h == 0 else lax.ppermute(tie(two, from_one), "seq", backward)
        one, two = add(grad_kv_one[own], from_one), add(grad_kv_two[own], from_two)
    late_deps = (hop_two, moe_from_x, moe_from_y)
    glow_out_t, glow_sgu_t, out_low_t, shared_rows_t, low_sdown_t, grad_q = tie_all(
        [glow_out, glow_sgu, out_low, back[rows:], low_sdown, jnp.concatenate([grad_q_one, grad_q_two], axis=1)],
        *late_deps,
    )
    hidden_out = (mid + moe + dot_nn(low_sdown_t, b_parts[6])).astype(BF16)[None]

    early = [
        jnp.concatenate([dot_tn(attn, glow_out_t), dot_tn(normed2, glow_sgu_t)], axis=1),
        jnp.concatenate(
            [
                jnp.zeros((query_width + 2 * kv_width, rank), F32),
                dot_tn(grad_mid_b, out_low_t),
                shared_columns(shared_rows_t[:rank]),
                shared_columns(shared_rows_t[rank:]),
                dot_tn(grad_out_b, low_sdown_t),
            ],
            axis=0,
        ),
    ]
    early_packed = pack_for_owners(early)
    early_flat = lax.all_to_all(early_packed, ("seq", "dp"), split_axis=0, concat_axis=0, tiled=True)
    one, two = tie_all([one, two], early_packed)
    grad_kvs = [half_[:, 2 * n * HEAD_DIM : 2 * (n + 1) * HEAD_DIM] for half_ in (one, two) for n in range(count)]
    glow_q = dot_nt(grad_q, b_parts[0]).astype(BF16)
    grad_normed = dot_nt(grad_q, q_w) + dot_nt(glow_q, first_q)
    grad_k = jnp.concatenate([piece[:, :HEAD_DIM] for piece in grad_kvs], axis=1)
    grad_v = jnp.concatenate([piece[:, HEAD_DIM:] for piece in grad_kvs], axis=1)
    glow_kv = jnp.concatenate([dot_nt(grad_k, b_parts[1]), dot_nt(grad_v, b_parts[2])], axis=1).astype(BF16)
    late = [
        jnp.concatenate([dot_tn(normed, glow_q), dot_tn(normed, glow_kv)], axis=1).astype(BF16),
        jnp.concatenate(
            [
                dot_tn(grad_q, low_q).astype(BF16),
                dot_tn(grad_k, low_kv[:, :rank]).astype(BF16),
                dot_tn(grad_v, low_kv[:, rank:]).astype(BF16),
                jnp.zeros((edges[-1] - edges[3], rank), BF16),
            ],
            axis=0,
        ),
    ]
    late_flat = lax.all_to_all(pack_for_owners(late), ("seq", "dp"), split_axis=0, concat_axis=0, tiled=True)
    grad_normed = grad_normed + dot_nt(jnp.concatenate([grad_k, grad_v], axis=1), kv_w) + dot_nt(glow_kv, first_kv)
    _, norm1_back = jax.vjp(lambda values_in: rms_norm(values_in, gains[0]), x_flat)
    grad_hidden = (grad_mid + norm1_back(grad_normed)[0])[None]
    early_parts, late_parts = spread_out(early_flat, early), spread_out(late_flat, late)
    grad_first = jnp.concatenate([late_parts[0], early_parts[0]], axis=2)
    grad_first = grad_first.reshape(-1, shard_rows, 6, rank).transpose(1, 2, 0, 3).reshape(shard_rows, 6, rank_all)
    grad_second = (early_parts[1] + late_parts[1]).transpose(0, 2, 1).reshape(rank_all, second_columns)
    return (
        hidden_out,
        grad_hidden,
        grad_first,
        grad_first_down,
        grad_second,
        grad_expert_a,
        grad_expert_a_down,
        grad_expert_b,
    )


def solution(mesh):
    in_specs = (
        P("dp", "seq", None),
        P("dp", "seq"),
        P("dp", "seq"),
        P("dp", "seq", None),
        P("dp"),
        P("dp", "seq", None),
        P(None, ("seq", "dp")),
        P(("seq", "dp"), None),
        P(("seq", "dp"), None),
        P(("seq", "dp"), None),
        P(("seq", "dp"), None, None),
        P(("seq", "dp"), None),
        P("dp", "seq", None, None),
        P("dp", "seq", None),
        P(("seq", "dp"), None, None),
        P(("seq", "dp"), None),
        P(None, ("seq", "dp")),
        P("dp", "seq", None, None),
        P("dp", "seq", None),
        P("dp", None, "seq"),
    )
    out_specs = (
        P("dp", "seq", None),
        P("dp", "seq", None),
        P(("seq", "dp"), None, None),
        P(("seq", "dp"), None),
        P(None, ("seq", "dp")),
        P("dp", "seq", None, None),
        P("dp", "seq", None),
        P("dp", None, "seq"),
    )
    return jax.shard_map(
        functools.partial(per_device, mesh.shape["seq"], mesh.shape["dp"]),
        mesh=mesh,
        in_specs=in_specs,
        out_specs=out_specs,
        check_vma=False,
    )
```

time: 1050 us -> 848 us (0.81)
  waiting for transfers between devices: 371 us -> 143 us
  matrix products: 110 us -> 62.5 us
  other arithmetic: 56.9 us -> 85.6 us
  Pallas kernels: 233 us -> 258 us
  local copies, waits for them, and re-layouts: 146 us -> 163 us
    ppermute x48 -> x52, waiting for transfers between devices: 261 us -> 55.4 us  [swap(): return lax.ppermute(array, 'dp', [(i, i ^ bit) for i in range(size)])]
    unnamed x1 -> x0, blocking collectives: 25.3 us -> none
    pallas_call x6 -> x31, Pallas kernels: 233 us -> 258 us  [the longest x8 182 us: expert_call(): pl.pallas_call(functools.partial(expert_kernel, count, splits, experts, c...]
    dot_general x15 -> x12, matrix products: 47.5 us -> 25.4 us  [dot_nt(): lax.dot_general(left, right, (((1,), (1,)), ((), ())), preferred_element_...]
    reshape x6 -> x23, local copies, waits for them, and re-layouts: 5.21 us -> 26 us  [the longest x6 5.42 us: per_device(): grads[2].astype(BF16).reshape(rank_all, depth, -1).transpose(1, 0, 2)]
    slice x28 -> x49, local copies, waits for them, and re-layouts: 18.8 us -> 39.3 us  [the longest x2 5.53 us: weights_of(): seq_down[j][:, :, :wide].reshape(EXPERT_HIDDEN, wide)]
    all_gather x0 -> x1, blocking collectives: none -> 18.7 us  [over_seq(): return lax.all_gather(shard, 'seq', axis=0)]
    ppermute x4 -> x6, waiting for transfers between devices: 84.6 us -> 66.6 us  [the longest x2 33.3 us: per_device(): kv_blocks.append(lax.ppermute(block, 'seq', forward))]
  transfers between devices with their start and end apart: 66 -> 69, of which waited for: 22 -> 16; matrix products, arithmetic and copies ran while one was open for 28% -> 33% of each run, Pallas kernels for 22% -> 26%
where the time goes in v2:
time: 848 us; the launch traced here: 835 us
  Pallas kernels  258 us (30%)
  local copies, waits for them, and re-layouts  163 us (19%)
  waiting for transfers between devices  143 us (17%)
  starting transfers between devices  86.6 us (10%)
  other arithmetic  85.6 us (10%)
  matrix products  62.5 us (7%)
  blocking collectives  18.7 us (2%)
  between operations  17.1 us (2%)
    pallas_call x8, Pallas kernels, expert_call(): pl.pallas_call(functools.partial(expert_kernel, count, splits, experts, c...  182 us
    ppermute x52, waiting for transfers between devices, swap(): return lax.ppermute(array, 'dp', [(i, i ^ bit) for i in range(size)])  55.4 us
    unnamed x291, local copies, waits for them, and re-layouts  49.4 us
    pallas_call x2, Pallas kernels, attend_back(): pl.pallas_call(functools.partial(attend_back_kernel, spans, hops * rows,...  36.8 us
    ppermute x2, waiting for transfers between devices, per_device(): kv_blocks.append(lax.ppermute(block, 'seq', forward))  33.3 us
    ppermute x1, waiting for transfers between devices, per_device(): lax.ppermute(tie(two, from_one), 'seq', backward)  33.2 us
    ppermute x52, starting transfers between devices, swap(): return lax.ppermute(array, 'dp', [(i, i ^ bit) for i in range(size)])  33.2 us
    dot_general x14, matrix products, dot_nn(): return jnp.dot(left, right, preferred_element_type=F32)  25.9 us
  transfers between devices with their start and end apart: 69, of which 16 were waited for; matrix products, arithmetic and copies ran while one was open for 33% of the time, Pallas kernels for 26%

profile of v2, /device:TPU:0, one launch (start us, length us, event | category | flops | bytes accessed | tf_op | source)
XLA Modules:
  0.0 834.7 jit_solution(2230706003668052292)
XLA Ops:
  12.5 3.5 collective-permute-start.12
  18.6 18.7 %all-gather = bf16[192,2048]{1,0:T(8,128)(2,1)} all-gather(bf16[48,2048]{1,0:T(8,128)(2,1)S(1)} %fusion.52), channel_id=2, replica_groups=mesh['seq'=4,'dp'=8] {'seq'}, dimensions={0}, use_global_device_ids=true | all-gather | bytes 983040 | tf_op jit(solution)/shard_map/all_gather | solution.py:620
  41.4 3.6 collective-permute-done.1.refs_2_.refs_1_
  50.3 14.5 %collective-permute-done.5.refs_4_.refs_3_.refs_2_ = bf16[4,48,2048]{2,1,0:T(8,128)(2,1)S(1)} collective-permute-done((bf16[4,48,2048]{2,1,0:T(8,128)(2,1)}, bf16[4,48,2048]{2,1,0:T(8,128)(2,1)S(1)}, u32[]{:S(2)}, u32[]{:S(2)}) %collective-permute-start.5) | collective-permute-done | bytes 786464 | tf_op jit(solution)/shard_map/ppermute | solution.py:487
  76.9 4.5 collective-permute-start.11
  95.3 4.0 all-to-all-start
  100.6 4.9 all-to-all-done
  109.1 6.0 assemble.2
  124.8 4.4 collective-permute-start.24
  129.1 10.8 %collective-permute-done.18.refs_4_.refs_2_ = bf16[4,48,3584]{2,1,0:T(8,128)(2,1)} collective-permute-done((bf16[4,48,3584]{2,1,0:T(8,128)(2,1)}, bf16[4,48,3584]{2,1,0:T(8,128)(2,1)}, u32[]{:S(2)}, u32[]{:S(2)}) %collective-permute-start.18) | collective-permute-done | bytes 1376288 | tf_op jit(solution)/shard_map/ppermute | solution.py:487
  142.6 30.8 %collective-permute-done.24.refs_0_ = bf16[512,1024]{1,0:T(8,128)(2,1)} collective-permute-done((bf16[512,1024]{1,0:T(8,128)(2,1)S(1)}, bf16[512,1024]{1,0:T(8,128)(2,1)}, u32[]{:S(2)}, u32[]{:S(2)}) %collective-permute-start.24) | collective-permute-done | bytes 1048608 | tf_op jit(solution)/shard_map/ppermute | solution.py:693
  173.4 12.4 %collective-permute-start.25 = (bf16[512,1024]{1,0:T(8,128)(2,1)}, bf16[512,1024]{1,0:T(8,128)(2,1)}, u32[]{:S(2)}, u32[]{:S(2)}) collective-permute-start(bf16[512,1024]{1,0:T(8,128)(2,1)} %tie.22), channel_id=1, source_target_pairs={{0,8},{8,16},{16,24},{1,9},{9,17},{17,25},{2,10},{10,18},{18,26},{... | collective-permute-start | bytes 3145736 | tf_op jit(solution)/shard_map/ppermute | solution.py:693
  191.4 13.4 %collective-permute-done.21.refs_7_ = bf16[2,48,3584]{2,1,0:T(8,128)(2,1)} collective-permute-done((bf16[2,48,3584]{2,1,0:T(8,128)(2,1)}, bf16[2,48,3584]{2,1,0:T(8,128)(2,1)}, u32[]{:S(2)}, u32[]{:S(2)}) %collective-permute-start.21) | collective-permute-done | bytes 688160 | tf_op jit(solution)/shard_map/ppermute | solution.py:487
  211.5 3.4 pad_maximum_fusion.k_ref.v_ref
  216.1 9.1 %assemble.3 = (bf16[4,8,1,48,1536]{4,3,2,1,0:T(8,128)(2,1)}, bf16[4,8,1,48,512]{4,3,2,1,0:T(8,128)(2,1)}, bf16[4,8,1,48,1536]{4,3,2,1,0:T(8,128)(2,1)}) custom-call(s32[1]{0:T(128)} %bitcast.1.me_ref, bf16[4,48,3584]{2,1,0:T(8,128)(2,1)} %tie.21.refs_0_, bf16[4,48,3584]{2,1,0:T(8,128)(2,1)} %collective-permute-done.15.refs_1_, ...), custom_call_target="tpu_custom_call" | custom-call | tf_op jit(solution)/shard_map/assemble/pallas_call | solution.py:560
  234.5 3.9 fusion.18.q_ref
  238.4 23.7 %attend.1 = (bf16[512,1536]{1,0:T(8,128)(2,1)}, f32[4,3,512]{2,1,0:T(4,128)}) custom-call(bf16[512,1536]{1,0:T(8,128)(2,1)} %fusion.18.q_ref, bf16[1536,1024]{1,0:T(8,128)(2,1)} %pad_maximum_fusion.k_ref.v_ref, bf16[1536,1024]{1,0:T(8,128)(2,1)} %pad_maximum_fusion.k_ref.v_ref, f32[1,512]{1,0:T(1,128)} %convert_element_type.356.qt_ref, ...), custom_call_target="tpu_custom_call" | custom-call | flops 26530500608 | bytes 1000000 | tf_op jit(solution)/shard_map/attend/pallas_call | solution.py:96
  266.0 4.8 multiply_reduce_fusion.3
  277.5 3.6 concatenate.128.refs_6_.refs_4_
  296.0 5.4 all-gather.14.cloned.1.call-done.refs_1_
  301.4 8.8 %all-gather.16.cloned.1.call-start = ((), (), s32[]{:S(2)}) async-start(), calls=%async_computation.7 | async-start | bytes 4915200 | tf_op jit(solution)/shard_map/all_gather | solution.py:620
  310.3 24.7 %expert.8 = (bf16[512,1536]{1,0:T(8,128)(2,1)}, bf16[512,1536]{1,0:T(8,128)(2,1)}, bf16[544,1664]{1,0:T(8,128)(2,1)}, bf16[544,1664]{1,0:T(8,128)(2,1)}, f32[153...) custom-call(s32[2]{0:T(128)} %pad_add_fusion.1.refs_0_, ...), custom_call_target="tpu_custom_call" | custom-call | flops 27683999744 | bytes 1000000 | tf_op jit(solution)/shard_map/expert/pallas_call | solution.py:458
  343.7 24.4 %expert.9 = (bf16[512,1536]{1,0:T(8,128)(2,1)}, bf16[512,1536]{1,0:T(8,128)(2,1)}, bf16[544,1664]{1,0:T(8,128)(2,1)}, bf16[544,1664]{1,0:T(8,128)(2,1)}, f32[153...) custom-call(s32[2]{0:T(128)} %pad_add_fusion.1.refs_0_, ...), custom_call_target="tpu_custom_call" | custom-call | flops 27683999744 | bytes 1000000 | tf_op jit(solution)/shard_map/expert/pallas_call | solution.py:458
  369.8 24.5 %expert.10 = (bf16[512,1536]{1,0:T(8,128)(2,1)}, bf16[512,1536]{1,0:T(8,128)(2,1)}, bf16[544,1664]{1,0:T(8,128)(2,1)}, bf16[544,1664]{1,0:T(8,128)(2,1)}, f32[15...) custom-call(s32[2]{0:T(128)} %pad_add_fusion.1.refs_0_, ...), custom_call_target="tpu_custom_call" | custom-call | flops 27683999744 | bytes 1000000 | tf_op jit(solution)/shard_map/expert/pallas_call | solution.py:458
  395.5 24.7 %expert.11 = (bf16[512,1536]{1,0:T(8,128)(2,1)}, bf16[512,1536]{1,0:T(8,128)(2,1)}, bf16[544,1664]{1,0:T(8,128)(2,1)}, bf16[544,1664]{1,0:T(8,128)(2,1)}, f32[15...) custom-call(s32[2]{0:T(128)} %pad_add_fusion.1.refs_0_, ...), custom_call_target="tpu_custom_call" | custom-call | flops 27683999744 | bytes 1000000 | tf_op jit(solution)/shard_map/expert/pallas_call | solution.py:458
  428.5 20.6 %expert.12 = (bf16[512,1536]{1,0:T(8,128)(2,1)}, bf16[512,1536]{1,0:T(8,128)(2,1)}, bf16[544,1664]{1,0:T(8,128)(2,1)}, bf16[544,1664]{1,0:T(8,128)(2,1)}, f32[15...) custom-call(s32[2]{0:T(128)} %pad_add_fusion.refs_0_, ...), custom_call_target="tpu_custom_call" | custom-call | flops 27683999744 | bytes 1000000 | tf_op jit(solution)/shard_map/expert/pallas_call | solution.py:458
  449.2 3.9 collective-permute-done.40
  456.3 21.5 %expert.13 = (bf16[512,1536]{1,0:T(8,128)(2,1)}, bf16[512,1536]{1,0:T(8,128)(2,1)}, bf16[544,1664]{1,0:T(8,128)(2,1)}, bf16[544,1664]{1,0:T(8,128)(2,1)}, f32[15...) custom-call(s32[2]{0:T(128)} %pad_add_fusion.refs_0_, ...), custom_call_target="tpu_custom_call" | custom-call | flops 27683999744 | bytes 1000000 | tf_op jit(solution)/shard_map/expert/pallas_call | solution.py:458
  487.9 21.0 %expert.14 = (bf16[512,1536]{1,0:T(8,128)(2,1)}, bf16[512,1536]{1,0:T(8,128)(2,1)}, bf16[544,1664]{1,0:T(8,128)(2,1)}, bf16[544,1664]{1,0:T(8,128)(2,1)}, f32[15...) custom-call(s32[2]{0:T(128)} %pad_add_fusion.refs_0_, ...), custom_call_target="tpu_custom_call" | custom-call | flops 27683999744 | bytes 1000000 | tf_op jit(solution)/shard_map/expert/pallas_call | solution.py:458
  523.7 20.9 %expert.15 = (bf16[512,1536]{1,0:T(8,128)(2,1)}, bf16[512,1536]{1,0:T(8,128)(2,1)}, bf16[544,1664]{1,0:T(8,128)(2,1)}, bf16[544,1664]{1,0:T(8,128)(2,1)}, f32[15...) custom-call(s32[2]{0:T(128)} %pad_add_fusion.refs_0_, ...), custom_call_target="tpu_custom_call" | custom-call | flops 27683999744 | bytes 1000000 | tf_op jit(solution)/shard_map/expert/pallas_call | solution.py:458
  553.1 3.9 add_convert_fusion.11
  557.0 3.6 collective-permute-done.46
  560.5 4.1 collective-permute-done.47
  564.6 3.5 fusion.93
  570.8 3.9 multiply_reduce_fusion.2
  575.3 3.9 fusion.15
  581.6 6.2 fusion.19.g_ref
  595.0 18.3 %attend_back.2 = (bf16[512,768]{1,0:T(8,128)(2,1)}, bf16[1536,512]{1,0:T(8,128)(2,1)}) custom-call(bf16[512,1536]{1,0:T(8,128)(2,1)} %fusion.18.q_ref, bf16[1536,1024]{1,0:T(8,128)(2,1)} %pad_maximum_fusion.k_ref.v_ref, bf16[1536,1024]{1,0:T(8,128)(2,1)} %pad_maximum_fusion.k_ref.v_ref, bf16[512,1536]{1,0:T(8,128)(2,1)} %fusion.19.g_ref, ...), custom_call_target="tpu_custom_call" | custom-call | flops 4614000128 | bytes 1000000 | tf_op jit(solution)/shard_map/attend_back/pallas_call | solution.py:159
  623.7 18.5 %attend_back.3 = (bf16[512,768]{1,0:T(8,128)(2,1)}, bf16[1536,512]{1,0:T(8,128)(2,1)}) custom-call(bf16[512,1536]{1,0:T(8,128)(2,1)} %fusion.18.q_ref, bf16[1536,1024]{1,0:T(8,128)(2,1)} %pad_maximum_fusion.k_ref.v_ref, bf16[1536,1024]{1,0:T(8,128)(2,1)} %pad_maximum_fusion.k_ref.v_ref, bf16[512,1536]{1,0:T(8,128)(2,1)} %fusion.19.g_ref, ...), custom_call_target="tpu_custom_call" | custom-call | flops 4614000128 | bytes 1000000 | tf_op jit(solution)/shard_map/attend_back/pallas_call | solution.py:159
  658.6 6.7 concatenate.153
  679.9 33.2 %collective-permute-done.59 = bf16[512,512]{1,0:T(8,128)(2,1)S(1)} collective-permute-done((bf16[512,512]{1,0:T(8,128)(2,1)}, bf16[512,512]{1,0:T(8,128)(2,1)S(1)}, u32[]{:S(2)}, u32[]{:S(2)}) %collective-permute-start.59) | collective-permute-done | bytes 524320 | tf_op jit(solution)/shard_map/ppermute | solution.py:900
  737.7 3.5 convert_element_type.432
  759.6 4.0 all-to-all-start.2
  771.9 3.5 reshape.354
  784.7 4.7 convolution_add_fusion.2
  791.8 4.8 fusion.24
  802.2 6.2 all-to-all-start.1
  814.7 7.1 all-to-all-done.1
  (650 shorter events, 297.9 us)
Async XLA Ops:
  7.2 93.4 %all-gather.12.cloned.1.call-start = ((), (), s32[]{:S(2)}) async-start(), calls=%async_computation.5 | async-start | bytes 1720320 | tf_op jit(solution)/shard_map/all_gather | solution.py:620
  7.3 37.7 %collective-permute-start.1 = (bf16[512,1536]{1,0:T(8,128)(2,1)}, bf16[512,1536]{1,0:T(8,128)(2,1)}, u32[]{:S(2)}, u32[]{:S(2)}) collective-permute-start(bf16[512,1536]{1,0:T(8,128)(2,1)} %bitcast.215), channel_id=1, source_target_pairs={{0,4},{1,5},{2,6},{3,7},{4,0},{5,1},{6,2},{7,3},{8,12},{9,13},{10,... | collective-permute-start | bytes 4718600 | tf_op jit(solution)/shard_map/ppermute | solution.py:487
  10.3 36.2 %collective-permute-start = (bf16[512,1536]{1,0:T(8,128)(2,1)}, bf16[512,1536]{1,0:T(8,128)(2,1)}, u32[]{:S(2)}, u32[]{:S(2)}) collective-permute-start(bf16[512,1536]{1,0:T(8,128)(2,1)} %bitcast.216), channel_id=1, source_target_pairs={{0,2},{1,3},{2,0},{3,1},{4,6},{5,7},{6,4},{7,5},{8,10},{9,11},{10,... | collective-permute-start | bytes 4718600 | tf_op jit(solution)/shard_map/ppermute | solution.py:487
  12.5 64.4 %collective-permute-start.12 = (f32[1,512]{1,0:T(1,128)S(1)}, f32[1,512]{1,0:T(1,128)S(1)}, u32[]{:S(2)}, u32[]{:S(2)}) collective-permute-start(f32[1,512]{1,0:T(1,128)S(1)} %get-tuple-element.239), channel_id=1, source_target_pairs={{0,8},{8,16},{16,24},{1,9},{9,17},{17,25},{2,10},{10,18},{18,26},{... | collective-permute-start | bytes 6152 | tf_op jit(solution)/shard_map/ppermute | solution.py:650
  73.9 25.5 %collective-permute-start.14 = (bf16[256,1536]{1,0:T(8,128)(2,1)}, bf16[256,1536]{1,0:T(8,128)(2,1)}, u32[]{:S(2)}, u32[]{:S(2)}) collective-permute-start(bf16[256,1536]{1,0:T(8,128)(2,1)} %slice.334), channel_id=1, source_target_pairs={{0,4},{1,5},{2,6},{3,7},{4,0},{5,1},{6,2},{7,3},{8,12},{9,13},{10,... | collective-permute-start | bytes 2359304 | tf_op jit(solution)/shard_map/ppermute | solution.py:487
  75.3 24.6 %collective-permute-start.13 = (bf16[256,1536]{1,0:T(8,128)(2,1)}, bf16[256,1536]{1,0:T(8,128)(2,1)}, u32[]{:S(2)}, u32[]{:S(2)}) collective-permute-start(bf16[256,1536]{1,0:T(8,128)(2,1)} %slice.333), channel_id=1, source_target_pairs={{0,2},{1,3},{2,0},{3,1},{4,6},{5,7},{6,4},{7,5},{8,10},{9,11},{10,... | collective-permute-start | bytes 2359304 | tf_op jit(solution)/shard_map/ppermute | solution.py:487
  82.7 25.3 %collective-permute-start.2 = (bf16[4,48,2048]{2,1,0:T(8,128)(2,1)S(1)}, bf16[4,48,2048]{2,1,0:T(8,128)(2,1)}, u32[]{:S(2)}, u32[]{:S(2)}) collective-permute-start(bf16[4,48,2048]{2,1,0:T(8,128)(2,1)S(1)} %copy-done.15), channel_id=1, source_target_pairs={{0,1},{1,0},{2,3},{3,2},{4,5},{5,4},{6,7},{7,6},{8,9},{9,8},{10,11... | collective-permute-start | bytes 2359304 | tf_op jit(solution)/shard_map/ppermute | solution.py:487
  82.7 26.4 %collective-permute-start.6 = (bf16[4,48,2048]{2,1,0:T(8,128)(2,1)S(1)}, bf16[4,48,2048]{2,1,0:T(8,128)(2,1)}, u32[]{:S(2)}, u32[]{:S(2)}) collective-permute-start(bf16[4,48,2048]{2,1,0:T(8,128)(2,1)S(1)} %copy-done.19), channel_id=1, source_target_pairs={{0,1},{1,0},{2,3},{3,2},{4,5},{5,4},{6,7},{7,6},{8,9},{9,8},{10,11... | collective-permute-start | bytes 2359304 | tf_op jit(solution)/shard_map/ppermute | solution.py:487
  83.2 25.9 %collective-permute-start.4 = (bf16[4,48,2048]{2,1,0:T(8,128)(2,1)}, bf16[4,48,2048]{2,1,0:T(8,128)(2,1)}, u32[]{:S(2)}, u32[]{:S(2)}) collective-permute-start(bf16[4,48,2048]{2,1,0:T(8,128)(2,1)} %collective-permute-done.3.refs_2_.refs_1_), channel_id=1, source_target_pairs={{0,1},{1,0},{2,3},{3,2},{4,5},{5,4},{6,7},{7,6},{8,9},{9,8},{10,11... | collective-permute-start | bytes 2359304 | tf_op jit(solution)/shard_map/ppermute | solution.py:487
  99.3 189.4 %all-gather.20.cloned.1.call-start = ((), (), s32[]{:S(2)}) async-start(), calls=%async_computation.9 | async-start | bytes 3604480 | tf_op jit(solution)/shard_map/all_gather | solution.py:620
  100.6 200.8 %all-gather.14.cloned.1.call-start = ((), (), s32[]{:S(2)}) async-start(), calls=%async_computation.6 | async-start | bytes 5898240 | tf_op jit(solution)/shard_map/all_gather | solution.py:620
  107.9 31.9 %collective-permute-start.18 = (bf16[4,48,3584]{2,1,0:T(8,128)(2,1)}, bf16[4,48,3584]{2,1,0:T(8,128)(2,1)}, u32[]{:S(2)}, u32[]{:S(2)}) collective-permute-start(bf16[4,48,3584]{2,1,0:T(8,128)(2,1)} %tie.21.refs_0_), channel_id=1, source_target_pairs={{0,4},{1,5},{2,6},{3,7},{4,0},{5,1},{6,2},{7,3},{8,12},{9,13},{10,... | collective-permute-start | bytes 4128776 | tf_op jit(solution)/shard_map/ppermute | solution.py:487
  108.5 64.9 %collective-permute-start.16 = (bf16[4,48,3584]{2,1,0:T(8,128)(2,1)}, bf16[4,48,3584]{2,1,0:T(8,128)(2,1)}, u32[]{:S(2)}, u32[]{:S(2)}) collective-permute-start(bf16[4,48,3584]{2,1,0:T(8,128)(2,1)} %tie.21.refs_0_), channel_id=1, source_target_pairs={{0,2},{1,3},{2,0},{3,1},{4,6},{5,7},{6,4},{7,5},{8,10},{9,11},{10,... | collective-permute-start | bytes 4128776 | tf_op jit(solution)/shard_map/ppermute | solution.py:487
  124.8 48.6 %collective-permute-start.24 = (bf16[512,1024]{1,0:T(8,128)(2,1)S(1)}, bf16[512,1024]{1,0:T(8,128)(2,1)}, u32[]{:S(2)}, u32[]{:S(2)}) collective-permute-start(bf16[512,1024]{1,0:T(8,128)(2,1)S(1)} %fusion.23), channel_id=1, source_target_pairs={{0,8},{8,16},{16,24},{1,9},{9,17},{17,25},{2,10},{10,18},{18,26},{... | collective-permute-start | bytes 3145736 | tf_op jit(solution)/shard_map/ppermute | solution.py:693
  141.9 48.1 %collective-permute-start.20 = (bf16[2,48,3584]{2,1,0:T(8,128)(2,1)}, bf16[2,48,3584]{2,1,0:T(8,128)(2,1)}, u32[]{:S(2)}, u32[]{:S(2)}) collective-permute-start(bf16[2,48,3584]{2,1,0:T(8,128)(2,1)} %slice.428), channel_id=1, source_target_pairs={{0,2},{1,3},{2,0},{3,1},{4,6},{5,7},{6,4},{7,5},{8,10},{9,11},{10,... | collective-permute-start | bytes 2064392 | tf_op jit(solution)/shard_map/ppermute | solution.py:487
  173.4 34.0 %collective-permute-start.25 = (bf16[512,1024]{1,0:T(8,128)(2,1)}, bf16[512,1024]{1,0:T(8,128)(2,1)}, u32[]{:S(2)}, u32[]{:S(2)}) collective-permute-start(bf16[512,1024]{1,0:T(8,128)(2,1)} %tie.22), channel_id=1, source_target_pairs={{0,8},{8,16},{16,24},{1,9},{9,17},{17,25},{2,10},{10,18},{18,26},{... | collective-permute-start | bytes 3145736 | tf_op jit(solution)/shard_map/ppermute | solution.py:693
  189.5 25.5 %collective-permute-start.15 = (bf16[4,48,3584]{2,1,0:T(8,128)(2,1)}, bf16[4,48,3584]{2,1,0:T(8,128)(2,1)}, u32[]{:S(2)}, u32[]{:S(2)}) collective-permute-start(bf16[4,48,3584]{2,1,0:T(8,128)(2,1)} %tie.21.refs_0_), channel_id=1, source_target_pairs={{0,1},{1,0},{2,3},{3,2},{4,5},{5,4},{6,7},{7,6},{8,9},{9,8},{10,11... | collective-permute-start | bytes 4128776 | tf_op jit(solution)/shard_map/ppermute | solution.py:487
  189.5 26.5 %collective-permute-start.19 = (bf16[4,48,3584]{2,1,0:T(8,128)(2,1)}, bf16[4,48,3584]{2,1,0:T(8,128)(2,1)}, u32[]{:S(2)}, u32[]{:S(2)}) collective-permute-start(bf16[4,48,3584]{2,1,0:T(8,128)(2,1)} %collective-permute-done.18.refs_4_.refs_2_), channel_id=1, source_target_pairs={{0,1},{1,0},{2,3},{3,2},{4,5},{5,4},{6,7},{7,6},{8,9},{9,8},{10,11... | collective-permute-start | bytes 4128776 | tf_op jit(solution)/shard_map/ppermute | solution.py:487
  190.0 26.1 %collective-permute-start.17 = (bf16[4,48,3584]{2,1,0:T(8,128)(2,1)}, bf16[4,48,3584]{2,1,0:T(8,128)(2,1)}, u32[]{:S(2)}, u32[]{:S(2)}) collective-permute-start(bf16[4,48,3584]{2,1,0:T(8,128)(2,1)} %collective-permute-done.16.refs_2_.refs_1_), channel_id=1, source_target_pairs={{0,1},{1,0},{2,3},{3,2},{4,5},{5,4},{6,7},{7,6},{8,9},{9,8},{10,11... | collective-permute-start | bytes 4128776 | tf_op jit(solution)/shard_map/ppermute | solution.py:487
  208.6 211.6 %all-gather.18.cloned.1.call-start = ((), (), s32[]{:S(2)}) async-start(), calls=%async_computation.8 | async-start | bytes 2949120 | tf_op jit(solution)/shard_map/all_gather | solution.py:620
  214.9 23.5 %collective-permute-start.27 = (bf16[512,1536]{1,0:T(8,128)(2,1)}, bf16[512,1536]{1,0:T(8,128)(2,1)}, u32[]{:S(2)}, u32[]{:S(2)}) collective-permute-start(bf16[512,1536]{1,0:T(8,128)(2,1)} %get-tuple-element.100.refs_8_.refs_6_), channel_id=1, source_target_pairs={{0,1},{1,0},{2,3},{3,2},{4,5},{5,4},{6,7},{7,6},{8,9},{9,8},{10,11... | collective-permute-start | bytes 4718600 | tf_op jit(solution)/shard_map/ppermute | solution.py:487
  215.5 23.0 %collective-permute-start.26 = (bf16[512,1536]{1,0:T(8,128)(2,1)}, bf16[512,1536]{1,0:T(8,128)(2,1)}, u32[]{:S(2)}, u32[]{:S(2)}) collective-permute-start(bf16[512,1536]{1,0:T(8,128)(2,1)} %get-tuple-element.101.refs_8_.refs_6_), channel_id=1, source_target_pairs={{0,1},{1,0},{2,3},{3,2},{4,5},{5,4},{6,7},{7,6},{8,9},{9,8},{10,11... | collective-permute-start | bytes 4718600 | tf_op jit(solution)/shard_map/ppermute | solution.py:487
  215.5 22.9 %collective-permute-start.29 = (bf16[256,1536]{1,0:T(8,128)(2,1)}, bf16[256,1536]{1,0:T(8,128)(2,1)}, u32[]{:S(2)}, u32[]{:S(2)}) collective-permute-start(bf16[256,1536]{1,0:T(8,128)(2,1)} %collective-permute-done.14.refs_2_.refs_11_.refs_9_), channel_id=1, source_target_pairs={{0,1},{1,0},{2,3},{3,2},{4,5},{5,4},{6,7},{7,6},{8,9},{9,8},{10,11... | collective-permute-start | bytes 2359304 | tf_op jit(solution)/shard_map/ppermute | solution.py:487
  281.0 29.2 %collective-permute-start.30 = (bf16[512,1664]{1,0:T(8,128)(2,1)}, bf16[512,1664]{1,0:T(8,128)(2,1)}, u32[]{:S(2)}, u32[]{:S(2)}) collective-permute-start(bf16[512,1664]{1,0:T(8,128)(2,1)} %concatenate.128.refs_6_.refs_4_), channel_id=1, source_target_pairs={{0,1},{1,0},{2,3},{3,2},{4,5},{5,4},{6,7},{7,6},{8,9},{9,8},{10,11... | collective-permute-start | bytes 5111816 | tf_op jit(solution)/shard_map/ppermute | solution.py:487
  281.5 28.8 %collective-permute-start.31 = (bf16[512,1536]{1,0:T(8,128)(2,1)S(1)}, bf16[512,1536]{1,0:T(8,128)(2,1)}, u32[]{:S(2)}, u32[]{:S(2)}) collective-permute-start(bf16[512,1536]{1,0:T(8,128)(2,1)S(1)} %bitcast.219), channel_id=1, source_target_pairs={{0,1},{1,0},{2,3},{3,2},{4,5},{5,4},{6,7},{7,6},{8,9},{9,8},{10,11... | collective-permute-start | bytes 4718600 | tf_op jit(solution)/shard_map/ppermute | solution.py:487
  285.8 49.2 %collective-permute-start.33 = (bf16[512,1664]{1,0:T(8,128)(2,1)}, bf16[512,1664]{1,0:T(8,128)(2,1)}, u32[]{:S(2)}, u32[]{:S(2)}) collective-permute-start(bf16[512,1664]{1,0:T(8,128)(2,1)} %concatenate.128.refs_6_.refs_4_), channel_id=1, source_target_pairs={{0,4},{1,5},{2,6},{3,7},{4,0},{5,1},{6,2},{7,3},{8,12},{9,13},{10,... | collective-permute-start | bytes 5111816 | tf_op jit(solution)/shard_map/ppermute | solution.py:487
  287.3 47.6 %collective-permute-start.32 = (bf16[512,1664]{1,0:T(8,128)(2,1)}, bf16[512,1664]{1,0:T(8,128)(2,1)}, u32[]{:S(2)}, u32[]{:S(2)}) collective-permute-start(bf16[512,1664]{1,0:T(8,128)(2,1)} %concatenate.128.refs_6_.refs_4_), channel_id=1, source_target_pairs={{0,2},{1,3},{2,0},{3,1},{4,6},{5,7},{6,4},{7,5},{8,10},{9,11},{10,... | collective-permute-start | bytes 5111816 | tf_op jit(solution)/shard_map/ppermute | solution.py:487
  301.4 127.1 %all-gather.16.cloned.1.call-start = ((), (), s32[]{:S(2)}) async-start(), calls=%async_computation.7 | async-start | bytes 4915200 | tf_op jit(solution)/shard_map/all_gather | solution.py:620
  340.5 29.4 %collective-permute-start.39 = (bf16[512,1664]{1,0:T(8,128)(2,1)}, bf16[512,1664]{1,0:T(8,128)(2,1)}, u32[]{:S(2)}, u32[]{:S(2)}) collective-permute-start(bf16[512,1664]{1,0:T(8,128)(2,1)} %get-tuple-element.118.refs_6_.refs_4_), channel_id=1, source_target_pairs={{0,1},{1,0},{2,3},{3,2},{4,5},{5,4},{6,7},{7,6},{8,9},{9,8},{10,11... | collective-permute-start | bytes 5111816 | tf_op jit(solution)/shard_map/ppermute | solution.py:487
  340.5 27.5 %collective-permute-start.35 = (bf16[256,1664]{1,0:T(8,128)(2,1)S(1)}, bf16[256,1664]{1,0:T(8,128)(2,1)S(1)}, u32[]{:S(2)}, u32[]{:S(2)}) collective-permute-start(bf16[256,1664]{1,0:T(8,128)(2,1)S(1)} %slice.369), channel_id=1, source_target_pairs={{0,2},{1,3},{2,0},{3,1},{4,6},{5,7},{6,4},{7,5},{8,10},{9,11},{10,... | collective-permute-start | bytes 2555912 | tf_op jit(solution)/shard_map/ppermute | solution.py:487
  342.1 26.0 %collective-permute-start.36 = (bf16[256,1664]{1,0:T(8,128)(2,1)S(1)}, bf16[256,1664]{1,0:T(8,128)(2,1)S(1)}, u32[]{:S(2)}, u32[]{:S(2)}) collective-permute-start(bf16[256,1664]{1,0:T(8,128)(2,1)S(1)} %slice.370), channel_id=1, source_target_pairs={{0,4},{1,5},{2,6},{3,7},{4,0},{5,1},{6,2},{7,3},{8,12},{9,13},{10,... | collective-permute-start | bytes 2555912 | tf_op jit(solution)/shard_map/ppermute | solution.py:487
  343.6 455.3 %reduce-scatter.2.cloned.1.call-start = ((), (), s32[]{:S(2)}) async-start(), calls=%async_computation.4 | async-start | bytes 4259840 | tf_op jit(solution)/shard_map/reduce_scatter | solution.py:843
  369.3 25.0 %collective-permute-start.37 = (bf16[256,1664]{1,0:T(8,128)(2,1)}, bf16[256,1664]{1,0:T(8,128)(2,1)S(1)}, u32[]{:S(2)}, u32[]{:S(2)}) collective-permute-start(bf16[256,1664]{1,0:T(8,128)(2,1)} %get-tuple-element.119.refs_6_.refs_4_), channel_id=1, source_target_pairs={{0,1},{1,0},{2,3},{3,2},{4,5},{5,4},{6,7},{7,6},{8,9},{9,8},{10,11... | collective-permute-start | bytes 2555912 | tf_op jit(solution)/shard_map/ppermute | solution.py:487
  369.3 25.0 %collective-permute-start.38 = (bf16[256,1664]{1,0:T(8,128)(2,1)}, bf16[256,1664]{1,0:T(8,128)(2,1)S(1)}, u32[]{:S(2)}, u32[]{:S(2)}) collective-permute-start(bf16[256,1664]{1,0:T(8,128)(2,1)} %get-tuple-element.120.refs_7_.refs_5_), channel_id=1, source_target_pairs={{0,1},{1,0},{2,3},{3,2},{4,5},{5,4},{6,7},{7,6},{8,9},{9,8},{10,11... | collective-permute-start | bytes 2555912 | tf_op jit(solution)/shard_map/ppermute | solution.py:487
  481.8 27.1 %collective-permute-start.43 = (bf16[272,1664]{1,0:T(8,128)(2,1)}, bf16[272,1664]{1,0:T(8,128)(2,1)S(1)}, u32[]{:S(2)}, u32[]{:S(2)}) collective-permute-start(bf16[272,1664]{1,0:T(8,128)(2,1)} %get-tuple-element.243), channel_id=1, source_target_pairs={{0,2},{1,3},{2,0},{3,1},{4,6},{5,7},{6,4},{7,5},{8,10},{9,11},{10,... | collective-permute-start | bytes 2715656 | tf_op jit(solution)/shard_map/ppermute | solution.py:487
  483.3 25.7 %collective-permute-start.42 = (bf16[272,1664]{1,0:T(8,128)(2,1)S(1)}, bf16[272,1664]{1,0:T(8,128)(2,1)S(1)}, u32[]{:S(2)}, u32[]{:S(2)}) collective-permute-start(bf16[272,1664]{1,0:T(8,128)(2,1)S(1)} %get-tuple-element.244), channel_id=1, source_target_pairs={{0,4},{1,5},{2,6},{3,7},{4,0},{5,1},{6,2},{7,3},{8,12},{9,13},{10,... | collective-permute-start | bytes 2715656 | tf_op jit(solution)/shard_map/ppermute | solution.py:487
  519.0 41.5 %collective-permute-start.46 = (bf16[544,1664]{1,0:T(8,128)(2,1)}, bf16[544,1664]{1,0:T(8,128)(2,1)}, u32[]{:S(2)}, u32[]{:S(2)}) collective-permute-start(bf16[544,1664]{1,0:T(8,128)(2,1)} %pad_maximum_fusion.1.refs_12_), channel_id=1, source_target_pairs={{0,2},{1,3},{2,0},{3,1},{4,6},{5,7},{6,4},{7,5},{8,10},{9,11},{10,... | collective-permute-start | bytes 5431304 | tf_op jit(solution)/shard_map/ppermute | solution.py:487
  523.1 41.5 %collective-permute-start.47 = (bf16[544,1664]{1,0:T(8,128)(2,1)}, bf16[544,1664]{1,0:T(8,128)(2,1)}, u32[]{:S(2)}, u32[]{:S(2)}) collective-permute-start(bf16[544,1664]{1,0:T(8,128)(2,1)} %pad_maximum_fusion.2.refs_13_), channel_id=1, source_target_pairs={{0,4},{1,5},{2,6},{3,7},{4,0},{5,1},{6,2},{7,3},{8,12},{9,13},{10,... | collective-permute-start | bytes 5431304 | tf_op jit(solution)/shard_map/ppermute | solution.py:487
  591.9 23.8 %collective-permute-start.51 = (bf16[256,1536]{1,0:T(8,128)(2,1)}, bf16[256,1536]{1,0:T(8,128)(2,1)}, u32[]{:S(2)}, u32[]{:S(2)}) collective-permute-start(bf16[256,1536]{1,0:T(8,128)(2,1)} %get-tuple-element.245), channel_id=1, source_target_pairs={{0,4},{1,5},{2,6},{3,7},{4,0},{5,1},{6,2},{7,3},{8,12},{9,13},{10,... | collective-permute-start | bytes 2359304 | tf_op jit(solution)/shard_map/ppermute | solution.py:487
  592.4 27.2 %collective-permute-start.54 = (bf16[256,1536]{1,0:T(8,128)(2,1)}, bf16[256,1536]{1,0:T(8,128)(2,1)}, u32[]{:S(2)}, u32[]{:S(2)}) collective-permute-start(bf16[256,1536]{1,0:T(8,128)(2,1)} %get-tuple-element.246), channel_id=1, source_target_pairs={{0,2},{1,3},{2,0},{3,1},{4,6},{5,7},{6,4},{7,5},{8,10},{9,11},{10,... | collective-permute-start | bytes 2359304 | tf_op jit(solution)/shard_map/ppermute | solution.py:487
  614.4 29.7 %collective-permute-start.56 = (bf16[512,512]{1,0:T(8,128)(2,1)S(1)}, bf16[512,512]{1,0:T(8,128)(2,1)}, u32[]{:S(2)}, u32[]{:S(2)}) collective-permute-start(bf16[512,512]{1,0:T(8,128)(2,1)S(1)} %slice.390), channel_id=1, source_target_pairs={{8,0},{16,8},{24,16},{9,1},{17,9},{25,17},{10,2},{18,10},{26,18},{... | collective-permute-start | bytes 1572872 | tf_op jit(solution)/shard_map/ppermute | solution.py:891
  618.6 96.6 %collective-permute-start.52 = (bf16[512,1536]{1,0:T(8,128)(2,1)}, bf16[512,1536]{1,0:T(8,128)(2,1)}, u32[]{:S(2)}, u32[]{:S(2)}) collective-permute-start(bf16[512,1536]{1,0:T(8,128)(2,1)} %pad_maximum_fusion.3.rest_0_), channel_id=1, source_target_pairs={{0,2},{1,3},{2,0},{3,1},{4,6},{5,7},{6,4},{7,5},{8,10},{9,11},{10,... | collective-permute-start | bytes 4718600 | tf_op jit(solution)/shard_map/ppermute | solution.py:487
  622.2 92.9 %collective-permute-start.55 = (bf16[512,1536]{1,0:T(8,128)(2,1)}, bf16[512,1536]{1,0:T(8,128)(2,1)}, u32[]{:S(2)}, u32[]{:S(2)}) collective-permute-start(bf16[512,1536]{1,0:T(8,128)(2,1)} %pad_maximum_fusion.4.rest_1_), channel_id=1, source_target_pairs={{0,4},{1,5},{2,6},{3,7},{4,0},{5,1},{6,2},{7,3},{8,12},{9,13},{10,... | collective-permute-start | bytes 4718600 | tf_op jit(solution)/shard_map/ppermute | solution.py:487
  644.1 26.9 %collective-permute-start.57 = (bf16[512,512]{1,0:T(8,128)(2,1)}, bf16[512,512]{1,0:T(8,128)(2,1)}, u32[]{:S(2)}, u32[]{:S(2)}) collective-permute-start(bf16[512,512]{1,0:T(8,128)(2,1)} %tie.32), channel_id=1, source_target_pairs={{8,0},{16,8},{24,16},{9,1},{17,9},{25,17},{10,2},{18,10},{26,18},{... | collective-permute-start | bytes 1572872 | tf_op jit(solution)/shard_map/ppermute | solution.py:896
  647.5 25.6 %collective-permute-start.58 = (bf16[512,512]{1,0:T(8,128)(2,1)}, bf16[512,512]{1,0:T(8,128)(2,1)}, u32[]{:S(2)}, u32[]{:S(2)}) collective-permute-start(bf16[512,512]{1,0:T(8,128)(2,1)} %add_convert_fusion.20), channel_id=1, source_target_pairs={{8,0},{16,8},{24,16},{9,1},{17,9},{25,17},{10,2},{18,10},{26,18},{... | collective-permute-start | bytes 1572872 | tf_op jit(solution)/shard_map/ppermute | solution.py:899
  671.0 120.5 %collective-permute-start.48 = (bf16[512,1536]{1,0:T(8,128)(2,1)}, bf16[512,1536]{1,0:T(8,128)(2,1)}, u32[]{:S(2)}, u32[]{:S(2)}) collective-permute-start(bf16[512,1536]{1,0:T(8,128)(2,1)} %get-tuple-element.142), channel_id=1, source_target_pairs={{0,1},{1,0},{2,3},{3,2},{4,5},{5,4},{6,7},{7,6},{8,9},{9,8},{10,11... | collective-permute-start | bytes 4718600 | tf_op jit(solution)/shard_map/ppermute | solution.py:487
  673.2 40.0 %collective-permute-start.59 = (bf16[512,512]{1,0:T(8,128)(2,1)}, bf16[512,512]{1,0:T(8,128)(2,1)S(1)}, u32[]{:S(2)}, u32[]{:S(2)}) collective-permute-start(bf16[512,512]{1,0:T(8,128)(2,1)} %tie.34), channel_id=1, source_target_pairs={{8,0},{16,8},{24,16},{9,1},{17,9},{25,17},{10,2},{18,10},{26,18},{... | collective-permute-start | bytes 1572872 | tf_op jit(solution)/shard_map/ppermute | solution.py:900
  759.6 42.5 %all-to-all-start.2 = ((bf16[32,2,3136]{2,1,0:T(2,128)(2,1)}), bf16[32,2,3136]{2,1,0:T(2,128)(2,1)}, u32[]{:S(2)}, u32[]{:S(2)}) async-start(bf16[32,2,3136]{2,1,0:T(2,128)(2,1)} %reshape.381), calls=%async_computation.2 | async-start | bytes 819200 | tf_op jit(solution)/shard_map/all_to_all | solution.py:923
  (153 other events, 1783.7 us)
Sparse Core Ops, SparseCore 0:
  38.3 30.9 all-gather.11
  101.8 79.8 all-gather.19
  208.7 92.6 all-gather.13
  302.8 48.9 all-gather.17
  353.2 75.2 all-gather.15
  665.5 79.2 reduce-scatter.1

commit v3 on v2

--- a/solution.py
+++ b/solution.py
@@ -191,7 +191,7 @@
 BACK_ROWS = 2 * ADAPTER_RANK
 
 
-def expert_kernel(count, splits, experts, capacity, with_prior, with_shared, waits, *refs):
+def expert_kernel(count, splits, experts, capacity, depth, with_prior, with_shared, with_sums, packed, waits, *refs):
     meta, refs = refs[0], refs[1:]
     weight_count = 5 if with_shared else 3
     weight_refs, refs = refs[:weight_count], refs[weight_count:]
@@ -206,15 +206,21 @@
     if with_prior:
         prior_moe, refs = refs[:count], refs[count:]
         prior_back, refs = refs[:count], refs[count:]
+    grad_count = 4 if with_shared else 3
+    sums_in = ()
+    if with_sums:
+        sums_in, refs = refs[:grad_count], refs[grad_count:]
     refs = refs[waits:]
     moe_refs, refs = refs[:count], refs[count:]
     back_refs, refs = refs[:count], refs[count:]
-    grad_count = 4 if with_shared else 3
-    grad_outs, refs = refs[:grad_count], refs[grad_count:]
+    out_count = 1 if packed else grad_count
+    grad_outs, refs = refs[:out_count], refs[out_count:]
     grad_sums, refs = refs[:grad_count], refs[grad_count:]
     first_grad, down_grad, second_grad = grad_sums[:3]
     weight_bufs, refs = refs[:weight_count], refs[weight_count:]
-    tokens_buf, grad_buf, moe_buf, back_buf, in_sem, out_sem, weight_sem, sum_sem = refs
+    if packed:
+        pack_buf, refs = refs[0], refs[1:]
+    tokens_buf, grad_buf, moe_buf, back_buf, in_sem, out_sem, weight_sem, sum_sem, sum_in_sem = refs
 
     step = pl.program_id(0)
     steps = count // 2
@@ -271,7 +277,10 @@
                     copy.start()
 
     def sum_copy(n):
-        return pltpu.make_async_copy(grad_sums[n], grad_outs[n], sum_sem.at[n])
+        return pltpu.make_async_copy(pack_buf if packed else grad_sums[n], grad_outs[n], sum_sem.at[n])
+
+    def sum_in(n):
+        return pltpu.make_async_copy(sums_in[n], grad_sums[n], sum_in_sem.at[n])
 
     @pl.when(step == 0)
     def _():
@@ -286,8 +295,11 @@
         for i in (0, 1):
             for copy in incoming(0, i, (2,)):
                 copy.start()
-        for total in grad_sums:
-            total[...] = jnp.zeros_like(total)
+        for n, total in enumerate(grad_sums):
+            if with_sums:
+                sum_in(n).start()
+            else:
+                total[...] = jnp.zeros_like(total)
 
     expert = meta[0]
     lane = lax.broadcasted_iota(jnp.int32, (1, LANES), 1)
@@ -340,6 +352,13 @@
     grad_gate = jnp.sum(output * grad_rows, axis=1, keepdims=True)
     weighted = (gate * output).astype(BF16)
 
+    if with_sums:
+
+        @pl.when(step == 0)
+        def _():
+            for n in range(grad_count):
+                sum_in(n).wait()
+
     grad_y = (gate * grad_rows).astype(BF16)
     glow_down = (dot_nt(grad_y, second_ref[:, 2 * hidden :]) * select).astype(BF16)
     second_grad[:, 2 * hidden :] += dot_tn(low_down, grad_y)
@@ -370,8 +389,18 @@
 
     @pl.when(step == steps - 1)
     def _():
-        for n in range(3):
-            sum_copy(n).start()
+        if not packed:
+            for n in range(3):
+                sum_copy(n).start()
+            return
+        second_t = second_grad[...].T
+        parts = [first_grad[:, :LANES], first_grad[:, LANES:], down_grad[...], second_t]
+        at = 0
+        for part in parts:
+            size = part.shape[0] // depth
+            for z in range(depth):
+                pack_buf[z, at : at + size, :] = part[z * size : (z + 1) * size].astype(BF16)
+            at += size
 
     for i in (0, 1):
         mine = slice(i * capacity, (i + 1) * capacity)
@@ -428,16 +457,23 @@
 
     @pl.when(step == steps - 1)
     def _():
-        for n in range(3, grad_count):
+        if packed and with_shared:
+            size = grad_sums[3].shape[0] // depth
+            for z in range(depth):
+                part = grad_sums[3][z * size : (z + 1) * size, :]
+                if size % 16:
+                    part = jnp.concatenate([part, jnp.zeros((16 - size % 16, LANES), F32)], axis=0)
+                pack_buf[z, pack_buf.shape[1] - part.shape[0] :, :] = part.astype(BF16)
+        for n in range(0 if packed else 3, out_count):
             sum_copy(n).start()
         for i in (0, 1):
             for copy in outgoing(steps - 1, i):
                 copy.wait()
-        for n in range(grad_count):
+        for n in range(out_count):
             sum_copy(n).wait()
 
 
-def expert_call(meta, weights, tokens, grads, prior, experts, capacity, deps=()):
+def expert_call(meta, weights, tokens, grads, prior, sums, packed, experts, capacity, depth, deps=()):
     count = len(tokens)
     with_shared = len(weights) > 3
     splits = [len(pieces) for pieces in tokens]
@@ -454,18 +490,28 @@
     ]
     if with_shared:
         grad_shapes.append(jax.ShapeDtypeStruct((weights[3].shape[0], LANES), F32))
+    out_shapes = grad_shapes
+    if packed:
+        lines = sum(s.shape[0] for s in grad_shapes[:2]) + model + weights[2].shape[1]
+        lines = lines // depth
+        if with_shared:
+            lines += -(-weights[3].shape[0] // depth // 16) * 16
+        out_shapes = [jax.ShapeDtypeStruct((depth, lines, LANES), BF16)]
     back_rows = rows + BACK_ROWS
     outs = pl.pallas_call(
-        functools.partial(expert_kernel, count, splits, experts, capacity, bool(prior), with_shared, len(deps)),
+        functools.partial(
+            expert_kernel, count, splits, experts, capacity, depth, bool(prior), with_shared, bool(sums), packed, len(deps)
+        ),
         grid=(count // 2,),
         in_specs=[pl.BlockSpec(memory_space=pltpu.SMEM)]
-        + [anywhere] * (len(weights) + len(flat) + len(prior) + len(deps)),
-        out_specs=[anywhere] * (2 * count + len(grad_shapes)),
+        + [anywhere] * (len(weights) + len(flat) + len(prior) + len(sums) + len(deps)),
+        out_specs=[anywhere] * (2 * count + len(out_shapes)),
         out_shape=[jax.ShapeDtypeStruct((rows, model), BF16)] * count
         + [jax.ShapeDtypeStruct((back_rows, wide), BF16)] * count
-        + grad_shapes,
+        + out_shapes,
         scratch_shapes=[pltpu.VMEM(s.shape, F32) for s in grad_shapes]
         + [pltpu.VMEM(w.shape, BF16) for w in weights]
+        + ([pltpu.VMEM(out_shapes[0].shape, BF16)] if packed else [])
         + [
             pltpu.VMEM((slots, 2, rows, wide), BF16),
             pltpu.VMEM((slots, 2, rows, model), BF16),
@@ -475,11 +521,12 @@
             pltpu.SemaphoreType.DMA((slots, 2, 2)),
             pltpu.SemaphoreType.DMA((len(weights),)),
             pltpu.SemaphoreType.DMA((len(grad_shapes),)),
+            pltpu.SemaphoreType.DMA((len(grad_shapes),)),
         ],
         compiler_params=pltpu.CompilerParams(vmem_limit_bytes=VMEM_LIMIT),
         cost_estimate=cost(12.0 * count),
         name="expert",
-    )(meta, *weights, *flat, *prior, *deps)
+    )(meta, *weights, *flat, *prior, *sums, *deps)
     return outs[:count], outs[count : 2 * count], outs[2 * count :]
 
 
@@ -571,6 +618,151 @@
         name="assemble",
     )(me.astype(jnp.int32).reshape(1), *flat, *deps)
     return [out.reshape(-1, out.shape[-1]) for out in outs]
+
+
+def query_back_kernel(q_one, q_two, normed, low_q, q_w, first_q, second_q, grad_normed, first_query, second_query):
+    half = q_one.shape[1]
+    glow_q = (dot_nt(q_one[...], second_q[:, :half]) + dot_nt(q_two[...], second_q[:, half:])).astype(BF16)
+    grad_normed[...] = (
+        dot_nt(q_one[...], q_w[:, :half]) + dot_nt(q_two[...], q_w[:, half:]) + dot_nt(glow_q, first_q[...])
+    )
+    first_query[...] = dot_tn(normed[...], glow_q)
+    second_query[:, :half] = dot_tn(low_q[...], q_one[...])
+    second_query[:, half:] = dot_tn(low_q[...], q_two[...])
+
+
+def query_back(args):
+    rows, model = args[2].shape
+    vmem = pl.BlockSpec(memory_space=pltpu.VMEM)
+    shapes = [(rows, model), (model, ADAPTER_RANK), (ADAPTER_RANK, HEADS * HEAD_DIM)]
+    return pl.pallas_call(
+        query_back_kernel,
+        in_specs=[vmem] * len(args),
+        out_specs=[vmem] * len(shapes),
+        out_shape=[jax.ShapeDtypeStruct(shape, F32) for shape in shapes],
+        compiler_params=pltpu.CompilerParams(vmem_limit_bytes=VMEM_LIMIT),
+        cost_estimate=cost(2.0),
+        name="query_back",
+    )(*args)
+
+
+def middle_kernel(waits, attn, glow_out, normed2, glow_sgu, grad_mid, out_low, grad_out, low_sdown, *rest):
+    first_early, second_out, second_down = rest[waits:]
+    rank = ADAPTER_RANK
+    first_early[:, :rank] = dot_tn(attn[...], glow_out[...])
+    first_early[:, rank:] = dot_tn(normed2[...], glow_sgu[...])
+    second_out[...] = dot_tn(out_low[...], grad_mid[...])
+    second_down[...] = dot_tn(low_sdown[...], grad_out[...])
+
+
+def middle(args, deps):
+    model = args[0].shape[1]
+    rank = ADAPTER_RANK
+    vmem = pl.BlockSpec(memory_space=pltpu.VMEM)
+    shapes = [(model, 3 * rank), (rank, model), (rank, model)]
+    return pl.pallas_call(
+        functools.partial(middle_kernel, len(deps)),
+        in_specs=[vmem] * len(args) + [pl.BlockSpec(memory_space=pl.ANY)] * len(deps),
+        out_specs=[vmem] * len(shapes),
+        out_shape=[jax.ShapeDtypeStruct(shape, F32) for shape in shapes],
+        compiler_params=pltpu.CompilerParams(vmem_limit_bytes=VMEM_LIMIT),
+        cost_estimate=cost(2.0),
+        name="middle",
+    )(*args, *deps)
+
+
+def last_kernel(
+    owners, one, two, normed, low_kv, kv_w, first_kv, second_k, second_v, hidden, gain, grad_mid, grad_normed_q,
+    first_query, first_early, second_query, second_early, adapter, grad_hidden, first_out, second_out
+):
+    rank = ADAPTER_RANK
+    count = one.shape[1] // (2 * HEAD_DIM)
+    heads = [(half, n) for half in (one, two) for n in range(count)]
+    grad_k = jnp.concatenate([half[:, 2 * n * HEAD_DIM : (2 * n + 1) * HEAD_DIM] for half, n in heads], axis=1)
+    grad_v = jnp.concatenate([half[:, (2 * n + 1) * HEAD_DIM : (2 * n + 2) * HEAD_DIM] for half, n in heads], axis=1)
+    width = grad_k.shape[1]
+    glow_k = dot_nt(grad_k, second_k[...]).astype(BF16)
+    glow_v = dot_nt(grad_v, second_v[...]).astype(BF16)
+    grad_normed = grad_normed_q[...] + dot_nt(grad_k, kv_w[:, :width]) + dot_nt(grad_v, kv_w[:, width:])
+    grad_normed = grad_normed + dot_nt(glow_k, first_kv[:, :rank]) + dot_nt(glow_v, first_kv[:, rank:])
+    values = hidden[...].astype(F32)
+    scale = lax.rsqrt(jnp.mean(values * values, axis=-1, keepdims=True) + EPSILON)
+    scaled = grad_normed * gain[...]
+    mean = jnp.mean(values * scaled, axis=-1, keepdims=True)
+    grad_hidden[...] = grad_mid[...] + scale * scaled - values * (scale * scale * scale * mean)
+    firsts = [first_query[...], dot_tn(normed[...], glow_k), dot_tn(normed[...], glow_v), first_early[...]]
+    tags = jnp.broadcast_to(adapter[...], (first_query.shape[0], LANES - 6 * rank))
+    first_out[...] = jnp.concatenate(firsts + [tags], axis=1).astype(BF16)
+    seconds = [second_query[...], dot_tn(low_kv[:, :rank], grad_k), dot_tn(low_kv[:, rank:], grad_v), second_early[...]]
+    seconds = jnp.concatenate(seconds, axis=1)
+    columns = seconds.shape[1] // owners
+    padding = jnp.zeros((rank, second_out.shape[1] // rank * LANES - columns), F32)
+    for n in range(owners):
+        piece = jnp.concatenate([seconds[:, n * columns : (n + 1) * columns], padding], axis=1).astype(BF16)
+        for c in range(piece.shape[1] // LANES):
+            second_out[n, c * rank : (c + 1) * rank, :] = piece[:, c * LANES : (c + 1) * LANES]
+
+
+def last(owners, args):
+    rows, model = args[8].shape
+    columns = (args[14].shape[1] + 2 * KV_HEADS * HEAD_DIM + args[15].shape[1]) // owners
+    vmem = pl.BlockSpec(memory_space=pltpu.VMEM)
+    return pl.pallas_call(
+        functools.partial(last_kernel, owners),
+        in_specs=[vmem] * len(args),
+        out_specs=[vmem] * 3,
+        out_shape=[
+            jax.ShapeDtypeStruct((rows, model), F32),
+            jax.ShapeDtypeStruct((model, LANES), BF16),
+            jax.ShapeDtypeStruct((owners, -(-columns // LANES) * ADAPTER_RANK, LANES), BF16),
+        ],
+        compiler_params=pltpu.CompilerParams(vmem_limit_bytes=VMEM_LIMIT),
+        cost_estimate=cost(2.0),
+        name="last",
+    )(*args)
+
+
+def spread_kernel(depth, lines, flat, first_out, second_out):
+    rank = ADAPTER_RANK
+    size = flat.shape[0] // depth
+    row = lax.broadcasted_iota(jnp.int32, (LANES, 1), 0).astype(F32)
+    column = lax.broadcasted_iota(jnp.int32, (1, first_out.shape[1]), 1)
+    inside = column % LANES
+    target = (column // LANES * rank + inside).astype(F32)
+    owner = (inside // rank).astype(F32)
+    short = lax.broadcasted_iota(jnp.int32, (1, rank), 1).astype(F32)
+    chunks = (flat.shape[1] - lines) // rank
+    first, second = None, [None] * chunks
+    for d in range(size):
+        adapter = flat[d, 0:1, 6 * rank : 6 * rank + 1].astype(F32)
+        total = flat[d].astype(F32)
+        for z in range(1, depth):
+            total = total + flat[z * size + d].astype(F32)
+        total = total.astype(BF16)
+        place = ((target - adapter * float(rank) == row) & (owner == adapter)).astype(F32).astype(BF16)
+        lift = (row - adapter * float(rank) == short).astype(F32).astype(BF16)
+        part = dot_nn(total[:lines], place)
+        first = part if first is None else first + part
+        for c in range(chunks):
+            part = dot_nn(lift, total[lines + c * rank : lines + (c + 1) * rank])
+            second[c] = part if second[c] is None else second[c] + part
+    first_out[...] = first
+    for c in range(chunks):
+        second_out[:, c * LANES : (c + 1) * LANES] = second[c]
+
+
+def spread(flat, depth, lines):
+    vmem = pl.BlockSpec(memory_space=pltpu.VMEM)
+    chunks = (flat.shape[1] - lines) // ADAPTER_RANK
+    return pl.pallas_call(
+        functools.partial(spread_kernel, depth, lines),
+        in_specs=[vmem],
+        out_specs=[vmem] * 2,
+        out_shape=[jax.ShapeDtypeStruct((lines, 6 * LANES), F32), jax.ShapeDtypeStruct((LANES, chunks * LANES), F32)],
+        compiler_params=pltpu.CompilerParams(vmem_limit_bytes=VMEM_LIMIT),
+        cost_estimate=cost(2.0),
+        name="spread",
+    )(flat)
 
 
 def per_device(
@@ -645,13 +837,6 @@
     seq_kv = over_seq(pack_kv)
     seq_q = over_seq(tie(pack_q, seq_kv))
 
-    present_tag = jnp.where(key_present == 1, document_number, -1).astype(F32)
-    tag_blocks = [
-        lax.ppermute(present_tag + 1.0, "seq", [(i, i + h) for i in range(depth - h)]) - 1.0 for h in range(hops, 0, -1)
-    ] + [present_tag]
-    key_tag = jnp.concatenate(tag_blocks, axis=1).reshape((hops + 1) * rows, 1)
-    query_tag = document_number.astype(F32)
-
     flags = jnp.sum((routes[0][..., None] == jnp.arange(experts, dtype=jnp.int32)).astype(F32), axis=1)
     before = (jnp.arange(rows)[:, None] > jnp.arange(rows)[None, :]).astype(BF16)
     slots = jnp.where(flags > 0, dot_nn(before, flags.astype(BF16)), -1.0).astype(BF16)
@@ -665,12 +850,15 @@
 
     grad_out_b = output_gradient[0]
     grads_x, grads_y = swap(grad_out_b, 2, size), swap(grad_out_b, 4, size)
-    kv_gathered = plane_gather(tie(seq_kv, grads_x, grads_y), size)
-    grads_x, grads_y = tie_all([grads_x, grads_y], kv_gathered[2][0], kv_gathered[4][0])
+    gate_up = shared_gate_up_weight.reshape(shard_rows, 2, depth, size, units // depth)
+    gate_up = gate_up.transpose(3, 0, 1, 2, 4).reshape(size, shard_rows, 2 * units)
+    gate_up = lax.all_to_all(gate_up, "dp", split_axis=0, concat_axis=0, tiled=True)
+    kv_gathered = plane_gather(tie(seq_kv, grads_x, grads_y, gate_up), size)
+    grads_x, grads_y = tie_all([grads_x, grads_y], *kv_gathered[6])
     far_grads = (swap(grads_y[: rows // 2], 2, size), swap(grads_x[rows // 2 :], 4, size))
     grad_blocks = [(grad_out_b,), None, (grads_x,), None, (grads_y,), None, far_grads, None]
     kv_w, kv_first, second_t, small = assemble(
-        kv_gathered, ((1, 2 * kv_width), (1, 2 * rank_all), (groups, rank_all), (1, LANES)), me, tag_blocks[:hops]
+        kv_gathered, ((1, 2 * kv_width), (1, 2 * rank_all), (groups, rank_all), (1, LANES)), me
     )
     router_w = small[:, :experts]
     gains = small[:, experts : experts + 2].astype(F32).T
@@ -684,7 +872,9 @@
     normed = rms_norm(x_flat, gains[0]).astype(BF16)
     low_kv = dot_nn(normed, first_kv).astype(BF16)
     kv_extra = jnp.concatenate([dot_nn(low_kv[:, :rank], b_parts[1]), dot_nn(low_kv[:, rank:], b_parts[2])], axis=1)
-    kv_blocks = [(dot_nn(normed, kv_w) + kv_extra).astype(BF16)]
+    present_tag = jnp.where(key_present == 1, document_number + 1, 0).astype(BF16)
+    tag_columns = jnp.broadcast_to(present_tag.reshape(rows, 1), (rows, LANES))
+    kv_blocks = [jnp.concatenate([(dot_nn(normed, kv_w) + kv_extra).astype(BF16), tag_columns], axis=1)]
     q_blocks = plane_gather(tie(seq_q, *far_grads), size)
     for k in range(1, size, 2):
         grad_blocks[k] = tuple(swap(piece, 1, size) for piece in grad_blocks[k - 1])
@@ -693,6 +883,8 @@
         kv_blocks.append(lax.ppermute(block, "seq", forward))
         kv_blocks[h] = block
     kv_all = jnp.concatenate(kv_blocks[::-1], axis=0)
+    key_tag = kv_all[:, 2 * kv_width : 2 * kv_width + 1].astype(F32)
+    query_tag = (document_number + 1).astype(F32)
 
     down_rows = routed_down_weight.shape[1]
     second_cut = rank_all * routed_second_factor.shape[2] // down_rows
@@ -708,9 +900,6 @@
             routed_second_factor[j].reshape(down_rows, -1),
         ]
         if j == 0:
-            gate_up = shared_gate_up_weight.reshape(shard_rows, 2, depth, size, units // depth)
-            gate_up = gate_up.transpose(3, 0, 1, 2, 4).reshape(size, shard_rows, 2 * units)
-            gate_up = lax.all_to_all(tie(gate_up, kv_gathered[2][0], kv_gathered[4][0]), "dp", split_axis=0, concat_axis=0, tiled=True)
             up_parts.append(gate_up.reshape(size * shard_rows, 2 * units))
             shared_down = jnp.concatenate([shared_down_weight, shared_down_first_factor], axis=1)
             down_parts.append(shared_down.reshape(down_rows, -1))
@@ -718,8 +907,8 @@
         down_shards.append(jnp.concatenate(down_parts, axis=1))
     seq_up, seq_down = [], []
     for j in range(local_experts):
-        seq_up.append(over_seq(tie(up_shards[j], seq_q if j == 0 else seq_up[j - 1])))
-        seq_down.append(over_seq(tie(down_shards[j], seq_q if j == 0 else seq_up[j - 1])))
+        seq_up.append(over_seq(tie(up_shards[j], seq_kv if j == 0 else seq_up[j - 1])))
+        seq_down.append(over_seq(tie(down_shards[j], seq_kv if j == 0 else seq_up[j - 1])))
 
     q_w, q_first, out_w = assemble(q_blocks, ((1, query_width), (1, 4 * rank_all), (1, model)), me)
     q_first = own_factors(q_first)
@@ -773,7 +962,7 @@
             args.append(jnp.concatenate([part.reshape(units, rank_all) for part in slices], axis=0))
         return args
 
-    def run_expert(j, args, group, prior, deps):
+    def run_expert(j, args, group, prior, deps, packed=False):
         meta = jnp.stack([me * local_experts + j, me]).astype(jnp.int32)
         prior = ([moe_parts[k] for k in group], [back_parts[k] for k in group]) if prior else None
         moe_out, back_out, grads = expert_call(
@@ -782,20 +971,23 @@
             [token_blocks[k] for k in group],
             [grad_blocks[k] for k in group],
             prior,
+            grad_sums[-1],
+            packed,
             experts,
             capacity,
+            depth,
             deps,
         )
         for n, k in enumerate(group):
             moe_parts[k], back_parts[k] = moe_out[n], back_out[n]
-        grad_sums[-1] = list(grads) if grad_sums[-1] is None else [a + b for a, b in zip(grad_sums[-1], grads)]
+        grad_sums[-1] = list(grads)
 
     for j in range(local_experts - 1):
-        grad_sums.append(None)
+        grad_sums.append([])
         args = weights_of(j)
         previous = ()
         for group in ((0, 1), (2, 3), (4, 5), (6, 7)):
-            run_expert(j, args, group, j > 0, previous)
+            run_expert(j, args, group, j > 0, previous, group == (6, 7))
             previous = (back_parts[group[0]],)
             if j == 0 and group == (0, 1):
                 far = gather_far(tokens_x, tokens_y, *previous)
@@ -803,7 +995,12 @@
                 gather_farthest(far, *previous)
     if local_experts == 1:
         gather_farthest(gather_far(tokens_x, tokens_y))
-    grad_sums.append(None)
+
+    def scatter(packed):
+        return lax.psum_scatter(packed, "seq", scatter_dimension=0, tiled=True)
+
+    packed_sums = [scatter(grads[0]) for grads in grad_sums]
+    grad_sums.append([])
     j, prior, half = local_experts - 1, local_experts > 1, (rows + BACK_ROWS) // 2
     args = weights_of(j)
     run_expert(j, args, (6, 7), prior, (back_parts[6],) if prior else ())
@@ -811,12 +1008,14 @@
     run_expert(j, args, (2, 3), prior, (pair_six,))
     from_diagonal_x, from_diagonal_y = swap(pair_six[:half], 2, size), swap(pair_six[half:], 4, size)
     pair_two = add(back_parts[2], swap(back_parts[3], 1, size))
-    run_expert(j, args, (4, 5), prior, (pair_two,))
+    run_expert(j, args, (4, 5), prior, (pair_two, *packed_sums))
     pair_four = add(back_parts[4], swap(tie(back_parts[5], from_diagonal_x, from_diagonal_y), 1, size))
     to_x = jnp.concatenate([pair_two[:half], add(pair_two[half:], from_diagonal_y)], axis=0)
     to_y = jnp.concatenate([add(pair_four[:half], from_diagonal_x), pair_four[half:]], axis=0)
-    run_expert(j, args, (0, 1), prior, (to_x, to_y))
-    back_sum = add(back_parts[0], swap(back_parts[1], 1, size), swap(to_x, 2, size), swap(to_y, 4, size))
+    run_expert(j, args, (0, 1), prior, (to_x, to_y), True)
+    packed_sums.append(scatter(grad_sums[-1][0]))
+    from_x, from_y = swap(to_x, 2, size), swap(to_y, 4, size)
+    back_sum = add(back_parts[0], swap(tie(back_parts[1], from_x, from_y), 1, size), from_x, from_y)
     back = back_sum.astype(F32)
 
     half = rows // 2
@@ -830,24 +1029,16 @@
     low_sdown = tail[:, 3 * experts + 2 * rank : 3 * experts + 3 * rank].astype(BF16)
 
     owner_rows = model // depth
-    packed = [grads[0].astype(BF16).reshape(depth, owner_rows, 2 * rank_all) for grads in grad_sums]
-    packed.append(
-        jnp.concatenate([g[1] for g in grad_sums], axis=1).astype(BF16).reshape(depth, -1, 2 * rank_all)
-    )
-    for grads in grad_sums:
-        packed.append(
-            grads[2].astype(BF16).reshape(rank_all, depth, -1).transpose(1, 0, 2).reshape(depth, -1, 2 * rank_all)
-        )
-    packed.append(grad_sums[0][3].astype(BF16).reshape(depth, -1, 2 * rank_all))
-    lines = [part.shape[1] for part in packed]
-    packed_sum = lax.psum_scatter(jnp.concatenate(packed, axis=1), "seq", scatter_dimension=0, tiled=True)
-    packed = packed_sum[0].astype(F32)
-    cuts = [sum(lines[:n]) for n in range(len(lines) + 1)]
-    pieces = [packed[cuts[n] : cuts[n + 1]] for n in range(len(lines))]
-    grad_expert_a = jnp.stack(pieces[:local_experts]).reshape(local_experts, owner_rows, 2, rank_all)
-    grad_expert_a_down = pieces[local_experts].reshape(down_rows, local_experts, rank_all).transpose(1, 0, 2)
-    grad_expert_b = jnp.stack(pieces[local_experts + 1 : -1]).reshape(local_experts, rank_all, -1)
-    grad_first_down = pieces[-1].reshape(shared_rows, rank_all)
+    firsts, downs, seconds = [], [], []
+    for packed in packed_sums:
+        packed = packed[0].astype(F32)
+        firsts.append(jnp.stack([packed[:owner_rows], packed[owner_rows : 2 * owner_rows]], axis=1))
+        at = 2 * owner_rows + down_rows
+        downs.append(packed[2 * owner_rows : at])
+        seconds.append(packed[at : at + routed_second_factor.shape[2]].T)
+    at += routed_second_factor.shape[2]
+    grad_expert_a, grad_expert_a_down, grad_expert_b = jnp.stack(firsts), jnp.stack(downs), jnp.stack(seconds)
+    grad_first_down = packed_sums[0][0, at : at + shared_rows].astype(F32)
 
     grad_out = grad_out_b.astype(F32)
     grad_gates = tail[:, :experts] + tail[:, experts : 2 * experts]
@@ -863,91 +1054,45 @@
     glow_out = dot_nt(grad_mid_b, b_parts[3]).astype(BF16)
     grad_attn = (dot_nt(grad_mid_b, out_w) + dot_nt(glow_out, first_o)).astype(BF16)
 
-    def spread_out(flat, pieces):
-        width = sum(p.size // (depth * size) for p in pieces)
-        flat = flat.astype(F32)
-        chosen = (flat[:, width : width + 1] == jnp.arange(rank_all // rank, dtype=F32)[None, :]).astype(F32)
-        spread = jnp.sum(chosen[:, :, None] * flat[:, None, :width], axis=0)
-        outs, at = [], 0
-        for p in pieces:
-            count = p.shape[0] // (depth * size)
-            outs.append(spread[:, at : at + count * p.shape[1]].reshape(-1, count, p.shape[1]))
-            at += count * p.shape[1]
-        return outs
-
-    def tagged(flat):
-        return jnp.concatenate([flat, jnp.full((flat.shape[0], LANES), adapter.astype(F32)).astype(flat.dtype)], axis=1)
-
     def shared_columns(block):
         block = block[:, :SHARED_HIDDEN].reshape(rank, size, depth, units // depth)
-        return block.transpose(0, 2, 1, 3).reshape(rank, SHARED_HIDDEN).T
-
-    def pack_for_owners(pieces):
-        return tagged(jnp.concatenate([p.astype(BF16).reshape(depth * size, -1) for p in pieces], axis=1))
+        return block.transpose(0, 2, 1, 3).reshape(rank, SHARED_HIDDEN)
 
     count = KV_HEADS // 2
     grad_q_one, grad_kv_one = attend_back(query, kv_all, grad_attn, lse, query_tag, key_tag, hops, 0, count, (pair[6], pair[2], pair[4]))
     one = grad_kv_one[:rows]
     hop_one = lax.ppermute(one, "seq", backward)
     grad_q_two, grad_kv_two = attend_back(
-        query, kv_all, grad_attn, lse, query_tag, key_tag, hops, count, count, (moe_to_x, moe_to_y)
+        query, kv_all, grad_attn, lse, query_tag, key_tag, hops, count, count, (moe_to_x, moe_to_y, packed_sums[-1])
     )
     two = tie(grad_kv_two[:rows], hop_one)
     hop_two = lax.ppermute(two, "seq", backward)
+    grad_normed_q, first_query, second_query = query_back(
+        [grad_q_one, grad_q_two, normed, low_q, q_w, first_q, b_parts[0]]
+    )
     for h in range(hops):
         own = slice((h + 1) * rows, (h + 2) * rows)
         from_one = hop_one if h == 0 else lax.ppermute(one, "seq", backward)
-        from_two = hop_two if h == 0 else lax.ppermute(tie(two, from_one), "seq", backward)
+        from_two = hop_two if h == 0 else lax.ppermute(tie(two, from_one, first_query), "seq", backward)
         one, two = add(grad_kv_one[own], from_one), add(grad_kv_two[own], from_two)
-    late_deps = (hop_two, moe_from_x, moe_from_y)
-    glow_out_t, glow_sgu_t, out_low_t, shared_rows_t, low_sdown_t, grad_q = tie_all(
-        [glow_out, glow_sgu, out_low, back[rows:], low_sdown, jnp.concatenate([grad_q_one, grad_q_two], axis=1)],
-        *late_deps,
-    )
-    hidden_out = (mid + moe + dot_nn(low_sdown_t, b_parts[6])).astype(BF16)[None]
-
-    early = [
-        jnp.concatenate([dot_tn(attn, glow_out_t), dot_tn(normed2, glow_sgu_t)], axis=1),
-        jnp.concatenate(
-            [
-                jnp.zeros((query_width + 2 * kv_width, rank), F32),
-                dot_tn(grad_mid_b, out_low_t),
-                shared_columns(shared_rows_t[:rank]),
-                shared_columns(shared_rows_t[rank:]),
-                dot_tn(grad_out_b, low_sdown_t),
-            ],
-            axis=0,
-        ),
-    ]
-    early_packed = pack_for_owners(early)
-    early_flat = lax.all_to_all(early_packed, ("seq", "dp"), split_axis=0, concat_axis=0, tiled=True)
-    one, two = tie_all([one, two], early_packed)
-    grad_kvs = [half_[:, 2 * n * HEAD_DIM : 2 * (n + 1) * HEAD_DIM] for half_ in (one, two) for n in range(count)]
-    glow_q = dot_nt(grad_q, b_parts[0]).astype(BF16)
-    grad_normed = dot_nt(grad_q, q_w) + dot_nt(glow_q, first_q)
-    grad_k = jnp.concatenate([piece[:, :HEAD_DIM] for piece in grad_kvs], axis=1)
-    grad_v = jnp.concatenate([piece[:, HEAD_DIM:] for piece in grad_kvs], axis=1)
-    glow_kv = jnp.concatenate([dot_nt(grad_k, b_parts[1]), dot_nt(grad_v, b_parts[2])], axis=1).astype(BF16)
-    late = [
-        jnp.concatenate([dot_tn(normed, glow_q), dot_tn(normed, glow_kv)], axis=1).astype(BF16),
-        jnp.concatenate(
-            [
-                dot_tn(grad_q, low_q).astype(BF16),
-                dot_tn(grad_k, low_kv[:, :rank]).astype(BF16),
-                dot_tn(grad_v, low_kv[:, rank:]).astype(BF16),
-                jnp.zeros((edges[-1] - edges[3], rank), BF16),
-            ],
-            axis=0,
-        ),
-    ]
-    late_flat = lax.all_to_all(pack_for_owners(late), ("seq", "dp"), split_axis=0, concat_axis=0, tiled=True)
-    grad_normed = grad_normed + dot_nt(jnp.concatenate([grad_k, grad_v], axis=1), kv_w) + dot_nt(glow_kv, first_kv)
-    _, norm1_back = jax.vjp(lambda values_in: rms_norm(values_in, gains[0]), x_flat)
-    grad_hidden = (grad_mid + norm1_back(grad_normed)[0])[None]
-    early_parts, late_parts = spread_out(early_flat, early), spread_out(late_flat, late)
-    grad_first = jnp.concatenate([late_parts[0], early_parts[0]], axis=2)
-    grad_first = grad_first.reshape(-1, shard_rows, 6, rank).transpose(1, 2, 0, 3).reshape(shard_rows, 6, rank_all)
-    grad_second = (early_parts[1] + late_parts[1]).transpose(0, 2, 1).reshape(rank_all, second_columns)
+    first_early, second_out, second_down = middle(
+        [attn, glow_out, normed2, glow_sgu, grad_mid_b, out_low, grad_out_b, low_sdown], (hop_two,)
+    )
+    hidden_out = (mid + moe + dot_nn(low_sdown, b_parts[6])).astype(BF16)[None]
+    second_early = jnp.concatenate(
+        [second_out, shared_columns(back[rows : rows + rank]), shared_columns(back[rows + rank :]), second_down], axis=1
+    )
+    grad_hidden, first_flat, second_flat = last(
+        depth * size,
+        [one, two, normed, low_kv, kv_w, first_kv, b_parts[1], b_parts[2], block_input[0], gains[0:1], grad_mid]
+        + [grad_normed_q, first_query, first_early, second_query, second_early, adapter.astype(F32).reshape(1, 1)],
+    )
+    flat = jnp.concatenate([first_flat.reshape(depth * size, shard_rows, LANES), second_flat], axis=1)
+    flat = lax.all_to_all(flat, ("seq", "dp"), split_axis=0, concat_axis=0, tiled=True)
+    grad_first, grad_second = spread(flat, depth, shard_rows)
+    grad_first = grad_first.reshape(shard_rows, 6, rank_all)
+    grad_second = grad_second[:, :second_columns]
+    grad_hidden = grad_hidden[None]
     return (
         hidden_out,
         grad_hidden,

time: 848 us -> 777 us (0.916)
  local copies, waits for them, and re-layouts: 163 us -> 113 us
  Pallas kernels: 258 us -> 299 us
  other arithmetic: 85.6 us -> 59.8 us
  matrix products: 62.5 us -> 37.3 us
  starting transfers between devices: 86.6 us -> 69.4 us
    pallas_call x0 -> x4, Pallas kernels: none -> 28.7 us  [the longest x1 12.1 us: last(): pl.pallas_call(functools.partial(last_kernel, owners), in_specs=[vmem] *...]
    ppermute x3 -> x1, waiting for transfers between devices: 34.1 us -> 8.91 us  [per_device(): lax.ppermute(tie(two, from_one, first_query), 'seq', backward)]
    concatenate x14 -> x1, local copies, waits for them, and re-layouts: 19.9 us -> 0.94 us  [own_factors(): jnp.concatenate([own_columns(matrix[:, n * rank_all:(n + 1) * rank_all])...]
    ppermute x2, waiting for transfers between devices: 33.3 us -> 50.8 us  [per_device(): kv_blocks.append(lax.ppermute(block, 'seq', forward))]
    dot_general x12 -> x5, matrix products: 25.4 us -> 10.1 us  [dot_nt(): lax.dot_general(left, right, (((1,), (1,)), ((), ())), preferred_element_...]
    reshape x15 -> x2, local copies, waits for them, and re-layouts: 17.8 us -> 2.8 us  [shared_columns(): return block.transpose(0, 2, 1, 3).reshape(rank, SHARED_HIDDEN)]
    unnamed x291 -> x207, local copies, waits for them, and re-layouts: 49.4 us -> 35.3 us
    pallas_call x8, Pallas kernels: 182 us -> 196 us  [expert_call(): pl.pallas_call(functools.partial(expert_kernel, count, splits, experts, c...]
  transfers between devices with their start and end apart: 69 -> 67, of which waited for: 16 -> 20; matrix products, arithmetic and copies ran while one was open for 33% -> 24% of each run, Pallas kernels for 26% -> 36%
where the time goes in v3:
time: 777 us; the launch traced here: 766 us
  Pallas kernels  299 us (38%)
  waiting for transfers between devices  150 us (19%)
  local copies, waits for them, and re-layouts  113 us (15%)
  starting transfers between devices  69.4 us (9%)
  other arithmetic  59.8 us (8%)
  matrix products  37.3 us (5%)
  blocking collectives  20.3 us (3%)
  between operations  16.8 us (2%)
    pallas_call x8, Pallas kernels, expert_call(): pl.pallas_call(functools.partial(expert_kernel, count, splits, experts, c...  196 us
    ppermute x52, waiting for transfers between devices, swap(): return lax.ppermute(array, 'dp', [(i, i ^ bit) for i in range(size)])  64.8 us
    ppermute x2, waiting for transfers between devices, per_device(): kv_blocks.append(lax.ppermute(block, 'seq', forward))  50.8 us
    pallas_call x2, Pallas kernels, attend_back(): pl.pallas_call(functools.partial(attend_back_kernel, spans, hops * rows,...  36.8 us
    ppermute x52, starting transfers between devices, swap(): return lax.ppermute(array, 'dp', [(i, i ^ bit) for i in range(size)])  35.8 us
    unnamed x207, local copies, waits for them, and re-layouts  35.3 us
    pallas_call x1, Pallas kernels, attend(): pl.pallas_call(functools.partial(attend_kernel, spans, hops * rows, len(d...  23.7 us
    dot_general x14, matrix products, dot_nn(): return jnp.dot(left, right, preferred_element_type=F32)  23.2 us
  transfers between devices with their start and end apart: 67, of which 20 were waited for; matrix products, arithmetic and copies ran while one was open for 24% of the time, Pallas kernels for 36%

profile of v3, /device:TPU:0, one launch (start us, length us, event | category | flops | bytes accessed | tf_op | source)
XLA Modules:
  0.0 765.6 jit_solution(16639502327853135471)
XLA Ops:
  7.2 3.0 collective-permute-start
  15.1 3.4 all-to-all-start
  18.8 20.3 %all-gather = bf16[192,2048]{1,0:T(8,128)(2,1)} all-gather(bf16[48,2048]{1,0:T(8,128)(2,1)S(1)} %fusion.23), channel_id=2, replica_groups=mesh['seq'=4,'dp'=8] {'seq'}, dimensions={0}, use_global_device_ids=true | all-gather | bytes 983040 | tf_op jit(solution)/shard_map/all_gather | solution.py:812
  51.7 17.2 %collective-permute-done.3.refs_2_ = bf16[4,48,2048]{2,1,0:T(8,128)(2,1)S(1)} collective-permute-done((bf16[4,48,2048]{2,1,0:T(8,128)(2,1)}, bf16[4,48,2048]{2,1,0:T(8,128)(2,1)S(1)}, u32[]{:S(2)}, u32[]{:S(2)}) %collective-permute-start.3) | collective-permute-done | bytes 786464 | tf_op jit(solution)/shard_map/ppermute | solution.py:534
  74.1 5.7 collective-permute-done.8.refs_7_.refs_3_
  87.9 5.6 assemble.2
  96.5 3.4 constant_dynamic-slice_fusion.6
  112.6 4.6 collective-permute-start.22
  117.2 37.9 %collective-permute-done.22.refs_0_ = bf16[512,1152]{1,0:T(8,128)(2,1)} collective-permute-done((bf16[512,1152]{1,0:T(8,128)(2,1)S(1)}, bf16[512,1152]{1,0:T(8,128)(2,1)}, u32[]{:S(2)}, u32[]{:S(2)}) %collective-permute-start.22) | collective-permute-done | bytes 1179680 | tf_op jit(solution)/shard_map/ppermute | solution.py:883
  155.1 5.6 collective-permute-start.23
  170.2 9.5 %collective-permute-done.18.refs_6_ = bf16[2,48,3584]{2,1,0:T(8,128)(2,1)} collective-permute-done((bf16[2,48,3584]{2,1,0:T(8,128)(2,1)}, bf16[2,48,3584]{2,1,0:T(8,128)(2,1)}, u32[]{:S(2)}, u32[]{:S(2)}) %collective-permute-start.18) | collective-permute-done | bytes 688160 | tf_op jit(solution)/shard_map/ppermute | solution.py:534
  183.1 12.9 %collective-permute-done.23 = bf16[512,1152]{1,0:T(8,128)(2,1)} collective-permute-done((bf16[512,1152]{1,0:T(8,128)(2,1)}, bf16[512,1152]{1,0:T(8,128)(2,1)}, u32[]{:S(2)}, u32[]{:S(2)}) %collective-permute-start.23) | collective-permute-done | bytes 1179680 | tf_op jit(solution)/shard_map/ppermute | solution.py:883
  202.1 8.4 %assemble.3 = (bf16[4,8,1,48,1536]{4,3,2,1,0:T(8,128)(2,1)}, bf16[4,8,1,48,512]{4,3,2,1,0:T(8,128)(2,1)}, bf16[4,8,1,48,1536]{4,3,2,1,0:T(8,128)(2,1)}) custom-call(s32[1]{0:T(128)} %bitcast.1.me_ref, bf16[4,48,3584]{2,1,0:T(8,128)(2,1)} %tie.19.refs_0_, bf16[4,48,3584]{2,1,0:T(8,128)(2,1)} %collective-permute-done.13.refs_1_, ...), custom_call_target="tpu_custom_call" | custom-call | tf_op jit(solution)/shard_map/assemble/pallas_call | solution.py:607
  220.7 3.8 fusion.6.q_ref
  224.6 23.7 %attend.1 = (bf16[512,1536]{1,0:T(8,128)(2,1)}, f32[4,3,512]{2,1,0:T(4,128)}) custom-call(bf16[512,1536]{1,0:T(8,128)(2,1)} %fusion.6.q_ref, bf16[1536,1152]{1,0:T(8,128)(2,1)} %copy-done.16, bf16[1536,1152]{1,0:T(8,128)(2,1)} %copy-done.16, f32[1,512]{1,0:T(1,128)} %add_convert_fusion.17.qt_ref, f32[1536,1]{1,0:T(8,128)} %slice_convert_fusion.kt_ref, ...), custom_call_target="tpu_custom_call" | custom-call | flops 26530500608 | bytes 1000000 | tf_op jit(solution)/shard_map/attend/pallas_call | solution.py:96
  251.8 4.7 multiply_reduce_fusion.1
  263.3 3.6 concatenate.74.refs_6_.refs_4_
  282.2 8.8 %all-gather.16.cloned.1.call-start = ((), (), s32[]{:S(2)}) async-start(), calls=%async_computation.8 | async-start | bytes 4915200 | tf_op jit(solution)/shard_map/all_gather | solution.py:812
  291.0 24.6 %expert.8 = (bf16[512,1536]{1,0:T(8,128)(2,1)}, bf16[512,1536]{1,0:T(8,128)(2,1)}, bf16[544,1664]{1,0:T(8,128)(2,1)}, bf16[544,1664]{1,0:T(8,128)(2,1)}, f32[153...) custom-call(s32[2]{0:T(128)} %pad_add_fusion.1.refs_0_, ...), custom_call_target="tpu_custom_call" | custom-call | flops 27683999744 | bytes 1000000 | tf_op jit(solution)/shard_map/expert/pallas_call | solution.py:501
  315.6 3.2 collective-permute-done.30.refs_0_
  327.9 26.7 %expert.9 = (bf16[512,1536]{1,0:T(8,128)(2,1)}, bf16[512,1536]{1,0:T(8,128)(2,1)}, bf16[544,1664]{1,0:T(8,128)(2,1)}, bf16[544,1664]{1,0:T(8,128)(2,1)}, f32[153...) custom-call(s32[2]{0:T(128)} %pad_add_fusion.1.refs_0_, ...), custom_call_target="tpu_custom_call" | custom-call | flops 27683999744 | bytes 1000000 | tf_op jit(solution)/shard_map/expert/pallas_call | solution.py:501
  356.4 26.7 %expert.10 = (bf16[512,1536]{1,0:T(8,128)(2,1)}, bf16[512,1536]{1,0:T(8,128)(2,1)}, bf16[544,1664]{1,0:T(8,128)(2,1)}, bf16[544,1664]{1,0:T(8,128)(2,1)}, f32[15...) custom-call(s32[2]{0:T(128)} %pad_add_fusion.1.refs_0_, ...), custom_call_target="tpu_custom_call" | custom-call | flops 27683999744 | bytes 1000000 | tf_op jit(solution)/shard_map/expert/pallas_call | solution.py:501
  384.3 27.2 %expert.11 = (bf16[512,1536]{1,0:T(8,128)(2,1)}, bf16[512,1536]{1,0:T(8,128)(2,1)}, bf16[544,1664]{1,0:T(8,128)(2,1)}, bf16[544,1664]{1,0:T(8,128)(2,1)}, bf16[4,1568,128]{2,1,0:T(8,128)(2,1)}) custom-call(s32[2]{0:T(128)} %pad_add_fusion.1.refs_0_, bf16[1536,1536]{1,0:T(8,128)(2,1)} %all-gather.14.cloned.1.call-done.refs_1_, bf16[512,1664]{1,0:T(8,128)(2,1)} %bitcast.200, ...), custom_call_target="tpu_custom_call" | custom-call | flops 27683999744 | bytes 1000000 | tf_op jit(solution)/shard_map/expert/pallas_call | solution.py:501
  417.0 4.2 all-gather.16.cloned.1.call-done.refs_1_
  421.2 21.0 %expert.12 = (bf16[512,1536]{1,0:T(8,128)(2,1)}, bf16[512,1536]{1,0:T(8,128)(2,1)}, bf16[544,1664]{1,0:T(8,128)(2,1)}, bf16[544,1664]{1,0:T(8,128)(2,1)}, f32[15...) custom-call(s32[2]{0:T(128)} %pad_add_fusion.refs_0_, ...), custom_call_target="tpu_custom_call" | custom-call | flops 27683999744 | bytes 1000000 | tf_op jit(solution)/shard_map/expert/pallas_call | solution.py:501
  442.3 3.9 collective-permute-done.38
  446.2 3.3 add_convert_fusion.3.refs_15_
  449.5 23.2 %expert.13 = (bf16[512,1536]{1,0:T(8,128)(2,1)}, bf16[512,1536]{1,0:T(8,128)(2,1)}, bf16[544,1664]{1,0:T(8,128)(2,1)}, bf16[544,1664]{1,0:T(8,128)(2,1)}, f32[15...) custom-call(s32[2]{0:T(128)} %pad_add_fusion.refs_0_, ...), custom_call_target="tpu_custom_call" | custom-call | flops 27683999744 | bytes 1000000 | tf_op jit(solution)/shard_map/expert/pallas_call | solution.py:501
  478.7 8.0 %reduce-scatter.3.cloned.1.call-done.refs_16_ = bf16[1,1568,128]{2,1,0:T(8,128)(2,1)} async-done(((bf16[4,1568,128]{2,1,0:T(8,128)(2,1)}), bf16[1,1568,128]{2,1,0:T(8,128)(2,1)}) %reduce-scatter.3.cloned.1.call-update) | async-done | bytes 401424 | tf_op jit(solution)/shard_map/reduce_scatter | solution.py:1000
  486.7 22.4 %expert.14 = (bf16[512,1536]{1,0:T(8,128)(2,1)}, bf16[512,1536]{1,0:T(8,128)(2,1)}, bf16[544,1664]{1,0:T(8,128)(2,1)}, bf16[544,1664]{1,0:T(8,128)(2,1)}, f32[15...) custom-call(s32[2]{0:T(128)} %pad_add_fusion.refs_0_, ...), custom_call_target="tpu_custom_call" | custom-call | flops 27683999744 | bytes 1000000 | tf_op jit(solution)/shard_map/expert/pallas_call | solution.py:501
  520.9 23.9 %expert.15 = (bf16[512,1536]{1,0:T(8,128)(2,1)}, bf16[512,1536]{1,0:T(8,128)(2,1)}, bf16[544,1664]{1,0:T(8,128)(2,1)}, bf16[544,1664]{1,0:T(8,128)(2,1)}, bf16[4,1536,128]{2,1,0:T(8,128)(2,1)}) custom-call(s32[2]{0:T(128)} %pad_add_fusion.refs_0_, bf16[1536,1280]{1,0:T(8,128)(2,1)} %all-gather.16.cloned.1.call-done.refs_1_, bf16[512,1664]{1,0:T(8,128)(2,1)} %bitcast.196, ...), custom_call_target="tpu_custom_call" | custom-call | flops 27683999744 | bytes 1000000 | tf_op jit(solution)/shard_map/expert/pallas_call | solution.py:501
  544.8 11.2 %collective-permute-done.43.refs_1_ = bf16[544,1664]{1,0:T(8,128)(2,1)S(1)} collective-permute-done((bf16[544,1664]{1,0:T(8,128)(2,1)}, bf16[544,1664]{1,0:T(8,128)(2,1)S(1)}, u32[]{:S(2)}, u32[]{:S(2)}) %collective-permute-start.43) | collective-permute-done | bytes 1810464 | tf_op jit(solution)/shard_map/ppermute | solution.py:534
  556.0 4.5 collective-permute-done.44.refs_2_
  565.5 3.7 fusion.58
  572.1 3.9 multiply_reduce_fusion
  576.8 4.9 fusion.56
  583.6 6.4 fusion.7.g_ref
  596.2 18.4 %attend_back.2 = (bf16[512,768]{1,0:T(8,128)(2,1)}, bf16[1536,512]{1,0:T(8,128)(2,1)}) custom-call(bf16[512,1536]{1,0:T(8,128)(2,1)} %fusion.6.q_ref, bf16[1536,1152]{1,0:T(8,128)(2,1)} %copy-done.16, bf16[1536,1152]{1,0:T(8,128)(2,1)} %copy-done.16, bf16[512,1536]{1,0:T(8,128)(2,1)} %fusion.7.g_ref, f32[4,3,512]{2,1,0:T(4,128)} %get-tuple-element.169.lse_ref, ...), custom_call_target="tpu_custom_call" | custom-call | flops 4614000128 | bytes 1000000 | tf_op jit(solution)/shard_map/attend_back/pallas_call | solution.py:159
  625.0 7.9 %collective-permute-done.54.refs_1_ = bf16[512,512]{1,0:T(8,128)(2,1)} collective-permute-done((bf16[512,512]{1,0:T(8,128)(2,1)}, bf16[512,512]{1,0:T(8,128)(2,1)}, u32[]{:S(2)}, u32[]{:S(2)}) %collective-permute-start.54) | collective-permute-done | bytes 524320 | tf_op jit(solution)/shard_map/ppermute | solution.py:1064
  638.9 5.0 collective-permute-done.52
  645.5 18.4 %attend_back.3 = (bf16[512,768]{1,0:T(8,128)(2,1)}, bf16[1536,512]{1,0:T(8,128)(2,1)}) custom-call(bf16[512,1536]{1,0:T(8,128)(2,1)} %fusion.6.q_ref, bf16[1536,1152]{1,0:T(8,128)(2,1)} %copy-done.16, bf16[1536,1152]{1,0:T(8,128)(2,1)} %copy-done.16, bf16[512,1536]{1,0:T(8,128)(2,1)} %fusion.7.g_ref, f32[4,3,512]{2,1,0:T(4,128)} %get-tuple-element.169.lse_ref, ...), custom_call_target="tpu_custom_call" | custom-call | flops 4614000128 | bytes 1000000 | tf_op jit(solution)/shard_map/attend_back/pallas_call | solution.py:159
  682.9 9.1 %query_back.1 = (f32[512,1536]{1,0:T(8,128)}, f32[1536,16]{1,0:T(8,128)}, f32[16,1536]{1,0:T(8,128)}) custom-call(bf16[512,768]{1,0:T(8,128)(2,1)} %get-tuple-element.173.q_one, bf16[512,768]{1,0:T(8,128)(2,1)} %get-tuple-element.174.q_two, bf16[512,1536]{1,0:T(8,128)(2,1)} %copy-done.5, bf16[512,16]{1,0:T(8,128)(2,1)} %copy-done.57, ...), custom_call_target="tpu_custom_call" | custom-call | flops 2307000064 | bytes 1000000 | tf_op jit(solution)/shard_map/query_back/pallas_call | solution.py:638
  697.7 5.2 middle.1
  704.6 8.9 %collective-permute-done.57 = bf16[512,512]{1,0:T(8,128)(2,1)S(1)} collective-permute-done((bf16[512,512]{1,0:T(8,128)(2,1)}, bf16[512,512]{1,0:T(8,128)(2,1)S(1)}, u32[]{:S(2)}, u32[]{:S(2)}) %collective-permute-start.57) | collective-permute-done | bytes 524320 | tf_op jit(solution)/shard_map/ppermute | solution.py:1076
  715.5 12.1 %last.1 = (f32[512,1536]{1,0:T(8,128)}, bf16[1536,128]{1,0:T(8,128)(2,1)}, bf16[32,32,128]{2,1,0:T(8,128)(2,1)}) custom-call(bf16[512,512]{1,0:T(8,128)(2,1)} %add_convert_fusion.15.one, bf16[512,512]{1,0:T(8,128)(2,1)} %add_convert_fusion.13.two, bf16[512,1536]{1,0:T(8,128)(2,1)} %copy-done.5, bf16[512,32]{1,0:T(8,128)(2,1)} %copy-done.45, ...), custom_call_target="tpu_custom_call" | custom-call | flops 2307000064 | bytes 1000000 | tf_op jit(solution)/shard_map/last/pallas_call | solution.py:710
  729.5 5.3 all-to-all-start.1
  744.1 4.8 fusion.10
  748.9 3.8 all-to-all-done.1.flat
  (490 shorter events, 214.9 us)
Async XLA Ops:
  7.2 42.3 %collective-permute-start = (bf16[512,1536]{1,0:T(8,128)(2,1)}, bf16[512,1536]{1,0:T(8,128)(2,1)}, u32[]{:S(2)}, u32[]{:S(2)}) collective-permute-start(bf16[512,1536]{1,0:T(8,128)(2,1)} %bitcast.169), channel_id=1, source_target_pairs={{0,2},{1,3},{2,0},{3,1},{4,6},{5,7},{6,4},{7,5},{8,10},{9,11},{10,... | collective-permute-start | bytes 4718600 | tf_op jit(solution)/shard_map/ppermute | solution.py:534
  10.2 39.3 %collective-permute-start.1 = (bf16[512,1536]{1,0:T(8,128)(2,1)}, bf16[512,1536]{1,0:T(8,128)(2,1)}, u32[]{:S(2)}, u32[]{:S(2)}) collective-permute-start(bf16[512,1536]{1,0:T(8,128)(2,1)} %bitcast.170), channel_id=1, source_target_pairs={{0,4},{1,5},{2,6},{3,7},{4,0},{5,1},{6,2},{7,3},{8,12},{9,13},{10,... | collective-permute-start | bytes 4718600 | tf_op jit(solution)/shard_map/ppermute | solution.py:534
  15.1 33.3 %all-to-all-start = ((bf16[8,48,256]{2,1,0:T(8,128)(2,1)}), bf16[8,48,256]{2,1,0:T(8,128)(2,1)S(1)}, u32[]{:S(2)}, u32[]{:S(2)}) async-start(bf16[8,48,256]{2,1,0:T(8,128)(2,1)} %copy.177), calls=%async_computation | async-start | bytes 393216 | tf_op jit(solution)/shard_map/all_to_all | solution.py:855
  18.5 89.1 %all-gather.12.cloned.1.call-start = ((), (), s32[]{:S(2)}) async-start(), calls=%async_computation.6 | async-start | bytes 1720320 | tf_op jit(solution)/shard_map/all_gather | solution.py:812
  40.0 231.7 %all-gather.20.cloned.1.call-start = ((), (), s32[]{:S(2)}) async-start(), calls=%async_computation.10 | async-start | bytes 3604480 | tf_op jit(solution)/shard_map/all_gather | solution.py:812
  49.6 19.3 %collective-permute-start.3 = (bf16[4,48,2048]{2,1,0:T(8,128)(2,1)}, bf16[4,48,2048]{2,1,0:T(8,128)(2,1)S(1)}, u32[]{:S(2)}, u32[]{:S(2)}) collective-permute-start(bf16[4,48,2048]{2,1,0:T(8,128)(2,1)} %tie.16.refs_0_), channel_id=1, source_target_pairs={{0,2},{1,3},{2,0},{3,1},{4,6},{5,7},{6,4},{7,5},{8,10},{9,11},{10,... | collective-permute-start | bytes 2359304 | tf_op jit(solution)/shard_map/ppermute | solution.py:534
  50.6 20.7 %collective-permute-start.5 = (bf16[4,48,2048]{2,1,0:T(8,128)(2,1)}, bf16[4,48,2048]{2,1,0:T(8,128)(2,1)S(1)}, u32[]{:S(2)}, u32[]{:S(2)}) collective-permute-start(bf16[4,48,2048]{2,1,0:T(8,128)(2,1)} %tie.16.refs_0_), channel_id=1, source_target_pairs={{0,4},{1,5},{2,6},{3,7},{4,0},{5,1},{6,2},{7,3},{8,12},{9,13},{10,... | collective-permute-start | bytes 2359304 | tf_op jit(solution)/shard_map/ppermute | solution.py:534
  73.4 208.7 %all-gather.14.cloned.1.call-start = ((), (), s32[]{:S(2)}) async-start(), calls=%async_computation.7 | async-start | bytes 5898240 | tf_op jit(solution)/shard_map/all_gather | solution.py:812
  86.7 20.8 %collective-permute-start.11 = (bf16[256,1536]{1,0:T(8,128)(2,1)}, bf16[256,1536]{1,0:T(8,128)(2,1)}, u32[]{:S(2)}, u32[]{:S(2)}) collective-permute-start(bf16[256,1536]{1,0:T(8,128)(2,1)} %slice.283), channel_id=1, source_target_pairs={{0,2},{1,3},{2,0},{3,1},{4,6},{5,7},{6,4},{7,5},{8,10},{9,11},{10,... | collective-permute-start | bytes 2359304 | tf_op jit(solution)/shard_map/ppermute | solution.py:534
  87.7 20.0 %collective-permute-start.12 = (bf16[256,1536]{1,0:T(8,128)(2,1)}, bf16[256,1536]{1,0:T(8,128)(2,1)}, u32[]{:S(2)}, u32[]{:S(2)}) collective-permute-start(bf16[256,1536]{1,0:T(8,128)(2,1)} %slice.284), channel_id=1, source_target_pairs={{0,4},{1,5},{2,6},{3,7},{4,0},{5,1},{6,2},{7,3},{8,12},{9,13},{10,... | collective-permute-start | bytes 2359304 | tf_op jit(solution)/shard_map/ppermute | solution.py:534
  107.6 47.5 %collective-permute-start.16 = (bf16[4,48,3584]{2,1,0:T(8,128)(2,1)}, bf16[4,48,3584]{2,1,0:T(8,128)(2,1)}, u32[]{:S(2)}, u32[]{:S(2)}) collective-permute-start(bf16[4,48,3584]{2,1,0:T(8,128)(2,1)} %tie.19.refs_0_), channel_id=1, source_target_pairs={{0,4},{1,5},{2,6},{3,7},{4,0},{5,1},{6,2},{7,3},{8,12},{9,13},{10,... | collective-permute-start | bytes 4128776 | tf_op jit(solution)/shard_map/ppermute | solution.py:534
  109.4 45.7 %collective-permute-start.14 = (bf16[4,48,3584]{2,1,0:T(8,128)(2,1)}, bf16[4,48,3584]{2,1,0:T(8,128)(2,1)}, u32[]{:S(2)}, u32[]{:S(2)}) collective-permute-start(bf16[4,48,3584]{2,1,0:T(8,128)(2,1)} %tie.19.refs_0_), channel_id=1, source_target_pairs={{0,2},{1,3},{2,0},{3,1},{4,6},{5,7},{6,4},{7,5},{8,10},{9,11},{10,... | collective-permute-start | bytes 4128776 | tf_op jit(solution)/shard_map/ppermute | solution.py:534
  112.6 42.5 %collective-permute-start.22 = (bf16[512,1152]{1,0:T(8,128)(2,1)S(1)}, bf16[512,1152]{1,0:T(8,128)(2,1)}, u32[]{:S(2)}, u32[]{:S(2)}) collective-permute-start(bf16[512,1152]{1,0:T(8,128)(2,1)S(1)} %pad_maximum_fusion.4), channel_id=1, source_target_pairs={{0,8},{8,16},{16,24},{1,9},{9,17},{17,25},{2,10},{10,18},{18,26},{... | collective-permute-start | bytes 3538952 | tf_op jit(solution)/shard_map/ppermute | solution.py:883
  155.1 40.8 %collective-permute-start.23 = (bf16[512,1152]{1,0:T(8,128)(2,1)}, bf16[512,1152]{1,0:T(8,128)(2,1)}, u32[]{:S(2)}, u32[]{:S(2)}) collective-permute-start(bf16[512,1152]{1,0:T(8,128)(2,1)} %tie.20), channel_id=1, source_target_pairs={{0,8},{8,16},{16,24},{1,9},{9,17},{17,25},{2,10},{10,18},{18,26},{... | collective-permute-start | bytes 3538952 | tf_op jit(solution)/shard_map/ppermute | solution.py:883
  169.3 242.2 %all-gather.18.cloned.1.call-start = ((), (), s32[]{:S(2)}) async-start(), calls=%async_computation.9 | async-start | bytes 2949120 | tf_op jit(solution)/shard_map/all_gather | solution.py:812
  169.6 31.3 %collective-permute-start.13 = (bf16[4,48,3584]{2,1,0:T(8,128)(2,1)}, bf16[4,48,3584]{2,1,0:T(8,128)(2,1)}, u32[]{:S(2)}, u32[]{:S(2)}) collective-permute-start(bf16[4,48,3584]{2,1,0:T(8,128)(2,1)} %tie.19.refs_0_), channel_id=1, source_target_pairs={{0,1},{1,0},{2,3},{3,2},{4,5},{5,4},{6,7},{7,6},{8,9},{9,8},{10,11... | collective-permute-start | bytes 4128776 | tf_op jit(solution)/shard_map/ppermute | solution.py:534
  169.7 32.3 %collective-permute-start.15 = (bf16[4,48,3584]{2,1,0:T(8,128)(2,1)}, bf16[4,48,3584]{2,1,0:T(8,128)(2,1)}, u32[]{:S(2)}, u32[]{:S(2)}) collective-permute-start(bf16[4,48,3584]{2,1,0:T(8,128)(2,1)} %collective-permute-done.14.refs_2_.refs_1_), channel_id=1, source_target_pairs={{0,1},{1,0},{2,3},{3,2},{4,5},{5,4},{6,7},{7,6},{8,9},{9,8},{10,11... | collective-permute-start | bytes 4128776 | tf_op jit(solution)/shard_map/ppermute | solution.py:534
  179.7 22.4 %collective-permute-start.17 = (bf16[4,48,3584]{2,1,0:T(8,128)(2,1)}, bf16[4,48,3584]{2,1,0:T(8,128)(2,1)}, u32[]{:S(2)}, u32[]{:S(2)}) collective-permute-start(bf16[4,48,3584]{2,1,0:T(8,128)(2,1)} %collective-permute-done.16.refs_4_.refs_2_), channel_id=1, source_target_pairs={{0,1},{1,0},{2,3},{3,2},{4,5},{5,4},{6,7},{7,6},{8,9},{9,8},{10,11... | collective-permute-start | bytes 4128776 | tf_op jit(solution)/shard_map/ppermute | solution.py:534
  183.1 18.4 %collective-permute-start.20 = (bf16[2,48,3584]{2,1,0:T(8,128)(2,1)}, bf16[2,48,3584]{2,1,0:T(8,128)(2,1)}, u32[]{:S(2)}, u32[]{:S(2)}) collective-permute-start(bf16[2,48,3584]{2,1,0:T(8,128)(2,1)} %collective-permute-done.18.refs_6_), channel_id=1, source_target_pairs={{0,1},{1,0},{2,3},{3,2},{4,5},{5,4},{6,7},{7,6},{8,9},{9,8},{10,11... | collective-permute-start | bytes 2064392 | tf_op jit(solution)/shard_map/ppermute | solution.py:534
  201.0 23.6 %collective-permute-start.24 = (bf16[512,1536]{1,0:T(8,128)(2,1)}, bf16[512,1536]{1,0:T(8,128)(2,1)}, u32[]{:S(2)}, u32[]{:S(2)}) collective-permute-start(bf16[512,1536]{1,0:T(8,128)(2,1)} %get-tuple-element.99.refs_8_.refs_6_), channel_id=1, source_target_pairs={{0,1},{1,0},{2,3},{3,2},{4,5},{5,4},{6,7},{7,6},{8,9},{9,8},{10,11... | collective-permute-start | bytes 4718600 | tf_op jit(solution)/shard_map/ppermute | solution.py:534
  201.5 23.1 %collective-permute-start.25 = (bf16[512,1536]{1,0:T(8,128)(2,1)}, bf16[512,1536]{1,0:T(8,128)(2,1)}, u32[]{:S(2)}, u32[]{:S(2)}) collective-permute-start(bf16[512,1536]{1,0:T(8,128)(2,1)} %get-tuple-element.98.refs_8_.refs_6_), channel_id=1, source_target_pairs={{0,1},{1,0},{2,3},{3,2},{4,5},{5,4},{6,7},{7,6},{8,9},{9,8},{10,11... | collective-permute-start | bytes 4718600 | tf_op jit(solution)/shard_map/ppermute | solution.py:534
  201.6 23.0 %collective-permute-start.26 = (bf16[256,1536]{1,0:T(8,128)(2,1)}, bf16[256,1536]{1,0:T(8,128)(2,1)}, u32[]{:S(2)}, u32[]{:S(2)}) collective-permute-start(bf16[256,1536]{1,0:T(8,128)(2,1)} %collective-permute-done.11.refs_1_.refs_10_.refs_8_), channel_id=1, source_target_pairs={{0,1},{1,0},{2,3},{3,2},{4,5},{5,4},{6,7},{7,6},{8,9},{9,8},{10,11... | collective-permute-start | bytes 2359304 | tf_op jit(solution)/shard_map/ppermute | solution.py:534
  202.0 22.6 %collective-permute-start.27 = (bf16[256,1536]{1,0:T(8,128)(2,1)}, bf16[256,1536]{1,0:T(8,128)(2,1)}, u32[]{:S(2)}, u32[]{:S(2)}) collective-permute-start(bf16[256,1536]{1,0:T(8,128)(2,1)} %collective-permute-done.12.refs_2_.refs_11_.refs_9_), channel_id=1, source_target_pairs={{0,1},{1,0},{2,3},{3,2},{4,5},{5,4},{6,7},{7,6},{8,9},{9,8},{10,11... | collective-permute-start | bytes 2359304 | tf_op jit(solution)/shard_map/ppermute | solution.py:534
  266.8 24.1 %collective-permute-start.28 = (bf16[512,1664]{1,0:T(8,128)(2,1)}, bf16[512,1664]{1,0:T(8,128)(2,1)}, u32[]{:S(2)}, u32[]{:S(2)}) collective-permute-start(bf16[512,1664]{1,0:T(8,128)(2,1)} %concatenate.74.refs_6_.refs_4_), channel_id=1, source_target_pairs={{0,1},{1,0},{2,3},{3,2},{4,5},{5,4},{6,7},{7,6},{8,9},{9,8},{10,11... | collective-permute-start | bytes 5111816 | tf_op jit(solution)/shard_map/ppermute | solution.py:534
  267.3 23.7 %collective-permute-start.29 = (bf16[512,1536]{1,0:T(8,128)(2,1)S(1)}, bf16[512,1536]{1,0:T(8,128)(2,1)}, u32[]{:S(2)}, u32[]{:S(2)}) collective-permute-start(bf16[512,1536]{1,0:T(8,128)(2,1)S(1)} %bitcast.174), channel_id=1, source_target_pairs={{0,1},{1,0},{2,3},{3,2},{4,5},{5,4},{6,7},{7,6},{8,9},{9,8},{10,11... | collective-permute-start | bytes 4718600 | tf_op jit(solution)/shard_map/ppermute | solution.py:534
  279.0 39.9 %collective-permute-start.30 = (bf16[512,1664]{1,0:T(8,128)(2,1)}, bf16[512,1664]{1,0:T(8,128)(2,1)}, u32[]{:S(2)}, u32[]{:S(2)}) collective-permute-start(bf16[512,1664]{1,0:T(8,128)(2,1)} %concatenate.74.refs_6_.refs_4_), channel_id=1, source_target_pairs={{0,2},{1,3},{2,0},{3,1},{4,6},{5,7},{6,4},{7,5},{8,10},{9,11},{10,... | collective-permute-start | bytes 5111816 | tf_op jit(solution)/shard_map/ppermute | solution.py:534
  280.6 39.6 %collective-permute-start.31 = (bf16[512,1664]{1,0:T(8,128)(2,1)}, bf16[512,1664]{1,0:T(8,128)(2,1)}, u32[]{:S(2)}, u32[]{:S(2)}) collective-permute-start(bf16[512,1664]{1,0:T(8,128)(2,1)} %concatenate.74.refs_6_.refs_4_), channel_id=1, source_target_pairs={{0,4},{1,5},{2,6},{3,7},{4,0},{5,1},{6,2},{7,3},{8,12},{9,13},{10,... | collective-permute-start | bytes 5111816 | tf_op jit(solution)/shard_map/ppermute | solution.py:534
  282.2 139.0 %all-gather.16.cloned.1.call-start = ((), (), s32[]{:S(2)}) async-start(), calls=%async_computation.8 | async-start | bytes 4915200 | tf_op jit(solution)/shard_map/all_gather | solution.py:812
  323.2 163.5 %reduce-scatter.3.cloned.1.call-start = ((), (), s32[]{:S(2)}) async-start(), calls=%async_computation.4 | async-start | bytes 2007040 | tf_op jit(solution)/shard_map/reduce_scatter | solution.py:1000
  323.3 33.1 %collective-permute-start.32 = (bf16[512,1664]{1,0:T(8,128)(2,1)}, bf16[512,1664]{1,0:T(8,128)(2,1)}, u32[]{:S(2)}, u32[]{:S(2)}) collective-permute-start(bf16[512,1664]{1,0:T(8,128)(2,1)} %get-tuple-element.111.refs_6_.refs_4_), channel_id=1, source_target_pairs={{0,1},{1,0},{2,3},{3,2},{4,5},{5,4},{6,7},{7,6},{8,9},{9,8},{10,11... | collective-permute-start | bytes 5111816 | tf_op jit(solution)/shard_map/ppermute | solution.py:534
  325.8 28.8 %collective-permute-start.34 = (bf16[256,1664]{1,0:T(8,128)(2,1)S(1)}, bf16[256,1664]{1,0:T(8,128)(2,1)S(1)}, u32[]{:S(2)}, u32[]{:S(2)}) collective-permute-start(bf16[256,1664]{1,0:T(8,128)(2,1)S(1)} %slice.320), channel_id=1, source_target_pairs={{0,2},{1,3},{2,0},{3,1},{4,6},{5,7},{6,4},{7,5},{8,10},{9,11},{10,... | collective-permute-start | bytes 2555912 | tf_op jit(solution)/shard_map/ppermute | solution.py:534
  326.3 28.4 %collective-permute-start.35 = (bf16[256,1664]{1,0:T(8,128)(2,1)S(1)}, bf16[256,1664]{1,0:T(8,128)(2,1)S(1)}, u32[]{:S(2)}, u32[]{:S(2)}) collective-permute-start(bf16[256,1664]{1,0:T(8,128)(2,1)S(1)} %slice.321), channel_id=1, source_target_pairs={{0,4},{1,5},{2,6},{3,7},{4,0},{5,1},{6,2},{7,3},{8,12},{9,13},{10,... | collective-permute-start | bytes 2555912 | tf_op jit(solution)/shard_map/ppermute | solution.py:534
  355.9 27.2 %collective-permute-start.36 = (bf16[256,1664]{1,0:T(8,128)(2,1)}, bf16[256,1664]{1,0:T(8,128)(2,1)S(1)}, u32[]{:S(2)}, u32[]{:S(2)}) collective-permute-start(bf16[256,1664]{1,0:T(8,128)(2,1)} %get-tuple-element.129.refs_6_.refs_4_), channel_id=1, source_target_pairs={{0,1},{1,0},{2,3},{3,2},{4,5},{5,4},{6,7},{7,6},{8,9},{9,8},{10,11... | collective-permute-start | bytes 2555912 | tf_op jit(solution)/shard_map/ppermute | solution.py:534
  355.9 27.2 %collective-permute-start.37 = (bf16[256,1664]{1,0:T(8,128)(2,1)}, bf16[256,1664]{1,0:T(8,128)(2,1)S(1)}, u32[]{:S(2)}, u32[]{:S(2)}) collective-permute-start(bf16[256,1664]{1,0:T(8,128)(2,1)} %get-tuple-element.130.refs_7_.refs_5_), channel_id=1, source_target_pairs={{0,1},{1,0},{2,3},{3,2},{4,5},{5,4},{6,7},{7,6},{8,9},{9,8},{10,11... | collective-permute-start | bytes 2555912 | tf_op jit(solution)/shard_map/ppermute | solution.py:534
  442.3 178.6 %reduce-scatter.5.cloned.1.call-start = ((), (), s32[]{:S(2)}) async-start(), calls=%async_computation.5 | async-start | bytes 1966080 | tf_op jit(solution)/shard_map/reduce_scatter | solution.py:1000
  474.2 34.9 %collective-permute-start.40 = (bf16[272,1664]{1,0:T(8,128)(2,1)}, bf16[272,1664]{1,0:T(8,128)(2,1)S(1)}, u32[]{:S(2)}, u32[]{:S(2)}) collective-permute-start(bf16[272,1664]{1,0:T(8,128)(2,1)} %get-tuple-element.242), channel_id=1, source_target_pairs={{0,4},{1,5},{2,6},{3,7},{4,0},{5,1},{6,2},{7,3},{8,12},{9,13},{10,... | collective-permute-start | bytes 2715656 | tf_op jit(solution)/shard_map/ppermute | solution.py:534
  475.6 33.5 %collective-permute-start.41 = (bf16[272,1664]{1,0:T(8,128)(2,1)}, bf16[272,1664]{1,0:T(8,128)(2,1)S(1)}, u32[]{:S(2)}, u32[]{:S(2)}) collective-permute-start(bf16[272,1664]{1,0:T(8,128)(2,1)} %get-tuple-element.241), channel_id=1, source_target_pairs={{0,2},{1,3},{2,0},{3,1},{4,6},{5,7},{6,4},{7,5},{8,10},{9,11},{10,... | collective-permute-start | bytes 2715656 | tf_op jit(solution)/shard_map/ppermute | solution.py:534
  514.7 41.3 %collective-permute-start.43 = (bf16[544,1664]{1,0:T(8,128)(2,1)}, bf16[544,1664]{1,0:T(8,128)(2,1)S(1)}, u32[]{:S(2)}, u32[]{:S(2)}) collective-permute-start(bf16[544,1664]{1,0:T(8,128)(2,1)} %pad_maximum_fusion.refs_15_), channel_id=1, source_target_pairs={{0,2},{1,3},{2,0},{3,1},{4,6},{5,7},{6,4},{7,5},{8,10},{9,11},{10,... | collective-permute-start | bytes 5431304 | tf_op jit(solution)/shard_map/ppermute | solution.py:534
  519.4 41.1 %collective-permute-start.44 = (bf16[544,1664]{1,0:T(8,128)(2,1)}, bf16[544,1664]{1,0:T(8,128)(2,1)}, u32[]{:S(2)}, u32[]{:S(2)}) collective-permute-start(bf16[544,1664]{1,0:T(8,128)(2,1)} %pad_maximum_fusion.1.refs_16_), channel_id=1, source_target_pairs={{0,4},{1,5},{2,6},{3,7},{4,0},{5,1},{6,2},{7,3},{8,12},{9,13},{10,... | collective-permute-start | bytes 5431304 | tf_op jit(solution)/shard_map/ppermute | solution.py:534
  576.7 17.9 %collective-permute-start.51 = (bf16[512,1536]{1,0:T(8,128)(2,1)}, bf16[512,1536]{1,0:T(8,128)(2,1)S(1)}, u32[]{:S(2)}, u32[]{:S(2)}) collective-permute-start(bf16[512,1536]{1,0:T(8,128)(2,1)} %get-tuple-element.168), channel_id=1, source_target_pairs={{0,1},{1,0},{2,3},{3,2},{4,5},{5,4},{6,7},{7,6},{8,9},{9,8},{10,11... | collective-permute-start | bytes 4718600 | tf_op jit(solution)/shard_map/ppermute | solution.py:534
  591.7 44.6 %collective-permute-start.49 = (bf16[256,1536]{1,0:T(8,128)(2,1)}, bf16[256,1536]{1,0:T(8,128)(2,1)}, u32[]{:S(2)}, u32[]{:S(2)}) collective-permute-start(bf16[256,1536]{1,0:T(8,128)(2,1)} %get-tuple-element.243), channel_id=1, source_target_pairs={{0,4},{1,5},{2,6},{3,7},{4,0},{5,1},{6,2},{7,3},{8,12},{9,13},{10,... | collective-permute-start | bytes 2359304 | tf_op jit(solution)/shard_map/ppermute | solution.py:534
  624.1 19.9 %collective-permute-start.52 = (bf16[256,1536]{1,0:T(8,128)(2,1)S(1)}, bf16[256,1536]{1,0:T(8,128)(2,1)S(1)}, u32[]{:S(2)}, u32[]{:S(2)}) collective-permute-start(bf16[256,1536]{1,0:T(8,128)(2,1)S(1)} %copy-done.51), channel_id=1, source_target_pairs={{0,2},{1,3},{2,0},{3,1},{4,6},{5,7},{6,4},{7,5},{8,10},{9,11},{10,... | collective-permute-start | bytes 2359304 | tf_op jit(solution)/shard_map/ppermute | solution.py:534
  635.0 57.0 %collective-permute-start.55 = (bf16[512,512]{1,0:T(8,128)(2,1)}, bf16[512,512]{1,0:T(8,128)(2,1)}, u32[]{:S(2)}, u32[]{:S(2)}) collective-permute-start(bf16[512,512]{1,0:T(8,128)(2,1)} %add_convert_fusion.16), channel_id=1, source_target_pairs={{8,0},{16,8},{24,16},{9,1},{17,9},{25,17},{10,2},{18,10},{26,18},{... | collective-permute-start | bytes 1572872 | tf_op jit(solution)/shard_map/ppermute | solution.py:1075
  665.8 28.4 %collective-permute-start.56 = (bf16[512,512]{1,0:T(8,128)(2,1)}, bf16[512,512]{1,0:T(8,128)(2,1)}, u32[]{:S(2)}, u32[]{:S(2)}) collective-permute-start(bf16[512,512]{1,0:T(8,128)(2,1)} %tie.30), channel_id=1, source_target_pairs={{8,0},{16,8},{24,16},{9,1},{17,9},{25,17},{10,2},{18,10},{26,18},{... | collective-permute-start | bytes 1572872 | tf_op jit(solution)/shard_map/ppermute | solution.py:1069
  680.8 63.3 %collective-permute-start.46 = (bf16[512,1536]{1,0:T(8,128)(2,1)}, bf16[512,1536]{1,0:T(8,128)(2,1)}, u32[]{:S(2)}, u32[]{:S(2)}) collective-permute-start(bf16[512,1536]{1,0:T(8,128)(2,1)} %get-tuple-element.162), channel_id=1, source_target_pairs={{0,1},{1,0},{2,3},{3,2},{4,5},{5,4},{6,7},{7,6},{8,9},{9,8},{10,11... | collective-permute-start | bytes 4718600 | tf_op jit(solution)/shard_map/ppermute | solution.py:534
  680.8 63.3 %collective-permute-start.50 = (bf16[512,1536]{1,0:T(8,128)(2,1)}, bf16[512,1536]{1,0:T(8,128)(2,1)}, u32[]{:S(2)}, u32[]{:S(2)}) collective-permute-start(bf16[512,1536]{1,0:T(8,128)(2,1)} %pad_maximum_fusion.2.rest_0_), channel_id=1, source_target_pairs={{0,2},{1,3},{2,0},{3,1},{4,6},{5,7},{6,4},{7,5},{8,10},{9,11},{10,... | collective-permute-start | bytes 4718600 | tf_op jit(solution)/shard_map/ppermute | solution.py:534
  681.5 62.6 %collective-permute-start.53 = (bf16[512,1536]{1,0:T(8,128)(2,1)}, bf16[512,1536]{1,0:T(8,128)(2,1)}, u32[]{:S(2)}, u32[]{:S(2)}) collective-permute-start(bf16[512,1536]{1,0:T(8,128)(2,1)} %pad_maximum_fusion.3.rest_1_), channel_id=1, source_target_pairs={{0,4},{1,5},{2,6},{3,7},{4,0},{5,1},{6,2},{7,3},{8,12},{9,13},{10,... | collective-permute-start | bytes 4718600 | tf_op jit(solution)/shard_map/ppermute | solution.py:534
  729.5 23.2 %all-to-all-start.1 = ((bf16[32,80,128]{2,1,0:T(8,128)(2,1)}), bf16[32,80,128]{2,1,0:T(8,128)(2,1)}, u32[]{:S(2)}, u32[]{:S(2)}) async-start(bf16[32,80,128]{2,1,0:T(8,128)(2,1)} %pad_maximum_fusion.9), calls=%async_computation.3 | async-start | bytes 1310720 | tf_op jit(solution)/shard_map/all_to_all | solution.py:1091
  (118 other events, 1265.8 us)
Sparse Core Ops, SparseCore 0:
  40.1 34.0 all-gather.11
  75.7 67.9 all-gather.19
  169.5 91.8 all-gather.13
  282.3 62.1 all-gather.17
  345.9 75.2 all-gather.15
  442.4 44.2 reduce-scatter.2
  565.6 35.0 reduce-scatter.4

commit v4 on v3

--- a/solution.py
+++ b/solution.py
@@ -620,30 +620,87 @@
     return [out.reshape(-1, out.shape[-1]) for out in outs]
 
 
-def query_back_kernel(q_one, q_two, normed, low_q, q_w, first_q, second_q, grad_normed, first_query, second_query):
-    half = q_one.shape[1]
-    glow_q = (dot_nt(q_one[...], second_q[:, :half]) + dot_nt(q_two[...], second_q[:, half:])).astype(BF16)
-    grad_normed[...] = (
-        dot_nt(q_one[...], q_w[:, :half]) + dot_nt(q_two[...], q_w[:, half:]) + dot_nt(glow_q, first_q[...])
-    )
+def turn_kernel(
+    own, other, from_x, from_y, hidden, gates, first_gu, router, gain, grad_out, second_o, out_w, first_o,
+    grad_mid_out, grad_mid_b_out, glow_out, glow_sgu, low_sdown, grad_attn, units_out
+):
+    rows, model = hidden.shape
+    experts = gates.shape[1]
+    rank = ADAPTER_RANK
+    total = own[...].astype(F32) + other[...].astype(F32) + from_x[...].astype(F32) + from_y[...].astype(F32)
+    units_out[...] = total[rows:, :]
+    tail = total[:rows, model:]
+    grad_gates = tail[:, :experts] + tail[:, experts : 2 * experts]
+    glow = tail[:, 3 * experts : 3 * experts + 2 * rank].astype(BF16)
+    glow_sgu[...] = glow
+    low_sdown[...] = tail[:, 3 * experts + 2 * rank : 3 * experts + 3 * rank].astype(BF16)
+    gate = gates[...]
+    grad_logits = gate * (grad_gates - jnp.sum(gate * grad_gates, axis=-1, keepdims=True))
+    logits_hi = grad_logits.astype(BF16)
+    rest = grad_logits - logits_hi.astype(F32)
+    logits_mid = rest.astype(BF16)
+    logits_lo = (rest - logits_mid.astype(F32)).astype(BF16)
+    grad_normed = total[:rows, :model] + dot_nt(glow, first_gu[...])
+    for part in (logits_hi, logits_mid, logits_lo):
+        grad_normed = grad_normed + dot_nt(part, router[...])
+    values = hidden[...]
+    scale = lax.rsqrt(jnp.mean(values * values, axis=-1, keepdims=True) + EPSILON)
+    scaled = grad_normed * gain[...]
+    mean = jnp.mean(values * scaled, axis=-1, keepdims=True)
+    grad_mid = grad_out[...].astype(F32) + scale * scaled - values * (scale * scale * scale * mean)
+    grad_mid_out[...] = grad_mid
+    grad_mid_b = grad_mid.astype(BF16)
+    grad_mid_b_out[...] = grad_mid_b
+    glow = dot_nt(grad_mid_b, second_o[...]).astype(BF16)
+    glow_out[...] = glow
+    grad_attn[...] = (dot_nt(grad_mid_b, out_w[...]) + dot_nt(glow, first_o[...])).astype(BF16)
+
+
+def turn(args):
+    rows, model = args[4].shape
+    rank = ADAPTER_RANK
+    vmem = pl.BlockSpec(memory_space=pltpu.VMEM)
+    shapes = [
+        ((rows, model), F32),
+        ((rows, model), BF16),
+        ((rows, rank), BF16),
+        ((rows, 2 * rank), BF16),
+        ((rows, rank), BF16),
+        ((rows, HEADS * HEAD_DIM), BF16),
+        ((BACK_ROWS, args[0].shape[1]), F32),
+    ]
+    return pl.pallas_call(
+        turn_kernel,
+        in_specs=[vmem] * len(args),
+        out_specs=[vmem] * len(shapes),
+        out_shape=[jax.ShapeDtypeStruct(shape, dtype) for shape, dtype in shapes],
+        compiler_params=pltpu.CompilerParams(vmem_limit_bytes=VMEM_LIMIT),
+        cost_estimate=cost(4.0),
+        name="turn",
+    )(*args)
+
+
+def query_back_kernel(waits, grad_q, normed, low_q, q_w, first_q, second_q, *rest):
+    grad_normed, first_query, second_query = rest[waits:]
+    glow_q = dot_nt(grad_q[...], second_q[...]).astype(BF16)
+    grad_normed[...] = dot_nt(grad_q[...], q_w[...]) + dot_nt(glow_q, first_q[...])
     first_query[...] = dot_tn(normed[...], glow_q)
-    second_query[:, :half] = dot_tn(low_q[...], q_one[...])
-    second_query[:, half:] = dot_tn(low_q[...], q_two[...])
-
-
-def query_back(args):
-    rows, model = args[2].shape
+    second_query[...] = dot_tn(low_q[...], grad_q[...])
+
+
+def query_back(args, deps):
+    rows, model = args[1].shape
     vmem = pl.BlockSpec(memory_space=pltpu.VMEM)
     shapes = [(rows, model), (model, ADAPTER_RANK), (ADAPTER_RANK, HEADS * HEAD_DIM)]
     return pl.pallas_call(
-        query_back_kernel,
-        in_specs=[vmem] * len(args),
+        functools.partial(query_back_kernel, len(deps)),
+        in_specs=[vmem] * len(args) + [pl.BlockSpec(memory_space=pl.ANY)] * len(deps),
         out_specs=[vmem] * len(shapes),
         out_shape=[jax.ShapeDtypeStruct(shape, F32) for shape in shapes],
         compiler_params=pltpu.CompilerParams(vmem_limit_bytes=VMEM_LIMIT),
-        cost_estimate=cost(2.0),
+        cost_estimate=cost(0.1),
         name="query_back",
-    )(*args)
+    )(*args, *deps)
 
 
 def middle_kernel(waits, attn, glow_out, normed2, glow_sgu, grad_mid, out_low, grad_out, low_sdown, *rest):
@@ -666,20 +723,19 @@
         out_specs=[vmem] * len(shapes),
         out_shape=[jax.ShapeDtypeStruct(shape, F32) for shape in shapes],
         compiler_params=pltpu.CompilerParams(vmem_limit_bytes=VMEM_LIMIT),
-        cost_estimate=cost(2.0),
+        cost_estimate=cost(0.1),
         name="middle",
     )(*args, *deps)
 
 
 def last_kernel(
-    owners, one, two, normed, low_kv, kv_w, first_kv, second_k, second_v, hidden, gain, grad_mid, grad_normed_q,
+    owners, grad_kv, normed, low_kv, kv_w, first_kv, second_k, second_v, hidden, gain, grad_mid, grad_normed_q,
     first_query, first_early, second_query, second_early, adapter, grad_hidden, first_out, second_out
 ):
     rank = ADAPTER_RANK
-    count = one.shape[1] // (2 * HEAD_DIM)
-    heads = [(half, n) for half in (one, two) for n in range(count)]
-    grad_k = jnp.concatenate([half[:, 2 * n * HEAD_DIM : (2 * n + 1) * HEAD_DIM] for half, n in heads], axis=1)
-    grad_v = jnp.concatenate([half[:, (2 * n + 1) * HEAD_DIM : (2 * n + 2) * HEAD_DIM] for half, n in heads], axis=1)
+    heads = range(grad_kv.shape[1] // (2 * HEAD_DIM))
+    grad_k = jnp.concatenate([grad_kv[:, 2 * n * HEAD_DIM : (2 * n + 1) * HEAD_DIM] for n in heads], axis=1)
+    grad_v = jnp.concatenate([grad_kv[:, (2 * n + 1) * HEAD_DIM : (2 * n + 2) * HEAD_DIM] for n in heads], axis=1)
     width = grad_k.shape[1]
     glow_k = dot_nt(grad_k, second_k[...]).astype(BF16)
     glow_v = dot_nt(grad_v, second_v[...]).astype(BF16)
@@ -704,8 +760,8 @@
 
 
 def last(owners, args):
-    rows, model = args[8].shape
-    columns = (args[14].shape[1] + 2 * KV_HEADS * HEAD_DIM + args[15].shape[1]) // owners
+    rows, model = args[7].shape
+    columns = (args[13].shape[1] + 2 * KV_HEADS * HEAD_DIM + args[14].shape[1]) // owners
     vmem = pl.BlockSpec(memory_space=pltpu.VMEM)
     return pl.pallas_call(
         functools.partial(last_kernel, owners),
@@ -908,7 +964,7 @@
     seq_up, seq_down = [], []
     for j in range(local_experts):
         seq_up.append(over_seq(tie(up_shards[j], seq_kv if j == 0 else seq_up[j - 1])))
-        seq_down.append(over_seq(tie(down_shards[j], seq_kv if j == 0 else seq_up[j - 1])))
+        seq_down.append(over_seq(tie(down_shards[j], kv_blocks[1] if j == 0 else seq_up[j - 1])))
 
     q_w, q_first, out_w = assemble(q_blocks, ((1, query_width), (1, 4 * rank_all), (1, model)), me)
     q_first = own_factors(q_first)
@@ -1008,26 +1064,49 @@
     run_expert(j, args, (2, 3), prior, (pair_six,))
     from_diagonal_x, from_diagonal_y = swap(pair_six[:half], 2, size), swap(pair_six[half:], 4, size)
     pair_two = add(back_parts[2], swap(back_parts[3], 1, size))
-    run_expert(j, args, (4, 5), prior, (pair_two, *packed_sums))
-    pair_four = add(back_parts[4], swap(tie(back_parts[5], from_diagonal_x, from_diagonal_y), 1, size))
+    run_expert(j, args, (4, 5), prior, (pair_two,))
+    pair_four = add(back_parts[4], swap(tie(back_parts[5], from_diagonal_x, from_diagonal_y, *packed_sums), 1, size))
     to_x = jnp.concatenate([pair_two[:half], add(pair_two[half:], from_diagonal_y)], axis=0)
     to_y = jnp.concatenate([add(pair_four[:half], from_diagonal_x), pair_four[half:]], axis=0)
     run_expert(j, args, (0, 1), prior, (to_x, to_y), True)
     packed_sums.append(scatter(grad_sums[-1][0]))
     from_x, from_y = swap(to_x, 2, size), swap(to_y, 4, size)
-    back_sum = add(back_parts[0], swap(tie(back_parts[1], from_x, from_y), 1, size), from_x, from_y)
-    back = back_sum.astype(F32)
+    grad_mid, grad_mid_b, glow_out, glow_sgu, low_sdown, grad_attn, shared_units = turn(
+        [back_parts[0], swap(tie(back_parts[1], from_x, from_y), 1, size), from_x, from_y, mid, gates, first_gu]
+        + [router_w, gains[1:2], grad_out_b, b_parts[3], out_w, first_o]
+    )
 
     half = rows // 2
-    far_parts = dict(zip((6, 2, 4, 0), tie_all([moe_parts[k + 1] for k in (6, 2, 4, 0)], back_sum)))
+    far_parts = dict(zip((6, 2, 4, 0), tie_all([moe_parts[k + 1] for k in (6, 2, 4, 0)], from_x, from_y)))
     pair = {k: add(moe_parts[k], swap(far_parts[k], 1, size)) for k in (6, 2, 4, 0)}
     moe_to_x = jnp.concatenate([pair[2][:half], add(pair[2][half:], swap(pair[6][half:], 4, size))], axis=0)
     moe_to_y = jnp.concatenate([add(pair[4][:half], swap(pair[6][:half], 2, size)), pair[4][half:]], axis=0)
     moe_from_x, moe_from_y = swap(moe_to_x, 2, size), swap(moe_to_y, 4, size)
     moe = pair[0].astype(F32) + moe_from_x.astype(F32) + moe_from_y.astype(F32)
-    tail = back[:rows, model:]
-    low_sdown = tail[:, 3 * experts + 2 * rank : 3 * experts + 3 * rank].astype(BF16)
-
+
+    def shared_columns(block):
+        block = block[:, :SHARED_HIDDEN].reshape(rank, size, depth, units // depth)
+        return block.transpose(0, 2, 1, 3).reshape(rank, SHARED_HIDDEN)
+
+    grad_q, grad_kv = attend_back(
+        query, kv_all, grad_attn, lse, query_tag, key_tag, hops, 0, KV_HEADS, (pair[6], pair[2], pair[4])
+    )
+    moving, early_received = grad_kv[:rows], grad_q
+    for h in range(hops):
+        if h == 1:
+            moving = tie(moving, moe_to_x, moe_to_y)
+        received = lax.ppermute(moving, "seq", backward)
+        moving = add(grad_kv[(h + 1) * rows : (h + 2) * rows], received)
+        if h == 0:
+            early_received = received
+    grad_normed_q, first_query, second_query = query_back(
+        [grad_q, normed, low_q, q_w, first_q, b_parts[0]], (early_received,)
+    )
+    first_early, second_out, second_down = middle(
+        [attn, glow_out, normed2, glow_sgu, grad_mid_b, out_low, grad_out_b, low_sdown],
+        (early_received,),
+    )
+    packed_sums = tie_all(packed_sums, early_received)
     owner_rows = model // depth
     firsts, downs, seconds = [], [], []
     for packed in packed_sums:
@@ -1040,51 +1119,13 @@
     grad_expert_a, grad_expert_a_down, grad_expert_b = jnp.stack(firsts), jnp.stack(downs), jnp.stack(seconds)
     grad_first_down = packed_sums[0][0, at : at + shared_rows].astype(F32)
 
-    grad_out = grad_out_b.astype(F32)
-    grad_gates = tail[:, :experts] + tail[:, experts : 2 * experts]
-    glow_sgu = tail[:, 3 * experts : 3 * experts + 2 * rank].astype(BF16)
-    grad_logits = gates * (grad_gates - jnp.sum(gates * grad_gates, axis=-1, keepdims=True))
-    grad_normed2 = back[:rows, :model] + dot_nt(glow_sgu, first_gu)
-    grad_normed2 = grad_normed2 + jnp.einsum(
-        "re,de->rd", grad_logits, router_w.astype(F32), precision=lax.Precision.HIGHEST
-    )
-    _, norm2_back = jax.vjp(lambda values_in: rms_norm(values_in, gains[1]), mid)
-    grad_mid = grad_out + norm2_back(grad_normed2)[0]
-    grad_mid_b = grad_mid.astype(BF16)
-    glow_out = dot_nt(grad_mid_b, b_parts[3]).astype(BF16)
-    grad_attn = (dot_nt(grad_mid_b, out_w) + dot_nt(glow_out, first_o)).astype(BF16)
-
-    def shared_columns(block):
-        block = block[:, :SHARED_HIDDEN].reshape(rank, size, depth, units // depth)
-        return block.transpose(0, 2, 1, 3).reshape(rank, SHARED_HIDDEN)
-
-    count = KV_HEADS // 2
-    grad_q_one, grad_kv_one = attend_back(query, kv_all, grad_attn, lse, query_tag, key_tag, hops, 0, count, (pair[6], pair[2], pair[4]))
-    one = grad_kv_one[:rows]
-    hop_one = lax.ppermute(one, "seq", backward)
-    grad_q_two, grad_kv_two = attend_back(
-        query, kv_all, grad_attn, lse, query_tag, key_tag, hops, count, count, (moe_to_x, moe_to_y, packed_sums[-1])
-    )
-    two = tie(grad_kv_two[:rows], hop_one)
-    hop_two = lax.ppermute(two, "seq", backward)
-    grad_normed_q, first_query, second_query = query_back(
-        [grad_q_one, grad_q_two, normed, low_q, q_w, first_q, b_parts[0]]
-    )
-    for h in range(hops):
-        own = slice((h + 1) * rows, (h + 2) * rows)
-        from_one = hop_one if h == 0 else lax.ppermute(one, "seq", backward)
-        from_two = hop_two if h == 0 else lax.ppermute(tie(two, from_one, first_query), "seq", backward)
-        one, two = add(grad_kv_one[own], from_one), add(grad_kv_two[own], from_two)
-    first_early, second_out, second_down = middle(
-        [attn, glow_out, normed2, glow_sgu, grad_mid_b, out_low, grad_out_b, low_sdown], (hop_two,)
-    )
     hidden_out = (mid + moe + dot_nn(low_sdown, b_parts[6])).astype(BF16)[None]
     second_early = jnp.concatenate(
-        [second_out, shared_columns(back[rows : rows + rank]), shared_columns(back[rows + rank :]), second_down], axis=1
+        [second_out, shared_columns(shared_units[:rank]), shared_columns(shared_units[rank:]), second_down], axis=1
     )
     grad_hidden, first_flat, second_flat = last(
         depth * size,
-        [one, two, normed, low_kv, kv_w, first_kv, b_parts[1], b_parts[2], block_input[0], gains[0:1], grad_mid]
+        [moving, normed, low_kv, kv_w, first_kv, b_parts[1], b_parts[2], block_input[0], gains[0:1], grad_mid]
         + [grad_normed_q, first_query, first_early, second_query, second_early, adapter.astype(F32).reshape(1, 1)],
     )
     flat = jnp.concatenate([first_flat.reshape(depth * size, shard_rows, LANES), second_flat], axis=1)

time: 777 us -> 764 us (0.983)
  local copies, waits for them, and re-layouts: 113 us -> 94.9 us
  Pallas kernels: 299 us -> 317 us
  matrix products: 37.3 us -> 24.9 us
  other arithmetic: 59.8 us -> 49.4 us
  starting transfers between devices: 69.4 us -> 78.8 us
    ppermute x2, starting transfers between devices: 10.2 us -> 33.6 us  [per_device(): kv_blocks.append(lax.ppermute(block, 'seq', forward))]
    pallas_call x1 -> x2, Pallas kernels: 9.13 us -> 28.5 us  [the longest x1 18.8 us: turn(): pl.pallas_call(turn_kernel, in_specs=[vmem] * len(args), out_specs=[vmem]...]
    convert_element_type x2 -> x0, other arithmetic: 8.56 us -> none  [the longest x1 4.87 us: per_device(): grad_mid_b = grad_mid.astype(BF16)]
    all_gather x5, starting transfers between devices: 9.22 us -> 0.79 us  [over_seq(): return lax.all_gather(shard, 'seq', axis=0)]
    dot_general x5 -> x1, matrix products: 10.1 us -> 1.91 us  [dot_nt(): lax.dot_general(left, right, (((1,), (1,)), ((), ())), preferred_element_...]
    ppermute x4 -> x2, waiting for transfers between devices: 16.8 us -> 22.1 us  [per_device(): received = lax.ppermute(moving, 'seq', backward)]
    pallas_call x2 -> x1, Pallas kernels: 36.8 us -> 33.4 us  [attend_back(): pl.pallas_call(functools.partial(attend_back_kernel, spans, hops * rows,...]
    unnamed x207 -> x195, local copies, waits for them, and re-layouts: 35.3 us -> 32.3 us
  transfers between devices with their start and end apart: 67 -> 65, of which waited for: 20 -> 17; matrix products, arithmetic and copies ran while one was open for 24% -> 19% of each run, Pallas kernels for 36% -> 36%
where the time goes in v4:
time: 764 us; the launch traced here: 753 us
  Pallas kernels  317 us (41%)
  waiting for transfers between devices  152 us (20%)
  local copies, waits for them, and re-layouts  94.9 us (12%)
  starting transfers between devices  78.8 us (10%)
  other arithmetic  49.4 us (6%)
  matrix products  24.9 us (3%)
  blocking collectives  20.3 us (3%)
  between operations  16.4 us (2%)
    pallas_call x8, Pallas kernels, expert_call(): pl.pallas_call(functools.partial(expert_kernel, count, splits, experts, c...  197 us
    ppermute x52, waiting for transfers between devices, swap(): return lax.ppermute(array, 'dp', [(i, i ^ bit) for i in range(size)])  57.2 us
    ppermute x2, waiting for transfers between devices, per_device(): kv_blocks.append(lax.ppermute(block, 'seq', forward))  48.6 us
    ppermute x52, starting transfers between devices, swap(): return lax.ppermute(array, 'dp', [(i, i ^ bit) for i in range(size)])  33.8 us
    ppermute x2, starting transfers between devices, per_device(): kv_blocks.append(lax.ppermute(block, 'seq', forward))  33.6 us
    pallas_call x1, Pallas kernels, attend_back(): pl.pallas_call(functools.partial(attend_back_kernel, spans, hops * rows,...  33.4 us
    unnamed x195, local copies, waits for them, and re-layouts  32.3 us
    pallas_call x1, Pallas kernels, attend(): pl.pallas_call(functools.partial(attend_kernel, spans, hops * rows, len(d...  23.6 us
  transfers between devices with their start and end apart: 65, of which 17 were waited for; matrix products, arithmetic and copies ran while one was open for 19% of the time, Pallas kernels for 36%

profile of v4, /device:TPU:0, one launch (start us, length us, event | category | flops | bytes accessed | tf_op | source)
XLA Modules:
  0.0 753.1 jit_solution(8248894912050436876)
XLA Ops:
  7.2 3.0 collective-permute-start
  15.1 3.4 all-to-all-start
  18.8 20.3 %all-gather = bf16[192,2048]{1,0:T(8,128)(2,1)} all-gather(bf16[48,2048]{1,0:T(8,128)(2,1)S(1)} %fusion.12), channel_id=2, replica_groups=mesh['seq'=4,'dp'=8] {'seq'}, dimensions={0}, use_global_device_ids=true | all-gather | bytes 983040 | tf_op jit(solution)/shard_map/all_gather | solution.py:868
  43.1 5.2 all-to-all-done.refs_3_
  51.6 17.2 %collective-permute-done.3.refs_2_ = bf16[4,48,2048]{2,1,0:T(8,128)(2,1)S(1)} collective-permute-done((bf16[4,48,2048]{2,1,0:T(8,128)(2,1)}, bf16[4,48,2048]{2,1,0:T(8,128)(2,1)S(1)}, u32[]{:S(2)}, u32[]{:S(2)}) %collective-permute-start.3) | collective-permute-done | bytes 786464 | tf_op jit(solution)/shard_map/ppermute | solution.py:534
  71.9 7.0 collective-permute-done.8.refs_7_.refs_3_
  87.5 6.1 assemble.2
  96.0 3.5 constant_dynamic-slice_fusion.7
  104.9 2.8 fusion.5
  112.0 4.5 collective-permute-start.22
  118.9 47.7 %collective-permute-done.22.refs_0_ = bf16[512,1152]{1,0:T(8,128)(2,1)} collective-permute-done((bf16[512,1152]{1,0:T(8,128)(2,1)S(1)}, bf16[512,1152]{1,0:T(8,128)(2,1)}, u32[]{:S(2)}, u32[]{:S(2)}) %collective-permute-start.22) | collective-permute-done | bytes 1179680 | tf_op jit(solution)/shard_map/ppermute | solution.py:939
  166.6 29.1 %collective-permute-start.23 = (bf16[512,1152]{1,0:T(8,128)(2,1)}, bf16[512,1152]{1,0:T(8,128)(2,1)}, u32[]{:S(2)}, u32[]{:S(2)}) collective-permute-start(bf16[512,1152]{1,0:T(8,128)(2,1)} %tie.20.refs_1_), channel_id=1, source_target_pairs={{0,8},{8,16},{16,24},{1,9},{9,17},{17,25},{2,10},{10,18},{18,26},{... | collective-permute-start | bytes 3538952 | tf_op jit(solution)/shard_map/ppermute | solution.py:939
  208.2 6.8 collective-permute-done.18.refs_6_
  225.8 8.6 %assemble.3 = (bf16[4,8,1,48,1536]{4,3,2,1,0:T(8,128)(2,1)}, bf16[4,8,1,48,512]{4,3,2,1,0:T(8,128)(2,1)}, bf16[4,8,1,48,1536]{4,3,2,1,0:T(8,128)(2,1)}) custom-call(s32[1]{0:T(128)} %bitcast.1.me_ref, bf16[4,48,3584]{2,1,0:T(8,128)(2,1)} %tie.19.refs_0_, bf16[4,48,3584]{2,1,0:T(8,128)(2,1)} %collective-permute-done.13.refs_1_, ...), custom_call_target="tpu_custom_call" | custom-call | tf_op jit(solution)/shard_map/assemble/pallas_call | solution.py:607
  240.3 3.8 fusion.4.q_ref
  244.2 23.6 %attend.1 = (bf16[512,1536]{1,0:T(8,128)(2,1)}, f32[4,3,512]{2,1,0:T(4,128)}) custom-call(bf16[512,1536]{1,0:T(8,128)(2,1)} %fusion.4.q_ref, bf16[1536,1152]{1,0:T(8,128)(2,1)} %copy-done.21, bf16[1536,1152]{1,0:T(8,128)(2,1)} %copy-done.21, f32[1,512]{1,0:T(1,128)} %add_convert_fusion.14.qt_ref, f32[1536,1]{1,0:T(8,128)} %slice_convert_fusion.kt_ref, ...), custom_call_target="tpu_custom_call" | custom-call | flops 26530500608 | bytes 1000000 | tf_op jit(solution)/shard_map/attend/pallas_call | solution.py:96
  271.3 4.8 multiply_reduce_fusion
  283.1 3.6 concatenate.74.refs_6_.refs_4_
  292.6 2.8 slice.347
  301.7 25.0 %expert.8 = (bf16[512,1536]{1,0:T(8,128)(2,1)}, bf16[512,1536]{1,0:T(8,128)(2,1)}, bf16[544,1664]{1,0:T(8,128)(2,1)}, bf16[544,1664]{1,0:T(8,128)(2,1)}, f32[153...) custom-call(s32[2]{0:T(128)} %pad_add_fusion.1.refs_0_, ...), custom_call_target="tpu_custom_call" | custom-call | flops 27683999744 | bytes 1000000 | tf_op jit(solution)/shard_map/expert/pallas_call | solution.py:501
  326.7 4.4 collective-permute-done.30.refs_0_
  338.2 7.8 %all-gather.18.cloned.1.call-done = bf16[512,2304]{1,0:T(8,128)(2,1)} async-done(((bf16[128,2304]{1,0:T(8,128)(2,1)}), bf16[512,2304]{1,0:T(8,128)(2,1)}) %all-gather.18.cloned.1.call-update) | async-done | bytes 2359312 | tf_op jit(solution)/shard_map/all_gather | solution.py:868
  347.1 2.8 slice.340
  351.3 27.4 %expert.9 = (bf16[512,1536]{1,0:T(8,128)(2,1)}, bf16[512,1536]{1,0:T(8,128)(2,1)}, bf16[544,1664]{1,0:T(8,128)(2,1)}, bf16[544,1664]{1,0:T(8,128)(2,1)}, f32[153...) custom-call(s32[2]{0:T(128)} %pad_add_fusion.1.refs_0_, ...), custom_call_target="tpu_custom_call" | custom-call | flops 27683999744 | bytes 1000000 | tf_op jit(solution)/shard_map/expert/pallas_call | solution.py:501
  380.5 26.6 %expert.10 = (bf16[512,1536]{1,0:T(8,128)(2,1)}, bf16[512,1536]{1,0:T(8,128)(2,1)}, bf16[544,1664]{1,0:T(8,128)(2,1)}, bf16[544,1664]{1,0:T(8,128)(2,1)}, f32[15...) custom-call(s32[2]{0:T(128)} %pad_add_fusion.1.refs_0_, ...), custom_call_target="tpu_custom_call" | custom-call | flops 27683999744 | bytes 1000000 | tf_op jit(solution)/shard_map/expert/pallas_call | solution.py:501
  408.4 26.8 %expert.11 = (bf16[512,1536]{1,0:T(8,128)(2,1)}, bf16[512,1536]{1,0:T(8,128)(2,1)}, bf16[544,1664]{1,0:T(8,128)(2,1)}, bf16[544,1664]{1,0:T(8,128)(2,1)}, bf16[4,1568,128]{2,1,0:T(8,128)(2,1)}) custom-call(s32[2]{0:T(128)} %pad_add_fusion.1.refs_0_, bf16[1536,1536]{1,0:T(8,128)(2,1)} %all-gather.14.cloned.1.call-done.refs_1_, bf16[512,1664]{1,0:T(8,128)(2,1)} %bitcast.200, ...), custom_call_target="tpu_custom_call" | custom-call | flops 27683999744 | bytes 1000000 | tf_op jit(solution)/shard_map/expert/pallas_call | solution.py:501
  435.2 20.7 %expert.12 = (bf16[512,1536]{1,0:T(8,128)(2,1)}, bf16[512,1536]{1,0:T(8,128)(2,1)}, bf16[544,1664]{1,0:T(8,128)(2,1)}, bf16[544,1664]{1,0:T(8,128)(2,1)}, f32[15...) custom-call(s32[2]{0:T(128)} %pad_add_fusion.refs_0_, ...), custom_call_target="tpu_custom_call" | custom-call | flops 27683999744 | bytes 1000000 | tf_op jit(solution)/shard_map/expert/pallas_call | solution.py:501
  456.0 3.9 collective-permute-done.38
  460.0 3.3 add_convert_fusion.2.refs_15_
  463.2 23.0 %expert.13 = (bf16[512,1536]{1,0:T(8,128)(2,1)}, bf16[512,1536]{1,0:T(8,128)(2,1)}, bf16[544,1664]{1,0:T(8,128)(2,1)}, bf16[544,1664]{1,0:T(8,128)(2,1)}, f32[15...) custom-call(s32[2]{0:T(128)} %pad_add_fusion.refs_0_, ...), custom_call_target="tpu_custom_call" | custom-call | flops 27683999744 | bytes 1000000 | tf_op jit(solution)/shard_map/expert/pallas_call | solution.py:501
  491.0 3.3 add_convert_fusion.1.refs_15_
  494.3 23.2 %expert.14 = (bf16[512,1536]{1,0:T(8,128)(2,1)}, bf16[512,1536]{1,0:T(8,128)(2,1)}, bf16[544,1664]{1,0:T(8,128)(2,1)}, bf16[544,1664]{1,0:T(8,128)(2,1)}, f32[15...) custom-call(s32[2]{0:T(128)} %pad_add_fusion.refs_0_, ...), custom_call_target="tpu_custom_call" | custom-call | flops 27683999744 | bytes 1000000 | tf_op jit(solution)/shard_map/expert/pallas_call | solution.py:501
  517.5 3.9 reduce-scatter.3.cloned.1.call-done.refs_3_.refs_0_
  533.1 23.7 %expert.15 = (bf16[512,1536]{1,0:T(8,128)(2,1)}, bf16[512,1536]{1,0:T(8,128)(2,1)}, bf16[544,1664]{1,0:T(8,128)(2,1)}, bf16[544,1664]{1,0:T(8,128)(2,1)}, bf16[4,1536,128]{2,1,0:T(8,128)(2,1)}) custom-call(s32[2]{0:T(128)} %pad_add_fusion.refs_0_, bf16[1536,1280]{1,0:T(8,128)(2,1)} %all-gather.16.cloned.1.call-done.refs_1_, bf16[512,1664]{1,0:T(8,128)(2,1)} %bitcast.196, ...), custom_call_target="tpu_custom_call" | custom-call | flops 27683999744 | bytes 1000000 | tf_op jit(solution)/shard_map/expert/pallas_call | solution.py:501
  556.8 11.4 %collective-permute-done.43.refs_4_.refs_1_.from_x = bf16[544,1664]{1,0:T(8,128)(2,1)S(1)} collective-permute-done((bf16[544,1664]{1,0:T(8,128)(2,1)}, bf16[544,1664]{1,0:T(8,128)(2,1)S(1)}, u32[]{:S(2)}, u32[]{:S(2)}) %collective-permute-start.43) | collective-permute-done | bytes 1810464 | tf_op jit(solution)/shard_map/ppermute | solution.py:534
  568.2 4.6 collective-permute-done.44.refs_5_.refs_2_.from_y
  585.9 18.8 %turn.1 = (f32[512,1536]{1,0:T(8,128)}, bf16[512,1536]{1,0:T(8,128)(2,1)}, bf16[512,16]{1,0:T(8,128)(2,1)}, bf16[512,32]{1,0:T(8,128)(2,1)}, bf16[512,16]{1,0:T(...) custom-call(bf16[544,1664]{1,0:T(8,128)(2,1)} %get-tuple-element.174.own, ...), custom_call_target="tpu_custom_call" | custom-call | flops 4614000128 | bytes 1000000 | tf_op jit(solution)/shard_map/turn/pallas_call | solution.py:672
  604.7 33.4 %attend_back.1 = (bf16[512,1536]{1,0:T(8,128)(2,1)}, bf16[1536,1024]{1,0:T(8,128)(2,1)}) custom-call(bf16[512,1536]{1,0:T(8,128)(2,1)} %fusion.4.q_ref, bf16[1536,1152]{1,0:T(8,128)(2,1)} %copy-done.21, bf16[1536,1152]{1,0:T(8,128)(2,1)} %copy-done.21, bf16[512,1536]{1,0:T(8,128)(2,1)} %get-tuple-element.177.g_ref, f32[4,3,512]{2,1,0:T(4,128)} %get-tuple-element.178.lse_ref, ...), custom_call_target="tpu_custom_call" | custom-call | flops 9228000256 | bytes 1000000 | tf_op jit(solution)/shard_map/attend_back/pallas_call | solution.py:159
  653.1 14.9 %collective-permute-done.54.rest_0_.refs_2_ = bf16[512,1024]{1,0:T(8,128)(2,1)S(1)} collective-permute-done((bf16[512,1024]{1,0:T(8,128)(2,1)}, bf16[512,1024]{1,0:T(8,128)(2,1)S(1)}, u32[]{:S(2)}, u32[]{:S(2)}) %collective-permute-start.54) | collective-permute-done | bytes 1048608 | tf_op jit(solution)/shard_map/ppermute | solution.py:1098
  671.7 2.5 add_convert_fusion.9.refs_0_
  675.8 5.2 middle.1
  684.3 9.7 %query_back.1 = (f32[512,1536]{1,0:T(8,128)}, f32[1536,16]{1,0:T(8,128)}, f32[16,1536]{1,0:T(8,128)}) custom-call(bf16[512,1536]{1,0:T(8,128)(2,1)} %get-tuple-element.181.grad_q, bf16[512,1536]{1,0:T(8,128)(2,1)} %copy-done.4, bf16[512,16]{1,0:T(8,128)(2,1)} %copy-done.52, bf16[1536,1536]{1,0:T(8,128)(2,1)} %bitcast.174, bf16[1536,16]{1,0:T(8,128)(2,1)} %copy-done.27, ...), custom_call_target="tpu_custom_call" | custom-call | flops 115350000 | bytes 1000000 | tf_op jit(solution)/shard_map/query_back/pallas_call | solution.py:695
  694.0 7.2 collective-permute-done.55
  701.1 3.0 add_convert_fusion.8.grad_kv
  704.1 12.2 %last.1 = (f32[512,1536]{1,0:T(8,128)}, bf16[1536,128]{1,0:T(8,128)(2,1)}, bf16[32,32,128]{2,1,0:T(8,128)(2,1)}) custom-call(bf16[512,1024]{1,0:T(8,128)(2,1)} %add_convert_fusion.8.grad_kv, bf16[512,1536]{1,0:T(8,128)(2,1)} %copy-done.4, bf16[512,32]{1,0:T(8,128)(2,1)} %copy-done.51, bf16[1536,1024]{1,0:T(8,128)(2,1)} %bitcast.183, ...), custom_call_target="tpu_custom_call" | custom-call | flops 2307000064 | bytes 1000000 | tf_op jit(solution)/shard_map/last/pallas_call | solution.py:766
  718.3 4.2 all-to-all-start.1
  729.0 4.6 fusion.7
  733.6 6.9 all-to-all-done.1.flat
  (460 shorter events, 168.5 us)
Async XLA Ops:
  7.2 42.3 %collective-permute-start = (bf16[512,1536]{1,0:T(8,128)(2,1)}, bf16[512,1536]{1,0:T(8,128)(2,1)}, u32[]{:S(2)}, u32[]{:S(2)}) collective-permute-start(bf16[512,1536]{1,0:T(8,128)(2,1)} %bitcast.164), channel_id=1, source_target_pairs={{0,2},{1,3},{2,0},{3,1},{4,6},{5,7},{6,4},{7,5},{8,10},{9,11},{10,... | collective-permute-start | bytes 4718600 | tf_op jit(solution)/shard_map/ppermute | solution.py:534
  10.2 39.3 %collective-permute-start.1 = (bf16[512,1536]{1,0:T(8,128)(2,1)}, bf16[512,1536]{1,0:T(8,128)(2,1)}, u32[]{:S(2)}, u32[]{:S(2)}) collective-permute-start(bf16[512,1536]{1,0:T(8,128)(2,1)} %bitcast.165), channel_id=1, source_target_pairs={{0,4},{1,5},{2,6},{3,7},{4,0},{5,1},{6,2},{7,3},{8,12},{9,13},{10,... | collective-permute-start | bytes 4718600 | tf_op jit(solution)/shard_map/ppermute | solution.py:534
  15.1 33.3 %all-to-all-start = ((bf16[8,48,256]{2,1,0:T(8,128)(2,1)}), bf16[8,48,256]{2,1,0:T(8,128)(2,1)S(1)}, u32[]{:S(2)}, u32[]{:S(2)}) async-start(bf16[8,48,256]{2,1,0:T(8,128)(2,1)} %copy.174), calls=%async_computation | async-start | bytes 393216 | tf_op jit(solution)/shard_map/all_to_all | solution.py:911
  18.5 89.3 %all-gather.12.cloned.1.call-start = ((), (), s32[]{:S(2)}) async-start(), calls=%async_computation.6 | async-start | bytes 1720320 | tf_op jit(solution)/shard_map/all_gather | solution.py:868
  39.9 252.3 %all-gather.14.cloned.1.call-start = ((), (), s32[]{:S(2)}) async-start(), calls=%async_computation.7 | async-start | bytes 5898240 | tf_op jit(solution)/shard_map/all_gather | solution.py:868
  49.5 19.3 %collective-permute-start.3 = (bf16[4,48,2048]{2,1,0:T(8,128)(2,1)}, bf16[4,48,2048]{2,1,0:T(8,128)(2,1)S(1)}, u32[]{:S(2)}, u32[]{:S(2)}) collective-permute-start(bf16[4,48,2048]{2,1,0:T(8,128)(2,1)} %tie.16.refs_0_), channel_id=1, source_target_pairs={{0,2},{1,3},{2,0},{3,1},{4,6},{5,7},{6,4},{7,5},{8,10},{9,11},{10,... | collective-permute-start | bytes 2359304 | tf_op jit(solution)/shard_map/ppermute | solution.py:534
  50.6 20.0 %collective-permute-start.5 = (bf16[4,48,2048]{2,1,0:T(8,128)(2,1)}, bf16[4,48,2048]{2,1,0:T(8,128)(2,1)S(1)}, u32[]{:S(2)}, u32[]{:S(2)}) collective-permute-start(bf16[4,48,2048]{2,1,0:T(8,128)(2,1)} %tie.16.refs_0_), channel_id=1, source_target_pairs={{0,4},{1,5},{2,6},{3,7},{4,0},{5,1},{6,2},{7,3},{8,12},{9,13},{10,... | collective-permute-start | bytes 2359304 | tf_op jit(solution)/shard_map/ppermute | solution.py:534
  71.4 16.2 %collective-permute-start.4 = (bf16[4,48,2048]{2,1,0:T(8,128)(2,1)S(1)}, bf16[4,48,2048]{2,1,0:T(8,128)(2,1)}, u32[]{:S(2)}, u32[]{:S(2)}) collective-permute-start(bf16[4,48,2048]{2,1,0:T(8,128)(2,1)S(1)} %collective-permute-done.3.refs_2_), channel_id=1, source_target_pairs={{0,1},{1,0},{2,3},{3,2},{4,5},{5,4},{6,7},{7,6},{8,9},{9,8},{10,11... | collective-permute-start | bytes 2359304 | tf_op jit(solution)/shard_map/ppermute | solution.py:534
  71.9 15.6 %collective-permute-start.6 = (bf16[4,48,2048]{2,1,0:T(8,128)(2,1)S(1)}, bf16[4,48,2048]{2,1,0:T(8,128)(2,1)}, u32[]{:S(2)}, u32[]{:S(2)}) collective-permute-start(bf16[4,48,2048]{2,1,0:T(8,128)(2,1)S(1)} %collective-permute-done.5.refs_4_), channel_id=1, source_target_pairs={{0,1},{1,0},{2,3},{3,2},{4,5},{5,4},{6,7},{7,6},{8,9},{9,8},{10,11... | collective-permute-start | bytes 2359304 | tf_op jit(solution)/shard_map/ppermute | solution.py:534
  80.9 211.7 %all-gather.20.cloned.1.call-start = ((), (), s32[]{:S(2)}) async-start(), calls=%async_computation.10 | async-start | bytes 3604480 | tf_op jit(solution)/shard_map/all_gather | solution.py:868
  85.9 21.8 %collective-permute-start.11 = (bf16[256,1536]{1,0:T(8,128)(2,1)}, bf16[256,1536]{1,0:T(8,128)(2,1)}, u32[]{:S(2)}, u32[]{:S(2)}) collective-permute-start(bf16[256,1536]{1,0:T(8,128)(2,1)} %slice.252), channel_id=1, source_target_pairs={{0,2},{1,3},{2,0},{3,1},{4,6},{5,7},{6,4},{7,5},{8,10},{9,11},{10,... | collective-permute-start | bytes 2359304 | tf_op jit(solution)/shard_map/ppermute | solution.py:534
  86.8 21.0 %collective-permute-start.12 = (bf16[256,1536]{1,0:T(8,128)(2,1)}, bf16[256,1536]{1,0:T(8,128)(2,1)}, u32[]{:S(2)}, u32[]{:S(2)}) collective-permute-start(bf16[256,1536]{1,0:T(8,128)(2,1)} %slice.253), channel_id=1, source_target_pairs={{0,4},{1,5},{2,6},{3,7},{4,0},{5,1},{6,2},{7,3},{8,12},{9,13},{10,... | collective-permute-start | bytes 2359304 | tf_op jit(solution)/shard_map/ppermute | solution.py:534
  107.8 58.7 %collective-permute-start.16 = (bf16[4,48,3584]{2,1,0:T(8,128)(2,1)}, bf16[4,48,3584]{2,1,0:T(8,128)(2,1)}, u32[]{:S(2)}, u32[]{:S(2)}) collective-permute-start(bf16[4,48,3584]{2,1,0:T(8,128)(2,1)} %tie.19.refs_0_), channel_id=1, source_target_pairs={{0,4},{1,5},{2,6},{3,7},{4,0},{5,1},{6,2},{7,3},{8,12},{9,13},{10,... | collective-permute-start | bytes 4128776 | tf_op jit(solution)/shard_map/ppermute | solution.py:534
  109.3 57.2 %collective-permute-start.14 = (bf16[4,48,3584]{2,1,0:T(8,128)(2,1)}, bf16[4,48,3584]{2,1,0:T(8,128)(2,1)}, u32[]{:S(2)}, u32[]{:S(2)}) collective-permute-start(bf16[4,48,3584]{2,1,0:T(8,128)(2,1)} %tie.19.refs_0_), channel_id=1, source_target_pairs={{0,2},{1,3},{2,0},{3,1},{4,6},{5,7},{6,4},{7,5},{8,10},{9,11},{10,... | collective-permute-start | bytes 4128776 | tf_op jit(solution)/shard_map/ppermute | solution.py:534
  112.0 54.6 %collective-permute-start.22 = (bf16[512,1152]{1,0:T(8,128)(2,1)S(1)}, bf16[512,1152]{1,0:T(8,128)(2,1)}, u32[]{:S(2)}, u32[]{:S(2)}) collective-permute-start(bf16[512,1152]{1,0:T(8,128)(2,1)S(1)} %pad_maximum_fusion.4), channel_id=1, source_target_pairs={{0,8},{8,16},{16,24},{1,9},{9,17},{17,25},{2,10},{10,18},{18,26},{... | collective-permute-start | bytes 3538952 | tf_op jit(solution)/shard_map/ppermute | solution.py:939
  166.6 53.1 %collective-permute-start.23 = (bf16[512,1152]{1,0:T(8,128)(2,1)}, bf16[512,1152]{1,0:T(8,128)(2,1)}, u32[]{:S(2)}, u32[]{:S(2)}) collective-permute-start(bf16[512,1152]{1,0:T(8,128)(2,1)} %tie.20.refs_1_), channel_id=1, source_target_pairs={{0,8},{8,16},{16,24},{1,9},{9,17},{17,25},{2,10},{10,18},{18,26},{... | collective-permute-start | bytes 3538952 | tf_op jit(solution)/shard_map/ppermute | solution.py:939
  198.2 16.7 %collective-permute-start.18 = (bf16[2,48,3584]{2,1,0:T(8,128)(2,1)}, bf16[2,48,3584]{2,1,0:T(8,128)(2,1)}, u32[]{:S(2)}, u32[]{:S(2)}) collective-permute-start(bf16[2,48,3584]{2,1,0:T(8,128)(2,1)} %slice.327), channel_id=1, source_target_pairs={{0,2},{1,3},{2,0},{3,1},{4,6},{5,7},{6,4},{7,5},{8,10},{9,11},{10,... | collective-permute-start | bytes 2064392 | tf_op jit(solution)/shard_map/ppermute | solution.py:534
  202.4 15.8 %collective-permute-start.19 = (bf16[2,48,3584]{2,1,0:T(8,128)(2,1)}, bf16[2,48,3584]{2,1,0:T(8,128)(2,1)}, u32[]{:S(2)}, u32[]{:S(2)}) collective-permute-start(bf16[2,48,3584]{2,1,0:T(8,128)(2,1)} %slice.328), channel_id=1, source_target_pairs={{0,4},{1,5},{2,6},{3,7},{4,0},{5,1},{6,2},{7,3},{8,12},{9,13},{10,... | collective-permute-start | bytes 2064392 | tf_op jit(solution)/shard_map/ppermute | solution.py:534
  207.7 17.0 %collective-permute-start.13 = (bf16[4,48,3584]{2,1,0:T(8,128)(2,1)}, bf16[4,48,3584]{2,1,0:T(8,128)(2,1)}, u32[]{:S(2)}, u32[]{:S(2)}) collective-permute-start(bf16[4,48,3584]{2,1,0:T(8,128)(2,1)} %tie.19.refs_0_), channel_id=1, source_target_pairs={{0,1},{1,0},{2,3},{3,2},{4,5},{5,4},{6,7},{7,6},{8,9},{9,8},{10,11... | collective-permute-start | bytes 4128776 | tf_op jit(solution)/shard_map/ppermute | solution.py:534
  207.7 18.0 %collective-permute-start.15 = (bf16[4,48,3584]{2,1,0:T(8,128)(2,1)}, bf16[4,48,3584]{2,1,0:T(8,128)(2,1)}, u32[]{:S(2)}, u32[]{:S(2)}) collective-permute-start(bf16[4,48,3584]{2,1,0:T(8,128)(2,1)} %collective-permute-done.14.refs_2_.refs_1_), channel_id=1, source_target_pairs={{0,1},{1,0},{2,3},{3,2},{4,5},{5,4},{6,7},{7,6},{8,9},{9,8},{10,11... | collective-permute-start | bytes 4128776 | tf_op jit(solution)/shard_map/ppermute | solution.py:534
  217.7 128.3 %all-gather.18.cloned.1.call-start = ((), (), s32[]{:S(2)}) async-start(), calls=%async_computation.9 | async-start | bytes 2949120 | tf_op jit(solution)/shard_map/all_gather | solution.py:868
  224.7 19.5 %collective-permute-start.24 = (bf16[512,1536]{1,0:T(8,128)(2,1)}, bf16[512,1536]{1,0:T(8,128)(2,1)}, u32[]{:S(2)}, u32[]{:S(2)}) collective-permute-start(bf16[512,1536]{1,0:T(8,128)(2,1)} %get-tuple-element.106.refs_8_.refs_6_), channel_id=1, source_target_pairs={{0,1},{1,0},{2,3},{3,2},{4,5},{5,4},{6,7},{7,6},{8,9},{9,8},{10,11... | collective-permute-start | bytes 4718600 | tf_op jit(solution)/shard_map/ppermute | solution.py:534
  225.2 19.0 %collective-permute-start.25 = (bf16[512,1536]{1,0:T(8,128)(2,1)}, bf16[512,1536]{1,0:T(8,128)(2,1)}, u32[]{:S(2)}, u32[]{:S(2)}) collective-permute-start(bf16[512,1536]{1,0:T(8,128)(2,1)} %get-tuple-element.105.refs_8_.refs_6_), channel_id=1, source_target_pairs={{0,1},{1,0},{2,3},{3,2},{4,5},{5,4},{6,7},{7,6},{8,9},{9,8},{10,11... | collective-permute-start | bytes 4718600 | tf_op jit(solution)/shard_map/ppermute | solution.py:534
  225.3 18.9 %collective-permute-start.26 = (bf16[256,1536]{1,0:T(8,128)(2,1)}, bf16[256,1536]{1,0:T(8,128)(2,1)}, u32[]{:S(2)}, u32[]{:S(2)}) collective-permute-start(bf16[256,1536]{1,0:T(8,128)(2,1)} %collective-permute-done.11.refs_1_.refs_10_.refs_8_), channel_id=1, source_target_pairs={{0,1},{1,0},{2,3},{3,2},{4,5},{5,4},{6,7},{7,6},{8,9},{9,8},{10,11... | collective-permute-start | bytes 2359304 | tf_op jit(solution)/shard_map/ppermute | solution.py:534
  225.7 18.4 %collective-permute-start.27 = (bf16[256,1536]{1,0:T(8,128)(2,1)}, bf16[256,1536]{1,0:T(8,128)(2,1)}, u32[]{:S(2)}, u32[]{:S(2)}) collective-permute-start(bf16[256,1536]{1,0:T(8,128)(2,1)} %collective-permute-done.12.refs_2_.refs_11_.refs_9_), channel_id=1, source_target_pairs={{0,1},{1,0},{2,3},{3,2},{4,5},{5,4},{6,7},{7,6},{8,9},{9,8},{10,11... | collective-permute-start | bytes 2359304 | tf_op jit(solution)/shard_map/ppermute | solution.py:534
  291.4 39.8 %collective-permute-start.30 = (bf16[512,1664]{1,0:T(8,128)(2,1)}, bf16[512,1664]{1,0:T(8,128)(2,1)S(1)}, u32[]{:S(2)}, u32[]{:S(2)}) collective-permute-start(bf16[512,1664]{1,0:T(8,128)(2,1)} %concatenate.74.refs_6_.refs_4_), channel_id=1, source_target_pairs={{0,2},{1,3},{2,0},{3,1},{4,6},{5,7},{6,4},{7,5},{8,10},{9,11},{10,... | collective-permute-start | bytes 5111816 | tf_op jit(solution)/shard_map/ppermute | solution.py:534
  291.9 39.5 %collective-permute-start.31 = (bf16[512,1664]{1,0:T(8,128)(2,1)}, bf16[512,1664]{1,0:T(8,128)(2,1)}, u32[]{:S(2)}, u32[]{:S(2)}) collective-permute-start(bf16[512,1664]{1,0:T(8,128)(2,1)} %concatenate.74.refs_6_.refs_4_), channel_id=1, source_target_pairs={{0,4},{1,5},{2,6},{3,7},{4,0},{5,1},{6,2},{7,3},{8,12},{9,13},{10,... | collective-permute-start | bytes 5111816 | tf_op jit(solution)/shard_map/ppermute | solution.py:534
  292.3 142.9 %all-gather.16.cloned.1.call-start = ((), (), s32[]{:S(2)}) async-start(), calls=%async_computation.8 | async-start | bytes 4915200 | tf_op jit(solution)/shard_map/all_gather | solution.py:868
  332.3 18.9 %collective-permute-start.33 = (bf16[512,1664]{1,0:T(8,128)(2,1)}, bf16[512,1664]{1,0:T(8,128)(2,1)}, u32[]{:S(2)}, u32[]{:S(2)}) collective-permute-start(bf16[512,1664]{1,0:T(8,128)(2,1)} %get-tuple-element.119.refs_6_.refs_4_), channel_id=1, source_target_pairs={{0,1},{1,0},{2,3},{3,2},{4,5},{5,4},{6,7},{7,6},{8,9},{9,8},{10,11... | collective-permute-start | bytes 5111816 | tf_op jit(solution)/shard_map/ppermute | solution.py:534
  335.4 186.0 %reduce-scatter.3.cloned.1.call-start = ((), (), s32[]{:S(2)}) async-start(), calls=%async_computation.4 | async-start | bytes 2007040 | tf_op jit(solution)/shard_map/reduce_scatter | solution.py:1056
  335.4 45.0 %collective-permute-start.32 = (bf16[512,1664]{1,0:T(8,128)(2,1)}, bf16[512,1664]{1,0:T(8,128)(2,1)}, u32[]{:S(2)}, u32[]{:S(2)}) collective-permute-start(bf16[512,1664]{1,0:T(8,128)(2,1)} %get-tuple-element.118.refs_6_.refs_4_), channel_id=1, source_target_pairs={{0,1},{1,0},{2,3},{3,2},{4,5},{5,4},{6,7},{7,6},{8,9},{9,8},{10,11... | collective-permute-start | bytes 5111816 | tf_op jit(solution)/shard_map/ppermute | solution.py:534
  337.1 41.6 %collective-permute-start.34 = (bf16[256,1664]{1,0:T(8,128)(2,1)S(1)}, bf16[256,1664]{1,0:T(8,128)(2,1)S(1)}, u32[]{:S(2)}, u32[]{:S(2)}) collective-permute-start(bf16[256,1664]{1,0:T(8,128)(2,1)S(1)} %slice.289), channel_id=1, source_target_pairs={{0,2},{1,3},{2,0},{3,1},{4,6},{5,7},{6,4},{7,5},{8,10},{9,11},{10,... | collective-permute-start | bytes 2555912 | tf_op jit(solution)/shard_map/ppermute | solution.py:534
  337.9 40.9 %collective-permute-start.35 = (bf16[256,1664]{1,0:T(8,128)(2,1)S(1)}, bf16[256,1664]{1,0:T(8,128)(2,1)S(1)}, u32[]{:S(2)}, u32[]{:S(2)}) collective-permute-start(bf16[256,1664]{1,0:T(8,128)(2,1)S(1)} %slice.290), channel_id=1, source_target_pairs={{0,4},{1,5},{2,6},{3,7},{4,0},{5,1},{6,2},{7,3},{8,12},{9,13},{10,... | collective-permute-start | bytes 2555912 | tf_op jit(solution)/shard_map/ppermute | solution.py:534
  379.9 27.2 %collective-permute-start.36 = (bf16[256,1664]{1,0:T(8,128)(2,1)}, bf16[256,1664]{1,0:T(8,128)(2,1)S(1)}, u32[]{:S(2)}, u32[]{:S(2)}) collective-permute-start(bf16[256,1664]{1,0:T(8,128)(2,1)} %get-tuple-element.136.refs_6_.refs_4_), channel_id=1, source_target_pairs={{0,1},{1,0},{2,3},{3,2},{4,5},{5,4},{6,7},{7,6},{8,9},{9,8},{10,11... | collective-permute-start | bytes 2555912 | tf_op jit(solution)/shard_map/ppermute | solution.py:534
  379.9 27.2 %collective-permute-start.37 = (bf16[256,1664]{1,0:T(8,128)(2,1)}, bf16[256,1664]{1,0:T(8,128)(2,1)S(1)}, u32[]{:S(2)}, u32[]{:S(2)}) collective-permute-start(bf16[256,1664]{1,0:T(8,128)(2,1)} %get-tuple-element.137.refs_7_.refs_5_), channel_id=1, source_target_pairs={{0,1},{1,0},{2,3},{3,2},{4,5},{5,4},{6,7},{7,6},{8,9},{9,8},{10,11... | collective-permute-start | bytes 2555912 | tf_op jit(solution)/shard_map/ppermute | solution.py:534
  486.5 166.7 %reduce-scatter.5.cloned.1.call-start = ((), (), s32[]{:S(2)}) async-start(), calls=%async_computation.5 | async-start | bytes 1966080 | tf_op jit(solution)/shard_map/reduce_scatter | solution.py:1056
  487.9 33.5 %collective-permute-start.40 = (bf16[272,1664]{1,0:T(8,128)(2,1)}, bf16[272,1664]{1,0:T(8,128)(2,1)S(1)}, u32[]{:S(2)}, u32[]{:S(2)}) collective-permute-start(bf16[272,1664]{1,0:T(8,128)(2,1)} %get-tuple-element.250), channel_id=1, source_target_pairs={{0,4},{1,5},{2,6},{3,7},{4,0},{5,1},{6,2},{7,3},{8,12},{9,13},{10,... | collective-permute-start | bytes 2715656 | tf_op jit(solution)/shard_map/ppermute | solution.py:534
  489.5 31.9 %collective-permute-start.41 = (bf16[272,1664]{1,0:T(8,128)(2,1)}, bf16[272,1664]{1,0:T(8,128)(2,1)S(1)}, u32[]{:S(2)}, u32[]{:S(2)}) collective-permute-start(bf16[272,1664]{1,0:T(8,128)(2,1)} %get-tuple-element.249), channel_id=1, source_target_pairs={{0,2},{1,3},{2,0},{3,1},{4,6},{5,7},{6,4},{7,5},{8,10},{9,11},{10,... | collective-permute-start | bytes 2715656 | tf_op jit(solution)/shard_map/ppermute | solution.py:534
  526.9 41.3 %collective-permute-start.43 = (bf16[544,1664]{1,0:T(8,128)(2,1)}, bf16[544,1664]{1,0:T(8,128)(2,1)S(1)}, u32[]{:S(2)}, u32[]{:S(2)}) collective-permute-start(bf16[544,1664]{1,0:T(8,128)(2,1)} %pad_maximum_fusion.refs_15_), channel_id=1, source_target_pairs={{0,2},{1,3},{2,0},{3,1},{4,6},{5,7},{6,4},{7,5},{8,10},{9,11},{10,... | collective-permute-start | bytes 5431304 | tf_op jit(solution)/shard_map/ppermute | solution.py:534
  531.7 41.1 %collective-permute-start.44 = (bf16[544,1664]{1,0:T(8,128)(2,1)}, bf16[544,1664]{1,0:T(8,128)(2,1)}, u32[]{:S(2)}, u32[]{:S(2)}) collective-permute-start(bf16[544,1664]{1,0:T(8,128)(2,1)} %pad_maximum_fusion.1.refs_16_), channel_id=1, source_target_pairs={{0,4},{1,5},{2,6},{3,7},{4,0},{5,1},{6,2},{7,3},{8,12},{9,13},{10,... | collective-permute-start | bytes 5431304 | tf_op jit(solution)/shard_map/ppermute | solution.py:534
  576.5 152.5 %collective-permute-start.45 = (bf16[512,1536]{1,0:T(8,128)(2,1)}, bf16[512,1536]{1,0:T(8,128)(2,1)}, u32[]{:S(2)}, u32[]{:S(2)}) collective-permute-start(bf16[512,1536]{1,0:T(8,128)(2,1)} %get-tuple-element.167), channel_id=1, source_target_pairs={{0,1},{1,0},{2,3},{3,2},{4,5},{5,4},{6,7},{7,6},{8,9},{9,8},{10,11... | collective-permute-start | bytes 4718600 | tf_op jit(solution)/shard_map/ppermute | solution.py:534
  580.3 65.6 %collective-permute-start.48 = (bf16[256,1536]{1,0:T(8,128)(2,1)}, bf16[256,1536]{1,0:T(8,128)(2,1)}, u32[]{:S(2)}, u32[]{:S(2)}) collective-permute-start(bf16[256,1536]{1,0:T(8,128)(2,1)} %get-tuple-element.251), channel_id=1, source_target_pairs={{0,4},{1,5},{2,6},{3,7},{4,0},{5,1},{6,2},{7,3},{8,12},{9,13},{10,... | collective-permute-start | bytes 2359304 | tf_op jit(solution)/shard_map/ppermute | solution.py:534
  583.6 65.0 %collective-permute-start.51 = (bf16[256,1536]{1,0:T(8,128)(2,1)}, bf16[256,1536]{1,0:T(8,128)(2,1)}, u32[]{:S(2)}, u32[]{:S(2)}) collective-permute-start(bf16[256,1536]{1,0:T(8,128)(2,1)} %get-tuple-element.252), channel_id=1, source_target_pairs={{0,2},{1,3},{2,0},{3,1},{4,6},{5,7},{6,4},{7,5},{8,10},{9,11},{10,... | collective-permute-start | bytes 2359304 | tf_op jit(solution)/shard_map/ppermute | solution.py:534
  640.4 27.6 %collective-permute-start.54 = (bf16[512,1024]{1,0:T(8,128)(2,1)}, bf16[512,1024]{1,0:T(8,128)(2,1)S(1)}, u32[]{:S(2)}, u32[]{:S(2)}) collective-permute-start(bf16[512,1024]{1,0:T(8,128)(2,1)} %slice.305), channel_id=1, source_target_pairs={{8,0},{16,8},{24,16},{9,1},{17,9},{25,17},{10,2},{18,10},{26,18},{... | collective-permute-start | bytes 3145736 | tf_op jit(solution)/shard_map/ppermute | solution.py:1098
  647.4 81.5 %collective-permute-start.49 = (bf16[512,1536]{1,0:T(8,128)(2,1)S(1)}, bf16[512,1536]{1,0:T(8,128)(2,1)}, u32[]{:S(2)}, u32[]{:S(2)}) collective-permute-start(bf16[512,1536]{1,0:T(8,128)(2,1)S(1)} %pad_maximum_fusion.2.refs_1_), channel_id=1, source_target_pairs={{0,2},{1,3},{2,0},{3,1},{4,6},{5,7},{6,4},{7,5},{8,10},{9,11},{10,... | collective-permute-start | bytes 4718600 | tf_op jit(solution)/shard_map/ppermute | solution.py:534
  651.8 77.1 %collective-permute-start.52 = (bf16[512,1536]{1,0:T(8,128)(2,1)}, bf16[512,1536]{1,0:T(8,128)(2,1)}, u32[]{:S(2)}, u32[]{:S(2)}) collective-permute-start(bf16[512,1536]{1,0:T(8,128)(2,1)} %pad_maximum_fusion.3.refs_2_), channel_id=1, source_target_pairs={{0,4},{1,5},{2,6},{3,7},{4,0},{5,1},{6,2},{7,3},{8,12},{9,13},{10,... | collective-permute-start | bytes 4718600 | tf_op jit(solution)/shard_map/ppermute | solution.py:534
  674.2 26.9 %collective-permute-start.55 = (bf16[512,1024]{1,0:T(8,128)(2,1)}, bf16[512,1024]{1,0:T(8,128)(2,1)}, u32[]{:S(2)}, u32[]{:S(2)}) collective-permute-start(bf16[512,1024]{1,0:T(8,128)(2,1)} %tie.30), channel_id=1, source_target_pairs={{8,0},{16,8},{24,16},{9,1},{17,9},{25,17},{10,2},{18,10},{26,18},{... | collective-permute-start | bytes 3145736 | tf_op jit(solution)/shard_map/ppermute | solution.py:1098
  718.3 22.1 %all-to-all-start.1 = ((bf16[32,80,128]{2,1,0:T(8,128)(2,1)}), bf16[32,80,128]{2,1,0:T(8,128)(2,1)}, u32[]{:S(2)}, u32[]{:S(2)}) async-start(bf16[32,80,128]{2,1,0:T(8,128)(2,1)} %pad_maximum_fusion.9), calls=%async_computation.2 | async-start | bytes 1310720 | tf_op jit(solution)/shard_map/all_to_all | solution.py:1132
  (110 other events, 1059.8 us)
Sparse Core Ops, SparseCore 0:
  40.1 34.0 all-gather.11
  81.0 110.4 all-gather.13
  217.8 58.5 all-gather.19
  292.4 53.4 all-gather.17
  347.4 75.2 all-gather.15
  486.6 34.7 reduce-scatter.2
  575.9 34.2 reduce-scatter.4

commit v5 on v4

--- a/solution.py
+++ b/solution.py
@@ -191,10 +191,13 @@
 BACK_ROWS = 2 * ADAPTER_RANK
 
 
-def expert_kernel(count, splits, experts, capacity, depth, with_prior, with_shared, with_sums, packed, waits, *refs):
+def expert_kernel(
+    count, splits, experts, capacity, depth, direct, with_prior, with_shared, with_sums, packed, waits, *refs
+):
     meta, refs = refs[0], refs[1:]
     weight_count = 5 if with_shared else 3
-    weight_refs, refs = refs[:weight_count], refs[weight_count:]
+    given = weight_count - (2 if with_shared else 1) if direct else weight_count
+    weight_refs, refs = refs[:given], refs[given:]
     token_refs, grad_refs = [], []
     for split in splits:
         token_refs.append(refs[:split])
@@ -232,8 +235,25 @@
     rank = ADAPTER_RANK
     up_ref, down_ref, second_ref = weight_bufs[:3]
 
-    def weight_copy(n):
-        return pltpu.make_async_copy(weight_refs[n], weight_bufs[n], weight_sem.at[n])
+    def weight_copies():
+        pairs = list(zip(weight_refs, weight_bufs))
+        if direct:
+            raw, lines = weight_refs[1], weight_refs[1].shape[1]
+            pairs, columns = pairs[:1], second_ref.shape[1] // depth
+            for z in range(depth):
+                pairs.append((raw.at[z, :, pl.ds(0, wide)], down_ref.at[pl.ds(z * lines, lines)]))
+                part = raw.at[z, :, pl.ds(wide, columns)]
+                pairs.append((part, second_ref.at[:, pl.ds(z * columns, columns)]))
+            if with_shared:
+                group, size = 4 * LANES, lines // 4
+                for z in range(depth):
+                    for q in range(4):
+                        width = min(group, wide - q * group)
+                        part = raw.at[z, pl.ds(q * size, size), pl.ds(wide + columns, width)]
+                        target = weight_bufs[3].at[pl.ds(z * size, size), pl.ds(q * group, width)]
+                        pairs.append((part, target))
+                pairs.append((weight_refs[2], weight_bufs[4]))
+        return [pltpu.make_async_copy(src, dst, weight_sem.at[n]) for n, (src, dst) in enumerate(pairs)]
 
     def incoming(k, i, kinds):
         copies = []
@@ -290,8 +310,8 @@
         for i in (0, 1):
             for copy in incoming(0, i, (1,)):
                 copy.start()
-        for n in range(weight_count):
-            weight_copy(n).start()
+        for copy in weight_copies():
+            copy.start()
         for i in (0, 1):
             for copy in incoming(0, i, (2,)):
                 copy.start()
@@ -338,8 +358,8 @@
 
     @pl.when(step == 0)
     def _():
-        for n in range(weight_count):
-            weight_copy(n).wait()
+        for copy in weight_copies():
+            copy.wait()
 
     low = (dot_nn(inputs, up_ref[:, 2 * hidden : 2 * hidden + 2 * LANES]) * select_two).astype(BF16)
     gate_part = dot_nn(inputs, up_ref[:, :hidden]) + dot_nn(low[:, :LANES], second_ref[:, :hidden])
@@ -473,9 +493,10 @@
             sum_copy(n).wait()
 
 
-def expert_call(meta, weights, tokens, grads, prior, sums, packed, experts, capacity, depth, deps=()):
+def expert_call(meta, weights, shapes, tokens, grads, prior, sums, packed, experts, capacity, depth, deps=()):
     count = len(tokens)
-    with_shared = len(weights) > 3
+    with_shared = len(shapes) > 3
+    direct = len(weights) < len(shapes)
     splits = [len(pieces) for pieces in tokens]
     rows, model = sum(piece.shape[0] for piece in grads[0]), grads[0][0].shape[1]
     wide = model + LANES
@@ -486,21 +507,22 @@
     grad_shapes = [
         jax.ShapeDtypeStruct((model, 2 * LANES), F32),
         jax.ShapeDtypeStruct((EXPERT_HIDDEN, LANES), F32),
-        jax.ShapeDtypeStruct(weights[2].shape, F32),
+        jax.ShapeDtypeStruct(shapes[2], F32),
     ]
     if with_shared:
-        grad_shapes.append(jax.ShapeDtypeStruct((weights[3].shape[0], LANES), F32))
+        grad_shapes.append(jax.ShapeDtypeStruct((shapes[3][0], LANES), F32))
     out_shapes = grad_shapes
     if packed:
-        lines = sum(s.shape[0] for s in grad_shapes[:2]) + model + weights[2].shape[1]
+        lines = sum(s.shape[0] for s in grad_shapes[:2]) + model + shapes[2][1]
         lines = lines // depth
         if with_shared:
-            lines += -(-weights[3].shape[0] // depth // 16) * 16
+            lines += -(-shapes[3][0] // depth // 16) * 16
         out_shapes = [jax.ShapeDtypeStruct((depth, lines, LANES), BF16)]
     back_rows = rows + BACK_ROWS
     outs = pl.pallas_call(
         functools.partial(
-            expert_kernel, count, splits, experts, capacity, depth, bool(prior), with_shared, bool(sums), packed, len(deps)
+            expert_kernel,
+            *(count, splits, experts, capacity, depth, direct, bool(prior), with_shared, bool(sums), packed, len(deps)),
         ),
         grid=(count // 2,),
         in_specs=[pl.BlockSpec(memory_space=pltpu.SMEM)]
@@ -510,7 +532,7 @@
         + [jax.ShapeDtypeStruct((back_rows, wide), BF16)] * count
         + out_shapes,
         scratch_shapes=[pltpu.VMEM(s.shape, F32) for s in grad_shapes]
-        + [pltpu.VMEM(w.shape, BF16) for w in weights]
+        + [pltpu.VMEM(shape, BF16) for shape in shapes]
         + ([pltpu.VMEM(out_shapes[0].shape, BF16)] if packed else [])
         + [
             pltpu.VMEM((slots, 2, rows, wide), BF16),
@@ -519,7 +541,7 @@
             pltpu.VMEM((slots, 2, back_rows, wide), BF16),
             pltpu.SemaphoreType.DMA((slots, 2, 6)),
             pltpu.SemaphoreType.DMA((slots, 2, 2)),
-            pltpu.SemaphoreType.DMA((len(weights),)),
+            pltpu.SemaphoreType.DMA((len(shapes) + 6 * depth,)),
             pltpu.SemaphoreType.DMA((len(grad_shapes),)),
             pltpu.SemaphoreType.DMA((len(grad_shapes),)),
         ],
@@ -924,24 +946,6 @@
     edges = [sum(widths[:n]) for n in range(len(widths) + 1)]
     b_parts = [second[:, edges[n] : edges[n + 1]] for n in range(len(widths))]
 
-    x_flat = block_input[0].astype(F32)
-    normed = rms_norm(x_flat, gains[0]).astype(BF16)
-    low_kv = dot_nn(normed, first_kv).astype(BF16)
-    kv_extra = jnp.concatenate([dot_nn(low_kv[:, :rank], b_parts[1]), dot_nn(low_kv[:, rank:], b_parts[2])], axis=1)
-    present_tag = jnp.where(key_present == 1, document_number + 1, 0).astype(BF16)
-    tag_columns = jnp.broadcast_to(present_tag.reshape(rows, 1), (rows, LANES))
-    kv_blocks = [jnp.concatenate([(dot_nn(normed, kv_w) + kv_extra).astype(BF16), tag_columns], axis=1)]
-    q_blocks = plane_gather(tie(seq_q, *far_grads), size)
-    for k in range(1, size, 2):
-        grad_blocks[k] = tuple(swap(piece, 1, size) for piece in grad_blocks[k - 1])
-    for h in range(hops):
-        block = kv_blocks[-1] if h == 0 else tie(kv_blocks[-1], q_blocks[2][0], q_blocks[4][0])
-        kv_blocks.append(lax.ppermute(block, "seq", forward))
-        kv_blocks[h] = block
-    kv_all = jnp.concatenate(kv_blocks[::-1], axis=0)
-    key_tag = kv_all[:, 2 * kv_width : 2 * kv_width + 1].astype(F32)
-    query_tag = (document_number + 1).astype(F32)
-
     down_rows = routed_down_weight.shape[1]
     second_cut = rank_all * routed_second_factor.shape[2] // down_rows
     up_shards, down_shards = [], []
@@ -958,13 +962,35 @@
         if j == 0:
             up_parts.append(gate_up.reshape(size * shard_rows, 2 * units))
             shared_down = jnp.concatenate([shared_down_weight, shared_down_first_factor], axis=1)
+            shared_down = jnp.pad(shared_down, ((0, 0), (0, 16 * LANES - shared_down.shape[1])))
+            shared_down = shared_down.reshape(shared_rows, 4, 4 * LANES).transpose(1, 0, 2)
             down_parts.append(shared_down.reshape(down_rows, -1))
         up_shards.append(jnp.concatenate(up_parts, axis=1))
         down_shards.append(jnp.concatenate(down_parts, axis=1))
-    seq_up, seq_down = [], []
-    for j in range(local_experts):
-        seq_up.append(over_seq(tie(up_shards[j], seq_kv if j == 0 else seq_up[j - 1])))
-        seq_down.append(over_seq(tie(down_shards[j], kv_blocks[1] if j == 0 else seq_up[j - 1])))
+    first_down = over_seq(tie(down_shards[0], seq_kv))
+
+    x_flat = block_input[0].astype(F32)
+    normed = rms_norm(x_flat, gains[0]).astype(BF16)
+    low_kv = dot_nn(normed, first_kv).astype(BF16)
+    kv_extra = jnp.concatenate([dot_nn(low_kv[:, :rank], b_parts[1]), dot_nn(low_kv[:, rank:], b_parts[2])], axis=1)
+    present_tag = jnp.where(key_present == 1, document_number + 1, 0).astype(BF16)
+    tag_columns = jnp.broadcast_to(present_tag.reshape(rows, 1), (rows, LANES))
+    kv_blocks = [jnp.concatenate([(dot_nn(normed, kv_w) + kv_extra).astype(BF16), tag_columns], axis=1)]
+    q_blocks = plane_gather(tie(seq_q, *far_grads), size)
+    for k in range(1, size, 2):
+        grad_blocks[k] = tuple(swap(piece, 1, size) for piece in grad_blocks[k - 1])
+    for h in range(hops):
+        block = kv_blocks[-1] if h == 0 else tie(kv_blocks[-1], q_blocks[2][0], q_blocks[4][0], first_down)
+        kv_blocks.append(lax.ppermute(block, "seq", forward))
+        kv_blocks[h] = block
+    kv_all = jnp.concatenate(kv_blocks[::-1], axis=0)
+    key_tag = kv_all[:, 2 * kv_width : 2 * kv_width + 1].astype(F32)
+    query_tag = (document_number + 1).astype(F32)
+
+    seq_up, seq_down = [over_seq(tie(up_shards[0], kv_blocks[hops]))], [first_down]
+    for j in range(1, local_experts):
+        seq_up.append(over_seq(tie(up_shards[j], seq_down[j - 1])))
+        seq_down.append(over_seq(tie(down_shards[j], seq_up[j - 1])))
 
     q_w, q_first, out_w = assemble(q_blocks, ((1, query_width), (1, 4 * rank_all), (1, model)), me)
     q_first = own_factors(q_first)
@@ -1005,17 +1031,28 @@
     moe_parts, back_parts, grad_sums = [None] * size, [None] * size, []
     wide = model + rank_all
 
+    direct = down_rows == rank_all
+    shapes = [None] * local_experts
+
     def weights_of(j):
-        second_j = seq_down[j][:, :, wide : wide + second_cut]
-        second_j = second_j.reshape(depth, rank_all, -1).transpose(1, 0, 2).reshape(rank_all, -1)
-        args = [seq_up[j].reshape(model, -1), seq_down[j][:, :, :wide].reshape(EXPERT_HIDDEN, wide), second_j]
+        args = [seq_up[j].reshape(model, -1)]
+        shapes[j] = [args[0].shape, (EXPERT_HIDDEN, wide), (rank_all, depth * second_cut * down_rows // rank_all)]
+        if direct:
+            args.append(seq_down[j])
+        else:
+            second_j = seq_down[j][:, :, wide : wide + second_cut]
+            second_j = second_j.reshape(depth, rank_all, -1).transpose(1, 0, 2).reshape(rank_all, -1)
+            args += [seq_down[j][:, :, :wide].reshape(EXPERT_HIDDEN, wide), second_j]
         if j == 0:
-            args.append(seq_down[j][:, :, wide + second_cut :].reshape(units, wide))
+            if not direct:
+                parts = seq_down[j][:, :, wide + second_cut :].reshape(depth, 4, shared_rows, 4 * LANES)
+                args.append(parts.transpose(0, 2, 1, 3).reshape(units, -1)[:, :wide])
             slices = [
                 lax.dynamic_slice_in_dim(second_t[edges[n] : edges[n + 1]].reshape(depth, size, -1, rank_all), me, 1, 1)
                 for n in (4, 5)
             ]
             args.append(jnp.concatenate([part.reshape(units, rank_all) for part in slices], axis=0))
+            shapes[j] += [(units, wide), args[-1].shape]
         return args
 
     def run_expert(j, args, group, prior, deps, packed=False):
@@ -1024,6 +1061,7 @@
         moe_out, back_out, grads = expert_call(
             meta,
             args,
+            shapes[j],
             [token_blocks[k] for k in group],
             [grad_blocks[k] for k in group],
             prior,

time: 764 us -> 730 us (0.955)
  starting transfers between devices: 78.8 us -> 59 us
  local copies, waits for them, and re-layouts: 94.9 us -> 80.7 us
    ppermute x2, starting transfers between devices: 33.6 us -> 10.5 us  [per_device(): kv_blocks.append(lax.ppermute(block, 'seq', forward))]
    all_gather x5, waiting for transfers between devices: 7.79 us -> 24 us  [over_seq(): return lax.all_gather(shard, 'seq', axis=0)]
    ppermute x2, waiting for transfers between devices: 48.6 us -> 35.4 us  [per_device(): kv_blocks.append(lax.ppermute(block, 'seq', forward))]
    slice x4 -> x0, local copies, waits for them, and re-layouts: 8.55 us -> none  [the longest x2 5.54 us: weights_of(): seq_down[j][:, :, :wide].reshape(EXPERT_HIDDEN, wide)]
    unnamed x195 -> x196, local copies, waits for them, and re-layouts: 32.3 us -> 34 us
  transfers between devices with their start and end apart: 65 -> 65, of which waited for: 17 -> 16; matrix products, arithmetic and copies ran while one was open for 19% -> 17% of each run, Pallas kernels for 36% -> 38%
where the time goes in v5:
time: 730 us; the launch traced here: 721 us
  Pallas kernels  317 us (43%)
  waiting for transfers between devices  154 us (21%)
  local copies, waits for them, and re-layouts  80.7 us (11%)
  starting transfers between devices  59 us (8%)
  other arithmetic  50.3 us (7%)
  matrix products  22.9 us (3%)
  blocking collectives  20.3 us (3%)
  between operations  16.5 us (2%)
    pallas_call x8, Pallas kernels, expert_call(): pl.pallas_call(functools.partial(expert_kernel, *(count, splits, experts,...  197 us
    ppermute x52, waiting for transfers between devices, swap(): return lax.ppermute(array, 'dp', [(i, i ^ bit) for i in range(size)])  56.1 us
    ppermute x52, starting transfers between devices, swap(): return lax.ppermute(array, 'dp', [(i, i ^ bit) for i in range(size)])  37.7 us
    ppermute x2, waiting for transfers between devices, per_device(): kv_blocks.append(lax.ppermute(block, 'seq', forward))  35.4 us
    unnamed x196, local copies, waits for them, and re-layouts  34 us
    pallas_call x1, Pallas kernels, attend_back(): pl.pallas_call(functools.partial(attend_back_kernel, spans, hops * rows,...  33.4 us
    all_gather x5, waiting for transfers between devices, over_seq(): return lax.all_gather(shard, 'seq', axis=0)  24 us
    pallas_call x1, Pallas kernels, attend(): pl.pallas_call(functools.partial(attend_kernel, spans, hops * rows, len(d...  23.7 us
  transfers between devices with their start and end apart: 65, of which 16 were waited for; matrix products, arithmetic and copies ran while one was open for 17% of the time, Pallas kernels for 38%

profile of v5, /device:TPU:0, one launch (start us, length us, event | category | flops | bytes accessed | tf_op | source)
XLA Modules:
  0.0 721.4 jit_solution(8571048925857403626)
XLA Ops:
  7.2 3.0 collective-permute-start
  15.1 3.4 all-to-all-start
  19.7 20.3 %all-gather = bf16[192,2048]{1,0:T(8,128)(2,1)} all-gather(bf16[48,2048]{1,0:T(8,128)(2,1)S(1)} %fusion.14), channel_id=2, replica_groups=mesh['seq'=4,'dp'=8] {'seq'}, dimensions={0}, use_global_device_ids=true | all-gather | bytes 983040 | tf_op jit(solution)/shard_map/all_gather | solution.py:890
  42.6 5.7 all-to-all-done.refs_3_
  51.1 17.2 %collective-permute-done.3.refs_2_ = bf16[4,48,2048]{2,1,0:T(8,128)(2,1)S(1)} collective-permute-done((bf16[4,48,2048]{2,1,0:T(8,128)(2,1)}, bf16[4,48,2048]{2,1,0:T(8,128)(2,1)S(1)}, u32[]{:S(2)}, u32[]{:S(2)}) %collective-permute-start.3) | collective-permute-done | bytes 786464 | tf_op jit(solution)/shard_map/ppermute | solution.py:556
  74.1 5.1 collective-permute-done.8.refs_7_.refs_3_
  88.0 5.6 assemble.2
  95.8 3.5 constant_dynamic-slice_fusion.7
  105.5 2.8 fusion.5
  114.5 4.5 collective-permute-start.22
  119.9 35.4 %collective-permute-done.22.refs_0_ = bf16[512,1152]{1,0:T(8,128)(2,1)} collective-permute-done((bf16[512,1152]{1,0:T(8,128)(2,1)}, bf16[512,1152]{1,0:T(8,128)(2,1)}, u32[]{:S(2)}, u32[]{:S(2)}) %collective-permute-start.22) | collective-permute-done | bytes 1179680 | tf_op jit(solution)/shard_map/ppermute | solution.py:984
  155.3 5.9 collective-permute-start.23
  161.2 2.5 fusion.44
  174.6 7.0 collective-permute-done.18.refs_6_
  183.8 3.8 collective-permute-done.19.refs_7_
  194.3 9.3 %assemble.3 = (bf16[4,8,1,48,1536]{4,3,2,1,0:T(8,128)(2,1)}, bf16[4,8,1,48,512]{4,3,2,1,0:T(8,128)(2,1)}, bf16[4,8,1,48,1536]{4,3,2,1,0:T(8,128)(2,1)}) custom-call(s32[1]{0:T(128)} %bitcast.1.me_ref, bf16[4,48,3584]{2,1,0:T(8,128)(2,1)} %tie.19.refs_0_, bf16[4,48,3584]{2,1,0:T(8,128)(2,1)} %collective-permute-done.13.refs_1_, ...), custom_call_target="tpu_custom_call" | custom-call | tf_op jit(solution)/shard_map/assemble/pallas_call | solution.py:629
  203.6 2.4 fusion.43
  209.3 3.8 fusion.4.q_ref
  213.4 23.7 %attend.1 = (bf16[512,1536]{1,0:T(8,128)(2,1)}, f32[4,3,512]{2,1,0:T(4,128)}) custom-call(bf16[512,1536]{1,0:T(8,128)(2,1)} %fusion.4.q_ref, bf16[1536,1152]{1,0:T(8,128)(2,1)} %copy-done.22, bf16[1536,1152]{1,0:T(8,128)(2,1)} %copy-done.22, f32[1,512]{1,0:T(1,128)} %add_convert_fusion.14.qt_ref, f32[1536,1]{1,0:T(8,128)} %slice_convert_fusion.kt_ref, ...), custom_call_target="tpu_custom_call" | custom-call | flops 26530500608 | bytes 1000000 | tf_op jit(solution)/shard_map/attend/pallas_call | solution.py:96
  240.6 4.8 multiply_reduce_fusion
  260.6 16.1 %all-gather.18.cloned.1.call-done.refs_1_ = bf16[1536,1536]{1,0:T(8,128)(2,1)} async-done(((bf16[384,1536]{1,0:T(8,128)(2,1)}), bf16[1536,1536]{1,0:T(8,128)(2,1)}) %all-gather.18.cloned.1.call-update) | async-done | bytes 4718608 | tf_op jit(solution)/shard_map/all_gather | solution.py:890
  276.7 25.6 %expert.8 = (bf16[512,1536]{1,0:T(8,128)(2,1)}, bf16[512,1536]{1,0:T(8,128)(2,1)}, bf16[544,1664]{1,0:T(8,128)(2,1)}, bf16[544,1664]{1,0:T(8,128)(2,1)}, f32[153...) custom-call(s32[2]{0:T(128)} %pad_add_fusion.1.refs_0_, ...), custom_call_target="tpu_custom_call" | custom-call | flops 27683999744 | bytes 1000000 | tf_op jit(solution)/shard_map/expert/pallas_call | solution.py:522
  311.0 27.3 %expert.9 = (bf16[512,1536]{1,0:T(8,128)(2,1)}, bf16[512,1536]{1,0:T(8,128)(2,1)}, bf16[544,1664]{1,0:T(8,128)(2,1)}, bf16[544,1664]{1,0:T(8,128)(2,1)}, f32[153...) custom-call(s32[2]{0:T(128)} %pad_add_fusion.1.refs_0_, ...), custom_call_target="tpu_custom_call" | custom-call | flops 27683999744 | bytes 1000000 | tf_op jit(solution)/shard_map/expert/pallas_call | solution.py:522
  340.0 27.2 %expert.10 = (bf16[512,1536]{1,0:T(8,128)(2,1)}, bf16[512,1536]{1,0:T(8,128)(2,1)}, bf16[544,1664]{1,0:T(8,128)(2,1)}, bf16[544,1664]{1,0:T(8,128)(2,1)}, f32[15...) custom-call(s32[2]{0:T(128)} %pad_add_fusion.1.refs_0_, ...), custom_call_target="tpu_custom_call" | custom-call | flops 27683999744 | bytes 1000000 | tf_op jit(solution)/shard_map/expert/pallas_call | solution.py:522
  368.5 27.7 %expert.11 = (bf16[512,1536]{1,0:T(8,128)(2,1)}, bf16[512,1536]{1,0:T(8,128)(2,1)}, bf16[544,1664]{1,0:T(8,128)(2,1)}, bf16[544,1664]{1,0:T(8,128)(2,1)}, bf16[4,1568,128]{2,1,0:T(8,128)(2,1)}) custom-call(s32[2]{0:T(128)} %pad_add_fusion.1.refs_0_, bf16[1536,1536]{1,0:T(8,128)(2,1)} %all-gather.18.cloned.1.call-done.refs_1_, ...), custom_call_target="tpu_custom_call" | custom-call | flops 27683999744 | bytes 1000000 | tf_op jit(solution)/shard_map/expert/pallas_call | solution.py:522
  396.3 7.9 %all-gather.20.cloned.1.call-done = bf16[512,2304]{1,0:T(8,128)(2,1)} async-done(((bf16[128,2304]{1,0:T(8,128)(2,1)}), bf16[512,2304]{1,0:T(8,128)(2,1)}) %all-gather.20.cloned.1.call-update) | async-done | bytes 2359312 | tf_op jit(solution)/shard_map/all_gather | solution.py:890
  404.1 21.0 %expert.12 = (bf16[512,1536]{1,0:T(8,128)(2,1)}, bf16[512,1536]{1,0:T(8,128)(2,1)}, bf16[544,1664]{1,0:T(8,128)(2,1)}, bf16[544,1664]{1,0:T(8,128)(2,1)}, f32[15...) custom-call(s32[2]{0:T(128)} %pad_add_fusion.refs_0_, ...), custom_call_target="tpu_custom_call" | custom-call | flops 27683999744 | bytes 1000000 | tf_op jit(solution)/shard_map/expert/pallas_call | solution.py:522
  425.2 3.9 collective-permute-done.38
  429.1 3.2 add_convert_fusion.2.refs_14_
  432.3 22.7 %expert.13 = (bf16[512,1536]{1,0:T(8,128)(2,1)}, bf16[512,1536]{1,0:T(8,128)(2,1)}, bf16[544,1664]{1,0:T(8,128)(2,1)}, bf16[544,1664]{1,0:T(8,128)(2,1)}, f32[15...) custom-call(s32[2]{0:T(128)} %pad_add_fusion.refs_0_, ...), custom_call_target="tpu_custom_call" | custom-call | flops 27683999744 | bytes 1000000 | tf_op jit(solution)/shard_map/expert/pallas_call | solution.py:522
  459.7 3.3 add_convert_fusion.1.refs_14_
  463.0 22.8 %expert.14 = (bf16[512,1536]{1,0:T(8,128)(2,1)}, bf16[512,1536]{1,0:T(8,128)(2,1)}, bf16[544,1664]{1,0:T(8,128)(2,1)}, bf16[544,1664]{1,0:T(8,128)(2,1)}, f32[15...) custom-call(s32[2]{0:T(128)} %pad_add_fusion.refs_0_, ...), custom_call_target="tpu_custom_call" | custom-call | flops 27683999744 | bytes 1000000 | tf_op jit(solution)/shard_map/expert/pallas_call | solution.py:522
  485.9 4.2 reduce-scatter.3.cloned.1.call-done.refs_3_.refs_0_
  501.9 23.0 %expert.15 = (bf16[512,1536]{1,0:T(8,128)(2,1)}, bf16[512,1536]{1,0:T(8,128)(2,1)}, bf16[544,1664]{1,0:T(8,128)(2,1)}, bf16[544,1664]{1,0:T(8,128)(2,1)}, bf16[4,1536,128]{2,1,0:T(8,128)(2,1)}) custom-call(s32[2]{0:T(128)} %pad_add_fusion.refs_0_, bf16[1536,1280]{1,0:T(8,128)(2,1)} %all-gather.16.cloned.1.call-done.refs_1_, bf16[4,128,2304]{2,1,0:T(8,128)(2,1)} %bitcast.227, ...), custom_call_target="tpu_custom_call" | custom-call | flops 27683999744 | bytes 1000000 | tf_op jit(solution)/shard_map/expert/pallas_call | solution.py:522
  524.9 12.0 %collective-permute-done.43.refs_4_.refs_1_.from_x = bf16[544,1664]{1,0:T(8,128)(2,1)S(1)} collective-permute-done((bf16[544,1664]{1,0:T(8,128)(2,1)}, bf16[544,1664]{1,0:T(8,128)(2,1)S(1)}, u32[]{:S(2)}, u32[]{:S(2)}) %collective-permute-start.43) | collective-permute-done | bytes 1810464 | tf_op jit(solution)/shard_map/ppermute | solution.py:556
  536.9 4.6 collective-permute-done.44.refs_5_.refs_2_.from_y
  554.7 18.8 %turn.1 = (f32[512,1536]{1,0:T(8,128)}, bf16[512,1536]{1,0:T(8,128)(2,1)}, bf16[512,16]{1,0:T(8,128)(2,1)}, bf16[512,32]{1,0:T(8,128)(2,1)}, bf16[512,16]{1,0:T(...) custom-call(bf16[544,1664]{1,0:T(8,128)(2,1)} %get-tuple-element.174.own, ...), custom_call_target="tpu_custom_call" | custom-call | flops 4614000128 | bytes 1000000 | tf_op jit(solution)/shard_map/turn/pallas_call | solution.py:694
  573.5 33.4 %attend_back.1 = (bf16[512,1536]{1,0:T(8,128)(2,1)}, bf16[1536,1024]{1,0:T(8,128)(2,1)}) custom-call(bf16[512,1536]{1,0:T(8,128)(2,1)} %fusion.4.q_ref, bf16[1536,1152]{1,0:T(8,128)(2,1)} %copy-done.22, bf16[1536,1152]{1,0:T(8,128)(2,1)} %copy-done.22, bf16[512,1536]{1,0:T(8,128)(2,1)} %get-tuple-element.177.g_ref, f32[4,3,512]{2,1,0:T(4,128)} %get-tuple-element.178.lse_ref, ...), custom_call_target="tpu_custom_call" | custom-call | flops 9228000256 | bytes 1000000 | tf_op jit(solution)/shard_map/attend_back/pallas_call | solution.py:159
  621.9 14.9 %collective-permute-done.54.rest_0_.refs_2_ = bf16[512,1024]{1,0:T(8,128)(2,1)S(1)} collective-permute-done((bf16[512,1024]{1,0:T(8,128)(2,1)}, bf16[512,1024]{1,0:T(8,128)(2,1)S(1)}, u32[]{:S(2)}, u32[]{:S(2)}) %collective-permute-start.54) | collective-permute-done | bytes 1048608 | tf_op jit(solution)/shard_map/ppermute | solution.py:1136
  640.5 2.5 add_convert_fusion.9.refs_0_
  644.7 5.2 middle.1
  653.2 9.7 %query_back.1 = (f32[512,1536]{1,0:T(8,128)}, f32[1536,16]{1,0:T(8,128)}, f32[16,1536]{1,0:T(8,128)}) custom-call(bf16[512,1536]{1,0:T(8,128)(2,1)} %get-tuple-element.181.grad_q, bf16[512,1536]{1,0:T(8,128)(2,1)} %copy-done.4, bf16[512,16]{1,0:T(8,128)(2,1)} %copy-done.53, bf16[1536,1536]{1,0:T(8,128)(2,1)} %bitcast.175, bf16[1536,16]{1,0:T(8,128)(2,1)} %copy-done.28, ...), custom_call_target="tpu_custom_call" | custom-call | flops 115350000 | bytes 1000000 | tf_op jit(solution)/shard_map/query_back/pallas_call | solution.py:717
  662.9 7.0 collective-permute-done.55
  669.9 2.9 add_convert_fusion.8.grad_kv
  672.8 12.1 %last.1 = (f32[512,1536]{1,0:T(8,128)}, bf16[1536,128]{1,0:T(8,128)(2,1)}, bf16[32,32,128]{2,1,0:T(8,128)(2,1)}) custom-call(bf16[512,1024]{1,0:T(8,128)(2,1)} %add_convert_fusion.8.grad_kv, bf16[512,1536]{1,0:T(8,128)(2,1)} %copy-done.4, bf16[512,32]{1,0:T(8,128)(2,1)} %copy-done.52, bf16[1536,1024]{1,0:T(8,128)(2,1)} %bitcast.185, ...), custom_call_target="tpu_custom_call" | custom-call | flops 2307000064 | bytes 1000000 | tf_op jit(solution)/shard_map/last/pallas_call | solution.py:788
  687.0 3.9 all-to-all-start.1
  697.3 4.6 fusion.7
  702.0 6.9 all-to-all-done.1.flat
  (455 shorter events, 160.6 us)
Async XLA Ops:
  7.2 41.2 %collective-permute-start = (bf16[512,1536]{1,0:T(8,128)(2,1)}, bf16[512,1536]{1,0:T(8,128)(2,1)}, u32[]{:S(2)}, u32[]{:S(2)}) collective-permute-start(bf16[512,1536]{1,0:T(8,128)(2,1)} %bitcast.160), channel_id=1, source_target_pairs={{0,2},{1,3},{2,0},{3,1},{4,6},{5,7},{6,4},{7,5},{8,10},{9,11},{10,... | collective-permute-start | bytes 4718600 | tf_op jit(solution)/shard_map/ppermute | solution.py:556
  10.2 38.2 %collective-permute-start.1 = (bf16[512,1536]{1,0:T(8,128)(2,1)}, bf16[512,1536]{1,0:T(8,128)(2,1)}, u32[]{:S(2)}, u32[]{:S(2)}) collective-permute-start(bf16[512,1536]{1,0:T(8,128)(2,1)} %bitcast.161), channel_id=1, source_target_pairs={{0,4},{1,5},{2,6},{3,7},{4,0},{5,1},{6,2},{7,3},{8,12},{9,13},{10,... | collective-permute-start | bytes 4718600 | tf_op jit(solution)/shard_map/ppermute | solution.py:556
  15.1 33.3 %all-to-all-start = ((bf16[8,48,256]{2,1,0:T(8,128)(2,1)}), bf16[8,48,256]{2,1,0:T(8,128)(2,1)S(1)}, u32[]{:S(2)}, u32[]{:S(2)}) async-start(bf16[8,48,256]{2,1,0:T(8,128)(2,1)} %copy.170), calls=%async_computation | async-start | bytes 393216 | tf_op jit(solution)/shard_map/all_to_all | solution.py:933
  18.5 89.9 %all-gather.12.cloned.1.call-start = ((), (), s32[]{:S(2)}) async-start(), calls=%async_computation.6 | async-start | bytes 1720320 | tf_op jit(solution)/shard_map/all_gather | solution.py:890
  40.0 115.2 %all-gather.14.cloned.1.call-start = ((), (), s32[]{:S(2)}) async-start(), calls=%async_computation.7 | async-start | bytes 3604480 | tf_op jit(solution)/shard_map/all_gather | solution.py:890
  49.1 19.2 %collective-permute-start.3 = (bf16[4,48,2048]{2,1,0:T(8,128)(2,1)}, bf16[4,48,2048]{2,1,0:T(8,128)(2,1)S(1)}, u32[]{:S(2)}, u32[]{:S(2)}) collective-permute-start(bf16[4,48,2048]{2,1,0:T(8,128)(2,1)} %tie.16.refs_0_), channel_id=1, source_target_pairs={{0,2},{1,3},{2,0},{3,1},{4,6},{5,7},{6,4},{7,5},{8,10},{9,11},{10,... | collective-permute-start | bytes 2359304 | tf_op jit(solution)/shard_map/ppermute | solution.py:556
  50.0 20.7 %collective-permute-start.5 = (bf16[4,48,2048]{2,1,0:T(8,128)(2,1)}, bf16[4,48,2048]{2,1,0:T(8,128)(2,1)S(1)}, u32[]{:S(2)}, u32[]{:S(2)}) collective-permute-start(bf16[4,48,2048]{2,1,0:T(8,128)(2,1)} %tie.16.refs_0_), channel_id=1, source_target_pairs={{0,4},{1,5},{2,6},{3,7},{4,0},{5,1},{6,2},{7,3},{8,12},{9,13},{10,... | collective-permute-start | bytes 2359304 | tf_op jit(solution)/shard_map/ppermute | solution.py:556
  72.3 14.4 %collective-permute-start.2 = (bf16[4,48,2048]{2,1,0:T(8,128)(2,1)}, bf16[4,48,2048]{2,1,0:T(8,128)(2,1)}, u32[]{:S(2)}, u32[]{:S(2)}) collective-permute-start(bf16[4,48,2048]{2,1,0:T(8,128)(2,1)} %tie.16.refs_0_), channel_id=1, source_target_pairs={{0,1},{1,0},{2,3},{3,2},{4,5},{5,4},{6,7},{7,6},{8,9},{9,8},{10,11... | collective-permute-start | bytes 2359304 | tf_op jit(solution)/shard_map/ppermute | solution.py:556
  72.3 15.6 %collective-permute-start.4 = (bf16[4,48,2048]{2,1,0:T(8,128)(2,1)S(1)}, bf16[4,48,2048]{2,1,0:T(8,128)(2,1)}, u32[]{:S(2)}, u32[]{:S(2)}) collective-permute-start(bf16[4,48,2048]{2,1,0:T(8,128)(2,1)S(1)} %collective-permute-done.3.refs_2_), channel_id=1, source_target_pairs={{0,1},{1,0},{2,3},{3,2},{4,5},{5,4},{6,7},{7,6},{8,9},{9,8},{10,11... | collective-permute-start | bytes 2359304 | tf_op jit(solution)/shard_map/ppermute | solution.py:556
  72.8 15.1 %collective-permute-start.6 = (bf16[4,48,2048]{2,1,0:T(8,128)(2,1)S(1)}, bf16[4,48,2048]{2,1,0:T(8,128)(2,1)}, u32[]{:S(2)}, u32[]{:S(2)}) collective-permute-start(bf16[4,48,2048]{2,1,0:T(8,128)(2,1)S(1)} %collective-permute-done.5.refs_4_), channel_id=1, source_target_pairs={{0,1},{1,0},{2,3},{3,2},{4,5},{5,4},{6,7},{7,6},{8,9},{9,8},{10,11... | collective-permute-start | bytes 2359304 | tf_op jit(solution)/shard_map/ppermute | solution.py:556
  72.8 203.9 %all-gather.18.cloned.1.call-start = ((), (), s32[]{:S(2)}) async-start(), calls=%async_computation.9 | async-start | bytes 5898240 | tf_op jit(solution)/shard_map/all_gather | solution.py:890
  86.7 21.7 %collective-permute-start.11 = (bf16[256,1536]{1,0:T(8,128)(2,1)}, bf16[256,1536]{1,0:T(8,128)(2,1)}, u32[]{:S(2)}, u32[]{:S(2)}) collective-permute-start(bf16[256,1536]{1,0:T(8,128)(2,1)} %slice.237), channel_id=1, source_target_pairs={{0,2},{1,3},{2,0},{3,1},{4,6},{5,7},{6,4},{7,5},{8,10},{9,11},{10,... | collective-permute-start | bytes 2359304 | tf_op jit(solution)/shard_map/ppermute | solution.py:556
  87.7 20.7 %collective-permute-start.12 = (bf16[256,1536]{1,0:T(8,128)(2,1)}, bf16[256,1536]{1,0:T(8,128)(2,1)}, u32[]{:S(2)}, u32[]{:S(2)}) collective-permute-start(bf16[256,1536]{1,0:T(8,128)(2,1)} %slice.238), channel_id=1, source_target_pairs={{0,4},{1,5},{2,6},{3,7},{4,0},{5,1},{6,2},{7,3},{8,12},{9,13},{10,... | collective-permute-start | bytes 2359304 | tf_op jit(solution)/shard_map/ppermute | solution.py:556
  108.4 46.8 %collective-permute-start.16 = (bf16[4,48,3584]{2,1,0:T(8,128)(2,1)}, bf16[4,48,3584]{2,1,0:T(8,128)(2,1)}, u32[]{:S(2)}, u32[]{:S(2)}) collective-permute-start(bf16[4,48,3584]{2,1,0:T(8,128)(2,1)} %tie.19.refs_0_), channel_id=1, source_target_pairs={{0,4},{1,5},{2,6},{3,7},{4,0},{5,1},{6,2},{7,3},{8,12},{9,13},{10,... | collective-permute-start | bytes 4128776 | tf_op jit(solution)/shard_map/ppermute | solution.py:556
  110.3 45.0 %collective-permute-start.14 = (bf16[4,48,3584]{2,1,0:T(8,128)(2,1)}, bf16[4,48,3584]{2,1,0:T(8,128)(2,1)}, u32[]{:S(2)}, u32[]{:S(2)}) collective-permute-start(bf16[4,48,3584]{2,1,0:T(8,128)(2,1)} %tie.19.refs_0_), channel_id=1, source_target_pairs={{0,2},{1,3},{2,0},{3,1},{4,6},{5,7},{6,4},{7,5},{8,10},{9,11},{10,... | collective-permute-start | bytes 4128776 | tf_op jit(solution)/shard_map/ppermute | solution.py:556
  114.5 40.8 %collective-permute-start.22 = (bf16[512,1152]{1,0:T(8,128)(2,1)}, bf16[512,1152]{1,0:T(8,128)(2,1)}, u32[]{:S(2)}, u32[]{:S(2)}) collective-permute-start(bf16[512,1152]{1,0:T(8,128)(2,1)} %pad_maximum_fusion.4), channel_id=1, source_target_pairs={{0,8},{8,16},{16,24},{1,9},{9,17},{17,25},{2,10},{10,18},{18,26},{... | collective-permute-start | bytes 3538952 | tf_op jit(solution)/shard_map/ppermute | solution.py:984
  155.3 32.4 %collective-permute-start.23 = (bf16[512,1152]{1,0:T(8,128)(2,1)}, bf16[512,1152]{1,0:T(8,128)(2,1)}, u32[]{:S(2)}, u32[]{:S(2)}) collective-permute-start(bf16[512,1152]{1,0:T(8,128)(2,1)} %tie.21), channel_id=1, source_target_pairs={{0,8},{8,16},{16,24},{1,9},{9,17},{17,25},{2,10},{10,18},{18,26},{... | collective-permute-start | bytes 3538952 | tf_op jit(solution)/shard_map/ppermute | solution.py:984
  164.9 16.7 %collective-permute-start.18 = (bf16[2,48,3584]{2,1,0:T(8,128)(2,1)S(1)}, bf16[2,48,3584]{2,1,0:T(8,128)(2,1)S(1)}, u32[]{:S(2)}, u32[]{:S(2)}) collective-permute-start(bf16[2,48,3584]{2,1,0:T(8,128)(2,1)S(1)} %slice.307), channel_id=1, source_target_pairs={{0,2},{1,3},{2,0},{3,1},{4,6},{5,7},{6,4},{7,5},{8,10},{9,11},{10,... | collective-permute-start | bytes 2064392 | tf_op jit(solution)/shard_map/ppermute | solution.py:556
  170.9 16.7 %collective-permute-start.19 = (bf16[2,48,3584]{2,1,0:T(8,128)(2,1)}, bf16[2,48,3584]{2,1,0:T(8,128)(2,1)}, u32[]{:S(2)}, u32[]{:S(2)}) collective-permute-start(bf16[2,48,3584]{2,1,0:T(8,128)(2,1)} %slice.308), channel_id=1, source_target_pairs={{0,4},{1,5},{2,6},{3,7},{4,0},{5,1},{6,2},{7,3},{8,12},{9,13},{10,... | collective-permute-start | bytes 2064392 | tf_op jit(solution)/shard_map/ppermute | solution.py:556
  174.1 19.1 %collective-permute-start.13 = (bf16[4,48,3584]{2,1,0:T(8,128)(2,1)}, bf16[4,48,3584]{2,1,0:T(8,128)(2,1)}, u32[]{:S(2)}, u32[]{:S(2)}) collective-permute-start(bf16[4,48,3584]{2,1,0:T(8,128)(2,1)} %tie.19.refs_0_), channel_id=1, source_target_pairs={{0,1},{1,0},{2,3},{3,2},{4,5},{5,4},{6,7},{7,6},{8,9},{9,8},{10,11... | collective-permute-start | bytes 4128776 | tf_op jit(solution)/shard_map/ppermute | solution.py:556
  174.1 19.7 %collective-permute-start.15 = (bf16[4,48,3584]{2,1,0:T(8,128)(2,1)}, bf16[4,48,3584]{2,1,0:T(8,128)(2,1)}, u32[]{:S(2)}, u32[]{:S(2)}) collective-permute-start(bf16[4,48,3584]{2,1,0:T(8,128)(2,1)} %collective-permute-done.14.refs_2_.refs_1_), channel_id=1, source_target_pairs={{0,1},{1,0},{2,3},{3,2},{4,5},{5,4},{6,7},{7,6},{8,9},{9,8},{10,11... | collective-permute-start | bytes 4128776 | tf_op jit(solution)/shard_map/ppermute | solution.py:556
  188.2 208.1 %all-gather.16.cloned.1.call-start = ((), (), s32[]{:S(2)}) async-start(), calls=%async_computation.8 | async-start | bytes 4915200 | tf_op jit(solution)/shard_map/all_gather | solution.py:890
  193.2 20.2 %collective-permute-start.24 = (bf16[512,1536]{1,0:T(8,128)(2,1)}, bf16[512,1536]{1,0:T(8,128)(2,1)}, u32[]{:S(2)}, u32[]{:S(2)}) collective-permute-start(bf16[512,1536]{1,0:T(8,128)(2,1)} %get-tuple-element.106.refs_6_.refs_5_), channel_id=1, source_target_pairs={{0,1},{1,0},{2,3},{3,2},{4,5},{5,4},{6,7},{7,6},{8,9},{9,8},{10,11... | collective-permute-start | bytes 4718600 | tf_op jit(solution)/shard_map/ppermute | solution.py:556
  193.2 20.2 %collective-permute-start.25 = (bf16[512,1536]{1,0:T(8,128)(2,1)}, bf16[512,1536]{1,0:T(8,128)(2,1)}, u32[]{:S(2)}, u32[]{:S(2)}) collective-permute-start(bf16[512,1536]{1,0:T(8,128)(2,1)} %get-tuple-element.105.refs_6_.refs_5_), channel_id=1, source_target_pairs={{0,1},{1,0},{2,3},{3,2},{4,5},{5,4},{6,7},{7,6},{8,9},{9,8},{10,11... | collective-permute-start | bytes 4718600 | tf_op jit(solution)/shard_map/ppermute | solution.py:556
  193.8 19.6 %collective-permute-start.26 = (bf16[256,1536]{1,0:T(8,128)(2,1)}, bf16[256,1536]{1,0:T(8,128)(2,1)}, u32[]{:S(2)}, u32[]{:S(2)}) collective-permute-start(bf16[256,1536]{1,0:T(8,128)(2,1)} %collective-permute-done.11.refs_1_.refs_8_.refs_7_), channel_id=1, source_target_pairs={{0,1},{1,0},{2,3},{3,2},{4,5},{5,4},{6,7},{7,6},{8,9},{9,8},{10,11... | collective-permute-start | bytes 2359304 | tf_op jit(solution)/shard_map/ppermute | solution.py:556
  193.8 19.6 %collective-permute-start.27 = (bf16[256,1536]{1,0:T(8,128)(2,1)}, bf16[256,1536]{1,0:T(8,128)(2,1)}, u32[]{:S(2)}, u32[]{:S(2)}) collective-permute-start(bf16[256,1536]{1,0:T(8,128)(2,1)} %collective-permute-done.12.refs_2_.refs_9_.refs_8_), channel_id=1, source_target_pairs={{0,1},{1,0},{2,3},{3,2},{4,5},{5,4},{6,7},{7,6},{8,9},{9,8},{10,11... | collective-permute-start | bytes 2359304 | tf_op jit(solution)/shard_map/ppermute | solution.py:556
  254.4 149.8 %all-gather.20.cloned.1.call-start = ((), (), s32[]{:S(2)}) async-start(), calls=%async_computation.10 | async-start | bytes 2949120 | tf_op jit(solution)/shard_map/all_gather | solution.py:890
  258.5 43.8 %collective-permute-start.30 = (bf16[512,1664]{1,0:T(8,128)(2,1)}, bf16[512,1664]{1,0:T(8,128)(2,1)S(1)}, u32[]{:S(2)}, u32[]{:S(2)}) collective-permute-start(bf16[512,1664]{1,0:T(8,128)(2,1)} %concatenate.76.refs_4_.refs_3_), channel_id=1, source_target_pairs={{0,2},{1,3},{2,0},{3,1},{4,6},{5,7},{6,4},{7,5},{8,10},{9,11},{10,... | collective-permute-start | bytes 5111816 | tf_op jit(solution)/shard_map/ppermute | solution.py:556
  258.9 43.4 %collective-permute-start.31 = (bf16[512,1664]{1,0:T(8,128)(2,1)}, bf16[512,1664]{1,0:T(8,128)(2,1)}, u32[]{:S(2)}, u32[]{:S(2)}) collective-permute-start(bf16[512,1664]{1,0:T(8,128)(2,1)} %concatenate.76.refs_4_.refs_3_), channel_id=1, source_target_pairs={{0,4},{1,5},{2,6},{3,7},{4,0},{5,1},{6,2},{7,3},{8,12},{9,13},{10,... | collective-permute-start | bytes 5111816 | tf_op jit(solution)/shard_map/ppermute | solution.py:556
  306.3 33.7 %collective-permute-start.32 = (bf16[512,1664]{1,0:T(8,128)(2,1)}, bf16[512,1664]{1,0:T(8,128)(2,1)}, u32[]{:S(2)}, u32[]{:S(2)}) collective-permute-start(bf16[512,1664]{1,0:T(8,128)(2,1)} %get-tuple-element.118.refs_4_.refs_3_), channel_id=1, source_target_pairs={{0,1},{1,0},{2,3},{3,2},{4,5},{5,4},{6,7},{7,6},{8,9},{9,8},{10,11... | collective-permute-start | bytes 5111816 | tf_op jit(solution)/shard_map/ppermute | solution.py:556
  307.9 30.4 %collective-permute-start.34 = (bf16[256,1664]{1,0:T(8,128)(2,1)S(1)}, bf16[256,1664]{1,0:T(8,128)(2,1)S(1)}, u32[]{:S(2)}, u32[]{:S(2)}) collective-permute-start(bf16[256,1664]{1,0:T(8,128)(2,1)S(1)} %slice.269), channel_id=1, source_target_pairs={{0,2},{1,3},{2,0},{3,1},{4,6},{5,7},{6,4},{7,5},{8,10},{9,11},{10,... | collective-permute-start | bytes 2555912 | tf_op jit(solution)/shard_map/ppermute | solution.py:556
  309.5 28.8 %collective-permute-start.35 = (bf16[256,1664]{1,0:T(8,128)(2,1)S(1)}, bf16[256,1664]{1,0:T(8,128)(2,1)S(1)}, u32[]{:S(2)}, u32[]{:S(2)}) collective-permute-start(bf16[256,1664]{1,0:T(8,128)(2,1)S(1)} %slice.270), channel_id=1, source_target_pairs={{0,4},{1,5},{2,6},{3,7},{4,0},{5,1},{6,2},{7,3},{8,12},{9,13},{10,... | collective-permute-start | bytes 2555912 | tf_op jit(solution)/shard_map/ppermute | solution.py:556
  311.0 179.1 %reduce-scatter.3.cloned.1.call-start = ((), (), s32[]{:S(2)}) async-start(), calls=%async_computation.4 | async-start | bytes 2007040 | tf_op jit(solution)/shard_map/reduce_scatter | solution.py:1094
  339.5 27.7 %collective-permute-start.36 = (bf16[256,1664]{1,0:T(8,128)(2,1)}, bf16[256,1664]{1,0:T(8,128)(2,1)S(1)}, u32[]{:S(2)}, u32[]{:S(2)}) collective-permute-start(bf16[256,1664]{1,0:T(8,128)(2,1)} %get-tuple-element.136.refs_4_.refs_3_), channel_id=1, source_target_pairs={{0,1},{1,0},{2,3},{3,2},{4,5},{5,4},{6,7},{7,6},{8,9},{9,8},{10,11... | collective-permute-start | bytes 2555912 | tf_op jit(solution)/shard_map/ppermute | solution.py:556
  339.5 27.8 %collective-permute-start.37 = (bf16[256,1664]{1,0:T(8,128)(2,1)}, bf16[256,1664]{1,0:T(8,128)(2,1)S(1)}, u32[]{:S(2)}, u32[]{:S(2)}) collective-permute-start(bf16[256,1664]{1,0:T(8,128)(2,1)} %get-tuple-element.137.refs_5_.refs_4_), channel_id=1, source_target_pairs={{0,1},{1,0},{2,3},{3,2},{4,5},{5,4},{6,7},{7,6},{8,9},{9,8},{10,11... | collective-permute-start | bytes 2555912 | tf_op jit(solution)/shard_map/ppermute | solution.py:556
  455.3 166.6 %reduce-scatter.5.cloned.1.call-start = ((), (), s32[]{:S(2)}) async-start(), calls=%async_computation.5 | async-start | bytes 1966080 | tf_op jit(solution)/shard_map/reduce_scatter | solution.py:1094
  456.7 33.4 %collective-permute-start.40 = (bf16[272,1664]{1,0:T(8,128)(2,1)}, bf16[272,1664]{1,0:T(8,128)(2,1)S(1)}, u32[]{:S(2)}, u32[]{:S(2)}) collective-permute-start(bf16[272,1664]{1,0:T(8,128)(2,1)} %get-tuple-element.250), channel_id=1, source_target_pairs={{0,4},{1,5},{2,6},{3,7},{4,0},{5,1},{6,2},{7,3},{8,12},{9,13},{10,... | collective-permute-start | bytes 2715656 | tf_op jit(solution)/shard_map/ppermute | solution.py:556
  458.2 31.9 %collective-permute-start.41 = (bf16[272,1664]{1,0:T(8,128)(2,1)}, bf16[272,1664]{1,0:T(8,128)(2,1)S(1)}, u32[]{:S(2)}, u32[]{:S(2)}) collective-permute-start(bf16[272,1664]{1,0:T(8,128)(2,1)} %get-tuple-element.249), channel_id=1, source_target_pairs={{0,2},{1,3},{2,0},{3,1},{4,6},{5,7},{6,4},{7,5},{8,10},{9,11},{10,... | collective-permute-start | bytes 2715656 | tf_op jit(solution)/shard_map/ppermute | solution.py:556
  495.6 41.3 %collective-permute-start.43 = (bf16[544,1664]{1,0:T(8,128)(2,1)}, bf16[544,1664]{1,0:T(8,128)(2,1)S(1)}, u32[]{:S(2)}, u32[]{:S(2)}) collective-permute-start(bf16[544,1664]{1,0:T(8,128)(2,1)} %pad_maximum_fusion.refs_14_), channel_id=1, source_target_pairs={{0,2},{1,3},{2,0},{3,1},{4,6},{5,7},{6,4},{7,5},{8,10},{9,11},{10,... | collective-permute-start | bytes 5431304 | tf_op jit(solution)/shard_map/ppermute | solution.py:556
  500.4 41.1 %collective-permute-start.44 = (bf16[544,1664]{1,0:T(8,128)(2,1)}, bf16[544,1664]{1,0:T(8,128)(2,1)}, u32[]{:S(2)}, u32[]{:S(2)}) collective-permute-start(bf16[544,1664]{1,0:T(8,128)(2,1)} %pad_maximum_fusion.1.refs_15_), channel_id=1, source_target_pairs={{0,4},{1,5},{2,6},{3,7},{4,0},{5,1},{6,2},{7,3},{8,12},{9,13},{10,... | collective-permute-start | bytes 5431304 | tf_op jit(solution)/shard_map/ppermute | solution.py:556
  545.2 152.1 %collective-permute-start.45 = (bf16[512,1536]{1,0:T(8,128)(2,1)}, bf16[512,1536]{1,0:T(8,128)(2,1)}, u32[]{:S(2)}, u32[]{:S(2)}) collective-permute-start(bf16[512,1536]{1,0:T(8,128)(2,1)} %get-tuple-element.167), channel_id=1, source_target_pairs={{0,1},{1,0},{2,3},{3,2},{4,5},{5,4},{6,7},{7,6},{8,9},{9,8},{10,11... | collective-permute-start | bytes 4718600 | tf_op jit(solution)/shard_map/ppermute | solution.py:556
  549.0 65.6 %collective-permute-start.48 = (bf16[256,1536]{1,0:T(8,128)(2,1)}, bf16[256,1536]{1,0:T(8,128)(2,1)}, u32[]{:S(2)}, u32[]{:S(2)}) collective-permute-start(bf16[256,1536]{1,0:T(8,128)(2,1)} %get-tuple-element.251), channel_id=1, source_target_pairs={{0,4},{1,5},{2,6},{3,7},{4,0},{5,1},{6,2},{7,3},{8,12},{9,13},{10,... | collective-permute-start | bytes 2359304 | tf_op jit(solution)/shard_map/ppermute | solution.py:556
  552.3 65.0 %collective-permute-start.51 = (bf16[256,1536]{1,0:T(8,128)(2,1)}, bf16[256,1536]{1,0:T(8,128)(2,1)}, u32[]{:S(2)}, u32[]{:S(2)}) collective-permute-start(bf16[256,1536]{1,0:T(8,128)(2,1)} %get-tuple-element.252), channel_id=1, source_target_pairs={{0,2},{1,3},{2,0},{3,1},{4,6},{5,7},{6,4},{7,5},{8,10},{9,11},{10,... | collective-permute-start | bytes 2359304 | tf_op jit(solution)/shard_map/ppermute | solution.py:556
  609.2 27.6 %collective-permute-start.54 = (bf16[512,1024]{1,0:T(8,128)(2,1)}, bf16[512,1024]{1,0:T(8,128)(2,1)S(1)}, u32[]{:S(2)}, u32[]{:S(2)}) collective-permute-start(bf16[512,1024]{1,0:T(8,128)(2,1)} %slice.285), channel_id=1, source_target_pairs={{8,0},{16,8},{24,16},{9,1},{17,9},{25,17},{10,2},{18,10},{26,18},{... | collective-permute-start | bytes 3145736 | tf_op jit(solution)/shard_map/ppermute | solution.py:1136
  616.1 81.2 %collective-permute-start.49 = (bf16[512,1536]{1,0:T(8,128)(2,1)S(1)}, bf16[512,1536]{1,0:T(8,128)(2,1)}, u32[]{:S(2)}, u32[]{:S(2)}) collective-permute-start(bf16[512,1536]{1,0:T(8,128)(2,1)S(1)} %pad_maximum_fusion.2.refs_1_), channel_id=1, source_target_pairs={{0,2},{1,3},{2,0},{3,1},{4,6},{5,7},{6,4},{7,5},{8,10},{9,11},{10,... | collective-permute-start | bytes 4718600 | tf_op jit(solution)/shard_map/ppermute | solution.py:556
  620.6 76.7 %collective-permute-start.52 = (bf16[512,1536]{1,0:T(8,128)(2,1)}, bf16[512,1536]{1,0:T(8,128)(2,1)}, u32[]{:S(2)}, u32[]{:S(2)}) collective-permute-start(bf16[512,1536]{1,0:T(8,128)(2,1)} %pad_maximum_fusion.3.refs_2_), channel_id=1, source_target_pairs={{0,4},{1,5},{2,6},{3,7},{4,0},{5,1},{6,2},{7,3},{8,12},{9,13},{10,... | collective-permute-start | bytes 4718600 | tf_op jit(solution)/shard_map/ppermute | solution.py:556
  643.0 26.9 %collective-permute-start.55 = (bf16[512,1024]{1,0:T(8,128)(2,1)}, bf16[512,1024]{1,0:T(8,128)(2,1)}, u32[]{:S(2)}, u32[]{:S(2)}) collective-permute-start(bf16[512,1024]{1,0:T(8,128)(2,1)} %tie.30), channel_id=1, source_target_pairs={{8,0},{16,8},{24,16},{9,1},{17,9},{25,17},{10,2},{18,10},{26,18},{... | collective-permute-start | bytes 3145736 | tf_op jit(solution)/shard_map/ppermute | solution.py:1136
  687.0 21.8 %all-to-all-start.1 = ((bf16[32,80,128]{2,1,0:T(8,128)(2,1)}), bf16[32,80,128]{2,1,0:T(8,128)(2,1)}, u32[]{:S(2)}, u32[]{:S(2)}) async-start(bf16[32,80,128]{2,1,0:T(8,128)(2,1)} %pad_maximum_fusion.9), calls=%async_computation.2 | async-start | bytes 1310720 | tf_op jit(solution)/shard_map/all_to_all | solution.py:1170
  (112 other events, 910.1 us)
Sparse Core Ops, SparseCore 0:
  40.1 34.0 all-gather.11
  75.7 65.9 all-gather.13
  188.3 88.3 all-gather.17
  278.1 74.8 all-gather.15
  355.0 49.0 all-gather.19
  455.4 34.6 reduce-scatter.2
  544.6 34.2 reduce-scatter.4

commit v6 on v5

--- a/solution.py
+++ b/solution.py
@@ -643,9 +643,9 @@
 
 
 def turn_kernel(
-    own, other, from_x, from_y, hidden, gates, first_gu, router, gain, grad_out, second_o, out_w, first_o,
-    grad_mid_out, grad_mid_b_out, glow_out, glow_sgu, low_sdown, grad_attn, units_out
+    waits, own, other, from_x, from_y, hidden, gates, first_gu, router, gain, grad_out, second_o, out_w, first_o, *rest
 ):
+    grad_mid_out, grad_mid_b_out, glow_out, glow_sgu, low_sdown, grad_attn, units_out = rest[waits:]
     rows, model = hidden.shape
     experts = gates.shape[1]
     rank = ADAPTER_RANK
@@ -659,9 +659,9 @@
     gate = gates[...]
     grad_logits = gate * (grad_gates - jnp.sum(gate * grad_gates, axis=-1, keepdims=True))
     logits_hi = grad_logits.astype(BF16)
-    rest = grad_logits - logits_hi.astype(F32)
-    logits_mid = rest.astype(BF16)
-    logits_lo = (rest - logits_mid.astype(F32)).astype(BF16)
+    left = grad_logits - logits_hi.astype(F32)
+    logits_mid = left.astype(BF16)
+    logits_lo = (left - logits_mid.astype(F32)).astype(BF16)
     grad_normed = total[:rows, :model] + dot_nt(glow, first_gu[...])
     for part in (logits_hi, logits_mid, logits_lo):
         grad_normed = grad_normed + dot_nt(part, router[...])
@@ -678,7 +678,7 @@
     grad_attn[...] = (dot_nt(grad_mid_b, out_w[...]) + dot_nt(glow, first_o[...])).astype(BF16)
 
 
-def turn(args):
+def turn(args, deps):
     rows, model = args[4].shape
     rank = ADAPTER_RANK
     vmem = pl.BlockSpec(memory_space=pltpu.VMEM)
@@ -692,14 +692,14 @@
         ((BACK_ROWS, args[0].shape[1]), F32),
     ]
     return pl.pallas_call(
-        turn_kernel,
-        in_specs=[vmem] * len(args),
+        functools.partial(turn_kernel, len(deps)),
+        in_specs=[vmem] * len(args) + [pl.BlockSpec(memory_space=pl.ANY)] * len(deps),
         out_specs=[vmem] * len(shapes),
         out_shape=[jax.ShapeDtypeStruct(shape, dtype) for shape, dtype in shapes],
         compiler_params=pltpu.CompilerParams(vmem_limit_bytes=VMEM_LIMIT),
         cost_estimate=cost(4.0),
         name="turn",
-    )(*args)
+    )(*args, *deps)
 
 
 def query_back_kernel(waits, grad_q, normed, low_q, q_w, first_q, second_q, *rest):
@@ -1099,10 +1099,10 @@
     args = weights_of(j)
     run_expert(j, args, (6, 7), prior, (back_parts[6],) if prior else ())
     pair_six = add(back_parts[6], swap(back_parts[7], 1, size))
-    run_expert(j, args, (2, 3), prior, (pair_six,))
+    run_expert(j, args, (2, 3), prior, (back_parts[6],))
     from_diagonal_x, from_diagonal_y = swap(pair_six[:half], 2, size), swap(pair_six[half:], 4, size)
     pair_two = add(back_parts[2], swap(back_parts[3], 1, size))
-    run_expert(j, args, (4, 5), prior, (pair_two,))
+    run_expert(j, args, (4, 5), prior, (back_parts[2], pair_six))
     pair_four = add(back_parts[4], swap(tie(back_parts[5], from_diagonal_x, from_diagonal_y, *packed_sums), 1, size))
     to_x = jnp.concatenate([pair_two[:half], add(pair_two[half:], from_diagonal_y)], axis=0)
     to_y = jnp.concatenate([add(pair_four[:half], from_diagonal_x), pair_four[half:]], axis=0)
@@ -1110,8 +1110,9 @@
     packed_sums.append(scatter(grad_sums[-1][0]))
     from_x, from_y = swap(to_x, 2, size), swap(to_y, 4, size)
     grad_mid, grad_mid_b, glow_out, glow_sgu, low_sdown, grad_attn, shared_units = turn(
-        [back_parts[0], swap(tie(back_parts[1], from_x, from_y), 1, size), from_x, from_y, mid, gates, first_gu]
-        + [router_w, gains[1:2], grad_out_b, b_parts[3], out_w, first_o]
+        [back_parts[0], swap(back_parts[1], 1, size), from_x, from_y, mid, gates, first_gu]
+        + [router_w, gains[1:2], grad_out_b, b_parts[3], out_w, first_o],
+        (swap(tie(gates_lo[:16], from_x, from_y), 1, size),),
     )
 
     half = rows // 2

time: 730 us -> 724 us (level)
    ppermute x52 -> x53, waiting for transfers between devices: 56.1 us -> 70.5 us  [swap(): return lax.ppermute(array, 'dp', [(i, i ^ bit) for i in range(size)])]
    ppermute x2, waiting for transfers between devices: 21.9 us -> 10.9 us  [per_device(): received = lax.ppermute(moving, 'seq', backward)]
    ppermute x52 -> x53, starting transfers between devices: 37.7 us -> 34.2 us  [swap(): return lax.ppermute(array, 'dp', [(i, i ^ bit) for i in range(size)])]
    unnamed x196 -> x198, local copies, waits for them, and re-layouts: 34 us -> 37 us
  transfers between devices with their start and end apart: 65 -> 66, of which waited for: 16 -> 15; matrix products, arithmetic and copies ran while one was open for 17% -> 17% of each run, Pallas kernels for 38% -> 44%
where the time goes in v6:
time: 724 us; the launch traced here: 716 us
  Pallas kernels  317 us (44%)
  waiting for transfers between devices  154 us (21%)
  local copies, waits for them, and re-layouts  82.3 us (11%)
  starting transfers between devices  54.9 us (8%)
  other arithmetic  47.5 us (7%)
  matrix products  22.9 us (3%)
  blocking collectives  20.3 us (3%)
  between operations  16.6 us (2%)
    pallas_call x8, Pallas kernels, expert_call(): pl.pallas_call(functools.partial(expert_kernel, *(count, splits, experts,...  197 us
    ppermute x53, waiting for transfers between devices, swap(): return lax.ppermute(array, 'dp', [(i, i ^ bit) for i in range(size)])  70.5 us
    unnamed x198, local copies, waits for them, and re-layouts  37 us
    ppermute x2, waiting for transfers between devices, per_device(): kv_blocks.append(lax.ppermute(block, 'seq', forward))  35.4 us
    ppermute x53, starting transfers between devices, swap(): return lax.ppermute(array, 'dp', [(i, i ^ bit) for i in range(size)])  34.2 us
    pallas_call x1, Pallas kernels, attend_back(): pl.pallas_call(functools.partial(attend_back_kernel, spans, hops * rows,...  33.3 us
    all_gather x5, waiting for transfers between devices, over_seq(): return lax.all_gather(shard, 'seq', axis=0)  24.3 us
    pallas_call x1, Pallas kernels, attend(): pl.pallas_call(functools.partial(attend_kernel, spans, hops * rows, len(d...  23.7 us
  transfers between devices with their start and end apart: 66, of which 15 were waited for; matrix products, arithmetic and copies ran while one was open for 17% of the time, Pallas kernels for 44%

profile of v6, /device:TPU:0, one launch (start us, length us, event | category | flops | bytes accessed | tf_op | source)
XLA Modules:
  0.0 715.8 jit_solution(7446556170919196625)
XLA Ops:
  7.2 3.0 collective-permute-start
  15.1 3.4 all-to-all-start
  19.6 20.3 %all-gather = bf16[192,2048]{1,0:T(8,128)(2,1)} all-gather(bf16[48,2048]{1,0:T(8,128)(2,1)S(1)} %fusion.14), channel_id=2, replica_groups=mesh['seq'=4,'dp'=8] {'seq'}, dimensions={0}, use_global_device_ids=true | all-gather | bytes 983040 | tf_op jit(solution)/shard_map/all_gather | solution.py:890
  42.5 5.9 all-to-all-done.refs_3_
  51.1 17.2 %collective-permute-done.3.refs_2_ = bf16[4,48,2048]{2,1,0:T(8,128)(2,1)S(1)} collective-permute-done((bf16[4,48,2048]{2,1,0:T(8,128)(2,1)}, bf16[4,48,2048]{2,1,0:T(8,128)(2,1)S(1)}, u32[]{:S(2)}, u32[]{:S(2)}) %collective-permute-start.3) | collective-permute-done | bytes 786464 | tf_op jit(solution)/shard_map/ppermute | solution.py:556
  74.1 5.1 collective-permute-done.8.refs_7_.refs_3_
  88.0 5.6 assemble.2
  95.9 3.5 constant_dynamic-slice_fusion.7
  105.5 2.9 fusion.5
  114.5 4.5 collective-permute-start.22
  119.8 35.4 %collective-permute-done.22.refs_0_ = bf16[512,1152]{1,0:T(8,128)(2,1)} collective-permute-done((bf16[512,1152]{1,0:T(8,128)(2,1)}, bf16[512,1152]{1,0:T(8,128)(2,1)}, u32[]{:S(2)}, u32[]{:S(2)}) %collective-permute-start.22) | collective-permute-done | bytes 1179680 | tf_op jit(solution)/shard_map/ppermute | solution.py:984
  155.2 5.6 collective-permute-start.23
  160.8 2.5 fusion.44
  174.2 7.1 collective-permute-done.18.refs_6_
  183.4 3.8 collective-permute-done.19.refs_7_
  193.9 9.4 %assemble.3 = (bf16[4,8,1,48,1536]{4,3,2,1,0:T(8,128)(2,1)}, bf16[4,8,1,48,512]{4,3,2,1,0:T(8,128)(2,1)}, bf16[4,8,1,48,1536]{4,3,2,1,0:T(8,128)(2,1)}) custom-call(s32[1]{0:T(128)} %bitcast.1.me_ref, bf16[4,48,3584]{2,1,0:T(8,128)(2,1)} %tie.19.refs_0_, bf16[4,48,3584]{2,1,0:T(8,128)(2,1)} %collective-permute-done.13.refs_1_, ...), custom_call_target="tpu_custom_call" | custom-call | tf_op jit(solution)/shard_map/assemble/pallas_call | solution.py:629
  203.3 2.4 fusion.43
  209.0 3.8 fusion.4.q_ref
  213.1 23.7 %attend.1 = (bf16[512,1536]{1,0:T(8,128)(2,1)}, f32[4,3,512]{2,1,0:T(4,128)}) custom-call(bf16[512,1536]{1,0:T(8,128)(2,1)} %fusion.4.q_ref, bf16[1536,1152]{1,0:T(8,128)(2,1)} %copy-done.21, bf16[1536,1152]{1,0:T(8,128)(2,1)} %copy-done.21, f32[1,512]{1,0:T(1,128)} %add_convert_fusion.14.qt_ref, f32[1536,1]{1,0:T(8,128)} %slice_convert_fusion.kt_ref, ...), custom_call_target="tpu_custom_call" | custom-call | flops 26530500608 | bytes 1000000 | tf_op jit(solution)/shard_map/attend/pallas_call | solution.py:96
  240.3 4.8 multiply_reduce_fusion
  260.1 16.6 %all-gather.18.cloned.1.call-done.refs_1_ = bf16[1536,1536]{1,0:T(8,128)(2,1)} async-done(((bf16[384,1536]{1,0:T(8,128)(2,1)}), bf16[1536,1536]{1,0:T(8,128)(2,1)}) %all-gather.18.cloned.1.call-update) | async-done | bytes 4718608 | tf_op jit(solution)/shard_map/all_gather | solution.py:890
  276.7 25.4 %expert.8 = (bf16[512,1536]{1,0:T(8,128)(2,1)}, bf16[512,1536]{1,0:T(8,128)(2,1)}, bf16[544,1664]{1,0:T(8,128)(2,1)}, bf16[544,1664]{1,0:T(8,128)(2,1)}, f32[153...) custom-call(s32[2]{0:T(128)} %pad_add_fusion.1.refs_0_, ...), custom_call_target="tpu_custom_call" | custom-call | flops 27683999744 | bytes 1000000 | tf_op jit(solution)/shard_map/expert/pallas_call | solution.py:522
  310.7 27.5 %expert.9 = (bf16[512,1536]{1,0:T(8,128)(2,1)}, bf16[512,1536]{1,0:T(8,128)(2,1)}, bf16[544,1664]{1,0:T(8,128)(2,1)}, bf16[544,1664]{1,0:T(8,128)(2,1)}, f32[153...) custom-call(s32[2]{0:T(128)} %pad_add_fusion.1.refs_0_, ...), custom_call_target="tpu_custom_call" | custom-call | flops 27683999744 | bytes 1000000 | tf_op jit(solution)/shard_map/expert/pallas_call | solution.py:522
  340.0 27.2 %expert.10 = (bf16[512,1536]{1,0:T(8,128)(2,1)}, bf16[512,1536]{1,0:T(8,128)(2,1)}, bf16[544,1664]{1,0:T(8,128)(2,1)}, bf16[544,1664]{1,0:T(8,128)(2,1)}, f32[15...) custom-call(s32[2]{0:T(128)} %pad_add_fusion.1.refs_0_, ...), custom_call_target="tpu_custom_call" | custom-call | flops 27683999744 | bytes 1000000 | tf_op jit(solution)/shard_map/expert/pallas_call | solution.py:522
  368.3 27.9 %expert.11 = (bf16[512,1536]{1,0:T(8,128)(2,1)}, bf16[512,1536]{1,0:T(8,128)(2,1)}, bf16[544,1664]{1,0:T(8,128)(2,1)}, bf16[544,1664]{1,0:T(8,128)(2,1)}, bf16[4,1568,128]{2,1,0:T(8,128)(2,1)}) custom-call(s32[2]{0:T(128)} %pad_add_fusion.1.refs_0_, bf16[1536,1536]{1,0:T(8,128)(2,1)} %all-gather.18.cloned.1.call-done.refs_1_, ...), custom_call_target="tpu_custom_call" | custom-call | flops 27683999744 | bytes 1000000 | tf_op jit(solution)/shard_map/expert/pallas_call | solution.py:522
  396.4 7.7 %all-gather.20.cloned.1.call-done = bf16[512,2304]{1,0:T(8,128)(2,1)} async-done(((bf16[128,2304]{1,0:T(8,128)(2,1)}), bf16[512,2304]{1,0:T(8,128)(2,1)}) %all-gather.20.cloned.1.call-update) | async-done | bytes 2359312 | tf_op jit(solution)/shard_map/all_gather | solution.py:890
  404.1 20.9 %expert.12 = (bf16[512,1536]{1,0:T(8,128)(2,1)}, bf16[512,1536]{1,0:T(8,128)(2,1)}, bf16[544,1664]{1,0:T(8,128)(2,1)}, bf16[544,1664]{1,0:T(8,128)(2,1)}, f32[15...) custom-call(s32[2]{0:T(128)} %pad_add_fusion.refs_0_, ...), custom_call_target="tpu_custom_call" | custom-call | flops 27683999744 | bytes 1000000 | tf_op jit(solution)/shard_map/expert/pallas_call | solution.py:522
  425.1 22.7 %expert.13 = (bf16[512,1536]{1,0:T(8,128)(2,1)}, bf16[512,1536]{1,0:T(8,128)(2,1)}, bf16[544,1664]{1,0:T(8,128)(2,1)}, bf16[544,1664]{1,0:T(8,128)(2,1)}, f32[15...) custom-call(s32[2]{0:T(128)} %pad_add_fusion.refs_0_, ...), custom_call_target="tpu_custom_call" | custom-call | flops 27683999744 | bytes 1000000 | tf_op jit(solution)/shard_map/expert/pallas_call | solution.py:522
  455.0 22.6 %expert.14 = (bf16[512,1536]{1,0:T(8,128)(2,1)}, bf16[512,1536]{1,0:T(8,128)(2,1)}, bf16[544,1664]{1,0:T(8,128)(2,1)}, bf16[544,1664]{1,0:T(8,128)(2,1)}, f32[15...) custom-call(s32[2]{0:T(128)} %pad_add_fusion.refs_0_, ...), custom_call_target="tpu_custom_call" | custom-call | flops 27683999744 | bytes 1000000 | tf_op jit(solution)/shard_map/expert/pallas_call | solution.py:522
  478.9 2.5 add_convert_fusion.1
  488.7 23.2 %expert.15 = (bf16[512,1536]{1,0:T(8,128)(2,1)}, bf16[512,1536]{1,0:T(8,128)(2,1)}, bf16[544,1664]{1,0:T(8,128)(2,1)}, bf16[544,1664]{1,0:T(8,128)(2,1)}, bf16[4,1536,128]{2,1,0:T(8,128)(2,1)}) custom-call(s32[2]{0:T(128)} %pad_add_fusion.refs_0_, bf16[1536,1280]{1,0:T(8,128)(2,1)} %all-gather.16.cloned.1.call-done.refs_1_, bf16[4,128,2304]{2,1,0:T(8,128)(2,1)} %bitcast.227, ...), custom_call_target="tpu_custom_call" | custom-call | flops 27683999744 | bytes 1000000 | tf_op jit(solution)/shard_map/expert/pallas_call | solution.py:522
  512.3 14.0 %collective-permute-done.43.refs_4_.refs_1_.from_x = bf16[544,1664]{1,0:T(8,128)(2,1)S(1)} collective-permute-done((bf16[544,1664]{1,0:T(8,128)(2,1)}, bf16[544,1664]{1,0:T(8,128)(2,1)S(1)}, u32[]{:S(2)}, u32[]{:S(2)}) %collective-permute-start.43) | collective-permute-done | bytes 1810464 | tf_op jit(solution)/shard_map/ppermute | solution.py:556
  526.3 4.1 collective-permute-done.44.refs_5_.refs_2_.from_y
  536.6 18.4 %turn.1 = (f32[512,1536]{1,0:T(8,128)}, bf16[512,1536]{1,0:T(8,128)(2,1)}, bf16[512,16]{1,0:T(8,128)(2,1)}, bf16[512,32]{1,0:T(8,128)(2,1)}, bf16[512,16]{1,0:T(...) custom-call(bf16[544,1664]{1,0:T(8,128)(2,1)} %get-tuple-element.174.own, ...), custom_call_target="tpu_custom_call" | custom-call | flops 4614000128 | bytes 1000000 | tf_op jit(solution)/shard_map/turn/pallas_call | solution.py:694
  567.9 33.3 %attend_back.1 = (bf16[512,1536]{1,0:T(8,128)(2,1)}, bf16[1536,1024]{1,0:T(8,128)(2,1)}) custom-call(bf16[512,1536]{1,0:T(8,128)(2,1)} %fusion.4.q_ref, bf16[1536,1152]{1,0:T(8,128)(2,1)} %copy-done.21, bf16[1536,1152]{1,0:T(8,128)(2,1)} %copy-done.21, bf16[512,1536]{1,0:T(8,128)(2,1)} %get-tuple-element.177.g_ref, f32[4,3,512]{2,1,0:T(4,128)} %get-tuple-element.178.lse_ref, ...), custom_call_target="tpu_custom_call" | custom-call | flops 9228000256 | bytes 1000000 | tf_op jit(solution)/shard_map/attend_back/pallas_call | solution.py:159
  601.3 2.4 slice.289
  608.6 16.8 %collective-permute-done.51 = bf16[256,1536]{1,0:T(8,128)(2,1)S(1)} collective-permute-done((bf16[256,1536]{1,0:T(8,128)(2,1)S(1)}, bf16[256,1536]{1,0:T(8,128)(2,1)S(1)}, u32[]{:S(2)}, u32[]{:S(2)}) %collective-permute-start.51) | collective-permute-done | bytes 786464 | tf_op jit(solution)/shard_map/ppermute | solution.py:556
  627.7 3.6 collective-permute-done.55.rest_0_.refs_2_
  635.0 2.5 add_convert_fusion.9.refs_0_
  639.0 5.2 middle.1
  647.4 9.7 %query_back.1 = (f32[512,1536]{1,0:T(8,128)}, f32[1536,16]{1,0:T(8,128)}, f32[16,1536]{1,0:T(8,128)}) custom-call(bf16[512,1536]{1,0:T(8,128)(2,1)} %get-tuple-element.181.grad_q, bf16[512,1536]{1,0:T(8,128)(2,1)} %copy-done.4, bf16[512,16]{1,0:T(8,128)(2,1)} %copy-done.53, bf16[1536,1536]{1,0:T(8,128)(2,1)} %bitcast.175, bf16[1536,16]{1,0:T(8,128)(2,1)} %copy-done.28, ...), custom_call_target="tpu_custom_call" | custom-call | flops 115350000 | bytes 1000000 | tf_op jit(solution)/shard_map/query_back/pallas_call | solution.py:717
  657.1 7.4 %collective-permute-done.56 = bf16[512,1024]{1,0:T(8,128)(2,1)} collective-permute-done((bf16[512,1024]{1,0:T(8,128)(2,1)}, bf16[512,1024]{1,0:T(8,128)(2,1)}, u32[]{:S(2)}, u32[]{:S(2)}) %collective-permute-start.56) | collective-permute-done | bytes 1048608 | tf_op jit(solution)/shard_map/ppermute | solution.py:1137
  664.5 2.9 add_convert_fusion.8.grad_kv
  667.4 12.0 %last.1 = (f32[512,1536]{1,0:T(8,128)}, bf16[1536,128]{1,0:T(8,128)(2,1)}, bf16[32,32,128]{2,1,0:T(8,128)(2,1)}) custom-call(bf16[512,1024]{1,0:T(8,128)(2,1)} %add_convert_fusion.8.grad_kv, bf16[512,1536]{1,0:T(8,128)(2,1)} %copy-done.4, bf16[512,32]{1,0:T(8,128)(2,1)} %copy-done.52, bf16[1536,1024]{1,0:T(8,128)(2,1)} %bitcast.185, ...), custom_call_target="tpu_custom_call" | custom-call | flops 2307000064 | bytes 1000000 | tf_op jit(solution)/shard_map/last/pallas_call | solution.py:788
  681.5 3.7 all-to-all-start.1
  691.6 4.6 fusion.7
  696.2 6.9 all-to-all-done.1.flat
  703.1 2.4 spread.1
  (459 shorter events, 155.3 us)
Async XLA Ops:
  7.2 41.2 %collective-permute-start = (bf16[512,1536]{1,0:T(8,128)(2,1)}, bf16[512,1536]{1,0:T(8,128)(2,1)}, u32[]{:S(2)}, u32[]{:S(2)}) collective-permute-start(bf16[512,1536]{1,0:T(8,128)(2,1)} %bitcast.160), channel_id=1, source_target_pairs={{0,2},{1,3},{2,0},{3,1},{4,6},{5,7},{6,4},{7,5},{8,10},{9,11},{10,... | collective-permute-start | bytes 4718600 | tf_op jit(solution)/shard_map/ppermute | solution.py:556
  10.2 38.2 %collective-permute-start.1 = (bf16[512,1536]{1,0:T(8,128)(2,1)}, bf16[512,1536]{1,0:T(8,128)(2,1)}, u32[]{:S(2)}, u32[]{:S(2)}) collective-permute-start(bf16[512,1536]{1,0:T(8,128)(2,1)} %bitcast.161), channel_id=1, source_target_pairs={{0,4},{1,5},{2,6},{3,7},{4,0},{5,1},{6,2},{7,3},{8,12},{9,13},{10,... | collective-permute-start | bytes 4718600 | tf_op jit(solution)/shard_map/ppermute | solution.py:556
  15.1 33.3 %all-to-all-start = ((bf16[8,48,256]{2,1,0:T(8,128)(2,1)}), bf16[8,48,256]{2,1,0:T(8,128)(2,1)S(1)}, u32[]{:S(2)}, u32[]{:S(2)}) async-start(bf16[8,48,256]{2,1,0:T(8,128)(2,1)} %copy.170), calls=%async_computation | async-start | bytes 393216 | tf_op jit(solution)/shard_map/all_to_all | solution.py:933
  18.5 89.9 %all-gather.12.cloned.1.call-start = ((), (), s32[]{:S(2)}) async-start(), calls=%async_computation.6 | async-start | bytes 1720320 | tf_op jit(solution)/shard_map/all_gather | solution.py:890
  40.0 115.2 %all-gather.14.cloned.1.call-start = ((), (), s32[]{:S(2)}) async-start(), calls=%async_computation.7 | async-start | bytes 3604480 | tf_op jit(solution)/shard_map/all_gather | solution.py:890
  49.1 19.2 %collective-permute-start.3 = (bf16[4,48,2048]{2,1,0:T(8,128)(2,1)}, bf16[4,48,2048]{2,1,0:T(8,128)(2,1)S(1)}, u32[]{:S(2)}, u32[]{:S(2)}) collective-permute-start(bf16[4,48,2048]{2,1,0:T(8,128)(2,1)} %tie.16.refs_0_), channel_id=1, source_target_pairs={{0,2},{1,3},{2,0},{3,1},{4,6},{5,7},{6,4},{7,5},{8,10},{9,11},{10,... | collective-permute-start | bytes 2359304 | tf_op jit(solution)/shard_map/ppermute | solution.py:556
  50.0 20.7 %collective-permute-start.5 = (bf16[4,48,2048]{2,1,0:T(8,128)(2,1)}, bf16[4,48,2048]{2,1,0:T(8,128)(2,1)S(1)}, u32[]{:S(2)}, u32[]{:S(2)}) collective-permute-start(bf16[4,48,2048]{2,1,0:T(8,128)(2,1)} %tie.16.refs_0_), channel_id=1, source_target_pairs={{0,4},{1,5},{2,6},{3,7},{4,0},{5,1},{6,2},{7,3},{8,12},{9,13},{10,... | collective-permute-start | bytes 2359304 | tf_op jit(solution)/shard_map/ppermute | solution.py:556
  72.8 203.8 %all-gather.18.cloned.1.call-start = ((), (), s32[]{:S(2)}) async-start(), calls=%async_computation.9 | async-start | bytes 5898240 | tf_op jit(solution)/shard_map/all_gather | solution.py:890
  86.7 21.7 %collective-permute-start.11 = (bf16[256,1536]{1,0:T(8,128)(2,1)}, bf16[256,1536]{1,0:T(8,128)(2,1)}, u32[]{:S(2)}, u32[]{:S(2)}) collective-permute-start(bf16[256,1536]{1,0:T(8,128)(2,1)} %slice.240), channel_id=1, source_target_pairs={{0,2},{1,3},{2,0},{3,1},{4,6},{5,7},{6,4},{7,5},{8,10},{9,11},{10,... | collective-permute-start | bytes 2359304 | tf_op jit(solution)/shard_map/ppermute | solution.py:556
  87.7 20.7 %collective-permute-start.12 = (bf16[256,1536]{1,0:T(8,128)(2,1)}, bf16[256,1536]{1,0:T(8,128)(2,1)}, u32[]{:S(2)}, u32[]{:S(2)}) collective-permute-start(bf16[256,1536]{1,0:T(8,128)(2,1)} %slice.241), channel_id=1, source_target_pairs={{0,4},{1,5},{2,6},{3,7},{4,0},{5,1},{6,2},{7,3},{8,12},{9,13},{10,... | collective-permute-start | bytes 2359304 | tf_op jit(solution)/shard_map/ppermute | solution.py:556
  108.4 46.8 %collective-permute-start.16 = (bf16[4,48,3584]{2,1,0:T(8,128)(2,1)}, bf16[4,48,3584]{2,1,0:T(8,128)(2,1)}, u32[]{:S(2)}, u32[]{:S(2)}) collective-permute-start(bf16[4,48,3584]{2,1,0:T(8,128)(2,1)} %tie.19.refs_0_), channel_id=1, source_target_pairs={{0,4},{1,5},{2,6},{3,7},{4,0},{5,1},{6,2},{7,3},{8,12},{9,13},{10,... | collective-permute-start | bytes 4128776 | tf_op jit(solution)/shard_map/ppermute | solution.py:556
  110.3 44.9 %collective-permute-start.14 = (bf16[4,48,3584]{2,1,0:T(8,128)(2,1)}, bf16[4,48,3584]{2,1,0:T(8,128)(2,1)}, u32[]{:S(2)}, u32[]{:S(2)}) collective-permute-start(bf16[4,48,3584]{2,1,0:T(8,128)(2,1)} %tie.19.refs_0_), channel_id=1, source_target_pairs={{0,2},{1,3},{2,0},{3,1},{4,6},{5,7},{6,4},{7,5},{8,10},{9,11},{10,... | collective-permute-start | bytes 4128776 | tf_op jit(solution)/shard_map/ppermute | solution.py:556
  114.5 40.7 %collective-permute-start.22 = (bf16[512,1152]{1,0:T(8,128)(2,1)}, bf16[512,1152]{1,0:T(8,128)(2,1)}, u32[]{:S(2)}, u32[]{:S(2)}) collective-permute-start(bf16[512,1152]{1,0:T(8,128)(2,1)} %pad_maximum_fusion.4), channel_id=1, source_target_pairs={{0,8},{8,16},{16,24},{1,9},{9,17},{17,25},{2,10},{10,18},{18,26},{... | collective-permute-start | bytes 3538952 | tf_op jit(solution)/shard_map/ppermute | solution.py:984
  155.2 32.0 %collective-permute-start.23 = (bf16[512,1152]{1,0:T(8,128)(2,1)}, bf16[512,1152]{1,0:T(8,128)(2,1)}, u32[]{:S(2)}, u32[]{:S(2)}) collective-permute-start(bf16[512,1152]{1,0:T(8,128)(2,1)} %tie.21), channel_id=1, source_target_pairs={{0,8},{8,16},{16,24},{1,9},{9,17},{17,25},{2,10},{10,18},{18,26},{... | collective-permute-start | bytes 3538952 | tf_op jit(solution)/shard_map/ppermute | solution.py:984
  173.7 19.7 %collective-permute-start.15 = (bf16[4,48,3584]{2,1,0:T(8,128)(2,1)}, bf16[4,48,3584]{2,1,0:T(8,128)(2,1)}, u32[]{:S(2)}, u32[]{:S(2)}) collective-permute-start(bf16[4,48,3584]{2,1,0:T(8,128)(2,1)} %collective-permute-done.14.refs_2_.refs_1_), channel_id=1, source_target_pairs={{0,1},{1,0},{2,3},{3,2},{4,5},{5,4},{6,7},{7,6},{8,9},{9,8},{10,11... | collective-permute-start | bytes 4128776 | tf_op jit(solution)/shard_map/ppermute | solution.py:556
  187.7 208.6 %all-gather.16.cloned.1.call-start = ((), (), s32[]{:S(2)}) async-start(), calls=%async_computation.8 | async-start | bytes 4915200 | tf_op jit(solution)/shard_map/all_gather | solution.py:890
  192.8 20.2 %collective-permute-start.24 = (bf16[512,1536]{1,0:T(8,128)(2,1)}, bf16[512,1536]{1,0:T(8,128)(2,1)}, u32[]{:S(2)}, u32[]{:S(2)}) collective-permute-start(bf16[512,1536]{1,0:T(8,128)(2,1)} %get-tuple-element.106.refs_6_.refs_5_), channel_id=1, source_target_pairs={{0,1},{1,0},{2,3},{3,2},{4,5},{5,4},{6,7},{7,6},{8,9},{9,8},{10,11... | collective-permute-start | bytes 4718600 | tf_op jit(solution)/shard_map/ppermute | solution.py:556
  192.8 20.2 %collective-permute-start.25 = (bf16[512,1536]{1,0:T(8,128)(2,1)}, bf16[512,1536]{1,0:T(8,128)(2,1)}, u32[]{:S(2)}, u32[]{:S(2)}) collective-permute-start(bf16[512,1536]{1,0:T(8,128)(2,1)} %get-tuple-element.105.refs_6_.refs_5_), channel_id=1, source_target_pairs={{0,1},{1,0},{2,3},{3,2},{4,5},{5,4},{6,7},{7,6},{8,9},{9,8},{10,11... | collective-permute-start | bytes 4718600 | tf_op jit(solution)/shard_map/ppermute | solution.py:556
  193.3 19.7 %collective-permute-start.26 = (bf16[256,1536]{1,0:T(8,128)(2,1)}, bf16[256,1536]{1,0:T(8,128)(2,1)}, u32[]{:S(2)}, u32[]{:S(2)}) collective-permute-start(bf16[256,1536]{1,0:T(8,128)(2,1)} %collective-permute-done.11.refs_1_.refs_8_.refs_7_), channel_id=1, source_target_pairs={{0,1},{1,0},{2,3},{3,2},{4,5},{5,4},{6,7},{7,6},{8,9},{9,8},{10,11... | collective-permute-start | bytes 2359304 | tf_op jit(solution)/shard_map/ppermute | solution.py:556
  193.4 19.6 %collective-permute-start.27 = (bf16[256,1536]{1,0:T(8,128)(2,1)}, bf16[256,1536]{1,0:T(8,128)(2,1)}, u32[]{:S(2)}, u32[]{:S(2)}) collective-permute-start(bf16[256,1536]{1,0:T(8,128)(2,1)} %collective-permute-done.12.refs_2_.refs_9_.refs_8_), channel_id=1, source_target_pairs={{0,1},{1,0},{2,3},{3,2},{4,5},{5,4},{6,7},{7,6},{8,9},{9,8},{10,11... | collective-permute-start | bytes 2359304 | tf_op jit(solution)/shard_map/ppermute | solution.py:556
  254.0 150.1 %all-gather.20.cloned.1.call-start = ((), (), s32[]{:S(2)}) async-start(), calls=%async_computation.10 | async-start | bytes 2949120 | tf_op jit(solution)/shard_map/all_gather | solution.py:890
  258.0 44.0 %collective-permute-start.30 = (bf16[512,1664]{1,0:T(8,128)(2,1)}, bf16[512,1664]{1,0:T(8,128)(2,1)S(1)}, u32[]{:S(2)}, u32[]{:S(2)}) collective-permute-start(bf16[512,1664]{1,0:T(8,128)(2,1)} %concatenate.76.refs_4_.refs_3_), channel_id=1, source_target_pairs={{0,2},{1,3},{2,0},{3,1},{4,6},{5,7},{6,4},{7,5},{8,10},{9,11},{10,... | collective-permute-start | bytes 5111816 | tf_op jit(solution)/shard_map/ppermute | solution.py:556
  258.3 43.8 %collective-permute-start.31 = (bf16[512,1664]{1,0:T(8,128)(2,1)}, bf16[512,1664]{1,0:T(8,128)(2,1)}, u32[]{:S(2)}, u32[]{:S(2)}) collective-permute-start(bf16[512,1664]{1,0:T(8,128)(2,1)} %concatenate.76.refs_4_.refs_3_), channel_id=1, source_target_pairs={{0,4},{1,5},{2,6},{3,7},{4,0},{5,1},{6,2},{7,3},{8,12},{9,13},{10,... | collective-permute-start | bytes 5111816 | tf_op jit(solution)/shard_map/ppermute | solution.py:556
  306.1 33.9 %collective-permute-start.32 = (bf16[512,1664]{1,0:T(8,128)(2,1)}, bf16[512,1664]{1,0:T(8,128)(2,1)}, u32[]{:S(2)}, u32[]{:S(2)}) collective-permute-start(bf16[512,1664]{1,0:T(8,128)(2,1)} %get-tuple-element.118.refs_4_.refs_3_), channel_id=1, source_target_pairs={{0,1},{1,0},{2,3},{3,2},{4,5},{5,4},{6,7},{7,6},{8,9},{9,8},{10,11... | collective-permute-start | bytes 5111816 | tf_op jit(solution)/shard_map/ppermute | solution.py:556
  307.6 30.6 %collective-permute-start.34 = (bf16[256,1664]{1,0:T(8,128)(2,1)S(1)}, bf16[256,1664]{1,0:T(8,128)(2,1)S(1)}, u32[]{:S(2)}, u32[]{:S(2)}) collective-permute-start(bf16[256,1664]{1,0:T(8,128)(2,1)S(1)} %slice.272), channel_id=1, source_target_pairs={{0,2},{1,3},{2,0},{3,1},{4,6},{5,7},{6,4},{7,5},{8,10},{9,11},{10,... | collective-permute-start | bytes 2555912 | tf_op jit(solution)/shard_map/ppermute | solution.py:556
  309.2 29.1 %collective-permute-start.35 = (bf16[256,1664]{1,0:T(8,128)(2,1)S(1)}, bf16[256,1664]{1,0:T(8,128)(2,1)S(1)}, u32[]{:S(2)}, u32[]{:S(2)}) collective-permute-start(bf16[256,1664]{1,0:T(8,128)(2,1)S(1)} %slice.273), channel_id=1, source_target_pairs={{0,4},{1,5},{2,6},{3,7},{4,0},{5,1},{6,2},{7,3},{8,12},{9,13},{10,... | collective-permute-start | bytes 2555912 | tf_op jit(solution)/shard_map/ppermute | solution.py:556
  310.7 167.0 %reduce-scatter.3.cloned.1.call-start = ((), (), s32[]{:S(2)}) async-start(), calls=%async_computation.4 | async-start | bytes 2007040 | tf_op jit(solution)/shard_map/reduce_scatter | solution.py:1094
  339.4 27.7 %collective-permute-start.36 = (bf16[256,1664]{1,0:T(8,128)(2,1)}, bf16[256,1664]{1,0:T(8,128)(2,1)S(1)}, u32[]{:S(2)}, u32[]{:S(2)}) collective-permute-start(bf16[256,1664]{1,0:T(8,128)(2,1)} %get-tuple-element.136.refs_4_.refs_3_), channel_id=1, source_target_pairs={{0,1},{1,0},{2,3},{3,2},{4,5},{5,4},{6,7},{7,6},{8,9},{9,8},{10,11... | collective-permute-start | bytes 2555912 | tf_op jit(solution)/shard_map/ppermute | solution.py:556
  339.4 27.7 %collective-permute-start.37 = (bf16[256,1664]{1,0:T(8,128)(2,1)}, bf16[256,1664]{1,0:T(8,128)(2,1)S(1)}, u32[]{:S(2)}, u32[]{:S(2)}) collective-permute-start(bf16[256,1664]{1,0:T(8,128)(2,1)} %get-tuple-element.137.refs_5_.refs_4_), channel_id=1, source_target_pairs={{0,1},{1,0},{2,3},{3,2},{4,5},{5,4},{6,7},{7,6},{8,9},{9,8},{10,11... | collective-permute-start | bytes 2555912 | tf_op jit(solution)/shard_map/ppermute | solution.py:556
  396.3 231.4 %reduce-scatter.5.cloned.1.call-start = ((), (), s32[]{:S(2)}) async-start(), calls=%async_computation.5 | async-start | bytes 1966080 | tf_op jit(solution)/shard_map/reduce_scatter | solution.py:1094
  425.0 23.3 %collective-permute-start.38 = (bf16[544,1664]{1,0:T(8,128)(2,1)}, bf16[544,1664]{1,0:T(8,128)(2,1)}, u32[]{:S(2)}, u32[]{:S(2)}) collective-permute-start(bf16[544,1664]{1,0:T(8,128)(2,1)} %get-tuple-element.154), channel_id=1, source_target_pairs={{0,1},{1,0},{2,3},{3,2},{4,5},{5,4},{6,7},{7,6},{8,9},{9,8},{10,11... | collective-permute-start | bytes 5431304 | tf_op jit(solution)/shard_map/ppermute | solution.py:556
  447.9 31.1 %collective-permute-start.39 = (bf16[544,1664]{1,0:T(8,128)(2,1)}, bf16[544,1664]{1,0:T(8,128)(2,1)}, u32[]{:S(2)}, u32[]{:S(2)}) collective-permute-start(bf16[544,1664]{1,0:T(8,128)(2,1)} %get-tuple-element.158), channel_id=1, source_target_pairs={{0,1},{1,0},{2,3},{3,2},{4,5},{5,4},{6,7},{7,6},{8,9},{9,8},{10,11... | collective-permute-start | bytes 5431304 | tf_op jit(solution)/shard_map/ppermute | solution.py:556
  452.1 25.6 %collective-permute-start.40 = (bf16[272,1664]{1,0:T(8,128)(2,1)}, bf16[272,1664]{1,0:T(8,128)(2,1)S(1)}, u32[]{:S(2)}, u32[]{:S(2)}) collective-permute-start(bf16[272,1664]{1,0:T(8,128)(2,1)} %get-tuple-element.250), channel_id=1, source_target_pairs={{0,4},{1,5},{2,6},{3,7},{4,0},{5,1},{6,2},{7,3},{8,12},{9,13},{10,... | collective-permute-start | bytes 2715656 | tf_op jit(solution)/shard_map/ppermute | solution.py:556
  453.6 24.2 %collective-permute-start.41 = (bf16[272,1664]{1,0:T(8,128)(2,1)}, bf16[272,1664]{1,0:T(8,128)(2,1)S(1)}, u32[]{:S(2)}, u32[]{:S(2)}) collective-permute-start(bf16[272,1664]{1,0:T(8,128)(2,1)} %get-tuple-element.249), channel_id=1, source_target_pairs={{0,2},{1,3},{2,0},{3,1},{4,6},{5,7},{6,4},{7,5},{8,10},{9,11},{10,... | collective-permute-start | bytes 2715656 | tf_op jit(solution)/shard_map/ppermute | solution.py:556
  484.2 42.1 %collective-permute-start.43 = (bf16[544,1664]{1,0:T(8,128)(2,1)}, bf16[544,1664]{1,0:T(8,128)(2,1)S(1)}, u32[]{:S(2)}, u32[]{:S(2)}) collective-permute-start(bf16[544,1664]{1,0:T(8,128)(2,1)} %pad_maximum_fusion.refs_14_), channel_id=1, source_target_pairs={{0,2},{1,3},{2,0},{3,1},{4,6},{5,7},{6,4},{7,5},{8,10},{9,11},{10,... | collective-permute-start | bytes 5431304 | tf_op jit(solution)/shard_map/ppermute | solution.py:556
  488.2 42.2 %collective-permute-start.44 = (bf16[544,1664]{1,0:T(8,128)(2,1)}, bf16[544,1664]{1,0:T(8,128)(2,1)}, u32[]{:S(2)}, u32[]{:S(2)}) collective-permute-start(bf16[544,1664]{1,0:T(8,128)(2,1)} %pad_maximum_fusion.1.refs_15_), channel_id=1, source_target_pairs={{0,4},{1,5},{2,6},{3,7},{4,0},{5,1},{6,2},{7,3},{8,12},{9,13},{10,... | collective-permute-start | bytes 5431304 | tf_op jit(solution)/shard_map/ppermute | solution.py:556
  512.0 24.0 %collective-permute-start.53 = (bf16[544,1664]{1,0:T(8,128)(2,1)}, bf16[544,1664]{1,0:T(8,128)(2,1)}, u32[]{:S(2)}, u32[]{:S(2)}) collective-permute-start(bf16[544,1664]{1,0:T(8,128)(2,1)} %get-tuple-element.175), channel_id=1, source_target_pairs={{0,1},{1,0},{2,3},{3,2},{4,5},{5,4},{6,7},{7,6},{8,9},{9,8},{10,11... | collective-permute-start | bytes 5431304 | tf_op jit(solution)/shard_map/ppermute | solution.py:556
  530.4 26.1 %collective-permute-start.47 = (bf16[512,1536]{1,0:T(8,128)(2,1)}, bf16[512,1536]{1,0:T(8,128)(2,1)}, u32[]{:S(2)}, u32[]{:S(2)}) collective-permute-start(bf16[512,1536]{1,0:T(8,128)(2,1)} %get-tuple-element.171), channel_id=1, source_target_pairs={{0,1},{1,0},{2,3},{3,2},{4,5},{5,4},{6,7},{7,6},{8,9},{9,8},{10,11... | collective-permute-start | bytes 4718600 | tf_op jit(solution)/shard_map/ppermute | solution.py:556
  535.5 25.0 %collective-permute-start.46 = (bf16[512,1536]{1,0:T(8,128)(2,1)S(1)}, bf16[512,1536]{1,0:T(8,128)(2,1)}, u32[]{:S(2)}, u32[]{:S(2)}) collective-permute-start(bf16[512,1536]{1,0:T(8,128)(2,1)S(1)} %copy-done.40), channel_id=1, source_target_pairs={{0,1},{1,0},{2,3},{3,2},{4,5},{5,4},{6,7},{7,6},{8,9},{9,8},{10,11... | collective-permute-start | bytes 4718600 | tf_op jit(solution)/shard_map/ppermute | solution.py:556
  535.5 27.5 %collective-permute-start.50 = (bf16[512,1536]{1,0:T(8,128)(2,1)}, bf16[512,1536]{1,0:T(8,128)(2,1)}, u32[]{:S(2)}, u32[]{:S(2)}) collective-permute-start(bf16[512,1536]{1,0:T(8,128)(2,1)} %get-tuple-element.173), channel_id=1, source_target_pairs={{0,1},{1,0},{2,3},{3,2},{4,5},{5,4},{6,7},{7,6},{8,9},{9,8},{10,11... | collective-permute-start | bytes 4718600 | tf_op jit(solution)/shard_map/ppermute | solution.py:556
  536.0 155.6 %collective-permute-start.45 = (bf16[512,1536]{1,0:T(8,128)(2,1)}, bf16[512,1536]{1,0:T(8,128)(2,1)}, u32[]{:S(2)}, u32[]{:S(2)}) collective-permute-start(bf16[512,1536]{1,0:T(8,128)(2,1)} %get-tuple-element.167), channel_id=1, source_target_pairs={{0,1},{1,0},{2,3},{3,2},{4,5},{5,4},{6,7},{7,6},{8,9},{9,8},{10,11... | collective-permute-start | bytes 4718600 | tf_op jit(solution)/shard_map/ppermute | solution.py:556
  559.9 46.1 %collective-permute-start.48 = (bf16[256,1536]{1,0:T(8,128)(2,1)}, bf16[256,1536]{1,0:T(8,128)(2,1)}, u32[]{:S(2)}, u32[]{:S(2)}) collective-permute-start(bf16[256,1536]{1,0:T(8,128)(2,1)} %get-tuple-element.251), channel_id=1, source_target_pairs={{0,4},{1,5},{2,6},{3,7},{4,0},{5,1},{6,2},{7,3},{8,12},{9,13},{10,... | collective-permute-start | bytes 2359304 | tf_op jit(solution)/shard_map/ppermute | solution.py:556
  603.7 27.6 %collective-permute-start.55 = (bf16[512,1024]{1,0:T(8,128)(2,1)}, bf16[512,1024]{1,0:T(8,128)(2,1)S(1)}, u32[]{:S(2)}, u32[]{:S(2)}) collective-permute-start(bf16[512,1024]{1,0:T(8,128)(2,1)} %slice.289), channel_id=1, source_target_pairs={{8,0},{16,8},{24,16},{9,1},{17,9},{25,17},{10,2},{18,10},{26,18},{... | collective-permute-start | bytes 3145736 | tf_op jit(solution)/shard_map/ppermute | solution.py:1137
  605.0 20.4 %collective-permute-start.51 = (bf16[256,1536]{1,0:T(8,128)(2,1)S(1)}, bf16[256,1536]{1,0:T(8,128)(2,1)S(1)}, u32[]{:S(2)}, u32[]{:S(2)}) collective-permute-start(bf16[256,1536]{1,0:T(8,128)(2,1)S(1)} %get-tuple-element.252), channel_id=1, source_target_pairs={{0,2},{1,3},{2,0},{3,1},{4,6},{5,7},{6,4},{7,5},{8,10},{9,11},{10,... | collective-permute-start | bytes 2359304 | tf_op jit(solution)/shard_map/ppermute | solution.py:556
  607.5 84.0 %collective-permute-start.49 = (bf16[512,1536]{1,0:T(8,128)(2,1)S(1)}, bf16[512,1536]{1,0:T(8,128)(2,1)}, u32[]{:S(2)}, u32[]{:S(2)}) collective-permute-start(bf16[512,1536]{1,0:T(8,128)(2,1)S(1)} %pad_maximum_fusion.2.refs_1_), channel_id=1, source_target_pairs={{0,2},{1,3},{2,0},{3,1},{4,6},{5,7},{6,4},{7,5},{8,10},{9,11},{10,... | collective-permute-start | bytes 4718600 | tf_op jit(solution)/shard_map/ppermute | solution.py:556
  626.9 64.7 %collective-permute-start.52 = (bf16[512,1536]{1,0:T(8,128)(2,1)}, bf16[512,1536]{1,0:T(8,128)(2,1)}, u32[]{:S(2)}, u32[]{:S(2)}) collective-permute-start(bf16[512,1536]{1,0:T(8,128)(2,1)} %pad_maximum_fusion.3.refs_2_), channel_id=1, source_target_pairs={{0,4},{1,5},{2,6},{3,7},{4,0},{5,1},{6,2},{7,3},{8,12},{9,13},{10,... | collective-permute-start | bytes 4718600 | tf_op jit(solution)/shard_map/ppermute | solution.py:556
  637.5 27.0 %collective-permute-start.56 = (bf16[512,1024]{1,0:T(8,128)(2,1)}, bf16[512,1024]{1,0:T(8,128)(2,1)}, u32[]{:S(2)}, u32[]{:S(2)}) collective-permute-start(bf16[512,1024]{1,0:T(8,128)(2,1)} %tie.30), channel_id=1, source_target_pairs={{8,0},{16,8},{24,16},{9,1},{17,9},{25,17},{10,2},{18,10},{26,18},{... | collective-permute-start | bytes 3145736 | tf_op jit(solution)/shard_map/ppermute | solution.py:1137
  681.5 21.6 %all-to-all-start.1 = ((bf16[32,80,128]{2,1,0:T(8,128)(2,1)}), bf16[32,80,128]{2,1,0:T(8,128)(2,1)}, u32[]{:S(2)}, u32[]{:S(2)}) async-start(bf16[32,80,128]{2,1,0:T(8,128)(2,1)} %pad_maximum_fusion.9), calls=%async_computation.2 | async-start | bytes 1310720 | tf_op jit(solution)/shard_map/all_to_all | solution.py:1171
  (113 other events, 992.0 us)
Sparse Core Ops, SparseCore 0:
  40.1 34.0 all-gather.11
  75.7 65.8 all-gather.13
  187.9 88.7 all-gather.17
  278.1 74.8 all-gather.15
  355.0 49.0 all-gather.19
  406.3 34.5 reduce-scatter.2
  535.0 32.8 reduce-scatter.4

commit v7 on v6

--- a/solution.py
+++ b/solution.py
@@ -971,11 +971,22 @@
 
     x_flat = block_input[0].astype(F32)
     normed = rms_norm(x_flat, gains[0]).astype(BF16)
-    low_kv = dot_nn(normed, first_kv).astype(BF16)
-    kv_extra = jnp.concatenate([dot_nn(low_kv[:, :rank], b_parts[1]), dot_nn(low_kv[:, rank:], b_parts[2])], axis=1)
+    select = (jnp.arange(rank_all, dtype=jnp.int32) // rank == adapter).astype(F32)[None, :]
+
+    def masked_low(inputs, factors):
+        low = dot_nn(inputs, factors)
+        return [
+            (low[:, at : at + rank_all] * select).astype(BF16) for at in range(0, factors.shape[1], rank_all)
+        ]
+
+    low_k, low_v = masked_low(normed, kv_first)
+    low_kv = own_factors(jnp.concatenate([low_k, low_v], axis=1))
+    kv_extra = jnp.concatenate(
+        [dot_nt(low_k, second_t[edges[1] : edges[2]]), dot_nt(low_v, second_t[edges[2] : edges[3]])], axis=1
+    )
     present_tag = jnp.where(key_present == 1, document_number + 1, 0).astype(BF16)
-    tag_columns = jnp.broadcast_to(present_tag.reshape(rows, 1), (rows, LANES))
-    kv_blocks = [jnp.concatenate([(dot_nn(normed, kv_w) + kv_extra).astype(BF16), tag_columns], axis=1)]
+    tag_rows = jnp.broadcast_to(jnp.pad(present_tag, ((0, 0), (0, 2 * kv_width - rows))), (16, 2 * kv_width))
+    kv_blocks = [jnp.concatenate([(dot_nn(normed, kv_w) + kv_extra).astype(BF16), tag_rows], axis=0)]
     q_blocks = plane_gather(tie(seq_q, *far_grads), size)
     for k in range(1, size, 2):
         grad_blocks[k] = tuple(swap(piece, 1, size) for piece in grad_blocks[k - 1])
@@ -983,8 +994,8 @@
         block = kv_blocks[-1] if h == 0 else tie(kv_blocks[-1], q_blocks[2][0], q_blocks[4][0], first_down)
         kv_blocks.append(lax.ppermute(block, "seq", forward))
         kv_blocks[h] = block
-    kv_all = jnp.concatenate(kv_blocks[::-1], axis=0)
-    key_tag = kv_all[:, 2 * kv_width : 2 * kv_width + 1].astype(F32)
+    kv_all = jnp.concatenate([block[:rows] for block in kv_blocks[::-1]], axis=0)
+    key_tag = jnp.concatenate([block[rows, :rows] for block in kv_blocks[::-1]]).astype(F32).reshape(-1, 1)
     query_tag = (document_number + 1).astype(F32)
 
     seq_up, seq_down = [over_seq(tie(up_shards[0], kv_blocks[hops]))], [first_down]
@@ -993,14 +1004,17 @@
         seq_down.append(over_seq(tie(down_shards[j], seq_up[j - 1])))
 
     q_w, q_first, out_w = assemble(q_blocks, ((1, query_width), (1, 4 * rank_all), (1, model)), me)
+    (low_q,) = masked_low(normed, q_first[:, :rank_all])
+    first_out = q_first[:, rank_all : 2 * rank_all]
     q_first = own_factors(q_first)
     first_q, first_o, first_gu = q_first[:, :rank], q_first[:, rank : 2 * rank], q_first[:, 2 * rank :]
-    low_q = dot_nn(normed, first_q).astype(BF16)
-    query = (dot_nn(normed, q_w) + dot_nn(low_q, b_parts[0])).astype(BF16)
+    query = (dot_nn(normed, q_w) + dot_nt(low_q, second_t[edges[0] : edges[1]])).astype(BF16)
+    low_q = own_columns(low_q)
     glow_sdown = dot_nt(grad_out_b, b_parts[6]).astype(BF16)
     attn, lse = attend(query, kv_all, query_tag, key_tag, hops, (*grad_blocks[3], *grad_blocks[5], *grad_blocks[7]))
-    out_low = dot_nn(attn, first_o).astype(BF16)
-    mid = x_flat + dot_nn(attn, out_w) + dot_nn(out_low, b_parts[3])
+    (out_low,) = masked_low(attn, first_out)
+    mid = x_flat + dot_nn(attn, out_w) + dot_nt(out_low, second_t[edges[3] : edges[4]])
+    out_low = own_columns(out_low)
     normed2 = rms_norm(mid, gains[1]).astype(BF16)
 
     logits = dot_nn(normed2, router_w)

time: 724 us -> 731 us (level)
  waiting for transfers between devices: 154 us -> 129 us
  local copies, waits for them, and re-layouts: 82.3 us -> 92.4 us
  matrix products: 22.9 us -> 32.5 us
  starting transfers between devices: 54.9 us -> 62.4 us
    ppermute x2, waiting for transfers between devices: 35.4 us -> 17.6 us  [per_device(): kv_blocks.append(lax.ppermute(block, 'seq', forward))]
    all_gather x5, starting transfers between devices: 0.61 us -> 8.96 us  [over_seq(): return lax.all_gather(shard, 'seq', axis=0)]
    unnamed x198 -> x216, local copies, waits for them, and re-layouts: 37 us -> 34.1 us
    dot_general x14 -> x10, matrix products: 22.4 us -> 24.7 us  [dot_nn(): return jnp.dot(left, right, preferred_element_type=F32)]
  transfers between devices with their start and end apart: 66 -> 66, of which waited for: 15 -> 17; matrix products, arithmetic and copies ran while one was open for 17% -> 21% of each run, Pallas kernels for 44% -> 44%
where the time goes in v7:
time: 731 us; the launch traced here: 721 us
  Pallas kernels  317 us (43%)
  waiting for transfers between devices  129 us (18%)
  local copies, waits for them, and re-layouts  92.4 us (13%)
  starting transfers between devices  62.4 us (9%)
  other arithmetic  51.3 us (7%)
  matrix products  32.5 us (4%)
  blocking collectives  20.3 us (3%)
  between operations  16.8 us (2%)
    pallas_call x8, Pallas kernels, expert_call(): pl.pallas_call(functools.partial(expert_kernel, *(count, splits, experts,...  198 us
    ppermute x53, waiting for transfers between devices, swap(): return lax.ppermute(array, 'dp', [(i, i ^ bit) for i in range(size)])  70.3 us
    unnamed x216, local copies, waits for them, and re-layouts  34.1 us
    ppermute x53, starting transfers between devices, swap(): return lax.ppermute(array, 'dp', [(i, i ^ bit) for i in range(size)])  33.4 us
    pallas_call x1, Pallas kernels, attend_back(): pl.pallas_call(functools.partial(attend_back_kernel, spans, hops * rows,...  33.4 us
    dot_general x10, matrix products, dot_nn(): return jnp.dot(left, right, preferred_element_type=F32)  24.7 us
    pallas_call x1, Pallas kernels, attend(): pl.pallas_call(functools.partial(attend_kernel, spans, hops * rows, len(d...  23.7 us
    all_gather x5, waiting for transfers between devices, over_seq(): return lax.all_gather(shard, 'seq', axis=0)  21.4 us
  transfers between devices with their start and end apart: 66, of which 17 were waited for; matrix products, arithmetic and copies ran while one was open for 21% of the time, Pallas kernels for 44%

profile of v7, /device:TPU:0, one launch (start us, length us, event | category | flops | bytes accessed | tf_op | source)
XLA Modules:
  0.0 721.4 jit_solution(325211617724301255)
XLA Ops:
  7.2 3.0 collective-permute-start
  15.1 3.4 all-to-all-start
  19.6 20.3 %all-gather = bf16[192,2048]{1,0:T(8,128)(2,1)} all-gather(bf16[48,2048]{1,0:T(8,128)(2,1)S(1)} %fusion.20), channel_id=2, replica_groups=mesh['seq'=4,'dp'=8] {'seq'}, dimensions={0}, use_global_device_ids=true | all-gather | bytes 983040 | tf_op jit(solution)/shard_map/all_gather | solution.py:890
  43.1 5.3 all-to-all-done.refs_3_
  51.2 17.2 %collective-permute-done.3.refs_2_ = bf16[4,48,2048]{2,1,0:T(8,128)(2,1)S(1)} collective-permute-done((bf16[4,48,2048]{2,1,0:T(8,128)(2,1)}, bf16[4,48,2048]{2,1,0:T(8,128)(2,1)S(1)}, u32[]{:S(2)}, u32[]{:S(2)}) %collective-permute-start.3) | collective-permute-done | bytes 786464 | tf_op jit(solution)/shard_map/ppermute | solution.py:556
  76.3 2.9 collective-permute-done.8.refs_7_.refs_3_
  79.2 3.2 collective-permute-done.7.refs_6_.refs_2_
  88.9 5.6 assemble.2
  101.8 6.2 collective-permute-done.11.refs_1_.refs_8_.refs_7_
  110.0 4.4 fusion.5
  116.4 4.5 collective-permute-start.22
  123.8 2.5 fusion.49
  130.0 2.5 pad_maximum_fusion.5.refs_0_
  132.5 7.9 %collective-permute-done.16.refs_4_.refs_2_ = bf16[4,48,3584]{2,1,0:T(8,128)(2,1)} collective-permute-done((bf16[4,48,3584]{2,1,0:T(8,128)(2,1)}, bf16[4,48,3584]{2,1,0:T(8,128)(2,1)}, u32[]{:S(2)}, u32[]{:S(2)}) %collective-permute-start.16) | collective-permute-done | bytes 1376288 | tf_op jit(solution)/shard_map/ppermute | solution.py:556
  145.7 7.3 %collective-permute-done.22.refs_0_ = bf16[528,1024]{1,0:T(8,128)(2,1)} collective-permute-done((bf16[528,1024]{1,0:T(8,128)(2,1)}, bf16[528,1024]{1,0:T(8,128)(2,1)}, u32[]{:S(2)}, u32[]{:S(2)}) %collective-permute-start.22) | collective-permute-done | bytes 1081376 | tf_op jit(solution)/shard_map/ppermute | solution.py:995
  153.1 5.7 collective-permute-start.23
  170.3 10.3 %collective-permute-done.23.refs_1_ = bf16[528,1024]{1,0:T(8,128)(2,1)} collective-permute-done((bf16[528,1024]{1,0:T(8,128)(2,1)}, bf16[528,1024]{1,0:T(8,128)(2,1)}, u32[]{:S(2)}, u32[]{:S(2)}) %collective-permute-start.23) | collective-permute-done | bytes 1081376 | tf_op jit(solution)/shard_map/ppermute | solution.py:995
  188.4 8.7 %assemble.3 = (bf16[4,8,1,48,1536]{4,3,2,1,0:T(8,128)(2,1)}, bf16[4,8,1,48,512]{4,3,2,1,0:T(8,128)(2,1)}, bf16[4,8,1,48,1536]{4,3,2,1,0:T(8,128)(2,1)}) custom-call(s32[1]{0:T(128)} %bitcast.1.me_ref, bf16[4,48,3584]{2,1,0:T(8,128)(2,1)} %tie.19.refs_0_, bf16[4,48,3584]{2,1,0:T(8,128)(2,1)} %collective-permute-done.13.refs_1_, ...), custom_call_target="tpu_custom_call" | custom-call | tf_op jit(solution)/shard_map/assemble/pallas_call | solution.py:629
  200.5 3.9 fusion.4.q_ref
  204.4 23.7 %attend.1 = (bf16[512,1536]{1,0:T(8,128)(2,1)}, f32[4,3,512]{2,1,0:T(4,128)}) custom-call(bf16[512,1536]{1,0:T(8,128)(2,1)} %fusion.4.q_ref, bf16[1536,1024]{1,0:T(8,128)(2,1)} %pad_maximum_fusion.k_ref.v_ref, bf16[1536,1024]{1,0:T(8,128)(2,1)} %pad_maximum_fusion.k_ref.v_ref, f32[1,512]{1,0:T(1,128)} %get-tuple-element.283.qt_ref, ...), custom_call_target="tpu_custom_call" | custom-call | flops 26530500608 | bytes 1000000 | tf_op jit(solution)/shard_map/attend/pallas_call | solution.py:96
  231.8 4.8 multiply_reduce_fusion
  246.6 8.8 %all-gather.20.cloned.1.call-start = ((), (), s32[]{:S(2)}) async-start(), calls=%async_computation.10 | async-start | bytes 2949120 | tf_op jit(solution)/shard_map/all_gather | solution.py:890
  261.2 14.3 %all-gather.18.cloned.1.call-done.refs_1_ = bf16[1536,1536]{1,0:T(8,128)(2,1)} async-done(((bf16[384,1536]{1,0:T(8,128)(2,1)}), bf16[1536,1536]{1,0:T(8,128)(2,1)}) %all-gather.18.cloned.1.call-update) | async-done | bytes 4718608 | tf_op jit(solution)/shard_map/all_gather | solution.py:890
  275.5 25.6 %expert.8 = (bf16[512,1536]{1,0:T(8,128)(2,1)}, bf16[512,1536]{1,0:T(8,128)(2,1)}, bf16[544,1664]{1,0:T(8,128)(2,1)}, bf16[544,1664]{1,0:T(8,128)(2,1)}, f32[153...) custom-call(s32[2]{0:T(128)} %pad_add_fusion.1.refs_0_, ...), custom_call_target="tpu_custom_call" | custom-call | flops 27683999744 | bytes 1000000 | tf_op jit(solution)/shard_map/expert/pallas_call | solution.py:522
  310.6 27.2 %expert.9 = (bf16[512,1536]{1,0:T(8,128)(2,1)}, bf16[512,1536]{1,0:T(8,128)(2,1)}, bf16[544,1664]{1,0:T(8,128)(2,1)}, bf16[544,1664]{1,0:T(8,128)(2,1)}, f32[153...) custom-call(s32[2]{0:T(128)} %pad_add_fusion.1.refs_0_, ...), custom_call_target="tpu_custom_call" | custom-call | flops 27683999744 | bytes 1000000 | tf_op jit(solution)/shard_map/expert/pallas_call | solution.py:522
  339.5 27.2 %expert.10 = (bf16[512,1536]{1,0:T(8,128)(2,1)}, bf16[512,1536]{1,0:T(8,128)(2,1)}, bf16[544,1664]{1,0:T(8,128)(2,1)}, bf16[544,1664]{1,0:T(8,128)(2,1)}, f32[15...) custom-call(s32[2]{0:T(128)} %pad_add_fusion.1.refs_0_, ...), custom_call_target="tpu_custom_call" | custom-call | flops 27683999744 | bytes 1000000 | tf_op jit(solution)/shard_map/expert/pallas_call | solution.py:522
  368.0 27.7 %expert.11 = (bf16[512,1536]{1,0:T(8,128)(2,1)}, bf16[512,1536]{1,0:T(8,128)(2,1)}, bf16[544,1664]{1,0:T(8,128)(2,1)}, bf16[544,1664]{1,0:T(8,128)(2,1)}, bf16[4,1568,128]{2,1,0:T(8,128)(2,1)}) custom-call(s32[2]{0:T(128)} %pad_add_fusion.1.refs_0_, bf16[1536,1536]{1,0:T(8,128)(2,1)} %all-gather.18.cloned.1.call-done.refs_1_, ...), custom_call_target="tpu_custom_call" | custom-call | flops 27683999744 | bytes 1000000 | tf_op jit(solution)/shard_map/expert/pallas_call | solution.py:522
  395.8 7.1 all-gather.20.cloned.1.call-done
  402.9 21.0 %expert.12 = (bf16[512,1536]{1,0:T(8,128)(2,1)}, bf16[512,1536]{1,0:T(8,128)(2,1)}, bf16[544,1664]{1,0:T(8,128)(2,1)}, bf16[544,1664]{1,0:T(8,128)(2,1)}, f32[15...) custom-call(s32[2]{0:T(128)} %pad_add_fusion.refs_0_, ...), custom_call_target="tpu_custom_call" | custom-call | flops 27683999744 | bytes 1000000 | tf_op jit(solution)/shard_map/expert/pallas_call | solution.py:522
  424.0 22.6 %expert.13 = (bf16[512,1536]{1,0:T(8,128)(2,1)}, bf16[512,1536]{1,0:T(8,128)(2,1)}, bf16[544,1664]{1,0:T(8,128)(2,1)}, bf16[544,1664]{1,0:T(8,128)(2,1)}, f32[15...) custom-call(s32[2]{0:T(128)} %pad_add_fusion.refs_0_, ...), custom_call_target="tpu_custom_call" | custom-call | flops 27683999744 | bytes 1000000 | tf_op jit(solution)/shard_map/expert/pallas_call | solution.py:522
  447.2 2.5 add_convert_fusion.2.refs_15_
  454.5 22.7 %expert.14 = (bf16[512,1536]{1,0:T(8,128)(2,1)}, bf16[512,1536]{1,0:T(8,128)(2,1)}, bf16[544,1664]{1,0:T(8,128)(2,1)}, bf16[544,1664]{1,0:T(8,128)(2,1)}, f32[15...) custom-call(s32[2]{0:T(128)} %pad_add_fusion.refs_0_, ...), custom_call_target="tpu_custom_call" | custom-call | flops 27683999744 | bytes 1000000 | tf_op jit(solution)/shard_map/expert/pallas_call | solution.py:522
  491.2 23.6 %expert.15 = (bf16[512,1536]{1,0:T(8,128)(2,1)}, bf16[512,1536]{1,0:T(8,128)(2,1)}, bf16[544,1664]{1,0:T(8,128)(2,1)}, bf16[544,1664]{1,0:T(8,128)(2,1)}, bf16[4,1536,128]{2,1,0:T(8,128)(2,1)}) custom-call(s32[2]{0:T(128)} %pad_add_fusion.refs_0_, bf16[1536,1280]{1,0:T(8,128)(2,1)} %all-gather.16.cloned.1.call-done.refs_1_, bf16[4,128,2304]{2,1,0:T(8,128)(2,1)} %bitcast.239, ...), custom_call_target="tpu_custom_call" | custom-call | flops 27683999744 | bytes 1000000 | tf_op jit(solution)/shard_map/expert/pallas_call | solution.py:522
  517.5 9.6 %collective-permute-done.43.refs_4_.refs_1_.from_x = bf16[544,1664]{1,0:T(8,128)(2,1)S(1)} collective-permute-done((bf16[544,1664]{1,0:T(8,128)(2,1)}, bf16[544,1664]{1,0:T(8,128)(2,1)S(1)}, u32[]{:S(2)}, u32[]{:S(2)}) %collective-permute-start.43) | collective-permute-done | bytes 1810464 | tf_op jit(solution)/shard_map/ppermute | solution.py:556
  527.0 5.7 collective-permute-done.44.refs_5_.refs_2_.from_y
  540.7 18.4 %turn.1 = (f32[512,1536]{1,0:T(8,128)}, bf16[512,1536]{1,0:T(8,128)(2,1)}, bf16[512,16]{1,0:T(8,128)(2,1)}, bf16[512,32]{1,0:T(8,128)(2,1)}, bf16[512,16]{1,0:T(...) custom-call(bf16[544,1664]{1,0:T(8,128)(2,1)} %get-tuple-element.174.own, ...), custom_call_target="tpu_custom_call" | custom-call | flops 4614000128 | bytes 1000000 | tf_op jit(solution)/shard_map/turn/pallas_call | solution.py:694
  572.9 33.4 %attend_back.1 = (bf16[512,1536]{1,0:T(8,128)(2,1)}, bf16[1536,1024]{1,0:T(8,128)(2,1)}) custom-call(bf16[512,1536]{1,0:T(8,128)(2,1)} %fusion.4.q_ref, bf16[1536,1024]{1,0:T(8,128)(2,1)} %pad_maximum_fusion.k_ref.v_ref, bf16[1536,1024]{1,0:T(8,128)(2,1)} %pad_maximum_fusion.k_ref.v_ref, bf16[512,1536]{1,0:T(8,128)(2,1)} %get-tuple-element.177.g_ref, ...), custom_call_target="tpu_custom_call" | custom-call | flops 9228000256 | bytes 1000000 | tf_op jit(solution)/shard_map/attend_back/pallas_call | solution.py:159
  613.7 17.0 %collective-permute-done.51 = bf16[256,1536]{1,0:T(8,128)(2,1)S(1)} collective-permute-done((bf16[256,1536]{1,0:T(8,128)(2,1)}, bf16[256,1536]{1,0:T(8,128)(2,1)S(1)}, u32[]{:S(2)}, u32[]{:S(2)}) %collective-permute-start.51) | collective-permute-done | bytes 786464 | tf_op jit(solution)/shard_map/ppermute | solution.py:556
  632.9 3.0 collective-permute-done.55.rest_0_.refs_2_
  640.7 2.6 add_convert_fusion.9.refs_0_
  644.9 5.2 middle.1
  654.4 9.7 %query_back.1 = (f32[512,1536]{1,0:T(8,128)}, f32[1536,16]{1,0:T(8,128)}, f32[16,1536]{1,0:T(8,128)}) custom-call(bf16[512,1536]{1,0:T(8,128)(2,1)} %get-tuple-element.181.grad_q, bf16[512,1536]{1,0:T(8,128)(2,1)} %copy-done.9, bf16[512,16]{1,0:T(8,128)(2,1)} %constant_dynamic-slice_fusion.2.low_q, bf16[1536,1536]{1,0:T(8,128)(2,1)} %bitcast.189, ...), custom_call_target="tpu_custom_call" | custom-call | flops 115350000 | bytes 1000000 | tf_op jit(solution)/shard_map/query_back/pallas_call | solution.py:717
  664.1 5.9 collective-permute-done.56
  669.9 2.9 add_convert_fusion.8.grad_kv
  672.9 12.2 %last.1 = (f32[512,1536]{1,0:T(8,128)}, bf16[1536,128]{1,0:T(8,128)(2,1)}, bf16[32,32,128]{2,1,0:T(8,128)(2,1)}) custom-call(bf16[512,1024]{1,0:T(8,128)(2,1)} %add_convert_fusion.8.grad_kv, bf16[512,1536]{1,0:T(8,128)(2,1)} %copy-done.9, bf16[512,32]{1,0:T(8,128)(2,1)} %pad_maximum_fusion.16.low_kv, bf16[1536,1024]{1,0:T(8,128)(2,1)} %bitcast.198, ...), custom_call_target="tpu_custom_call" | custom-call | flops 2307000064 | bytes 1000000 | tf_op jit(solution)/shard_map/last/pallas_call | solution.py:788
  687.1 3.6 all-to-all-start.1
  698.7 4.6 fusion.7
  703.4 5.2 all-to-all-done.1.flat
  (489 shorter events, 182.2 us)
Async XLA Ops:
  7.2 41.2 %collective-permute-start = (bf16[512,1536]{1,0:T(8,128)(2,1)}, bf16[512,1536]{1,0:T(8,128)(2,1)}, u32[]{:S(2)}, u32[]{:S(2)}) collective-permute-start(bf16[512,1536]{1,0:T(8,128)(2,1)} %bitcast.168), channel_id=1, source_target_pairs={{0,2},{1,3},{2,0},{3,1},{4,6},{5,7},{6,4},{7,5},{8,10},{9,11},{10,... | collective-permute-start | bytes 4718600 | tf_op jit(solution)/shard_map/ppermute | solution.py:556
  10.2 38.2 %collective-permute-start.1 = (bf16[512,1536]{1,0:T(8,128)(2,1)}, bf16[512,1536]{1,0:T(8,128)(2,1)}, u32[]{:S(2)}, u32[]{:S(2)}) collective-permute-start(bf16[512,1536]{1,0:T(8,128)(2,1)} %bitcast.169), channel_id=1, source_target_pairs={{0,4},{1,5},{2,6},{3,7},{4,0},{5,1},{6,2},{7,3},{8,12},{9,13},{10,... | collective-permute-start | bytes 4718600 | tf_op jit(solution)/shard_map/ppermute | solution.py:556
  15.1 33.3 %all-to-all-start = ((bf16[8,48,256]{2,1,0:T(8,128)(2,1)}), bf16[8,48,256]{2,1,0:T(8,128)(2,1)S(1)}, u32[]{:S(2)}, u32[]{:S(2)}) async-start(bf16[8,48,256]{2,1,0:T(8,128)(2,1)} %copy.182), calls=%async_computation | async-start | bytes 393216 | tf_op jit(solution)/shard_map/all_to_all | solution.py:933
  18.5 83.3 %all-gather.12.cloned.1.call-start = ((), (), s32[]{:S(2)}) async-start(), calls=%async_computation.6 | async-start | bytes 1720320 | tf_op jit(solution)/shard_map/all_gather | solution.py:890
  39.9 113.1 %all-gather.14.cloned.1.call-start = ((), (), s32[]{:S(2)}) async-start(), calls=%async_computation.7 | async-start | bytes 3604480 | tf_op jit(solution)/shard_map/all_gather | solution.py:890
  49.1 19.3 %collective-permute-start.3 = (bf16[4,48,2048]{2,1,0:T(8,128)(2,1)}, bf16[4,48,2048]{2,1,0:T(8,128)(2,1)S(1)}, u32[]{:S(2)}, u32[]{:S(2)}) collective-permute-start(bf16[4,48,2048]{2,1,0:T(8,128)(2,1)} %tie.16.refs_0_), channel_id=1, source_target_pairs={{0,2},{1,3},{2,0},{3,1},{4,6},{5,7},{6,4},{7,5},{8,10},{9,11},{10,... | collective-permute-start | bytes 2359304 | tf_op jit(solution)/shard_map/ppermute | solution.py:556
  50.1 20.7 %collective-permute-start.5 = (bf16[4,48,2048]{2,1,0:T(8,128)(2,1)}, bf16[4,48,2048]{2,1,0:T(8,128)(2,1)S(1)}, u32[]{:S(2)}, u32[]{:S(2)}) collective-permute-start(bf16[4,48,2048]{2,1,0:T(8,128)(2,1)} %tie.16.refs_0_), channel_id=1, source_target_pairs={{0,4},{1,5},{2,6},{3,7},{4,0},{5,1},{6,2},{7,3},{8,12},{9,13},{10,... | collective-permute-start | bytes 2359304 | tf_op jit(solution)/shard_map/ppermute | solution.py:556
  73.2 202.3 %all-gather.18.cloned.1.call-start = ((), (), s32[]{:S(2)}) async-start(), calls=%async_computation.9 | async-start | bytes 5898240 | tf_op jit(solution)/shard_map/all_gather | solution.py:890
  87.7 20.3 %collective-permute-start.11 = (bf16[256,1536]{1,0:T(8,128)(2,1)}, bf16[256,1536]{1,0:T(8,128)(2,1)}, u32[]{:S(2)}, u32[]{:S(2)}) collective-permute-start(bf16[256,1536]{1,0:T(8,128)(2,1)} %slice.266), channel_id=1, source_target_pairs={{0,2},{1,3},{2,0},{3,1},{4,6},{5,7},{6,4},{7,5},{8,10},{9,11},{10,... | collective-permute-start | bytes 2359304 | tf_op jit(solution)/shard_map/ppermute | solution.py:556
  88.5 20.0 %collective-permute-start.12 = (bf16[256,1536]{1,0:T(8,128)(2,1)}, bf16[256,1536]{1,0:T(8,128)(2,1)}, u32[]{:S(2)}, u32[]{:S(2)}) collective-permute-start(bf16[256,1536]{1,0:T(8,128)(2,1)} %slice.267), channel_id=1, source_target_pairs={{0,4},{1,5},{2,6},{3,7},{4,0},{5,1},{6,2},{7,3},{8,12},{9,13},{10,... | collective-permute-start | bytes 2359304 | tf_op jit(solution)/shard_map/ppermute | solution.py:556
  108.5 31.8 %collective-permute-start.16 = (bf16[4,48,3584]{2,1,0:T(8,128)(2,1)}, bf16[4,48,3584]{2,1,0:T(8,128)(2,1)}, u32[]{:S(2)}, u32[]{:S(2)}) collective-permute-start(bf16[4,48,3584]{2,1,0:T(8,128)(2,1)} %tie.19.refs_0_), channel_id=1, source_target_pairs={{0,4},{1,5},{2,6},{3,7},{4,0},{5,1},{6,2},{7,3},{8,12},{9,13},{10,... | collective-permute-start | bytes 4128776 | tf_op jit(solution)/shard_map/ppermute | solution.py:556
  108.8 34.6 %collective-permute-start.14 = (bf16[4,48,3584]{2,1,0:T(8,128)(2,1)}, bf16[4,48,3584]{2,1,0:T(8,128)(2,1)}, u32[]{:S(2)}, u32[]{:S(2)}) collective-permute-start(bf16[4,48,3584]{2,1,0:T(8,128)(2,1)} %tie.19.refs_0_), channel_id=1, source_target_pairs={{0,2},{1,3},{2,0},{3,1},{4,6},{5,7},{6,4},{7,5},{8,10},{9,11},{10,... | collective-permute-start | bytes 4128776 | tf_op jit(solution)/shard_map/ppermute | solution.py:556
  116.4 36.7 %collective-permute-start.22 = (bf16[528,1024]{1,0:T(8,128)(2,1)}, bf16[528,1024]{1,0:T(8,128)(2,1)}, u32[]{:S(2)}, u32[]{:S(2)}) collective-permute-start(bf16[528,1024]{1,0:T(8,128)(2,1)} %pad_maximum_fusion.6), channel_id=1, source_target_pairs={{0,8},{8,16},{16,24},{1,9},{9,17},{17,25},{2,10},{10,18},{18,26},{... | collective-permute-start | bytes 3244040 | tf_op jit(solution)/shard_map/ppermute | solution.py:995
  153.1 27.5 %collective-permute-start.23 = (bf16[528,1024]{1,0:T(8,128)(2,1)}, bf16[528,1024]{1,0:T(8,128)(2,1)}, u32[]{:S(2)}, u32[]{:S(2)}) collective-permute-start(bf16[528,1024]{1,0:T(8,128)(2,1)} %tie.21), channel_id=1, source_target_pairs={{0,8},{8,16},{16,24},{1,9},{9,17},{17,25},{2,10},{10,18},{18,26},{... | collective-permute-start | bytes 3244040 | tf_op jit(solution)/shard_map/ppermute | solution.py:995
  160.7 24.6 %collective-permute-start.13 = (bf16[4,48,3584]{2,1,0:T(8,128)(2,1)}, bf16[4,48,3584]{2,1,0:T(8,128)(2,1)}, u32[]{:S(2)}, u32[]{:S(2)}) collective-permute-start(bf16[4,48,3584]{2,1,0:T(8,128)(2,1)} %tie.19.refs_0_), channel_id=1, source_target_pairs={{0,1},{1,0},{2,3},{3,2},{4,5},{5,4},{6,7},{7,6},{8,9},{9,8},{10,11... | collective-permute-start | bytes 4128776 | tf_op jit(solution)/shard_map/ppermute | solution.py:556
  160.7 27.6 %collective-permute-start.15 = (bf16[4,48,3584]{2,1,0:T(8,128)(2,1)}, bf16[4,48,3584]{2,1,0:T(8,128)(2,1)}, u32[]{:S(2)}, u32[]{:S(2)}) collective-permute-start(bf16[4,48,3584]{2,1,0:T(8,128)(2,1)} %collective-permute-done.14.refs_2_.refs_1_), channel_id=1, source_target_pairs={{0,1},{1,0},{2,3},{3,2},{4,5},{5,4},{6,7},{7,6},{8,9},{9,8},{10,11... | collective-permute-start | bytes 4128776 | tf_op jit(solution)/shard_map/ppermute | solution.py:556
  161.2 27.2 %collective-permute-start.17 = (bf16[4,48,3584]{2,1,0:T(8,128)(2,1)}, bf16[4,48,3584]{2,1,0:T(8,128)(2,1)}, u32[]{:S(2)}, u32[]{:S(2)}) collective-permute-start(bf16[4,48,3584]{2,1,0:T(8,128)(2,1)} %collective-permute-done.16.refs_4_.refs_2_), channel_id=1, source_target_pairs={{0,1},{1,0},{2,3},{3,2},{4,5},{5,4},{6,7},{7,6},{8,9},{9,8},{10,11... | collective-permute-start | bytes 4128776 | tf_op jit(solution)/shard_map/ppermute | solution.py:556
  164.1 21.9 %collective-permute-start.20 = (bf16[2,48,3584]{2,1,0:T(8,128)(2,1)}, bf16[2,48,3584]{2,1,0:T(8,128)(2,1)}, u32[]{:S(2)}, u32[]{:S(2)}) collective-permute-start(bf16[2,48,3584]{2,1,0:T(8,128)(2,1)} %collective-permute-done.18.refs_6_), channel_id=1, source_target_pairs={{0,1},{1,0},{2,3},{3,2},{4,5},{5,4},{6,7},{7,6},{8,9},{9,8},{10,11... | collective-permute-start | bytes 2064392 | tf_op jit(solution)/shard_map/ppermute | solution.py:556
  183.8 212.0 %all-gather.16.cloned.1.call-start = ((), (), s32[]{:S(2)}) async-start(), calls=%async_computation.8 | async-start | bytes 4915200 | tf_op jit(solution)/shard_map/all_gather | solution.py:890
  185.3 19.0 %collective-permute-start.24 = (bf16[512,1536]{1,0:T(8,128)(2,1)}, bf16[512,1536]{1,0:T(8,128)(2,1)}, u32[]{:S(2)}, u32[]{:S(2)}) collective-permute-start(bf16[512,1536]{1,0:T(8,128)(2,1)} %get-tuple-element.106.refs_6_.refs_5_), channel_id=1, source_target_pairs={{0,1},{1,0},{2,3},{3,2},{4,5},{5,4},{6,7},{7,6},{8,9},{9,8},{10,11... | collective-permute-start | bytes 4718600 | tf_op jit(solution)/shard_map/ppermute | solution.py:556
  246.6 156.3 %all-gather.20.cloned.1.call-start = ((), (), s32[]{:S(2)}) async-start(), calls=%async_computation.10 | async-start | bytes 2949120 | tf_op jit(solution)/shard_map/all_gather | solution.py:890
  257.9 43.2 %collective-permute-start.30 = (bf16[512,1664]{1,0:T(8,128)(2,1)}, bf16[512,1664]{1,0:T(8,128)(2,1)S(1)}, u32[]{:S(2)}, u32[]{:S(2)}) collective-permute-start(bf16[512,1664]{1,0:T(8,128)(2,1)} %concatenate.98.refs_4_.refs_3_), channel_id=1, source_target_pairs={{0,2},{1,3},{2,0},{3,1},{4,6},{5,7},{6,4},{7,5},{8,10},{9,11},{10,... | collective-permute-start | bytes 5111816 | tf_op jit(solution)/shard_map/ppermute | solution.py:556
  259.7 41.4 %collective-permute-start.31 = (bf16[512,1664]{1,0:T(8,128)(2,1)}, bf16[512,1664]{1,0:T(8,128)(2,1)}, u32[]{:S(2)}, u32[]{:S(2)}) collective-permute-start(bf16[512,1664]{1,0:T(8,128)(2,1)} %concatenate.98.refs_4_.refs_3_), channel_id=1, source_target_pairs={{0,4},{1,5},{2,6},{3,7},{4,0},{5,1},{6,2},{7,3},{8,12},{9,13},{10,... | collective-permute-start | bytes 5111816 | tf_op jit(solution)/shard_map/ppermute | solution.py:556
  304.3 35.3 %collective-permute-start.32 = (bf16[512,1664]{1,0:T(8,128)(2,1)}, bf16[512,1664]{1,0:T(8,128)(2,1)}, u32[]{:S(2)}, u32[]{:S(2)}) collective-permute-start(bf16[512,1664]{1,0:T(8,128)(2,1)} %get-tuple-element.118.refs_4_.refs_3_), channel_id=1, source_target_pairs={{0,1},{1,0},{2,3},{3,2},{4,5},{5,4},{6,7},{7,6},{8,9},{9,8},{10,11... | collective-permute-start | bytes 5111816 | tf_op jit(solution)/shard_map/ppermute | solution.py:556
  307.5 30.3 %collective-permute-start.34 = (bf16[256,1664]{1,0:T(8,128)(2,1)}, bf16[256,1664]{1,0:T(8,128)(2,1)S(1)}, u32[]{:S(2)}, u32[]{:S(2)}) collective-permute-start(bf16[256,1664]{1,0:T(8,128)(2,1)} %slice.299), channel_id=1, source_target_pairs={{0,2},{1,3},{2,0},{3,1},{4,6},{5,7},{6,4},{7,5},{8,10},{9,11},{10,... | collective-permute-start | bytes 2555912 | tf_op jit(solution)/shard_map/ppermute | solution.py:556
  309.1 28.8 %collective-permute-start.35 = (bf16[256,1664]{1,0:T(8,128)(2,1)}, bf16[256,1664]{1,0:T(8,128)(2,1)S(1)}, u32[]{:S(2)}, u32[]{:S(2)}) collective-permute-start(bf16[256,1664]{1,0:T(8,128)(2,1)} %slice.300), channel_id=1, source_target_pairs={{0,4},{1,5},{2,6},{3,7},{4,0},{5,1},{6,2},{7,3},{8,12},{9,13},{10,... | collective-permute-start | bytes 2555912 | tf_op jit(solution)/shard_map/ppermute | solution.py:556
  310.6 166.6 %reduce-scatter.3.cloned.1.call-start = ((), (), s32[]{:S(2)}) async-start(), calls=%async_computation.4 | async-start | bytes 2007040 | tf_op jit(solution)/shard_map/reduce_scatter | solution.py:1108
  339.0 27.8 %collective-permute-start.36 = (bf16[256,1664]{1,0:T(8,128)(2,1)}, bf16[256,1664]{1,0:T(8,128)(2,1)S(1)}, u32[]{:S(2)}, u32[]{:S(2)}) collective-permute-start(bf16[256,1664]{1,0:T(8,128)(2,1)} %get-tuple-element.136.refs_4_.refs_3_), channel_id=1, source_target_pairs={{0,1},{1,0},{2,3},{3,2},{4,5},{5,4},{6,7},{7,6},{8,9},{9,8},{10,11... | collective-permute-start | bytes 2555912 | tf_op jit(solution)/shard_map/ppermute | solution.py:556
  339.0 27.8 %collective-permute-start.37 = (bf16[256,1664]{1,0:T(8,128)(2,1)}, bf16[256,1664]{1,0:T(8,128)(2,1)S(1)}, u32[]{:S(2)}, u32[]{:S(2)}) collective-permute-start(bf16[256,1664]{1,0:T(8,128)(2,1)} %get-tuple-element.137.refs_5_.refs_4_), channel_id=1, source_target_pairs={{0,1},{1,0},{2,3},{3,2},{4,5},{5,4},{6,7},{7,6},{8,9},{9,8},{10,11... | collective-permute-start | bytes 2555912 | tf_op jit(solution)/shard_map/ppermute | solution.py:556
  395.7 237.2 %reduce-scatter.5.cloned.1.call-start = ((), (), s32[]{:S(2)}) async-start(), calls=%async_computation.5 | async-start | bytes 1966080 | tf_op jit(solution)/shard_map/reduce_scatter | solution.py:1108
  424.0 23.2 %collective-permute-start.38 = (bf16[544,1664]{1,0:T(8,128)(2,1)}, bf16[544,1664]{1,0:T(8,128)(2,1)}, u32[]{:S(2)}, u32[]{:S(2)}) collective-permute-start(bf16[544,1664]{1,0:T(8,128)(2,1)} %get-tuple-element.154), channel_id=1, source_target_pairs={{0,1},{1,0},{2,3},{3,2},{4,5},{5,4},{6,7},{7,6},{8,9},{9,8},{10,11... | collective-permute-start | bytes 5431304 | tf_op jit(solution)/shard_map/ppermute | solution.py:556
  446.7 33.7 %collective-permute-start.39 = (bf16[544,1664]{1,0:T(8,128)(2,1)}, bf16[544,1664]{1,0:T(8,128)(2,1)}, u32[]{:S(2)}, u32[]{:S(2)}) collective-permute-start(bf16[544,1664]{1,0:T(8,128)(2,1)} %get-tuple-element.158), channel_id=1, source_target_pairs={{0,1},{1,0},{2,3},{3,2},{4,5},{5,4},{6,7},{7,6},{8,9},{9,8},{10,11... | collective-permute-start | bytes 5431304 | tf_op jit(solution)/shard_map/ppermute | solution.py:556
  451.5 25.6 %collective-permute-start.40 = (bf16[272,1664]{1,0:T(8,128)(2,1)}, bf16[272,1664]{1,0:T(8,128)(2,1)S(1)}, u32[]{:S(2)}, u32[]{:S(2)}) collective-permute-start(bf16[272,1664]{1,0:T(8,128)(2,1)} %get-tuple-element.250), channel_id=1, source_target_pairs={{0,4},{1,5},{2,6},{3,7},{4,0},{5,1},{6,2},{7,3},{8,12},{9,13},{10,... | collective-permute-start | bytes 2715656 | tf_op jit(solution)/shard_map/ppermute | solution.py:556
  453.0 24.2 %collective-permute-start.41 = (bf16[272,1664]{1,0:T(8,128)(2,1)}, bf16[272,1664]{1,0:T(8,128)(2,1)S(1)}, u32[]{:S(2)}, u32[]{:S(2)}) collective-permute-start(bf16[272,1664]{1,0:T(8,128)(2,1)} %get-tuple-element.249), channel_id=1, source_target_pairs={{0,2},{1,3},{2,0},{3,1},{4,6},{5,7},{6,4},{7,5},{8,10},{9,11},{10,... | collective-permute-start | bytes 2715656 | tf_op jit(solution)/shard_map/ppermute | solution.py:556
  485.1 42.0 %collective-permute-start.43 = (bf16[544,1664]{1,0:T(8,128)(2,1)}, bf16[544,1664]{1,0:T(8,128)(2,1)S(1)}, u32[]{:S(2)}, u32[]{:S(2)}) collective-permute-start(bf16[544,1664]{1,0:T(8,128)(2,1)} %pad_maximum_fusion.1.refs_14_), channel_id=1, source_target_pairs={{0,2},{1,3},{2,0},{3,1},{4,6},{5,7},{6,4},{7,5},{8,10},{9,11},{10,... | collective-permute-start | bytes 5431304 | tf_op jit(solution)/shard_map/ppermute | solution.py:556
  490.6 42.1 %collective-permute-start.44 = (bf16[544,1664]{1,0:T(8,128)(2,1)}, bf16[544,1664]{1,0:T(8,128)(2,1)}, u32[]{:S(2)}, u32[]{:S(2)}) collective-permute-start(bf16[544,1664]{1,0:T(8,128)(2,1)} %pad_maximum_fusion.2.refs_15_), channel_id=1, source_target_pairs={{0,4},{1,5},{2,6},{3,7},{4,0},{5,1},{6,2},{7,3},{8,12},{9,13},{10,... | collective-permute-start | bytes 5431304 | tf_op jit(solution)/shard_map/ppermute | solution.py:556
  514.8 24.8 %collective-permute-start.53 = (bf16[544,1664]{1,0:T(8,128)(2,1)}, bf16[544,1664]{1,0:T(8,128)(2,1)}, u32[]{:S(2)}, u32[]{:S(2)}) collective-permute-start(bf16[544,1664]{1,0:T(8,128)(2,1)} %get-tuple-element.175), channel_id=1, source_target_pairs={{0,1},{1,0},{2,3},{3,2},{4,5},{5,4},{6,7},{7,6},{8,9},{9,8},{10,11... | collective-permute-start | bytes 5431304 | tf_op jit(solution)/shard_map/ppermute | solution.py:556
  532.8 28.6 %collective-permute-start.47 = (bf16[512,1536]{1,0:T(8,128)(2,1)}, bf16[512,1536]{1,0:T(8,128)(2,1)}, u32[]{:S(2)}, u32[]{:S(2)}) collective-permute-start(bf16[512,1536]{1,0:T(8,128)(2,1)} %get-tuple-element.171), channel_id=1, source_target_pairs={{0,1},{1,0},{2,3},{3,2},{4,5},{5,4},{6,7},{7,6},{8,9},{9,8},{10,11... | collective-permute-start | bytes 4718600 | tf_op jit(solution)/shard_map/ppermute | solution.py:556
  539.0 26.4 %collective-permute-start.46 = (bf16[512,1536]{1,0:T(8,128)(2,1)S(1)}, bf16[512,1536]{1,0:T(8,128)(2,1)}, u32[]{:S(2)}, u32[]{:S(2)}) collective-permute-start(bf16[512,1536]{1,0:T(8,128)(2,1)S(1)} %copy-done.41), channel_id=1, source_target_pairs={{0,1},{1,0},{2,3},{3,2},{4,5},{5,4},{6,7},{7,6},{8,9},{9,8},{10,11... | collective-permute-start | bytes 4718600 | tf_op jit(solution)/shard_map/ppermute | solution.py:556
  539.6 28.4 %collective-permute-start.50 = (bf16[512,1536]{1,0:T(8,128)(2,1)}, bf16[512,1536]{1,0:T(8,128)(2,1)}, u32[]{:S(2)}, u32[]{:S(2)}) collective-permute-start(bf16[512,1536]{1,0:T(8,128)(2,1)} %get-tuple-element.173), channel_id=1, source_target_pairs={{0,1},{1,0},{2,3},{3,2},{4,5},{5,4},{6,7},{7,6},{8,9},{9,8},{10,11... | collective-permute-start | bytes 4718600 | tf_op jit(solution)/shard_map/ppermute | solution.py:556
  539.7 159.0 %collective-permute-start.45 = (bf16[512,1536]{1,0:T(8,128)(2,1)}, bf16[512,1536]{1,0:T(8,128)(2,1)}, u32[]{:S(2)}, u32[]{:S(2)}) collective-permute-start(bf16[512,1536]{1,0:T(8,128)(2,1)} %get-tuple-element.167), channel_id=1, source_target_pairs={{0,1},{1,0},{2,3},{3,2},{4,5},{5,4},{6,7},{7,6},{8,9},{9,8},{10,11... | collective-permute-start | bytes 4718600 | tf_op jit(solution)/shard_map/ppermute | solution.py:556
  564.9 46.2 %collective-permute-start.48 = (bf16[256,1536]{1,0:T(8,128)(2,1)}, bf16[256,1536]{1,0:T(8,128)(2,1)}, u32[]{:S(2)}, u32[]{:S(2)}) collective-permute-start(bf16[256,1536]{1,0:T(8,128)(2,1)} %get-tuple-element.255), channel_id=1, source_target_pairs={{0,4},{1,5},{2,6},{3,7},{4,0},{5,1},{6,2},{7,3},{8,12},{9,13},{10,... | collective-permute-start | bytes 2359304 | tf_op jit(solution)/shard_map/ppermute | solution.py:556
  608.7 27.2 %collective-permute-start.55 = (bf16[512,1024]{1,0:T(8,128)(2,1)}, bf16[512,1024]{1,0:T(8,128)(2,1)S(1)}, u32[]{:S(2)}, u32[]{:S(2)}) collective-permute-start(bf16[512,1024]{1,0:T(8,128)(2,1)} %slice.317), channel_id=1, source_target_pairs={{8,0},{16,8},{24,16},{9,1},{17,9},{25,17},{10,2},{18,10},{26,18},{... | collective-permute-start | bytes 3145736 | tf_op jit(solution)/shard_map/ppermute | solution.py:1151
  610.0 20.7 %collective-permute-start.51 = (bf16[256,1536]{1,0:T(8,128)(2,1)}, bf16[256,1536]{1,0:T(8,128)(2,1)S(1)}, u32[]{:S(2)}, u32[]{:S(2)}) collective-permute-start(bf16[256,1536]{1,0:T(8,128)(2,1)} %get-tuple-element.256), channel_id=1, source_target_pairs={{0,2},{1,3},{2,0},{3,1},{4,6},{5,7},{6,4},{7,5},{8,10},{9,11},{10,... | collective-permute-start | bytes 2359304 | tf_op jit(solution)/shard_map/ppermute | solution.py:556
  612.6 86.1 %collective-permute-start.49 = (bf16[512,1536]{1,0:T(8,128)(2,1)S(1)}, bf16[512,1536]{1,0:T(8,128)(2,1)}, u32[]{:S(2)}, u32[]{:S(2)}) collective-permute-start(bf16[512,1536]{1,0:T(8,128)(2,1)S(1)} %pad_maximum_fusion.3.refs_1_), channel_id=1, source_target_pairs={{0,2},{1,3},{2,0},{3,1},{4,6},{5,7},{6,4},{7,5},{8,10},{9,11},{10,... | collective-permute-start | bytes 4718600 | tf_op jit(solution)/shard_map/ppermute | solution.py:556
  632.1 66.6 %collective-permute-start.52 = (bf16[512,1536]{1,0:T(8,128)(2,1)}, bf16[512,1536]{1,0:T(8,128)(2,1)}, u32[]{:S(2)}, u32[]{:S(2)}) collective-permute-start(bf16[512,1536]{1,0:T(8,128)(2,1)} %pad_maximum_fusion.4.refs_2_), channel_id=1, source_target_pairs={{0,4},{1,5},{2,6},{3,7},{4,0},{5,1},{6,2},{7,3},{8,12},{9,13},{10,... | collective-permute-start | bytes 4718600 | tf_op jit(solution)/shard_map/ppermute | solution.py:556
  643.3 26.6 %collective-permute-start.56 = (bf16[512,1024]{1,0:T(8,128)(2,1)}, bf16[512,1024]{1,0:T(8,128)(2,1)}, u32[]{:S(2)}, u32[]{:S(2)}) collective-permute-start(bf16[512,1024]{1,0:T(8,128)(2,1)} %tie.30), channel_id=1, source_target_pairs={{8,0},{16,8},{24,16},{9,1},{17,9},{25,17},{10,2},{18,10},{26,18},{... | collective-permute-start | bytes 3145736 | tf_op jit(solution)/shard_map/ppermute | solution.py:1151
  687.1 21.5 %all-to-all-start.1 = ((bf16[32,80,128]{2,1,0:T(8,128)(2,1)}), bf16[32,80,128]{2,1,0:T(8,128)(2,1)}, u32[]{:S(2)}, u32[]{:S(2)}) async-start(bf16[32,80,128]{2,1,0:T(8,128)(2,1)} %pad_maximum_fusion.10), calls=%async_computation.2 | async-start | bytes 1310720 | tf_op jit(solution)/shard_map/all_to_all | solution.py:1185
  (122 other events, 913.4 us)
Sparse Core Ops, SparseCore 0:
  40.1 34.0 all-gather.11
  75.7 64.3 all-gather.13
  183.9 91.5 all-gather.17
  276.9 74.8 all-gather.15
  353.8 49.0 all-gather.19
  405.1 34.5 reduce-scatter.2
  539.2 32.8 reduce-scatter.4

commit v8 on v7

--- a/solution.py
+++ b/solution.py
@@ -998,7 +998,7 @@
     key_tag = jnp.concatenate([block[rows, :rows] for block in kv_blocks[::-1]]).astype(F32).reshape(-1, 1)
     query_tag = (document_number + 1).astype(F32)
 
-    seq_up, seq_down = [over_seq(tie(up_shards[0], kv_blocks[hops]))], [first_down]
+    seq_up, seq_down = [over_seq(tie(up_shards[0], kv_blocks[min(1, hops)]))], [first_down]
     for j in range(1, local_experts):
         seq_up.append(over_seq(tie(up_shards[j], seq_down[j - 1])))
         seq_down.append(over_seq(tie(down_shards[j], seq_up[j - 1])))

time: 731 us -> 722 us (0.988)
  starting transfers between devices: 62.4 us -> 53.7 us
    all_gather x5, waiting for transfers between devices: 21.4 us -> 3.5 us  [over_seq(): return lax.all_gather(shard, 'seq', axis=0)]
    ppermute x53, waiting for transfers between devices: 70.3 us -> 84.8 us  [swap(): return lax.ppermute(array, 'dp', [(i, i ^ bit) for i in range(size)])]
    all_gather x5, starting transfers between devices: 8.96 us -> 0.39 us  [over_seq(): return lax.all_gather(shard, 'seq', axis=0)]
    unnamed x216 -> x222, local copies, waits for them, and re-layouts: 34.1 us -> 33.4 us
  transfers between devices with their start and end apart: 66 -> 66, of which waited for: 17 -> 19; matrix products, arithmetic and copies ran while one was open for 21% -> 21% of each run, Pallas kernels for 44% -> 44%
where the time goes in v8:
time: 722 us; the launch traced here: 712 us
  Pallas kernels  317 us (44%)
  waiting for transfers between devices  130 us (18%)
  local copies, waits for them, and re-layouts  91.5 us (13%)
  starting transfers between devices  53.7 us (7%)
  other arithmetic  50.7 us (7%)
  matrix products  31.6 us (4%)
  blocking collectives  20.3 us (3%)
  between operations  16.9 us (2%)
    pallas_call x8, Pallas kernels, expert_call(): pl.pallas_call(functools.partial(expert_kernel, *(count, splits, experts,...  198 us
    ppermute x53, waiting for transfers between devices, swap(): return lax.ppermute(array, 'dp', [(i, i ^ bit) for i in range(size)])  84.8 us
    unnamed x222, local copies, waits for them, and re-layouts  33.4 us
    pallas_call x1, Pallas kernels, attend_back(): pl.pallas_call(functools.partial(attend_back_kernel, spans, hops * rows,...  33.4 us
    ppermute x53, starting transfers between devices, swap(): return lax.ppermute(array, 'dp', [(i, i ^ bit) for i in range(size)])  33.2 us
    pallas_call x1, Pallas kernels, attend(): pl.pallas_call(functools.partial(attend_kernel, spans, hops * rows, len(d...  23.7 us
    dot_general x10, matrix products, dot_nn(): return jnp.dot(left, right, preferred_element_type=F32)  23.1 us
    all_gather x1, blocking collectives, over_seq(): return lax.all_gather(shard, 'seq', axis=0)  20.3 us
  transfers between devices with their start and end apart: 66, of which 19 were waited for; matrix products, arithmetic and copies ran while one was open for 21% of the time, Pallas kernels for 44%

profile of v8, /device:TPU:0, one launch (start us, length us, event | category | flops | bytes accessed | tf_op | source)
XLA Modules:
  0.0 711.6 jit_solution(6311550235577213000)
XLA Ops:
  7.2 3.0 collective-permute-start
  15.1 3.4 all-to-all-start
  19.6 20.3 %all-gather = bf16[192,2048]{1,0:T(8,128)(2,1)} all-gather(bf16[48,2048]{1,0:T(8,128)(2,1)S(1)} %fusion.20), channel_id=2, replica_groups=mesh['seq'=4,'dp'=8] {'seq'}, dimensions={0}, use_global_device_ids=true | all-gather | bytes 983040 | tf_op jit(solution)/shard_map/all_gather | solution.py:890
  43.1 5.2 all-to-all-done.refs_3_
  51.2 17.2 %collective-permute-done.3.refs_2_ = bf16[4,48,2048]{2,1,0:T(8,128)(2,1)S(1)} collective-permute-done((bf16[4,48,2048]{2,1,0:T(8,128)(2,1)}, bf16[4,48,2048]{2,1,0:T(8,128)(2,1)S(1)}, u32[]{:S(2)}, u32[]{:S(2)}) %collective-permute-start.3) | collective-permute-done | bytes 786464 | tf_op jit(solution)/shard_map/ppermute | solution.py:556
  76.2 3.0 collective-permute-done.8.refs_7_.refs_3_
  79.2 3.2 collective-permute-done.7.refs_6_.refs_2_
  88.9 5.6 assemble.2
  101.4 6.5 collective-permute-done.11.refs_1_.refs_8_.refs_7_
  109.9 4.0 fusion.5
  116.0 3.5 collective-permute-start.22
  120.5 2.5 fusion.49
  128.0 12.3 %collective-permute-done.16.refs_4_.refs_2_ = bf16[4,48,3584]{2,1,0:T(8,128)(2,1)} collective-permute-done((bf16[4,48,3584]{2,1,0:T(8,128)(2,1)}, bf16[4,48,3584]{2,1,0:T(8,128)(2,1)}, u32[]{:S(2)}, u32[]{:S(2)}) %collective-permute-start.16) | collective-permute-done | bytes 1376288 | tf_op jit(solution)/shard_map/ppermute | solution.py:556
  145.0 8.1 %collective-permute-done.22.refs_0_ = bf16[528,1024]{1,0:T(8,128)(2,1)S(1)} collective-permute-done((bf16[528,1024]{1,0:T(8,128)(2,1)}, bf16[528,1024]{1,0:T(8,128)(2,1)S(1)}, u32[]{:S(2)}, u32[]{:S(2)}) %collective-permute-start.22) | collective-permute-done | bytes 1081376 | tf_op jit(solution)/shard_map/ppermute | solution.py:995
  154.1 5.3 collective-permute-start.23
  159.3 3.4 constant_dynamic-slice_fusion.10
  172.4 12.1 %collective-permute-done.23 = bf16[528,1024]{1,0:T(8,128)(2,1)} collective-permute-done((bf16[528,1024]{1,0:T(8,128)(2,1)}, bf16[528,1024]{1,0:T(8,128)(2,1)}, u32[]{:S(2)}, u32[]{:S(2)}) %collective-permute-start.23) | collective-permute-done | bytes 1081376 | tf_op jit(solution)/shard_map/ppermute | solution.py:995
  192.4 8.4 %assemble.3 = (bf16[4,8,1,48,1536]{4,3,2,1,0:T(8,128)(2,1)}, bf16[4,8,1,48,512]{4,3,2,1,0:T(8,128)(2,1)}, bf16[4,8,1,48,1536]{4,3,2,1,0:T(8,128)(2,1)}) custom-call(s32[1]{0:T(128)} %bitcast.1.me_ref, bf16[4,48,3584]{2,1,0:T(8,128)(2,1)} %tie.19.refs_0_, bf16[4,48,3584]{2,1,0:T(8,128)(2,1)} %collective-permute-done.13.refs_1_, ...), custom_call_target="tpu_custom_call" | custom-call | tf_op jit(solution)/shard_map/assemble/pallas_call | solution.py:629
  204.3 3.9 fusion.4.q_ref
  208.1 23.7 %attend.1 = (bf16[512,1536]{1,0:T(8,128)(2,1)}, f32[4,3,512]{2,1,0:T(4,128)}) custom-call(bf16[512,1536]{1,0:T(8,128)(2,1)} %fusion.4.q_ref, bf16[1536,1024]{1,0:T(8,128)(2,1)} %pad_maximum_fusion.k_ref.v_ref, bf16[1536,1024]{1,0:T(8,128)(2,1)} %pad_maximum_fusion.k_ref.v_ref, f32[1,512]{1,0:T(1,128)} %get-tuple-element.283.qt_ref, ...), custom_call_target="tpu_custom_call" | custom-call | flops 26530500608 | bytes 1000000 | tf_op jit(solution)/shard_map/attend/pallas_call | solution.py:96
  235.6 4.8 multiply_reduce_fusion
  257.4 2.8 all-gather.18.cloned.1.call-done.refs_1_
  260.2 25.6 %expert.8 = (bf16[512,1536]{1,0:T(8,128)(2,1)}, bf16[512,1536]{1,0:T(8,128)(2,1)}, bf16[544,1664]{1,0:T(8,128)(2,1)}, bf16[544,1664]{1,0:T(8,128)(2,1)}, f32[153...) custom-call(s32[2]{0:T(128)} %pad_add_fusion.1.refs_0_, ...), custom_call_target="tpu_custom_call" | custom-call | flops 27683999744 | bytes 1000000 | tf_op jit(solution)/shard_map/expert/pallas_call | solution.py:522
  285.8 8.1 %collective-permute-done.30.refs_0_ = bf16[512,1664]{1,0:T(8,128)(2,1)S(1)} collective-permute-done((bf16[512,1664]{1,0:T(8,128)(2,1)}, bf16[512,1664]{1,0:T(8,128)(2,1)S(1)}, u32[]{:S(2)}, u32[]{:S(2)}) %collective-permute-start.30) | collective-permute-done | bytes 1703968 | tf_op jit(solution)/shard_map/ppermute | solution.py:556
  303.6 27.2 %expert.9 = (bf16[512,1536]{1,0:T(8,128)(2,1)}, bf16[512,1536]{1,0:T(8,128)(2,1)}, bf16[544,1664]{1,0:T(8,128)(2,1)}, bf16[544,1664]{1,0:T(8,128)(2,1)}, f32[153...) custom-call(s32[2]{0:T(128)} %pad_add_fusion.1.refs_0_, ...), custom_call_target="tpu_custom_call" | custom-call | flops 27683999744 | bytes 1000000 | tf_op jit(solution)/shard_map/expert/pallas_call | solution.py:522
  332.5 27.3 %expert.10 = (bf16[512,1536]{1,0:T(8,128)(2,1)}, bf16[512,1536]{1,0:T(8,128)(2,1)}, bf16[544,1664]{1,0:T(8,128)(2,1)}, bf16[544,1664]{1,0:T(8,128)(2,1)}, f32[15...) custom-call(s32[2]{0:T(128)} %pad_add_fusion.1.refs_0_, ...), custom_call_target="tpu_custom_call" | custom-call | flops 27683999744 | bytes 1000000 | tf_op jit(solution)/shard_map/expert/pallas_call | solution.py:522
  361.1 27.7 %expert.11 = (bf16[512,1536]{1,0:T(8,128)(2,1)}, bf16[512,1536]{1,0:T(8,128)(2,1)}, bf16[544,1664]{1,0:T(8,128)(2,1)}, bf16[544,1664]{1,0:T(8,128)(2,1)}, bf16[4,1568,128]{2,1,0:T(8,128)(2,1)}) custom-call(s32[2]{0:T(128)} %pad_add_fusion.1.refs_0_, bf16[1536,1536]{1,0:T(8,128)(2,1)} %all-gather.18.cloned.1.call-done.refs_1_, ...), custom_call_target="tpu_custom_call" | custom-call | flops 27683999744 | bytes 1000000 | tf_op jit(solution)/shard_map/expert/pallas_call | solution.py:522
  389.6 21.0 %expert.12 = (bf16[512,1536]{1,0:T(8,128)(2,1)}, bf16[512,1536]{1,0:T(8,128)(2,1)}, bf16[544,1664]{1,0:T(8,128)(2,1)}, bf16[544,1664]{1,0:T(8,128)(2,1)}, f32[15...) custom-call(s32[2]{0:T(128)} %pad_add_fusion.refs_0_, ...), custom_call_target="tpu_custom_call" | custom-call | flops 27683999744 | bytes 1000000 | tf_op jit(solution)/shard_map/expert/pallas_call | solution.py:522
  410.6 22.6 %expert.13 = (bf16[512,1536]{1,0:T(8,128)(2,1)}, bf16[512,1536]{1,0:T(8,128)(2,1)}, bf16[544,1664]{1,0:T(8,128)(2,1)}, bf16[544,1664]{1,0:T(8,128)(2,1)}, f32[15...) custom-call(s32[2]{0:T(128)} %pad_add_fusion.refs_0_, ...), custom_call_target="tpu_custom_call" | custom-call | flops 27683999744 | bytes 1000000 | tf_op jit(solution)/shard_map/expert/pallas_call | solution.py:522
  433.8 2.5 add_convert_fusion.2.refs_15_
  441.0 22.7 %expert.14 = (bf16[512,1536]{1,0:T(8,128)(2,1)}, bf16[512,1536]{1,0:T(8,128)(2,1)}, bf16[544,1664]{1,0:T(8,128)(2,1)}, bf16[544,1664]{1,0:T(8,128)(2,1)}, f32[15...) custom-call(s32[2]{0:T(128)} %pad_add_fusion.refs_0_, ...), custom_call_target="tpu_custom_call" | custom-call | flops 27683999744 | bytes 1000000 | tf_op jit(solution)/shard_map/expert/pallas_call | solution.py:522
  477.8 23.6 %expert.15 = (bf16[512,1536]{1,0:T(8,128)(2,1)}, bf16[512,1536]{1,0:T(8,128)(2,1)}, bf16[544,1664]{1,0:T(8,128)(2,1)}, bf16[544,1664]{1,0:T(8,128)(2,1)}, bf16[4,1536,128]{2,1,0:T(8,128)(2,1)}) custom-call(s32[2]{0:T(128)} %pad_add_fusion.refs_0_, bf16[1536,1280]{1,0:T(8,128)(2,1)} %all-gather.16.cloned.1.call-done.refs_1_, bf16[4,128,2304]{2,1,0:T(8,128)(2,1)} %bitcast.239, ...), custom_call_target="tpu_custom_call" | custom-call | flops 27683999744 | bytes 1000000 | tf_op jit(solution)/shard_map/expert/pallas_call | solution.py:522
  504.0 9.6 %collective-permute-done.43.refs_4_.refs_1_.from_x = bf16[544,1664]{1,0:T(8,128)(2,1)S(1)} collective-permute-done((bf16[544,1664]{1,0:T(8,128)(2,1)}, bf16[544,1664]{1,0:T(8,128)(2,1)S(1)}, u32[]{:S(2)}, u32[]{:S(2)}) %collective-permute-start.43) | collective-permute-done | bytes 1810464 | tf_op jit(solution)/shard_map/ppermute | solution.py:556
  513.6 5.7 collective-permute-done.44.refs_5_.refs_2_.from_y
  527.3 18.2 %turn.1 = (f32[512,1536]{1,0:T(8,128)}, bf16[512,1536]{1,0:T(8,128)(2,1)}, bf16[512,16]{1,0:T(8,128)(2,1)}, bf16[512,32]{1,0:T(8,128)(2,1)}, bf16[512,16]{1,0:T(...) custom-call(bf16[544,1664]{1,0:T(8,128)(2,1)} %get-tuple-element.174.own, ...), custom_call_target="tpu_custom_call" | custom-call | flops 4614000128 | bytes 1000000 | tf_op jit(solution)/shard_map/turn/pallas_call | solution.py:694
  559.4 33.4 %attend_back.1 = (bf16[512,1536]{1,0:T(8,128)(2,1)}, bf16[1536,1024]{1,0:T(8,128)(2,1)}) custom-call(bf16[512,1536]{1,0:T(8,128)(2,1)} %fusion.4.q_ref, bf16[1536,1024]{1,0:T(8,128)(2,1)} %pad_maximum_fusion.k_ref.v_ref, bf16[1536,1024]{1,0:T(8,128)(2,1)} %pad_maximum_fusion.k_ref.v_ref, bf16[512,1536]{1,0:T(8,128)(2,1)} %get-tuple-element.177.g_ref, ...), custom_call_target="tpu_custom_call" | custom-call | flops 9228000256 | bytes 1000000 | tf_op jit(solution)/shard_map/attend_back/pallas_call | solution.py:159
  592.7 2.4 slice.317
  600.1 17.0 %collective-permute-done.51 = bf16[256,1536]{1,0:T(8,128)(2,1)S(1)} collective-permute-done((bf16[256,1536]{1,0:T(8,128)(2,1)}, bf16[256,1536]{1,0:T(8,128)(2,1)S(1)}, u32[]{:S(2)}, u32[]{:S(2)}) %collective-permute-start.51) | collective-permute-done | bytes 786464 | tf_op jit(solution)/shard_map/ppermute | solution.py:556
  619.3 4.3 collective-permute-done.55.rest_0_.refs_2_
  628.5 2.6 add_convert_fusion.9.refs_0_
  632.6 5.2 middle.1
  642.1 9.7 %query_back.1 = (f32[512,1536]{1,0:T(8,128)}, f32[1536,16]{1,0:T(8,128)}, f32[16,1536]{1,0:T(8,128)}) custom-call(bf16[512,1536]{1,0:T(8,128)(2,1)} %get-tuple-element.181.grad_q, bf16[512,1536]{1,0:T(8,128)(2,1)} %copy-done.9, bf16[512,16]{1,0:T(8,128)(2,1)} %constant_dynamic-slice_fusion.2.low_q, bf16[1536,1536]{1,0:T(8,128)(2,1)} %bitcast.189, ...), custom_call_target="tpu_custom_call" | custom-call | flops 115350000 | bytes 1000000 | tf_op jit(solution)/shard_map/query_back/pallas_call | solution.py:717
  651.9 6.7 collective-permute-done.56
  658.5 2.9 add_convert_fusion.8.grad_kv
  661.4 12.3 %last.1 = (f32[512,1536]{1,0:T(8,128)}, bf16[1536,128]{1,0:T(8,128)(2,1)}, bf16[32,32,128]{2,1,0:T(8,128)(2,1)}) custom-call(bf16[512,1024]{1,0:T(8,128)(2,1)} %add_convert_fusion.8.grad_kv, bf16[512,1536]{1,0:T(8,128)(2,1)} %copy-done.9, bf16[512,32]{1,0:T(8,128)(2,1)} %pad_maximum_fusion.16.low_kv, bf16[1536,1024]{1,0:T(8,128)(2,1)} %bitcast.198, ...), custom_call_target="tpu_custom_call" | custom-call | flops 2307000064 | bytes 1000000 | tf_op jit(solution)/shard_map/last/pallas_call | solution.py:788
  675.8 5.0 all-to-all-start.1
  688.9 4.6 fusion.7
  693.5 5.2 all-to-all-done.1.flat
  (495 shorter events, 179.2 us)
Async XLA Ops:
  7.2 41.2 %collective-permute-start = (bf16[512,1536]{1,0:T(8,128)(2,1)}, bf16[512,1536]{1,0:T(8,128)(2,1)}, u32[]{:S(2)}, u32[]{:S(2)}) collective-permute-start(bf16[512,1536]{1,0:T(8,128)(2,1)} %bitcast.168), channel_id=1, source_target_pairs={{0,2},{1,3},{2,0},{3,1},{4,6},{5,7},{6,4},{7,5},{8,10},{9,11},{10,... | collective-permute-start | bytes 4718600 | tf_op jit(solution)/shard_map/ppermute | solution.py:556
  10.2 38.2 %collective-permute-start.1 = (bf16[512,1536]{1,0:T(8,128)(2,1)}, bf16[512,1536]{1,0:T(8,128)(2,1)}, u32[]{:S(2)}, u32[]{:S(2)}) collective-permute-start(bf16[512,1536]{1,0:T(8,128)(2,1)} %bitcast.169), channel_id=1, source_target_pairs={{0,4},{1,5},{2,6},{3,7},{4,0},{5,1},{6,2},{7,3},{8,12},{9,13},{10,... | collective-permute-start | bytes 4718600 | tf_op jit(solution)/shard_map/ppermute | solution.py:556
  15.1 33.3 %all-to-all-start = ((bf16[8,48,256]{2,1,0:T(8,128)(2,1)}), bf16[8,48,256]{2,1,0:T(8,128)(2,1)S(1)}, u32[]{:S(2)}, u32[]{:S(2)}) async-start(bf16[8,48,256]{2,1,0:T(8,128)(2,1)} %copy.182), calls=%async_computation | async-start | bytes 393216 | tf_op jit(solution)/shard_map/all_to_all | solution.py:933
  18.5 82.9 %all-gather.12.cloned.1.call-start = ((), (), s32[]{:S(2)}) async-start(), calls=%async_computation.6 | async-start | bytes 1720320 | tf_op jit(solution)/shard_map/all_gather | solution.py:890
  40.0 113.1 %all-gather.14.cloned.1.call-start = ((), (), s32[]{:S(2)}) async-start(), calls=%async_computation.7 | async-start | bytes 3604480 | tf_op jit(solution)/shard_map/all_gather | solution.py:890
  50.1 20.7 %collective-permute-start.5 = (bf16[4,48,2048]{2,1,0:T(8,128)(2,1)}, bf16[4,48,2048]{2,1,0:T(8,128)(2,1)S(1)}, u32[]{:S(2)}, u32[]{:S(2)}) collective-permute-start(bf16[4,48,2048]{2,1,0:T(8,128)(2,1)} %tie.16.refs_0_), channel_id=1, source_target_pairs={{0,4},{1,5},{2,6},{3,7},{4,0},{5,1},{6,2},{7,3},{8,12},{9,13},{10,... | collective-permute-start | bytes 2359304 | tf_op jit(solution)/shard_map/ppermute | solution.py:556
  73.2 187.0 %all-gather.18.cloned.1.call-start = ((), (), s32[]{:S(2)}) async-start(), calls=%async_computation.9 | async-start | bytes 5898240 | tf_op jit(solution)/shard_map/all_gather | solution.py:890
  87.6 20.3 %collective-permute-start.11 = (bf16[256,1536]{1,0:T(8,128)(2,1)}, bf16[256,1536]{1,0:T(8,128)(2,1)}, u32[]{:S(2)}, u32[]{:S(2)}) collective-permute-start(bf16[256,1536]{1,0:T(8,128)(2,1)} %slice.266), channel_id=1, source_target_pairs={{0,2},{1,3},{2,0},{3,1},{4,6},{5,7},{6,4},{7,5},{8,10},{9,11},{10,... | collective-permute-start | bytes 2359304 | tf_op jit(solution)/shard_map/ppermute | solution.py:556
  88.5 20.0 %collective-permute-start.12 = (bf16[256,1536]{1,0:T(8,128)(2,1)}, bf16[256,1536]{1,0:T(8,128)(2,1)}, u32[]{:S(2)}, u32[]{:S(2)}) collective-permute-start(bf16[256,1536]{1,0:T(8,128)(2,1)} %slice.267), channel_id=1, source_target_pairs={{0,4},{1,5},{2,6},{3,7},{4,0},{5,1},{6,2},{7,3},{8,12},{9,13},{10,... | collective-permute-start | bytes 2359304 | tf_op jit(solution)/shard_map/ppermute | solution.py:556
  108.5 31.8 %collective-permute-start.16 = (bf16[4,48,3584]{2,1,0:T(8,128)(2,1)}, bf16[4,48,3584]{2,1,0:T(8,128)(2,1)}, u32[]{:S(2)}, u32[]{:S(2)}) collective-permute-start(bf16[4,48,3584]{2,1,0:T(8,128)(2,1)} %tie.19.refs_0_), channel_id=1, source_target_pairs={{0,4},{1,5},{2,6},{3,7},{4,0},{5,1},{6,2},{7,3},{8,12},{9,13},{10,... | collective-permute-start | bytes 4128776 | tf_op jit(solution)/shard_map/ppermute | solution.py:556
  108.8 33.8 %collective-permute-start.14 = (bf16[4,48,3584]{2,1,0:T(8,128)(2,1)}, bf16[4,48,3584]{2,1,0:T(8,128)(2,1)}, u32[]{:S(2)}, u32[]{:S(2)}) collective-permute-start(bf16[4,48,3584]{2,1,0:T(8,128)(2,1)} %tie.19.refs_0_), channel_id=1, source_target_pairs={{0,2},{1,3},{2,0},{3,1},{4,6},{5,7},{6,4},{7,5},{8,10},{9,11},{10,... | collective-permute-start | bytes 4128776 | tf_op jit(solution)/shard_map/ppermute | solution.py:556
  116.0 37.1 %collective-permute-start.22 = (bf16[528,1024]{1,0:T(8,128)(2,1)}, bf16[528,1024]{1,0:T(8,128)(2,1)S(1)}, u32[]{:S(2)}, u32[]{:S(2)}) collective-permute-start(bf16[528,1024]{1,0:T(8,128)(2,1)} %pad_maximum_fusion.6), channel_id=1, source_target_pairs={{0,8},{8,16},{16,24},{1,9},{9,17},{17,25},{2,10},{10,18},{18,26},{... | collective-permute-start | bytes 3244040 | tf_op jit(solution)/shard_map/ppermute | solution.py:995
  141.5 21.8 %collective-permute-start.18 = (bf16[2,48,3584]{2,1,0:T(8,128)(2,1)S(1)}, bf16[2,48,3584]{2,1,0:T(8,128)(2,1)}, u32[]{:S(2)}, u32[]{:S(2)}) collective-permute-start(bf16[2,48,3584]{2,1,0:T(8,128)(2,1)S(1)} %slice.344), channel_id=1, source_target_pairs={{0,2},{1,3},{2,0},{3,1},{4,6},{5,7},{6,4},{7,5},{8,10},{9,11},{10,... | collective-permute-start | bytes 2064392 | tf_op jit(solution)/shard_map/ppermute | solution.py:556
  144.7 21.5 %collective-permute-start.19 = (bf16[2,48,3584]{2,1,0:T(8,128)(2,1)}, bf16[2,48,3584]{2,1,0:T(8,128)(2,1)}, u32[]{:S(2)}, u32[]{:S(2)}) collective-permute-start(bf16[2,48,3584]{2,1,0:T(8,128)(2,1)} %slice.345), channel_id=1, source_target_pairs={{0,4},{1,5},{2,6},{3,7},{4,0},{5,1},{6,2},{7,3},{8,12},{9,13},{10,... | collective-permute-start | bytes 2064392 | tf_op jit(solution)/shard_map/ppermute | solution.py:556
  154.1 30.4 %collective-permute-start.23 = (bf16[528,1024]{1,0:T(8,128)(2,1)}, bf16[528,1024]{1,0:T(8,128)(2,1)}, u32[]{:S(2)}, u32[]{:S(2)}) collective-permute-start(bf16[528,1024]{1,0:T(8,128)(2,1)} %tie.21.refs_1_), channel_id=1, source_target_pairs={{0,8},{8,16},{16,24},{1,9},{9,17},{17,25},{2,10},{10,18},{18,26},{... | collective-permute-start | bytes 3244040 | tf_op jit(solution)/shard_map/ppermute | solution.py:995
  162.8 26.3 %collective-permute-start.13 = (bf16[4,48,3584]{2,1,0:T(8,128)(2,1)}, bf16[4,48,3584]{2,1,0:T(8,128)(2,1)}, u32[]{:S(2)}, u32[]{:S(2)}) collective-permute-start(bf16[4,48,3584]{2,1,0:T(8,128)(2,1)} %tie.19.refs_0_), channel_id=1, source_target_pairs={{0,1},{1,0},{2,3},{3,2},{4,5},{5,4},{6,7},{7,6},{8,9},{9,8},{10,11... | collective-permute-start | bytes 4128776 | tf_op jit(solution)/shard_map/ppermute | solution.py:556
  162.8 29.5 %collective-permute-start.15 = (bf16[4,48,3584]{2,1,0:T(8,128)(2,1)}, bf16[4,48,3584]{2,1,0:T(8,128)(2,1)}, u32[]{:S(2)}, u32[]{:S(2)}) collective-permute-start(bf16[4,48,3584]{2,1,0:T(8,128)(2,1)} %collective-permute-done.14.refs_2_.refs_1_), channel_id=1, source_target_pairs={{0,1},{1,0},{2,3},{3,2},{4,5},{5,4},{6,7},{7,6},{8,9},{9,8},{10,11... | collective-permute-start | bytes 4128776 | tf_op jit(solution)/shard_map/ppermute | solution.py:556
  163.3 29.1 %collective-permute-start.17 = (bf16[4,48,3584]{2,1,0:T(8,128)(2,1)}, bf16[4,48,3584]{2,1,0:T(8,128)(2,1)}, u32[]{:S(2)}, u32[]{:S(2)}) collective-permute-start(bf16[4,48,3584]{2,1,0:T(8,128)(2,1)} %collective-permute-done.16.refs_4_.refs_2_), channel_id=1, source_target_pairs={{0,1},{1,0},{2,3},{3,2},{4,5},{5,4},{6,7},{7,6},{8,9},{9,8},{10,11... | collective-permute-start | bytes 4128776 | tf_op jit(solution)/shard_map/ppermute | solution.py:556
  166.1 23.5 %collective-permute-start.20 = (bf16[2,48,3584]{2,1,0:T(8,128)(2,1)}, bf16[2,48,3584]{2,1,0:T(8,128)(2,1)}, u32[]{:S(2)}, u32[]{:S(2)}) collective-permute-start(bf16[2,48,3584]{2,1,0:T(8,128)(2,1)} %collective-permute-done.18.refs_6_), channel_id=1, source_target_pairs={{0,1},{1,0},{2,3},{3,2},{4,5},{5,4},{6,7},{7,6},{8,9},{9,8},{10,11... | collective-permute-start | bytes 2064392 | tf_op jit(solution)/shard_map/ppermute | solution.py:556
  171.7 217.2 %all-gather.16.cloned.1.call-start = ((), (), s32[]{:S(2)}) async-start(), calls=%async_computation.8 | async-start | bytes 4915200 | tf_op jit(solution)/shard_map/all_gather | solution.py:890
  250.3 139.2 %all-gather.20.cloned.1.call-start = ((), (), s32[]{:S(2)}) async-start(), calls=%async_computation.10 | async-start | bytes 2949120 | tf_op jit(solution)/shard_map/all_gather | solution.py:890
  254.2 39.7 %collective-permute-start.30 = (bf16[512,1664]{1,0:T(8,128)(2,1)}, bf16[512,1664]{1,0:T(8,128)(2,1)S(1)}, u32[]{:S(2)}, u32[]{:S(2)}) collective-permute-start(bf16[512,1664]{1,0:T(8,128)(2,1)} %concatenate.98.refs_4_.refs_3_), channel_id=1, source_target_pairs={{0,2},{1,3},{2,0},{3,1},{4,6},{5,7},{6,4},{7,5},{8,10},{9,11},{10,... | collective-permute-start | bytes 5111816 | tf_op jit(solution)/shard_map/ppermute | solution.py:556
  255.9 39.6 %collective-permute-start.31 = (bf16[512,1664]{1,0:T(8,128)(2,1)}, bf16[512,1664]{1,0:T(8,128)(2,1)}, u32[]{:S(2)}, u32[]{:S(2)}) collective-permute-start(bf16[512,1664]{1,0:T(8,128)(2,1)} %concatenate.98.refs_4_.refs_3_), channel_id=1, source_target_pairs={{0,4},{1,5},{2,6},{3,7},{4,0},{5,1},{6,2},{7,3},{8,12},{9,13},{10,... | collective-permute-start | bytes 5111816 | tf_op jit(solution)/shard_map/ppermute | solution.py:556
  297.4 35.2 %collective-permute-start.32 = (bf16[512,1664]{1,0:T(8,128)(2,1)}, bf16[512,1664]{1,0:T(8,128)(2,1)}, u32[]{:S(2)}, u32[]{:S(2)}) collective-permute-start(bf16[512,1664]{1,0:T(8,128)(2,1)} %get-tuple-element.118.refs_4_.refs_3_), channel_id=1, source_target_pairs={{0,1},{1,0},{2,3},{3,2},{4,5},{5,4},{6,7},{7,6},{8,9},{9,8},{10,11... | collective-permute-start | bytes 5111816 | tf_op jit(solution)/shard_map/ppermute | solution.py:556
  300.6 30.2 %collective-permute-start.34 = (bf16[256,1664]{1,0:T(8,128)(2,1)}, bf16[256,1664]{1,0:T(8,128)(2,1)S(1)}, u32[]{:S(2)}, u32[]{:S(2)}) collective-permute-start(bf16[256,1664]{1,0:T(8,128)(2,1)} %slice.299), channel_id=1, source_target_pairs={{0,2},{1,3},{2,0},{3,1},{4,6},{5,7},{6,4},{7,5},{8,10},{9,11},{10,... | collective-permute-start | bytes 2555912 | tf_op jit(solution)/shard_map/ppermute | solution.py:556
  302.0 28.8 %collective-permute-start.35 = (bf16[256,1664]{1,0:T(8,128)(2,1)}, bf16[256,1664]{1,0:T(8,128)(2,1)S(1)}, u32[]{:S(2)}, u32[]{:S(2)}) collective-permute-start(bf16[256,1664]{1,0:T(8,128)(2,1)} %slice.300), channel_id=1, source_target_pairs={{0,4},{1,5},{2,6},{3,7},{4,0},{5,1},{6,2},{7,3},{8,12},{9,13},{10,... | collective-permute-start | bytes 2555912 | tf_op jit(solution)/shard_map/ppermute | solution.py:556
  303.5 160.2 %reduce-scatter.3.cloned.1.call-start = ((), (), s32[]{:S(2)}) async-start(), calls=%async_computation.4 | async-start | bytes 2007040 | tf_op jit(solution)/shard_map/reduce_scatter | solution.py:1108
  332.0 27.8 %collective-permute-start.36 = (bf16[256,1664]{1,0:T(8,128)(2,1)}, bf16[256,1664]{1,0:T(8,128)(2,1)S(1)}, u32[]{:S(2)}, u32[]{:S(2)}) collective-permute-start(bf16[256,1664]{1,0:T(8,128)(2,1)} %get-tuple-element.136.refs_4_.refs_3_), channel_id=1, source_target_pairs={{0,1},{1,0},{2,3},{3,2},{4,5},{5,4},{6,7},{7,6},{8,9},{9,8},{10,11... | collective-permute-start | bytes 2555912 | tf_op jit(solution)/shard_map/ppermute | solution.py:556
  332.0 27.9 %collective-permute-start.37 = (bf16[256,1664]{1,0:T(8,128)(2,1)}, bf16[256,1664]{1,0:T(8,128)(2,1)S(1)}, u32[]{:S(2)}, u32[]{:S(2)}) collective-permute-start(bf16[256,1664]{1,0:T(8,128)(2,1)} %get-tuple-element.137.refs_5_.refs_4_), channel_id=1, source_target_pairs={{0,1},{1,0},{2,3},{3,2},{4,5},{5,4},{6,7},{7,6},{8,9},{9,8},{10,11... | collective-permute-start | bytes 2555912 | tf_op jit(solution)/shard_map/ppermute | solution.py:556
  388.8 230.5 %reduce-scatter.5.cloned.1.call-start = ((), (), s32[]{:S(2)}) async-start(), calls=%async_computation.5 | async-start | bytes 1966080 | tf_op jit(solution)/shard_map/reduce_scatter | solution.py:1108
  410.5 23.2 %collective-permute-start.38 = (bf16[544,1664]{1,0:T(8,128)(2,1)}, bf16[544,1664]{1,0:T(8,128)(2,1)}, u32[]{:S(2)}, u32[]{:S(2)}) collective-permute-start(bf16[544,1664]{1,0:T(8,128)(2,1)} %get-tuple-element.154), channel_id=1, source_target_pairs={{0,1},{1,0},{2,3},{3,2},{4,5},{5,4},{6,7},{7,6},{8,9},{9,8},{10,11... | collective-permute-start | bytes 5431304 | tf_op jit(solution)/shard_map/ppermute | solution.py:556
  433.2 33.6 %collective-permute-start.39 = (bf16[544,1664]{1,0:T(8,128)(2,1)}, bf16[544,1664]{1,0:T(8,128)(2,1)}, u32[]{:S(2)}, u32[]{:S(2)}) collective-permute-start(bf16[544,1664]{1,0:T(8,128)(2,1)} %get-tuple-element.158), channel_id=1, source_target_pairs={{0,1},{1,0},{2,3},{3,2},{4,5},{5,4},{6,7},{7,6},{8,9},{9,8},{10,11... | collective-permute-start | bytes 5431304 | tf_op jit(solution)/shard_map/ppermute | solution.py:556
  438.1 25.6 %collective-permute-start.40 = (bf16[272,1664]{1,0:T(8,128)(2,1)}, bf16[272,1664]{1,0:T(8,128)(2,1)S(1)}, u32[]{:S(2)}, u32[]{:S(2)}) collective-permute-start(bf16[272,1664]{1,0:T(8,128)(2,1)} %get-tuple-element.250), channel_id=1, source_target_pairs={{0,4},{1,5},{2,6},{3,7},{4,0},{5,1},{6,2},{7,3},{8,12},{9,13},{10,... | collective-permute-start | bytes 2715656 | tf_op jit(solution)/shard_map/ppermute | solution.py:556
  439.6 24.2 %collective-permute-start.41 = (bf16[272,1664]{1,0:T(8,128)(2,1)}, bf16[272,1664]{1,0:T(8,128)(2,1)S(1)}, u32[]{:S(2)}, u32[]{:S(2)}) collective-permute-start(bf16[272,1664]{1,0:T(8,128)(2,1)} %get-tuple-element.249), channel_id=1, source_target_pairs={{0,2},{1,3},{2,0},{3,1},{4,6},{5,7},{6,4},{7,5},{8,10},{9,11},{10,... | collective-permute-start | bytes 2715656 | tf_op jit(solution)/shard_map/ppermute | solution.py:556
  471.6 42.0 %collective-permute-start.43 = (bf16[544,1664]{1,0:T(8,128)(2,1)}, bf16[544,1664]{1,0:T(8,128)(2,1)S(1)}, u32[]{:S(2)}, u32[]{:S(2)}) collective-permute-start(bf16[544,1664]{1,0:T(8,128)(2,1)} %pad_maximum_fusion.1.refs_14_), channel_id=1, source_target_pairs={{0,2},{1,3},{2,0},{3,1},{4,6},{5,7},{6,4},{7,5},{8,10},{9,11},{10,... | collective-permute-start | bytes 5431304 | tf_op jit(solution)/shard_map/ppermute | solution.py:556
  477.2 42.1 %collective-permute-start.44 = (bf16[544,1664]{1,0:T(8,128)(2,1)}, bf16[544,1664]{1,0:T(8,128)(2,1)}, u32[]{:S(2)}, u32[]{:S(2)}) collective-permute-start(bf16[544,1664]{1,0:T(8,128)(2,1)} %pad_maximum_fusion.2.refs_15_), channel_id=1, source_target_pairs={{0,4},{1,5},{2,6},{3,7},{4,0},{5,1},{6,2},{7,3},{8,12},{9,13},{10,... | collective-permute-start | bytes 5431304 | tf_op jit(solution)/shard_map/ppermute | solution.py:556
  501.4 24.9 %collective-permute-start.53 = (bf16[544,1664]{1,0:T(8,128)(2,1)}, bf16[544,1664]{1,0:T(8,128)(2,1)}, u32[]{:S(2)}, u32[]{:S(2)}) collective-permute-start(bf16[544,1664]{1,0:T(8,128)(2,1)} %get-tuple-element.175), channel_id=1, source_target_pairs={{0,1},{1,0},{2,3},{3,2},{4,5},{5,4},{6,7},{7,6},{8,9},{9,8},{10,11... | collective-permute-start | bytes 5431304 | tf_op jit(solution)/shard_map/ppermute | solution.py:556
  519.3 28.4 %collective-permute-start.47 = (bf16[512,1536]{1,0:T(8,128)(2,1)}, bf16[512,1536]{1,0:T(8,128)(2,1)}, u32[]{:S(2)}, u32[]{:S(2)}) collective-permute-start(bf16[512,1536]{1,0:T(8,128)(2,1)} %get-tuple-element.171), channel_id=1, source_target_pairs={{0,1},{1,0},{2,3},{3,2},{4,5},{5,4},{6,7},{7,6},{8,9},{9,8},{10,11... | collective-permute-start | bytes 4718600 | tf_op jit(solution)/shard_map/ppermute | solution.py:556
  525.6 26.2 %collective-permute-start.46 = (bf16[512,1536]{1,0:T(8,128)(2,1)S(1)}, bf16[512,1536]{1,0:T(8,128)(2,1)}, u32[]{:S(2)}, u32[]{:S(2)}) collective-permute-start(bf16[512,1536]{1,0:T(8,128)(2,1)S(1)} %copy-done.41), channel_id=1, source_target_pairs={{0,1},{1,0},{2,3},{3,2},{4,5},{5,4},{6,7},{7,6},{8,9},{9,8},{10,11... | collective-permute-start | bytes 4718600 | tf_op jit(solution)/shard_map/ppermute | solution.py:556
  526.2 28.2 %collective-permute-start.50 = (bf16[512,1536]{1,0:T(8,128)(2,1)}, bf16[512,1536]{1,0:T(8,128)(2,1)}, u32[]{:S(2)}, u32[]{:S(2)}) collective-permute-start(bf16[512,1536]{1,0:T(8,128)(2,1)} %get-tuple-element.173), channel_id=1, source_target_pairs={{0,1},{1,0},{2,3},{3,2},{4,5},{5,4},{6,7},{7,6},{8,9},{9,8},{10,11... | collective-permute-start | bytes 4718600 | tf_op jit(solution)/shard_map/ppermute | solution.py:556
  526.3 162.6 %collective-permute-start.45 = (bf16[512,1536]{1,0:T(8,128)(2,1)}, bf16[512,1536]{1,0:T(8,128)(2,1)}, u32[]{:S(2)}, u32[]{:S(2)}) collective-permute-start(bf16[512,1536]{1,0:T(8,128)(2,1)} %get-tuple-element.167), channel_id=1, source_target_pairs={{0,1},{1,0},{2,3},{3,2},{4,5},{5,4},{6,7},{7,6},{8,9},{9,8},{10,11... | collective-permute-start | bytes 4718600 | tf_op jit(solution)/shard_map/ppermute | solution.py:556
  551.3 46.2 %collective-permute-start.48 = (bf16[256,1536]{1,0:T(8,128)(2,1)}, bf16[256,1536]{1,0:T(8,128)(2,1)}, u32[]{:S(2)}, u32[]{:S(2)}) collective-permute-start(bf16[256,1536]{1,0:T(8,128)(2,1)} %get-tuple-element.255), channel_id=1, source_target_pairs={{0,4},{1,5},{2,6},{3,7},{4,0},{5,1},{6,2},{7,3},{8,12},{9,13},{10,... | collective-permute-start | bytes 2359304 | tf_op jit(solution)/shard_map/ppermute | solution.py:556
  595.2 28.5 %collective-permute-start.55 = (bf16[512,1024]{1,0:T(8,128)(2,1)}, bf16[512,1024]{1,0:T(8,128)(2,1)S(1)}, u32[]{:S(2)}, u32[]{:S(2)}) collective-permute-start(bf16[512,1024]{1,0:T(8,128)(2,1)} %slice.317), channel_id=1, source_target_pairs={{8,0},{16,8},{24,16},{9,1},{17,9},{25,17},{10,2},{18,10},{26,18},{... | collective-permute-start | bytes 3145736 | tf_op jit(solution)/shard_map/ppermute | solution.py:1151
  596.5 20.7 %collective-permute-start.51 = (bf16[256,1536]{1,0:T(8,128)(2,1)}, bf16[256,1536]{1,0:T(8,128)(2,1)S(1)}, u32[]{:S(2)}, u32[]{:S(2)}) collective-permute-start(bf16[256,1536]{1,0:T(8,128)(2,1)} %get-tuple-element.256), channel_id=1, source_target_pairs={{0,2},{1,3},{2,0},{3,1},{4,6},{5,7},{6,4},{7,5},{8,10},{9,11},{10,... | collective-permute-start | bytes 2359304 | tf_op jit(solution)/shard_map/ppermute | solution.py:556
  599.0 89.9 %collective-permute-start.49 = (bf16[512,1536]{1,0:T(8,128)(2,1)S(1)}, bf16[512,1536]{1,0:T(8,128)(2,1)}, u32[]{:S(2)}, u32[]{:S(2)}) collective-permute-start(bf16[512,1536]{1,0:T(8,128)(2,1)S(1)} %pad_maximum_fusion.3.refs_1_), channel_id=1, source_target_pairs={{0,2},{1,3},{2,0},{3,1},{4,6},{5,7},{6,4},{7,5},{8,10},{9,11},{10,... | collective-permute-start | bytes 4718600 | tf_op jit(solution)/shard_map/ppermute | solution.py:556
  618.6 70.3 %collective-permute-start.52 = (bf16[512,1536]{1,0:T(8,128)(2,1)}, bf16[512,1536]{1,0:T(8,128)(2,1)}, u32[]{:S(2)}, u32[]{:S(2)}) collective-permute-start(bf16[512,1536]{1,0:T(8,128)(2,1)} %pad_maximum_fusion.4.refs_2_), channel_id=1, source_target_pairs={{0,4},{1,5},{2,6},{3,7},{4,0},{5,1},{6,2},{7,3},{8,12},{9,13},{10,... | collective-permute-start | bytes 4718600 | tf_op jit(solution)/shard_map/ppermute | solution.py:556
  631.1 27.4 %collective-permute-start.56 = (bf16[512,1024]{1,0:T(8,128)(2,1)}, bf16[512,1024]{1,0:T(8,128)(2,1)}, u32[]{:S(2)}, u32[]{:S(2)}) collective-permute-start(bf16[512,1024]{1,0:T(8,128)(2,1)} %tie.30), channel_id=1, source_target_pairs={{8,0},{16,8},{24,16},{9,1},{17,9},{25,17},{10,2},{18,10},{26,18},{... | collective-permute-start | bytes 3145736 | tf_op jit(solution)/shard_map/ppermute | solution.py:1151
  675.8 23.0 %all-to-all-start.1 = ((bf16[32,80,128]{2,1,0:T(8,128)(2,1)}), bf16[32,80,128]{2,1,0:T(8,128)(2,1)}, u32[]{:S(2)}, u32[]{:S(2)}) async-start(bf16[32,80,128]{2,1,0:T(8,128)(2,1)} %pad_maximum_fusion.10), calls=%async_computation.2 | async-start | bytes 1310720 | tf_op jit(solution)/shard_map/all_to_all | solution.py:1185
  (125 other events, 901.2 us)
Sparse Core Ops, SparseCore 0:
  40.1 34.0 all-gather.11
  75.7 64.7 all-gather.13
  171.8 88.3 all-gather.17
  261.6 76.8 all-gather.15
  340.5 49.0 all-gather.19
  391.7 35.5 reduce-scatter.2
  525.7 37.4 reduce-scatter.4

commit v9 on v8

--- a/solution.py
+++ b/solution.py
@@ -307,11 +307,11 @@
         for i in (0, 1):
             for copy in incoming(0, i, (0,)):
                 copy.start()
+        for copy in weight_copies():
+            copy.start()
         for i in (0, 1):
             for copy in incoming(0, i, (1,)):
                 copy.start()
-        for copy in weight_copies():
-            copy.start()
         for i in (0, 1):
             for copy in incoming(0, i, (2,)):
                 copy.start()
@@ -346,24 +346,31 @@
         places.append(place)
         adapters.append(adapter)
         selects.append(jnp.broadcast_to(select, (capacity, LANES)))
+    inputs = jnp.concatenate(inputs, axis=0)
+    gate = jnp.concatenate(gates_of, axis=0)
+    select = jnp.concatenate(selects, axis=0)
+    select_two = jnp.concatenate([select, select], axis=1)
+
+    @pl.when(step == 0)
+    def _():
+        weight_copies()[0].wait()
+
+    low = (dot_nn(inputs, up_ref[:, 2 * hidden : 2 * hidden + 2 * LANES]) * select_two).astype(BF16)
+    gate_part = dot_nn(inputs, up_ref[:, :hidden])
+    up_part = dot_nn(inputs, up_ref[:, hidden : 2 * hidden])
+
+    @pl.when(step == 0)
+    def _():
+        for copy in weight_copies()[1:]:
+            copy.wait()
+
     for i in (0, 1):
         wait_in(i, 1)
         grad_rows.append(dot_nn(picks[i], grad_buf[slot, i]))
     at_step(turn)
-    inputs = jnp.concatenate(inputs, axis=0)
     grad_rows = jnp.concatenate(grad_rows, axis=0)
-    gate = jnp.concatenate(gates_of, axis=0)
-    select = jnp.concatenate(selects, axis=0)
-    select_two = jnp.concatenate([select, select], axis=1)
-
-    @pl.when(step == 0)
-    def _():
-        for copy in weight_copies():
-            copy.wait()
-
-    low = (dot_nn(inputs, up_ref[:, 2 * hidden : 2 * hidden + 2 * LANES]) * select_two).astype(BF16)
-    gate_part = dot_nn(inputs, up_ref[:, :hidden]) + dot_nn(low[:, :LANES], second_ref[:, :hidden])
-    up_part = dot_nn(inputs, up_ref[:, hidden : 2 * hidden]) + dot_nn(low[:, LANES:], second_ref[:, hidden : 2 * hidden])
+    gate_part = gate_part + dot_nn(low[:, :LANES], second_ref[:, :hidden])
+    up_part = up_part + dot_nn(low[:, LANES:], second_ref[:, hidden : 2 * hidden])
     sigmoid = 1.0 / (1.0 + jnp.exp(-gate_part))
     silu = gate_part * sigmoid
     act = (silu * up_part).astype(BF16)

time: 722 us -> 723 us (level)
  no operation moved by 1% of the time
where the time goes in v9:
time: 723 us; the launch traced here: 712 us
  Pallas kernels  318 us (44%)
  waiting for transfers between devices  130 us (18%)
  local copies, waits for them, and re-layouts  91.5 us (13%)
  starting transfers between devices  53.8 us (7%)
  other arithmetic  50.7 us (7%)
  matrix products  31.7 us (4%)
  blocking collectives  20.3 us (3%)
  between operations  17 us (2%)
    pallas_call x8, Pallas kernels, expert_call(): pl.pallas_call(functools.partial(expert_kernel, *(count, splits, experts,...  199 us
    ppermute x53, waiting for transfers between devices, swap(): return lax.ppermute(array, 'dp', [(i, i ^ bit) for i in range(size)])  84.3 us
    pallas_call x1, Pallas kernels, attend_back(): pl.pallas_call(functools.partial(attend_back_kernel, spans, hops * rows,...  33.6 us
    unnamed x222, local copies, waits for them, and re-layouts  33.4 us
    ppermute x53, starting transfers between devices, swap(): return lax.ppermute(array, 'dp', [(i, i ^ bit) for i in range(size)])  33.3 us
    pallas_call x1, Pallas kernels, attend(): pl.pallas_call(functools.partial(attend_kernel, spans, hops * rows, len(d...  23.7 us
    dot_general x10, matrix products, dot_nn(): return jnp.dot(left, right, preferred_element_type=F32)  23.1 us
    all_gather x1, blocking collectives, over_seq(): return lax.all_gather(shard, 'seq', axis=0)  20.3 us
  transfers between devices with their start and end apart: 66, of which 19 were waited for; matrix products, arithmetic and copies ran while one was open for 21% of the time, Pallas kernels for 44%

profile of v9, /device:TPU:0, one launch (start us, length us, event | category | flops | bytes accessed | tf_op | source)
XLA Modules:
  0.0 712.2 jit_solution(7374015381704804388)
XLA Ops:
  7.2 3.0 collective-permute-start
  15.1 3.4 all-to-all-start
  19.6 20.3 %all-gather = bf16[192,2048]{1,0:T(8,128)(2,1)} all-gather(bf16[48,2048]{1,0:T(8,128)(2,1)S(1)} %fusion.20), channel_id=2, replica_groups=mesh['seq'=4,'dp'=8] {'seq'}, dimensions={0}, use_global_device_ids=true | all-gather | bytes 983040 | tf_op jit(solution)/shard_map/all_gather | solution.py:897
  43.1 5.2 all-to-all-done.refs_3_
  51.2 17.2 %collective-permute-done.3.refs_2_ = bf16[4,48,2048]{2,1,0:T(8,128)(2,1)S(1)} collective-permute-done((bf16[4,48,2048]{2,1,0:T(8,128)(2,1)}, bf16[4,48,2048]{2,1,0:T(8,128)(2,1)S(1)}, u32[]{:S(2)}, u32[]{:S(2)}) %collective-permute-start.3) | collective-permute-done | bytes 786464 | tf_op jit(solution)/shard_map/ppermute | solution.py:563
  76.2 3.0 collective-permute-done.8.refs_7_.refs_3_
  79.2 3.2 collective-permute-done.7.refs_6_.refs_2_
  88.9 5.6 assemble.2
  101.4 6.5 collective-permute-done.11.refs_1_.refs_8_.refs_7_
  110.0 4.0 fusion.5
  116.0 3.5 collective-permute-start.22
  120.5 2.5 fusion.49
  128.0 12.3 %collective-permute-done.16.refs_4_.refs_2_ = bf16[4,48,3584]{2,1,0:T(8,128)(2,1)} collective-permute-done((bf16[4,48,3584]{2,1,0:T(8,128)(2,1)}, bf16[4,48,3584]{2,1,0:T(8,128)(2,1)}, u32[]{:S(2)}, u32[]{:S(2)}) %collective-permute-start.16) | collective-permute-done | bytes 1376288 | tf_op jit(solution)/shard_map/ppermute | solution.py:563
  145.0 8.1 %collective-permute-done.22.refs_0_ = bf16[528,1024]{1,0:T(8,128)(2,1)S(1)} collective-permute-done((bf16[528,1024]{1,0:T(8,128)(2,1)}, bf16[528,1024]{1,0:T(8,128)(2,1)S(1)}, u32[]{:S(2)}, u32[]{:S(2)}) %collective-permute-start.22) | collective-permute-done | bytes 1081376 | tf_op jit(solution)/shard_map/ppermute | solution.py:1002
  154.1 5.3 collective-permute-start.23
  159.3 3.4 constant_dynamic-slice_fusion.10
  172.4 12.1 %collective-permute-done.23 = bf16[528,1024]{1,0:T(8,128)(2,1)} collective-permute-done((bf16[528,1024]{1,0:T(8,128)(2,1)}, bf16[528,1024]{1,0:T(8,128)(2,1)}, u32[]{:S(2)}, u32[]{:S(2)}) %collective-permute-start.23) | collective-permute-done | bytes 1081376 | tf_op jit(solution)/shard_map/ppermute | solution.py:1002
  192.4 8.4 %assemble.3 = (bf16[4,8,1,48,1536]{4,3,2,1,0:T(8,128)(2,1)}, bf16[4,8,1,48,512]{4,3,2,1,0:T(8,128)(2,1)}, bf16[4,8,1,48,1536]{4,3,2,1,0:T(8,128)(2,1)}) custom-call(s32[1]{0:T(128)} %bitcast.1.me_ref, bf16[4,48,3584]{2,1,0:T(8,128)(2,1)} %tie.19.refs_0_, bf16[4,48,3584]{2,1,0:T(8,128)(2,1)} %collective-permute-done.13.refs_1_, ...), custom_call_target="tpu_custom_call" | custom-call | tf_op jit(solution)/shard_map/assemble/pallas_call | solution.py:636
  204.3 3.9 fusion.4.q_ref
  208.1 23.7 %attend.1 = (bf16[512,1536]{1,0:T(8,128)(2,1)}, f32[4,3,512]{2,1,0:T(4,128)}) custom-call(bf16[512,1536]{1,0:T(8,128)(2,1)} %fusion.4.q_ref, bf16[1536,1024]{1,0:T(8,128)(2,1)} %pad_maximum_fusion.k_ref.v_ref, bf16[1536,1024]{1,0:T(8,128)(2,1)} %pad_maximum_fusion.k_ref.v_ref, f32[1,512]{1,0:T(1,128)} %get-tuple-element.283.qt_ref, ...), custom_call_target="tpu_custom_call" | custom-call | flops 26530500608 | bytes 1000000 | tf_op jit(solution)/shard_map/attend/pallas_call | solution.py:96
  235.6 4.8 multiply_reduce_fusion
  257.4 2.8 all-gather.18.cloned.1.call-done.refs_1_
  260.2 26.1 %expert.8 = (bf16[512,1536]{1,0:T(8,128)(2,1)}, bf16[512,1536]{1,0:T(8,128)(2,1)}, bf16[544,1664]{1,0:T(8,128)(2,1)}, bf16[544,1664]{1,0:T(8,128)(2,1)}, f32[153...) custom-call(s32[2]{0:T(128)} %pad_add_fusion.1.refs_0_, ...), custom_call_target="tpu_custom_call" | custom-call | flops 27683999744 | bytes 1000000 | tf_op jit(solution)/shard_map/expert/pallas_call | solution.py:529
  286.3 7.6 %collective-permute-done.30.refs_0_ = bf16[512,1664]{1,0:T(8,128)(2,1)S(1)} collective-permute-done((bf16[512,1664]{1,0:T(8,128)(2,1)}, bf16[512,1664]{1,0:T(8,128)(2,1)S(1)}, u32[]{:S(2)}, u32[]{:S(2)}) %collective-permute-start.30) | collective-permute-done | bytes 1703968 | tf_op jit(solution)/shard_map/ppermute | solution.py:563
  303.6 27.2 %expert.9 = (bf16[512,1536]{1,0:T(8,128)(2,1)}, bf16[512,1536]{1,0:T(8,128)(2,1)}, bf16[544,1664]{1,0:T(8,128)(2,1)}, bf16[544,1664]{1,0:T(8,128)(2,1)}, f32[153...) custom-call(s32[2]{0:T(128)} %pad_add_fusion.1.refs_0_, ...), custom_call_target="tpu_custom_call" | custom-call | flops 27683999744 | bytes 1000000 | tf_op jit(solution)/shard_map/expert/pallas_call | solution.py:529
  332.6 27.4 %expert.10 = (bf16[512,1536]{1,0:T(8,128)(2,1)}, bf16[512,1536]{1,0:T(8,128)(2,1)}, bf16[544,1664]{1,0:T(8,128)(2,1)}, bf16[544,1664]{1,0:T(8,128)(2,1)}, f32[15...) custom-call(s32[2]{0:T(128)} %pad_add_fusion.1.refs_0_, ...), custom_call_target="tpu_custom_call" | custom-call | flops 27683999744 | bytes 1000000 | tf_op jit(solution)/shard_map/expert/pallas_call | solution.py:529
  361.2 27.5 %expert.11 = (bf16[512,1536]{1,0:T(8,128)(2,1)}, bf16[512,1536]{1,0:T(8,128)(2,1)}, bf16[544,1664]{1,0:T(8,128)(2,1)}, bf16[544,1664]{1,0:T(8,128)(2,1)}, bf16[4,1568,128]{2,1,0:T(8,128)(2,1)}) custom-call(s32[2]{0:T(128)} %pad_add_fusion.1.refs_0_, bf16[1536,1536]{1,0:T(8,128)(2,1)} %all-gather.18.cloned.1.call-done.refs_1_, ...), custom_call_target="tpu_custom_call" | custom-call | flops 27683999744 | bytes 1000000 | tf_op jit(solution)/shard_map/expert/pallas_call | solution.py:529
  389.6 21.5 %expert.12 = (bf16[512,1536]{1,0:T(8,128)(2,1)}, bf16[512,1536]{1,0:T(8,128)(2,1)}, bf16[544,1664]{1,0:T(8,128)(2,1)}, bf16[544,1664]{1,0:T(8,128)(2,1)}, f32[15...) custom-call(s32[2]{0:T(128)} %pad_add_fusion.refs_0_, ...), custom_call_target="tpu_custom_call" | custom-call | flops 27683999744 | bytes 1000000 | tf_op jit(solution)/shard_map/expert/pallas_call | solution.py:529
  411.2 22.7 %expert.13 = (bf16[512,1536]{1,0:T(8,128)(2,1)}, bf16[512,1536]{1,0:T(8,128)(2,1)}, bf16[544,1664]{1,0:T(8,128)(2,1)}, bf16[544,1664]{1,0:T(8,128)(2,1)}, f32[15...) custom-call(s32[2]{0:T(128)} %pad_add_fusion.refs_0_, ...), custom_call_target="tpu_custom_call" | custom-call | flops 27683999744 | bytes 1000000 | tf_op jit(solution)/shard_map/expert/pallas_call | solution.py:529
  434.4 2.5 add_convert_fusion.2.refs_15_
  441.7 22.7 %expert.14 = (bf16[512,1536]{1,0:T(8,128)(2,1)}, bf16[512,1536]{1,0:T(8,128)(2,1)}, bf16[544,1664]{1,0:T(8,128)(2,1)}, bf16[544,1664]{1,0:T(8,128)(2,1)}, f32[15...) custom-call(s32[2]{0:T(128)} %pad_add_fusion.refs_0_, ...), custom_call_target="tpu_custom_call" | custom-call | flops 27683999744 | bytes 1000000 | tf_op jit(solution)/shard_map/expert/pallas_call | solution.py:529
  478.5 23.6 %expert.15 = (bf16[512,1536]{1,0:T(8,128)(2,1)}, bf16[512,1536]{1,0:T(8,128)(2,1)}, bf16[544,1664]{1,0:T(8,128)(2,1)}, bf16[544,1664]{1,0:T(8,128)(2,1)}, bf16[4,1536,128]{2,1,0:T(8,128)(2,1)}) custom-call(s32[2]{0:T(128)} %pad_add_fusion.refs_0_, bf16[1536,1280]{1,0:T(8,128)(2,1)} %all-gather.16.cloned.1.call-done.refs_1_, bf16[4,128,2304]{2,1,0:T(8,128)(2,1)} %bitcast.239, ...), custom_call_target="tpu_custom_call" | custom-call | flops 27683999744 | bytes 1000000 | tf_op jit(solution)/shard_map/expert/pallas_call | solution.py:529
  504.7 9.6 %collective-permute-done.43.refs_4_.refs_1_.from_x = bf16[544,1664]{1,0:T(8,128)(2,1)S(1)} collective-permute-done((bf16[544,1664]{1,0:T(8,128)(2,1)}, bf16[544,1664]{1,0:T(8,128)(2,1)S(1)}, u32[]{:S(2)}, u32[]{:S(2)}) %collective-permute-start.43) | collective-permute-done | bytes 1810464 | tf_op jit(solution)/shard_map/ppermute | solution.py:563
  514.3 5.7 collective-permute-done.44.refs_5_.refs_2_.from_y
  528.0 18.3 %turn.1 = (f32[512,1536]{1,0:T(8,128)}, bf16[512,1536]{1,0:T(8,128)(2,1)}, bf16[512,16]{1,0:T(8,128)(2,1)}, bf16[512,32]{1,0:T(8,128)(2,1)}, bf16[512,16]{1,0:T(...) custom-call(bf16[544,1664]{1,0:T(8,128)(2,1)} %get-tuple-element.174.own, ...), custom_call_target="tpu_custom_call" | custom-call | flops 4614000128 | bytes 1000000 | tf_op jit(solution)/shard_map/turn/pallas_call | solution.py:701
  560.1 33.6 %attend_back.1 = (bf16[512,1536]{1,0:T(8,128)(2,1)}, bf16[1536,1024]{1,0:T(8,128)(2,1)}) custom-call(bf16[512,1536]{1,0:T(8,128)(2,1)} %fusion.4.q_ref, bf16[1536,1024]{1,0:T(8,128)(2,1)} %pad_maximum_fusion.k_ref.v_ref, bf16[1536,1024]{1,0:T(8,128)(2,1)} %pad_maximum_fusion.k_ref.v_ref, bf16[512,1536]{1,0:T(8,128)(2,1)} %get-tuple-element.177.g_ref, ...), custom_call_target="tpu_custom_call" | custom-call | flops 9228000256 | bytes 1000000 | tf_op jit(solution)/shard_map/attend_back/pallas_call | solution.py:159
  593.7 2.4 slice.317
  601.1 17.0 %collective-permute-done.51 = bf16[256,1536]{1,0:T(8,128)(2,1)S(1)} collective-permute-done((bf16[256,1536]{1,0:T(8,128)(2,1)}, bf16[256,1536]{1,0:T(8,128)(2,1)S(1)}, u32[]{:S(2)}, u32[]{:S(2)}) %collective-permute-start.51) | collective-permute-done | bytes 786464 | tf_op jit(solution)/shard_map/ppermute | solution.py:563
  620.3 4.1 collective-permute-done.55.rest_0_.refs_2_
  629.1 2.6 add_convert_fusion.9.refs_0_
  633.3 5.2 middle.1
  642.8 9.7 %query_back.1 = (f32[512,1536]{1,0:T(8,128)}, f32[1536,16]{1,0:T(8,128)}, f32[16,1536]{1,0:T(8,128)}) custom-call(bf16[512,1536]{1,0:T(8,128)(2,1)} %get-tuple-element.181.grad_q, bf16[512,1536]{1,0:T(8,128)(2,1)} %copy-done.9, bf16[512,16]{1,0:T(8,128)(2,1)} %constant_dynamic-slice_fusion.2.low_q, bf16[1536,1536]{1,0:T(8,128)(2,1)} %bitcast.189, ...), custom_call_target="tpu_custom_call" | custom-call | flops 115350000 | bytes 1000000 | tf_op jit(solution)/shard_map/query_back/pallas_call | solution.py:724
  652.6 6.7 collective-permute-done.56
  659.3 2.9 add_convert_fusion.8.grad_kv
  662.2 12.1 %last.1 = (f32[512,1536]{1,0:T(8,128)}, bf16[1536,128]{1,0:T(8,128)(2,1)}, bf16[32,32,128]{2,1,0:T(8,128)(2,1)}) custom-call(bf16[512,1024]{1,0:T(8,128)(2,1)} %add_convert_fusion.8.grad_kv, bf16[512,1536]{1,0:T(8,128)(2,1)} %copy-done.9, bf16[512,32]{1,0:T(8,128)(2,1)} %pad_maximum_fusion.16.low_kv, bf16[1536,1024]{1,0:T(8,128)(2,1)} %bitcast.198, ...), custom_call_target="tpu_custom_call" | custom-call | flops 2307000064 | bytes 1000000 | tf_op jit(solution)/shard_map/last/pallas_call | solution.py:795
  676.3 5.0 all-to-all-start.1
  689.4 4.6 fusion.7
  694.0 5.2 all-to-all-done.1.flat
  (495 shorter events, 179.4 us)
Async XLA Ops:
  7.2 41.2 %collective-permute-start = (bf16[512,1536]{1,0:T(8,128)(2,1)}, bf16[512,1536]{1,0:T(8,128)(2,1)}, u32[]{:S(2)}, u32[]{:S(2)}) collective-permute-start(bf16[512,1536]{1,0:T(8,128)(2,1)} %bitcast.168), channel_id=1, source_target_pairs={{0,2},{1,3},{2,0},{3,1},{4,6},{5,7},{6,4},{7,5},{8,10},{9,11},{10,... | collective-permute-start | bytes 4718600 | tf_op jit(solution)/shard_map/ppermute | solution.py:563
  10.2 38.2 %collective-permute-start.1 = (bf16[512,1536]{1,0:T(8,128)(2,1)}, bf16[512,1536]{1,0:T(8,128)(2,1)}, u32[]{:S(2)}, u32[]{:S(2)}) collective-permute-start(bf16[512,1536]{1,0:T(8,128)(2,1)} %bitcast.169), channel_id=1, source_target_pairs={{0,4},{1,5},{2,6},{3,7},{4,0},{5,1},{6,2},{7,3},{8,12},{9,13},{10,... | collective-permute-start | bytes 4718600 | tf_op jit(solution)/shard_map/ppermute | solution.py:563
  15.1 33.3 %all-to-all-start = ((bf16[8,48,256]{2,1,0:T(8,128)(2,1)}), bf16[8,48,256]{2,1,0:T(8,128)(2,1)S(1)}, u32[]{:S(2)}, u32[]{:S(2)}) async-start(bf16[8,48,256]{2,1,0:T(8,128)(2,1)} %copy.182), calls=%async_computation | async-start | bytes 393216 | tf_op jit(solution)/shard_map/all_to_all | solution.py:940
  18.5 82.9 %all-gather.12.cloned.1.call-start = ((), (), s32[]{:S(2)}) async-start(), calls=%async_computation.6 | async-start | bytes 1720320 | tf_op jit(solution)/shard_map/all_gather | solution.py:897
  40.0 113.1 %all-gather.14.cloned.1.call-start = ((), (), s32[]{:S(2)}) async-start(), calls=%async_computation.7 | async-start | bytes 3604480 | tf_op jit(solution)/shard_map/all_gather | solution.py:897
  50.1 20.7 %collective-permute-start.5 = (bf16[4,48,2048]{2,1,0:T(8,128)(2,1)}, bf16[4,48,2048]{2,1,0:T(8,128)(2,1)S(1)}, u32[]{:S(2)}, u32[]{:S(2)}) collective-permute-start(bf16[4,48,2048]{2,1,0:T(8,128)(2,1)} %tie.16.refs_0_), channel_id=1, source_target_pairs={{0,4},{1,5},{2,6},{3,7},{4,0},{5,1},{6,2},{7,3},{8,12},{9,13},{10,... | collective-permute-start | bytes 2359304 | tf_op jit(solution)/shard_map/ppermute | solution.py:563
  73.2 187.0 %all-gather.18.cloned.1.call-start = ((), (), s32[]{:S(2)}) async-start(), calls=%async_computation.9 | async-start | bytes 5898240 | tf_op jit(solution)/shard_map/all_gather | solution.py:897
  87.7 20.3 %collective-permute-start.11 = (bf16[256,1536]{1,0:T(8,128)(2,1)}, bf16[256,1536]{1,0:T(8,128)(2,1)}, u32[]{:S(2)}, u32[]{:S(2)}) collective-permute-start(bf16[256,1536]{1,0:T(8,128)(2,1)} %slice.266), channel_id=1, source_target_pairs={{0,2},{1,3},{2,0},{3,1},{4,6},{5,7},{6,4},{7,5},{8,10},{9,11},{10,... | collective-permute-start | bytes 2359304 | tf_op jit(solution)/shard_map/ppermute | solution.py:563
  88.5 20.0 %collective-permute-start.12 = (bf16[256,1536]{1,0:T(8,128)(2,1)}, bf16[256,1536]{1,0:T(8,128)(2,1)}, u32[]{:S(2)}, u32[]{:S(2)}) collective-permute-start(bf16[256,1536]{1,0:T(8,128)(2,1)} %slice.267), channel_id=1, source_target_pairs={{0,4},{1,5},{2,6},{3,7},{4,0},{5,1},{6,2},{7,3},{8,12},{9,13},{10,... | collective-permute-start | bytes 2359304 | tf_op jit(solution)/shard_map/ppermute | solution.py:563
  108.5 31.8 %collective-permute-start.16 = (bf16[4,48,3584]{2,1,0:T(8,128)(2,1)}, bf16[4,48,3584]{2,1,0:T(8,128)(2,1)}, u32[]{:S(2)}, u32[]{:S(2)}) collective-permute-start(bf16[4,48,3584]{2,1,0:T(8,128)(2,1)} %tie.19.refs_0_), channel_id=1, source_target_pairs={{0,4},{1,5},{2,6},{3,7},{4,0},{5,1},{6,2},{7,3},{8,12},{9,13},{10,... | collective-permute-start | bytes 4128776 | tf_op jit(solution)/shard_map/ppermute | solution.py:563
  108.9 33.8 %collective-permute-start.14 = (bf16[4,48,3584]{2,1,0:T(8,128)(2,1)}, bf16[4,48,3584]{2,1,0:T(8,128)(2,1)}, u32[]{:S(2)}, u32[]{:S(2)}) collective-permute-start(bf16[4,48,3584]{2,1,0:T(8,128)(2,1)} %tie.19.refs_0_), channel_id=1, source_target_pairs={{0,2},{1,3},{2,0},{3,1},{4,6},{5,7},{6,4},{7,5},{8,10},{9,11},{10,... | collective-permute-start | bytes 4128776 | tf_op jit(solution)/shard_map/ppermute | solution.py:563
  116.0 37.1 %collective-permute-start.22 = (bf16[528,1024]{1,0:T(8,128)(2,1)}, bf16[528,1024]{1,0:T(8,128)(2,1)S(1)}, u32[]{:S(2)}, u32[]{:S(2)}) collective-permute-start(bf16[528,1024]{1,0:T(8,128)(2,1)} %pad_maximum_fusion.6), channel_id=1, source_target_pairs={{0,8},{8,16},{16,24},{1,9},{9,17},{17,25},{2,10},{10,18},{18,26},{... | collective-permute-start | bytes 3244040 | tf_op jit(solution)/shard_map/ppermute | solution.py:1002
  141.5 21.8 %collective-permute-start.18 = (bf16[2,48,3584]{2,1,0:T(8,128)(2,1)S(1)}, bf16[2,48,3584]{2,1,0:T(8,128)(2,1)}, u32[]{:S(2)}, u32[]{:S(2)}) collective-permute-start(bf16[2,48,3584]{2,1,0:T(8,128)(2,1)S(1)} %slice.344), channel_id=1, source_target_pairs={{0,2},{1,3},{2,0},{3,1},{4,6},{5,7},{6,4},{7,5},{8,10},{9,11},{10,... | collective-permute-start | bytes 2064392 | tf_op jit(solution)/shard_map/ppermute | solution.py:563
  144.7 21.4 %collective-permute-start.19 = (bf16[2,48,3584]{2,1,0:T(8,128)(2,1)}, bf16[2,48,3584]{2,1,0:T(8,128)(2,1)}, u32[]{:S(2)}, u32[]{:S(2)}) collective-permute-start(bf16[2,48,3584]{2,1,0:T(8,128)(2,1)} %slice.345), channel_id=1, source_target_pairs={{0,4},{1,5},{2,6},{3,7},{4,0},{5,1},{6,2},{7,3},{8,12},{9,13},{10,... | collective-permute-start | bytes 2064392 | tf_op jit(solution)/shard_map/ppermute | solution.py:563
  154.1 30.4 %collective-permute-start.23 = (bf16[528,1024]{1,0:T(8,128)(2,1)}, bf16[528,1024]{1,0:T(8,128)(2,1)}, u32[]{:S(2)}, u32[]{:S(2)}) collective-permute-start(bf16[528,1024]{1,0:T(8,128)(2,1)} %tie.21.refs_1_), channel_id=1, source_target_pairs={{0,8},{8,16},{16,24},{1,9},{9,17},{17,25},{2,10},{10,18},{18,26},{... | collective-permute-start | bytes 3244040 | tf_op jit(solution)/shard_map/ppermute | solution.py:1002
  162.8 26.3 %collective-permute-start.13 = (bf16[4,48,3584]{2,1,0:T(8,128)(2,1)}, bf16[4,48,3584]{2,1,0:T(8,128)(2,1)}, u32[]{:S(2)}, u32[]{:S(2)}) collective-permute-start(bf16[4,48,3584]{2,1,0:T(8,128)(2,1)} %tie.19.refs_0_), channel_id=1, source_target_pairs={{0,1},{1,0},{2,3},{3,2},{4,5},{5,4},{6,7},{7,6},{8,9},{9,8},{10,11... | collective-permute-start | bytes 4128776 | tf_op jit(solution)/shard_map/ppermute | solution.py:563
  162.8 29.5 %collective-permute-start.15 = (bf16[4,48,3584]{2,1,0:T(8,128)(2,1)}, bf16[4,48,3584]{2,1,0:T(8,128)(2,1)}, u32[]{:S(2)}, u32[]{:S(2)}) collective-permute-start(bf16[4,48,3584]{2,1,0:T(8,128)(2,1)} %collective-permute-done.14.refs_2_.refs_1_), channel_id=1, source_target_pairs={{0,1},{1,0},{2,3},{3,2},{4,5},{5,4},{6,7},{7,6},{8,9},{9,8},{10,11... | collective-permute-start | bytes 4128776 | tf_op jit(solution)/shard_map/ppermute | solution.py:563
  163.3 29.1 %collective-permute-start.17 = (bf16[4,48,3584]{2,1,0:T(8,128)(2,1)}, bf16[4,48,3584]{2,1,0:T(8,128)(2,1)}, u32[]{:S(2)}, u32[]{:S(2)}) collective-permute-start(bf16[4,48,3584]{2,1,0:T(8,128)(2,1)} %collective-permute-done.16.refs_4_.refs_2_), channel_id=1, source_target_pairs={{0,1},{1,0},{2,3},{3,2},{4,5},{5,4},{6,7},{7,6},{8,9},{9,8},{10,11... | collective-permute-start | bytes 4128776 | tf_op jit(solution)/shard_map/ppermute | solution.py:563
  166.1 23.5 %collective-permute-start.20 = (bf16[2,48,3584]{2,1,0:T(8,128)(2,1)}, bf16[2,48,3584]{2,1,0:T(8,128)(2,1)}, u32[]{:S(2)}, u32[]{:S(2)}) collective-permute-start(bf16[2,48,3584]{2,1,0:T(8,128)(2,1)} %collective-permute-done.18.refs_6_), channel_id=1, source_target_pairs={{0,1},{1,0},{2,3},{3,2},{4,5},{5,4},{6,7},{7,6},{8,9},{9,8},{10,11... | collective-permute-start | bytes 2064392 | tf_op jit(solution)/shard_map/ppermute | solution.py:563
  171.7 217.0 %all-gather.16.cloned.1.call-start = ((), (), s32[]{:S(2)}) async-start(), calls=%async_computation.8 | async-start | bytes 4915200 | tf_op jit(solution)/shard_map/all_gather | solution.py:897
  250.3 139.2 %all-gather.20.cloned.1.call-start = ((), (), s32[]{:S(2)}) async-start(), calls=%async_computation.10 | async-start | bytes 2949120 | tf_op jit(solution)/shard_map/all_gather | solution.py:897
  254.2 39.7 %collective-permute-start.30 = (bf16[512,1664]{1,0:T(8,128)(2,1)}, bf16[512,1664]{1,0:T(8,128)(2,1)S(1)}, u32[]{:S(2)}, u32[]{:S(2)}) collective-permute-start(bf16[512,1664]{1,0:T(8,128)(2,1)} %concatenate.98.refs_4_.refs_3_), channel_id=1, source_target_pairs={{0,2},{1,3},{2,0},{3,1},{4,6},{5,7},{6,4},{7,5},{8,10},{9,11},{10,... | collective-permute-start | bytes 5111816 | tf_op jit(solution)/shard_map/ppermute | solution.py:563
  255.9 39.5 %collective-permute-start.31 = (bf16[512,1664]{1,0:T(8,128)(2,1)}, bf16[512,1664]{1,0:T(8,128)(2,1)}, u32[]{:S(2)}, u32[]{:S(2)}) collective-permute-start(bf16[512,1664]{1,0:T(8,128)(2,1)} %concatenate.98.refs_4_.refs_3_), channel_id=1, source_target_pairs={{0,4},{1,5},{2,6},{3,7},{4,0},{5,1},{6,2},{7,3},{8,12},{9,13},{10,... | collective-permute-start | bytes 5111816 | tf_op jit(solution)/shard_map/ppermute | solution.py:563
  297.3 35.2 %collective-permute-start.32 = (bf16[512,1664]{1,0:T(8,128)(2,1)}, bf16[512,1664]{1,0:T(8,128)(2,1)}, u32[]{:S(2)}, u32[]{:S(2)}) collective-permute-start(bf16[512,1664]{1,0:T(8,128)(2,1)} %get-tuple-element.118.refs_4_.refs_3_), channel_id=1, source_target_pairs={{0,1},{1,0},{2,3},{3,2},{4,5},{5,4},{6,7},{7,6},{8,9},{9,8},{10,11... | collective-permute-start | bytes 5111816 | tf_op jit(solution)/shard_map/ppermute | solution.py:563
  300.6 30.3 %collective-permute-start.34 = (bf16[256,1664]{1,0:T(8,128)(2,1)}, bf16[256,1664]{1,0:T(8,128)(2,1)S(1)}, u32[]{:S(2)}, u32[]{:S(2)}) collective-permute-start(bf16[256,1664]{1,0:T(8,128)(2,1)} %slice.299), channel_id=1, source_target_pairs={{0,2},{1,3},{2,0},{3,1},{4,6},{5,7},{6,4},{7,5},{8,10},{9,11},{10,... | collective-permute-start | bytes 2555912 | tf_op jit(solution)/shard_map/ppermute | solution.py:563
  302.0 28.9 %collective-permute-start.35 = (bf16[256,1664]{1,0:T(8,128)(2,1)}, bf16[256,1664]{1,0:T(8,128)(2,1)S(1)}, u32[]{:S(2)}, u32[]{:S(2)}) collective-permute-start(bf16[256,1664]{1,0:T(8,128)(2,1)} %slice.300), channel_id=1, source_target_pairs={{0,4},{1,5},{2,6},{3,7},{4,0},{5,1},{6,2},{7,3},{8,12},{9,13},{10,... | collective-permute-start | bytes 2555912 | tf_op jit(solution)/shard_map/ppermute | solution.py:563
  303.5 160.9 %reduce-scatter.3.cloned.1.call-start = ((), (), s32[]{:S(2)}) async-start(), calls=%async_computation.4 | async-start | bytes 2007040 | tf_op jit(solution)/shard_map/reduce_scatter | solution.py:1115
  332.1 27.9 %collective-permute-start.36 = (bf16[256,1664]{1,0:T(8,128)(2,1)}, bf16[256,1664]{1,0:T(8,128)(2,1)S(1)}, u32[]{:S(2)}, u32[]{:S(2)}) collective-permute-start(bf16[256,1664]{1,0:T(8,128)(2,1)} %get-tuple-element.136.refs_4_.refs_3_), channel_id=1, source_target_pairs={{0,1},{1,0},{2,3},{3,2},{4,5},{5,4},{6,7},{7,6},{8,9},{9,8},{10,11... | collective-permute-start | bytes 2555912 | tf_op jit(solution)/shard_map/ppermute | solution.py:563
  332.1 27.9 %collective-permute-start.37 = (bf16[256,1664]{1,0:T(8,128)(2,1)}, bf16[256,1664]{1,0:T(8,128)(2,1)S(1)}, u32[]{:S(2)}, u32[]{:S(2)}) collective-permute-start(bf16[256,1664]{1,0:T(8,128)(2,1)} %get-tuple-element.137.refs_5_.refs_4_), channel_id=1, source_target_pairs={{0,1},{1,0},{2,3},{3,2},{4,5},{5,4},{6,7},{7,6},{8,9},{9,8},{10,11... | collective-permute-start | bytes 2555912 | tf_op jit(solution)/shard_map/ppermute | solution.py:563
  388.7 231.6 %reduce-scatter.5.cloned.1.call-start = ((), (), s32[]{:S(2)}) async-start(), calls=%async_computation.5 | async-start | bytes 1966080 | tf_op jit(solution)/shard_map/reduce_scatter | solution.py:1115
  411.1 23.3 %collective-permute-start.38 = (bf16[544,1664]{1,0:T(8,128)(2,1)}, bf16[544,1664]{1,0:T(8,128)(2,1)}, u32[]{:S(2)}, u32[]{:S(2)}) collective-permute-start(bf16[544,1664]{1,0:T(8,128)(2,1)} %get-tuple-element.154), channel_id=1, source_target_pairs={{0,1},{1,0},{2,3},{3,2},{4,5},{5,4},{6,7},{7,6},{8,9},{9,8},{10,11... | collective-permute-start | bytes 5431304 | tf_op jit(solution)/shard_map/ppermute | solution.py:563
  433.9 33.7 %collective-permute-start.39 = (bf16[544,1664]{1,0:T(8,128)(2,1)}, bf16[544,1664]{1,0:T(8,128)(2,1)}, u32[]{:S(2)}, u32[]{:S(2)}) collective-permute-start(bf16[544,1664]{1,0:T(8,128)(2,1)} %get-tuple-element.158), channel_id=1, source_target_pairs={{0,1},{1,0},{2,3},{3,2},{4,5},{5,4},{6,7},{7,6},{8,9},{9,8},{10,11... | collective-permute-start | bytes 5431304 | tf_op jit(solution)/shard_map/ppermute | solution.py:563
  438.7 25.7 %collective-permute-start.40 = (bf16[272,1664]{1,0:T(8,128)(2,1)}, bf16[272,1664]{1,0:T(8,128)(2,1)S(1)}, u32[]{:S(2)}, u32[]{:S(2)}) collective-permute-start(bf16[272,1664]{1,0:T(8,128)(2,1)} %get-tuple-element.250), channel_id=1, source_target_pairs={{0,4},{1,5},{2,6},{3,7},{4,0},{5,1},{6,2},{7,3},{8,12},{9,13},{10,... | collective-permute-start | bytes 2715656 | tf_op jit(solution)/shard_map/ppermute | solution.py:563
  440.2 24.3 %collective-permute-start.41 = (bf16[272,1664]{1,0:T(8,128)(2,1)}, bf16[272,1664]{1,0:T(8,128)(2,1)S(1)}, u32[]{:S(2)}, u32[]{:S(2)}) collective-permute-start(bf16[272,1664]{1,0:T(8,128)(2,1)} %get-tuple-element.249), channel_id=1, source_target_pairs={{0,2},{1,3},{2,0},{3,1},{4,6},{5,7},{6,4},{7,5},{8,10},{9,11},{10,... | collective-permute-start | bytes 2715656 | tf_op jit(solution)/shard_map/ppermute | solution.py:563
  472.3 42.0 %collective-permute-start.43 = (bf16[544,1664]{1,0:T(8,128)(2,1)}, bf16[544,1664]{1,0:T(8,128)(2,1)S(1)}, u32[]{:S(2)}, u32[]{:S(2)}) collective-permute-start(bf16[544,1664]{1,0:T(8,128)(2,1)} %pad_maximum_fusion.1.refs_14_), channel_id=1, source_target_pairs={{0,2},{1,3},{2,0},{3,1},{4,6},{5,7},{6,4},{7,5},{8,10},{9,11},{10,... | collective-permute-start | bytes 5431304 | tf_op jit(solution)/shard_map/ppermute | solution.py:563
  477.9 42.1 %collective-permute-start.44 = (bf16[544,1664]{1,0:T(8,128)(2,1)}, bf16[544,1664]{1,0:T(8,128)(2,1)}, u32[]{:S(2)}, u32[]{:S(2)}) collective-permute-start(bf16[544,1664]{1,0:T(8,128)(2,1)} %pad_maximum_fusion.2.refs_15_), channel_id=1, source_target_pairs={{0,4},{1,5},{2,6},{3,7},{4,0},{5,1},{6,2},{7,3},{8,12},{9,13},{10,... | collective-permute-start | bytes 5431304 | tf_op jit(solution)/shard_map/ppermute | solution.py:563
  502.1 24.9 %collective-permute-start.53 = (bf16[544,1664]{1,0:T(8,128)(2,1)}, bf16[544,1664]{1,0:T(8,128)(2,1)}, u32[]{:S(2)}, u32[]{:S(2)}) collective-permute-start(bf16[544,1664]{1,0:T(8,128)(2,1)} %get-tuple-element.175), channel_id=1, source_target_pairs={{0,1},{1,0},{2,3},{3,2},{4,5},{5,4},{6,7},{7,6},{8,9},{9,8},{10,11... | collective-permute-start | bytes 5431304 | tf_op jit(solution)/shard_map/ppermute | solution.py:563
  520.0 28.4 %collective-permute-start.47 = (bf16[512,1536]{1,0:T(8,128)(2,1)}, bf16[512,1536]{1,0:T(8,128)(2,1)}, u32[]{:S(2)}, u32[]{:S(2)}) collective-permute-start(bf16[512,1536]{1,0:T(8,128)(2,1)} %get-tuple-element.171), channel_id=1, source_target_pairs={{0,1},{1,0},{2,3},{3,2},{4,5},{5,4},{6,7},{7,6},{8,9},{9,8},{10,11... | collective-permute-start | bytes 4718600 | tf_op jit(solution)/shard_map/ppermute | solution.py:563
  526.3 26.2 %collective-permute-start.46 = (bf16[512,1536]{1,0:T(8,128)(2,1)S(1)}, bf16[512,1536]{1,0:T(8,128)(2,1)}, u32[]{:S(2)}, u32[]{:S(2)}) collective-permute-start(bf16[512,1536]{1,0:T(8,128)(2,1)S(1)} %copy-done.41), channel_id=1, source_target_pairs={{0,1},{1,0},{2,3},{3,2},{4,5},{5,4},{6,7},{7,6},{8,9},{9,8},{10,11... | collective-permute-start | bytes 4718600 | tf_op jit(solution)/shard_map/ppermute | solution.py:563
  526.9 28.3 %collective-permute-start.50 = (bf16[512,1536]{1,0:T(8,128)(2,1)}, bf16[512,1536]{1,0:T(8,128)(2,1)}, u32[]{:S(2)}, u32[]{:S(2)}) collective-permute-start(bf16[512,1536]{1,0:T(8,128)(2,1)} %get-tuple-element.173), channel_id=1, source_target_pairs={{0,1},{1,0},{2,3},{3,2},{4,5},{5,4},{6,7},{7,6},{8,9},{9,8},{10,11... | collective-permute-start | bytes 4718600 | tf_op jit(solution)/shard_map/ppermute | solution.py:563
  527.0 162.4 %collective-permute-start.45 = (bf16[512,1536]{1,0:T(8,128)(2,1)}, bf16[512,1536]{1,0:T(8,128)(2,1)}, u32[]{:S(2)}, u32[]{:S(2)}) collective-permute-start(bf16[512,1536]{1,0:T(8,128)(2,1)} %get-tuple-element.167), channel_id=1, source_target_pairs={{0,1},{1,0},{2,3},{3,2},{4,5},{5,4},{6,7},{7,6},{8,9},{9,8},{10,11... | collective-permute-start | bytes 4718600 | tf_op jit(solution)/shard_map/ppermute | solution.py:563
  552.0 46.4 %collective-permute-start.48 = (bf16[256,1536]{1,0:T(8,128)(2,1)}, bf16[256,1536]{1,0:T(8,128)(2,1)}, u32[]{:S(2)}, u32[]{:S(2)}) collective-permute-start(bf16[256,1536]{1,0:T(8,128)(2,1)} %get-tuple-element.255), channel_id=1, source_target_pairs={{0,4},{1,5},{2,6},{3,7},{4,0},{5,1},{6,2},{7,3},{8,12},{9,13},{10,... | collective-permute-start | bytes 2359304 | tf_op jit(solution)/shard_map/ppermute | solution.py:563
  596.1 28.2 %collective-permute-start.55 = (bf16[512,1024]{1,0:T(8,128)(2,1)}, bf16[512,1024]{1,0:T(8,128)(2,1)S(1)}, u32[]{:S(2)}, u32[]{:S(2)}) collective-permute-start(bf16[512,1024]{1,0:T(8,128)(2,1)} %slice.317), channel_id=1, source_target_pairs={{8,0},{16,8},{24,16},{9,1},{17,9},{25,17},{10,2},{18,10},{26,18},{... | collective-permute-start | bytes 3145736 | tf_op jit(solution)/shard_map/ppermute | solution.py:1158
  597.4 20.7 %collective-permute-start.51 = (bf16[256,1536]{1,0:T(8,128)(2,1)}, bf16[256,1536]{1,0:T(8,128)(2,1)S(1)}, u32[]{:S(2)}, u32[]{:S(2)}) collective-permute-start(bf16[256,1536]{1,0:T(8,128)(2,1)} %get-tuple-element.256), channel_id=1, source_target_pairs={{0,2},{1,3},{2,0},{3,1},{4,6},{5,7},{6,4},{7,5},{8,10},{9,11},{10,... | collective-permute-start | bytes 2359304 | tf_op jit(solution)/shard_map/ppermute | solution.py:563
  600.0 89.4 %collective-permute-start.49 = (bf16[512,1536]{1,0:T(8,128)(2,1)S(1)}, bf16[512,1536]{1,0:T(8,128)(2,1)}, u32[]{:S(2)}, u32[]{:S(2)}) collective-permute-start(bf16[512,1536]{1,0:T(8,128)(2,1)S(1)} %pad_maximum_fusion.3.refs_1_), channel_id=1, source_target_pairs={{0,2},{1,3},{2,0},{3,1},{4,6},{5,7},{6,4},{7,5},{8,10},{9,11},{10,... | collective-permute-start | bytes 4718600 | tf_op jit(solution)/shard_map/ppermute | solution.py:563
  619.5 69.8 %collective-permute-start.52 = (bf16[512,1536]{1,0:T(8,128)(2,1)}, bf16[512,1536]{1,0:T(8,128)(2,1)}, u32[]{:S(2)}, u32[]{:S(2)}) collective-permute-start(bf16[512,1536]{1,0:T(8,128)(2,1)} %pad_maximum_fusion.4.refs_2_), channel_id=1, source_target_pairs={{0,4},{1,5},{2,6},{3,7},{4,0},{5,1},{6,2},{7,3},{8,12},{9,13},{10,... | collective-permute-start | bytes 4718600 | tf_op jit(solution)/shard_map/ppermute | solution.py:563
  631.8 27.5 %collective-permute-start.56 = (bf16[512,1024]{1,0:T(8,128)(2,1)}, bf16[512,1024]{1,0:T(8,128)(2,1)}, u32[]{:S(2)}, u32[]{:S(2)}) collective-permute-start(bf16[512,1024]{1,0:T(8,128)(2,1)} %tie.30), channel_id=1, source_target_pairs={{8,0},{16,8},{24,16},{9,1},{17,9},{25,17},{10,2},{18,10},{26,18},{... | collective-permute-start | bytes 3145736 | tf_op jit(solution)/shard_map/ppermute | solution.py:1158
  676.3 23.0 %all-to-all-start.1 = ((bf16[32,80,128]{2,1,0:T(8,128)(2,1)}), bf16[32,80,128]{2,1,0:T(8,128)(2,1)}, u32[]{:S(2)}, u32[]{:S(2)}) async-start(bf16[32,80,128]{2,1,0:T(8,128)(2,1)} %pad_maximum_fusion.10), calls=%async_computation.2 | async-start | bytes 1310720 | tf_op jit(solution)/shard_map/all_to_all | solution.py:1192
  (125 other events, 901.1 us)
Sparse Core Ops, SparseCore 0:
  40.1 34.0 all-gather.11
  75.7 64.7 all-gather.13
  171.8 88.3 all-gather.17
  261.6 76.8 all-gather.15
  340.5 49.0 all-gather.19
  391.7 35.3 reduce-scatter.2
  526.4 37.2 reduce-scatter.4
